TPU v7x, 32 devices: a whole 2x2x4 slice. The times are simulated.
32 devices in a mesh: groups: 2 (over y), samp: 4 (over z), head: 4 (over x, core).
Axes of the slice: x: 2, y: 2, z: 4, core: 2. Of those that a mesh axis runs over, the one named last changes fastest.
Arguments:
- prompt_states: bfloat16 [8, 1024, 5120], P(('groups', 'samp'), None, 'head'), parts along dimension 0, may hold values from -6 to 6
- prompt_lengths: int32 [8], P('groups'), parts along dimension 0, may hold values from 1 to 1024, 2048 in all
- prompt_owner: int32 [8], P('groups'), parts along dimension 0, may hold values from 0 to 3, each once
- kv_weight: bfloat16 [5120, 2048], P('head'), may hold values from -0.078125 to 0.078125
- sampler_prompts: int32 [16], P(('groups', 'samp')), parts along dimension 0, may hold values from 0 to 3, as said below
- step_queries: bfloat16 [4, 512, 5120], P(None, ('groups', 'samp'), 'head'), parts along dimension 1, may hold values from -8 to 8
- step_kv: bfloat16 [4, 512, 2048], P(None, ('groups', 'samp'), 'head'), parts along dimension 1, may hold values from -8 to 8
- out_weight: bfloat16 [5120, 5120], P('head', 'samp'), may hold values from -0.625 to 0.625
Outputs:
- mixed: bfloat16 [4, 512, 5120], P(None, ('groups', 'samp'), 'head'), parts along dimension 1
There are 2 independent parts, one for each index of `groups`. A program takes and returns all parts, laid end to end along the dimension named above; an argument that names none is the same for every part. Nothing has to cross between parts.
Inputs may be any that keep to these rules, and one draw needn't show every extreme that they name: prompt_owner is a permutation: each owner slot holds exactly one prompt. `sampler_prompts`: entries s * 2 to s * 2 + 1 are 2 different prompts, one for each of sampler s's aligned blocks of 32 rows in order; every prompt is listed by at least one sampler.
All inputs are finite; a program needn't handle non-finite values.
Results may differ from a plain program's by a relative error of at most 0.017.
Values may be sent and summed in bfloat16 or wider, within the bound.
No kernel may reach another device: no remote copies, remote signals or barrier semaphores. Data moves between devices by JAX's collectives and lax.ppermute only.
A program may use at most 128 MiB of HBM per device.

v0:
```python
import math

import jax
import jax.numpy as jnp
from jax import lax
from jax.sharding import PartitionSpec as P

HD = 128
GQA = 5


masked_score = -1e30


def prompt_partial(queries, page_block, length):
    row_count = queries.shape[0]
    groups = page_block.shape[0] // (2 * HD)
    score_scale = 1.0 / math.sqrt(HD)
    query_heads = queries.reshape(row_count, groups, GQA, HD)
    page_heads = page_block.reshape(groups, 2, HD, page_block.shape[1])
    scores = (
        jnp.einsum(
            "rgjd,gdl->grjl", query_heads, page_heads[:, 0], preferred_element_type=jnp.float32
        )
        * score_scale
    )
    usable = lax.broadcasted_iota(jnp.int32, scores.shape, 3) < length
    peak_score = jnp.max(jnp.where(usable, scores, masked_score), axis=3)
    weights = jnp.where(usable, jnp.exp(scores - peak_score[..., None]), 0.0)
    totals = jnp.sum(weights, axis=3)
    summed = jnp.einsum(
        "grjl,gdl->grjd",
        weights.astype(jnp.bfloat16),
        page_heads[:, 1],
        preferred_element_type=jnp.float32,
    )
    summed = jnp.transpose(summed, (1, 0, 2, 3)).reshape(row_count, groups * GQA * HD)
    peak_score = jnp.transpose(peak_score, (1, 0, 2)).reshape(row_count, groups * GQA)
    totals = jnp.transpose(totals, (1, 0, 2)).reshape(row_count, groups * GQA)
    return (summed, peak_score, totals)


def on_device(
    prompt_states,
    prompt_lengths,
    prompt_owner,
    kv_weight,
    sampler_prompts,
    step_queries,
    step_kv,
    out_weight,
):
    states = prompt_states[0]
    own_pages = lax.psum_scatter(
        lax.dot_general(
            kv_weight, states, (((0,), (1,)), ((), ())), preferred_element_type=jnp.float32
        ).astype(jnp.bfloat16),
        "head",
        scatter_dimension=0,
        tiled=True,
    )
    step_count = step_queries.shape[0]
    row_total = step_queries.shape[1]
    prompt_count = sampler_prompts.shape[0]
    block_rows = row_total // prompt_count
    head_width = step_queries.shape[2]
    groups = own_pages.shape[0] // (2 * HD)
    owner_slots = jnp.take(prompt_owner, sampler_prompts)
    block_lengths = jnp.take(prompt_lengths, sampler_prompts)
    block_queries = [
        step_queries[:, position * block_rows : (position + 1) * block_rows].reshape(
            step_count * block_rows, head_width
        )
        for position in range(prompt_count)
    ]
    library = lax.all_gather(own_pages[None], "samp", axis=0, tiled=True)
    partials = []
    for position in range(prompt_count):
        page_block = lax.dynamic_index_in_dim(library, owner_slots[position], 0, keepdims=False)
        partials.append(
            prompt_partial(block_queries[position], page_block, block_lengths[position])
        )
    prompt_sum = jnp.concatenate(
        [entry[0].reshape(step_count, block_rows, groups, GQA, HD) for entry in partials], axis=1
    )
    prompt_peak = jnp.concatenate(
        [entry[1].reshape(step_count, block_rows, groups, GQA) for entry in partials], axis=1
    )
    prompt_total = jnp.concatenate(
        [entry[2].reshape(step_count, block_rows, groups, GQA) for entry in partials], axis=1
    )
    score_scale = 1.0 / math.sqrt(HD)
    query_all = step_queries.reshape(step_count, row_total, groups, GQA, HD)
    own_cache = step_kv.reshape(step_count, row_total, groups, 2, HD)
    near_scores = (
        jnp.einsum(
            "trgjd,urgd->trgju",
            query_all,
            own_cache[:, :, :, 0],
            preferred_element_type=jnp.float32,
        )
        * score_scale
    )
    causal = lax.broadcasted_iota(jnp.int32, near_scores.shape, 4) <= lax.broadcasted_iota(
        jnp.int32, near_scores.shape, 0
    )
    near_peak = jnp.max(jnp.where(causal, near_scores, masked_score), axis=4)
    near_weights = jnp.where(causal, jnp.exp(near_scores - near_peak[..., None]), 0.0)
    near_total = jnp.sum(near_weights, axis=4)
    near_sum = jnp.einsum(
        "trgju,urgd->trgjd",
        near_weights.astype(jnp.bfloat16),
        own_cache[:, :, :, 1],
        preferred_element_type=jnp.float32,
    )
    peak_all = jnp.maximum(prompt_peak, near_peak)
    far_factor = jnp.exp(prompt_peak - peak_all)
    near_factor = jnp.exp(near_peak - peak_all)
    numerator = prompt_sum * far_factor[..., None] + near_sum * near_factor[..., None]
    denominator = prompt_total * far_factor + near_total * near_factor
    attention = (numerator / denominator[..., None]).astype(jnp.bfloat16)
    attention = attention.reshape(step_count * row_total, groups * GQA * HD)
    terms = jnp.dot(
        attention,
        lax.all_gather(out_weight, "samp", axis=1, tiled=True),
        preferred_element_type=jnp.float32,
    )
    mixed = lax.psum_scatter(
        terms.astype(jnp.bfloat16), "head", scatter_dimension=1, tiled=True
    ).astype(jnp.float32)
    return mixed.astype(jnp.bfloat16).reshape(step_count, row_total, mixed.shape[1])


def solution(mesh):
    placed = (
        P(("groups", "samp"), None, "head"),
        P("groups"),
        P("groups"),
        P("head", None),
        P(("groups", "samp")),
        P(None, ("groups", "samp"), "head"),
        P(None, ("groups", "samp"), "head"),
        P("head", "samp"),
    )
    return jax.shard_map(
        on_device,
        mesh=mesh,
        in_specs=placed,
        out_specs=P(None, ("groups", "samp"), "head"),
        check_vma=False,
    )
```

profile of v0, /device:TPU:6, one launch (start us, length us, event | category | flops | bytes accessed | tf_op | source)
XLA Modules:
  0.0 421.6 jit_solution(5873810962759771176)
XLA Ops:
  6.5 0.0 copy-start
  6.5 0.0 reduce-scatter.3.cloned.1.call-start
  6.5 1.7 copy-done
  8.3 9.8 %convolution_convert_fusion.1 = bf16[2048,1024]{1,0:T(8,128)(2,1)} fusion(bf16[1280,2048]{1,0:T(8,128)(2,1)} %param.13, bf16[1,1024,1280]{2,1,0:T(8,128)(2,1)S(1)} %copy-done), kind=kOutput, calls=%fused_computation.11 | convolution fusion | flops 5370806272 | bytes 12058624 | tf_op jit(solution)/shard_map/dot_general | solution.py:55
  18.1 0.0 reduce-scatter.3.cloned.1.call-update
  18.1 0.0 all-gather.6.cloned.1.call-start
  18.1 44.9 %reduce-scatter.3.cloned.1.call-done = bf16[512,1024]{1,0:T(8,128)(2,1)} async-done(((bf16[2048,1024]{1,0:T(8,128)(2,1)}), bf16[512,1024]{1,0:T(8,128)(2,1)}) %reduce-scatter.3.cloned.1.call-update) | async-done | bytes 1048592 | tf_op jit(solution)/shard_map/reduce_scatter | solution.py:54
  63.0 0.0 all-gather.6.cloned.1.call-update
  63.1 0.0 all-gather.4.cloned.1.call-start
  63.1 0.7 all-gather.4.cloned.1.call-update
  63.8 0.0 reduce-scatter.5.cloned.1.call-start
  63.8 0.0 copy-done.15
  63.9 0.0 copy-done.1
  63.9 0.6 gather_fusion
  64.5 0.0 copy-done.2
  64.5 0.6 gather_fusion.1
  65.2 0.7 fusion.31
  68.3 0.0 copy-done.5
  68.3 1.7 reshape.123
  70.0 0.9 fusion.29
  70.9 2.1 reshape_reshape.16
  73.0 1.4 reshape_reshape.18
  74.4 1.0 reshape.122
  76.7 0.6 iota_compare_fusion.2
  77.3 0.0 copy-start.13
  77.3 1.2 iota_compare_fusion.1
  78.5 1.1 fusion.30
  79.6 6.0 %select_reduce_fusion.2 = (f32[4,64,2,5]{3,0,2,1:T(4,128)S(1)}, f32[4,64,2,5,4]{3,4,0,2,1:T(4,128)S(1)}) fusion(bf16[4,64,2,5,128]{4,3,2,1,0:T(8,128)(2,1)} %reshape.123, bf16[4,64,2,1,128]{4,3,2,1,0:T(2,128)(2,1)S(1)} %get-tuple-element.14), kind=kOutput, calls=%fused_computation.26 | convolution fusion | flops 2659840 | bytes 837632 | tf_op jit(solution)/shard_map/trgjd,urgd->trgju/dot_general | solution.py:96
  85.6 0.0 copy-start.8
  85.6 1.0 copy-done.8
  86.6 1.7 fusion.10
  88.3 58.1 %all-gather.6.cloned.1.call-done = bf16[2048,1024]{1,0:T(8,128)(2,1)} async-done(((bf16[512,1024]{1,0:T(8,128)(2,1)}), bf16[2048,1024]{1,0:T(8,128)(2,1)}) %all-gather.6.cloned.1.call-update) | async-done | bytes 4194320 | tf_op jit(solution)/shard_map/all_gather | solution.py:76
  146.4 2.8 constant_dynamic-slice_fusion.1
  149.2 2.9 select_reduce_fusion.1
  152.1 2.4 copy-done.3
  154.5 1.5 bitcast_reduce_fusion.1
  156.1 0.7 reshape.157
  156.8 0.9 copy.104
  157.6 2.6 select_reduce_fusion
  160.2 0.0 copy-start.4
  160.2 0.0 copy-start.14
  160.2 2.3 copy-done.4
  162.5 2.1 bitcast_reduce_fusion
  164.6 0.1 reshape.158
  164.7 0.1 copy.105
  164.9 0.1 reshape.155
  164.9 0.1 copy.97
  165.1 0.1 reshape.156
  165.2 0.1 copy.98
  165.3 0.0 copy-done.14
  165.3 0.0 copy-start.6
  165.3 4.3 %fusion.1 = f32[2,128,5,128]{3,1,2,0:T(8,128)S(1)} fusion(f32[2,1024,128,5]{2,1,3,0:T(8,128)} %copy-done.3, f32[2,128,5]{1,2,0:T(8,128)S(1)} %get-tuple-element.23, pred[1024]{0:T(1024)(128)(4,1)S(1)} %copy-done.14, bf16[2,2,128,1024]{3,2,1,0:T(8,128)(2,1)} %bitcast.99), kind=kOutput, calls=%fused_computation.13 | convolution fusion | flops 340787200 | bytes 6428672 | tf_op jit(solution)/shard_map/grjl,gdl->grjd/dot_general | solution.py:31
  169.7 0.4 copy.93
  170.1 4.3 %fusion.2 = f32[2,128,5,128]{3,1,2,0:T(8,128)S(1)} fusion(f32[2,1024,128,5]{2,1,3,0:T(8,128)} %copy-done.4, f32[2,128,5]{1,2,0:T(8,128)S(1)} %get-tuple-element.21, pred[1024]{0:T(1024)(128)(4,1)S(1)} %copy-done.12, bf16[2,2,128,1024]{3,2,1,0:T(8,128)(2,1)S(1)} %bitcast.97), kind=kOutput, calls=%fused_computation.14 | convolution fusion | flops 340787200 | bytes 6431744 | tf_op jit(solution)/shard_map/grjl,gdl->grjd/dot_general | solution.py:31
  174.4 0.4 copy.94
  174.8 0.0 copy-done.10
  174.8 0.3 fusion.21
  175.1 2.6 fusion.7
  177.7 1.2 copy.106
  178.9 1.9 reshape.124
  180.8 192.6 %all-gather.4.cloned.1.call-done = bf16[1280,5120]{1,0:T(8,128)(2,1)} async-done(((bf16[1280,1280]{1,0:T(8,128)(2,1)}), bf16[1280,5120]{1,0:T(8,128)(2,1)}) %all-gather.4.cloned.1.call-update) | async-done | bytes 13107216 | tf_op jit(solution)/shard_map/all_gather | solution.py:125
  373.4 9.6 %convolution_convert_fusion = bf16[256,5120]{1,0:T(8,128)(2,1)} fusion(bf16[256,1280]{1,0:T(8,128)(2,1)S(1)} %reshape.124, bf16[1280,5120]{1,0:T(8,128)(2,1)} %all-gather.4.cloned.1.call-done), kind=kOutput, calls=%fused_computation.2 | convolution fusion | flops 3356753920 | bytes 16384000 | tf_op jit(solution)/shard_map/dot_general | solution.py:123
  382.9 0.0 reduce-scatter.5.cloned.1.call-update
  383.0 32.1 %reduce-scatter.5.cloned.1.call-done = bf16[256,1280]{1,0:T(8,128)(2,1)} async-done(((bf16[256,5120]{1,0:T(8,128)(2,1)}), bf16[256,1280]{1,0:T(8,128)(2,1)}) %reduce-scatter.5.cloned.1.call-update) | async-done | bytes 655376 | tf_op jit(solution)/shard_map/reduce_scatter | solution.py:128
  (19 shorter events, 0.0 us)
Async XLA Ops:
  6.5 1.7 copy-start
  6.5 56.5 %reduce-scatter.3.cloned.1.call-start = ((), (), s32[]{:S(2)}) async-start(), calls=%async_computation.2 | async-start | bytes 5242880 | tf_op jit(solution)/shard_map/reduce_scatter | solution.py:54
  18.1 45.8 %copy-start.15 = (s32[2]{0:T(128)S(1)}, s32[2]{0:T(128)}, u32[]{:S(2)}) copy-start(s32[2]{0:T(128)} %param.14) | copy-start | bytes 28
  18.1 45.8 %copy-start.1 = (s32[4]{0:T(128)S(1)}, s32[4]{0:T(128)}, u32[]{:S(2)}) copy-start(s32[4]{0:T(128)} %param.11) | copy-start | bytes 52
  18.1 46.5 %copy-start.2 = (s32[4]{0:T(128)S(1)}, s32[4]{0:T(128)}, u32[]{:S(2)}) copy-start(s32[4]{0:T(128)} %param.12) | copy-start | bytes 52
  18.1 50.2 %copy-start.5 = (bf16[4,64,1280]{2,1,0:T(8,128)(2,1)S(1)}, bf16[4,64,1280]{2,1,0:T(8,128)(2,1)}, u32[]{:S(2)}) copy-start(bf16[4,64,1280]{2,1,0:T(8,128)(2,1)} %param.15) | copy-start | bytes 1966084
  18.1 128.3 %all-gather.6.cloned.1.call-start = ((), (), s32[]{:S(2)}) async-start(), calls=%async_computation.5 | async-start | bytes 5242880 | tf_op jit(solution)/shard_map/all_gather | solution.py:76
  63.1 310.3 %all-gather.4.cloned.1.call-start = ((), (), s32[]{:S(2)}) async-start(), calls=%async_computation.3 | async-start | bytes 16384000 | tf_op jit(solution)/shard_map/all_gather | solution.py:125
  63.8 351.3 %reduce-scatter.5.cloned.1.call-start = ((), (), s32[]{:S(2)}) async-start(), calls=%async_computation.4 | async-start | bytes 3276800 | tf_op jit(solution)/shard_map/reduce_scatter | solution.py:128
  77.3 74.7 %copy-start.13 = (pred[1024]{0:T(1024)(128)(4,1)}, pred[1024]{0:T(1024)(128)(4,1)S(1)}, u32[]{:S(2)}) copy-start(pred[1024]{0:T(1024)(128)(4,1)S(1)} %iota_compare_fusion.2) | copy-start | bytes 3076
  85.6 1.0 copy-start.8
  149.2 6.9 %copy-start.7 = (bf16[1,512,1024]{2,1,0:T(8,128)(2,1)}, bf16[1,512,1024]{2,1,0:T(8,128)(2,1)S(1)}, u32[]{:S(2)}) copy-start(bf16[1,512,1024]{2,1,0:T(8,128)(2,1)S(1)} %get-tuple-element.9) | copy-start | bytes 3145732
  152.0 2.5 copy-start.3
  160.2 2.3 copy-start.4
  160.2 5.1 %copy-start.14 = (pred[1024]{0:T(1024)(128)(4,1)S(1)}, pred[1024]{0:T(1024)(128)(4,1)}, u32[]{:S(2)}) copy-start(pred[1024]{0:T(1024)(128)(4,1)} %copy-done.13) | copy-start | bytes 3076
  164.8 5.2 %copy-start.12 = (pred[1024]{0:T(1024)(128)(4,1)S(1)}, pred[1024]{0:T(1024)(128)(4,1)}, u32[]{:S(2)}) copy-start(pred[1024]{0:T(1024)(128)(4,1)} %iota_compare_fusion.1) | copy-start | bytes 3076
  165.3 4.7 %copy-start.6 = (bf16[1,512,1024]{2,1,0:T(8,128)(2,1)S(1)}, bf16[1,512,1024]{2,1,0:T(8,128)(2,1)}, u32[]{:S(2)}) copy-start(bf16[1,512,1024]{2,1,0:T(8,128)(2,1)} %get-tuple-element.10) | copy-start | bytes 3145732
  170.1 4.7 %copy-start.10 = (f32[4,64,2,5]{3,0,2,1:T(4,128)S(1)}, f32[4,64,2,5]{3,0,2,1:T(4,128)}, u32[]{:S(2)}) copy-start(f32[4,64,2,5]{3,0,2,1:T(4,128)} %fusion.10) | copy-start | bytes 30724
  170.1 5.0 %copy-start.9 = (f32[4,64,2,5,4]{3,4,0,2,1:T(4,128)S(1)}, f32[4,64,2,5,4]{3,4,0,2,1:T(4,128)}, u32[]{:S(2)}) copy-start(f32[4,64,2,5,4]{3,4,0,2,1:T(4,128)} %copy-done.8) | copy-start | bytes 122884
  170.1 5.0 %copy-start.11 = (bf16[4,64,2,1,128]{4,3,2,1,0:T(2,128)(2,1)S(1)}, bf16[4,64,2,1,128]{4,3,2,1,0:T(2,128)(2,1)}, u32[]{:S(2)}) copy-start(bf16[4,64,2,1,128]{4,3,2,1,0:T(2,128)(2,1)} %get-tuple-element.13) | copy-start | bytes 393220
Sparse Core Ops, SparseCore 0:
  18.2 44.7 reduce-scatter.2
  64.7 81.6 all-gather.5
  148.1 225.2 all-gather.3
  383.1 31.9 reduce-scatter.4
where the time goes:
time: 425 us; the launch traced here: 422 us
  waiting for transfers between devices  328 us (77%)
  matrix products  41.9 us (10%)
  local copies, waits for them, and re-layouts  26.5 us (6%)
  between operations  17.2 us (4%)
  other arithmetic  7.45 us (2%)
    all_gather x1, waiting for transfers between devices, on_device(): lax.all_gather(out_weight, 'samp', axis=1, tiled=True)  193 us
    all_gather x1, waiting for transfers between devices, on_device(): library = lax.all_gather(own_pages[None], 'samp', axis=0, tiled=True)  58.1 us
    reduce_scatter x1, waiting for transfers between devices, on_device(): lax.psum_scatter(lax.dot_general(kv_weight, states, (((0,), (1,)), ((), (...  44.9 us
    reduce_scatter x1, waiting for transfers between devices, on_device(): lax.psum_scatter(terms.astype(jnp.bfloat16), 'head', scatter_dimension=1,...  32.1 us
    dot_general x1, matrix products, on_device(): lax.dot_general(kv_weight, states, (((0,), (1,)), ((), ())), preferred_el...  9.78 us
    dot_general x1, matrix products, on_device(): jnp.dot(attention, lax.all_gather(out_weight, 'samp', axis=1, tiled=True)...  9.55 us
    dot_general x2, matrix products, prompt_partial(): jnp.einsum('grjl,gdl->grjd', weights.astype(jnp.bfloat16), page_heads[:,...  8.57 us
  transfers between devices with their start and end apart: 4, of which 4 were waited for; matrix products, arithmetic and copies ran while one was open for 12% of the time, Pallas kernels for 0%

commit v1 on v0

--- a/solution.py
+++ b/solution.py
@@ -3,6 +3,8 @@
 import jax
 import jax.numpy as jnp
 from jax import lax
+from jax.experimental import pallas as pl
+from jax.experimental.pallas import tpu as pltpu
 from jax.sharding import PartitionSpec as P
 
 HD = 128
@@ -40,7 +42,7 @@
     return (summed, peak_score, totals)
 
 
-def on_device(
+def general_plan(
     prompt_states,
     prompt_lengths,
     prompt_owner,
@@ -131,7 +133,288 @@
     return mixed.astype(jnp.bfloat16).reshape(step_count, row_total, mixed.shape[1])
 
 
+CHUNKS = 4
+PIECES = 2
+VMEM = 56 * 1024 * 1024
+
+CORE = [(0, 1), (1, 0), (2, 3), (3, 2)]
+ACROSS_X = [(0, 2), (2, 0), (1, 3), (3, 1)]
+INWARD = [(0, 1), (3, 2)]
+OUTWARD = [(1, 0), (2, 3)]
+MIDDLE = [(1, 2), (2, 1)]
+BEYOND = [(1, 3), (2, 0)]
+
+
+def compiler_params():
+    return pltpu.CompilerParams(vmem_limit_bytes=VMEM)
+
+
+def project(states, weight, first, second):
+    tokens, features = states.shape
+    width = weight.shape[1] // 4
+    chunk = tokens // CHUNKS
+
+    def body(places, state_ref, first_ref, second_ref, *outs):
+        step = pl.program_id(0)
+        one = jnp.dot(state_ref[...], first_ref[...], preferred_element_type=jnp.float32)
+        two = jnp.dot(state_ref[...], second_ref[...], preferred_element_type=jnp.float32)
+        for at in range(CHUNKS):
+
+            @pl.when(step == at)
+            def _():
+                outs[at][...] = one.astype(jnp.bfloat16)
+                outs[CHUNKS + at][...] = two.astype(jnp.bfloat16)
+
+    whole = pl.BlockSpec((chunk, width), lambda i, places: (0, 0))
+    outs = pl.pallas_call(
+        body,
+        grid_spec=pltpu.PrefetchScalarGridSpec(
+            num_scalar_prefetch=1,
+            grid=(CHUNKS,),
+            in_specs=[
+                pl.BlockSpec((chunk, features), lambda i, places: (i, 0)),
+                pl.BlockSpec((features, width), lambda i, places: (0, places[0])),
+                pl.BlockSpec((features, width), lambda i, places: (0, places[1])),
+            ],
+            out_specs=[whole] * (2 * CHUNKS),
+        ),
+        out_shape=[jax.ShapeDtypeStruct((chunk, width), jnp.bfloat16)] * (2 * CHUNKS),
+        compiler_params=compiler_params(),
+        name="project",
+    )(jnp.stack([first, second]).astype(jnp.int32), states, weight, weight)
+    return outs[:CHUNKS], outs[CHUNKS:]
+
+
+def attend(places, lengths, queries, news, pages):
+    steps, rows, width = queries.shape
+    blocks = places.shape[0]
+    block_rows = rows // blocks
+    new_width = news.shape[2]
+    groups = new_width // (2 * HD)
+    chunk = pages[0][0].shape[0]
+    tokens = chunk * CHUNKS
+    flat = steps * block_rows
+    factor = math.log2(math.e) / math.sqrt(HD)
+
+    def body(places_ref, lengths_ref, query_ref, new_ref, *rest):
+        page_refs, out_ref, held = rest[: 4 * CHUNKS], rest[4 * CHUNKS], rest[4 * CHUNKS + 1]
+        block = pl.program_id(0)
+        place, length = places_ref[block], lengths_ref[block]
+        for which in range(4):
+
+            @pl.when(place == which)
+            def _():
+                for at in range(CHUNKS):
+                    held[at * chunk : (at + 1) * chunk] = page_refs[which * CHUNKS + at][...]
+
+        query = query_ref[...].reshape(flat, width)
+        new = new_ref[...].reshape(flat, new_width)
+        shape = (GQA * flat, flat)
+        asker = lax.broadcasted_iota(jnp.int32, shape, 0) % flat
+        holder = lax.broadcasted_iota(jnp.int32, shape, 1)
+        same_row = asker % block_rows == holder % block_rows
+        near_ok = jnp.logical_and(same_row, holder <= asker)
+        far_ok = lax.broadcasted_iota(jnp.int32, (GQA * flat, tokens), 1) < length
+        for group in range(groups):
+            key = slice(2 * group * HD, (2 * group + 1) * HD)
+            value = slice((2 * group + 1) * HD, (2 * group + 2) * HD)
+            asked = jnp.concatenate(
+                [
+                    query[:, (group * GQA + head) * HD : (group * GQA + head + 1) * HD]
+                    for head in range(GQA)
+                ],
+                axis=0,
+            )
+            far = lax.dot_general(
+                asked, held[:, key], (((1,), (1,)), ((), ())), preferred_element_type=jnp.float32
+            )
+            near = lax.dot_general(
+                asked, new[:, key], (((1,), (1,)), ((), ())), preferred_element_type=jnp.float32
+            )
+            far = jnp.where(far_ok, far * factor, masked_score)
+            near = jnp.where(near_ok, near * factor, masked_score)
+            peak = jnp.maximum(
+                jnp.max(far, axis=1, keepdims=True), jnp.max(near, axis=1, keepdims=True)
+            )
+            far = jnp.exp2(far - peak)
+            near = jnp.exp2(near - peak)
+            total = jnp.sum(far, axis=1, keepdims=True) + jnp.sum(near, axis=1, keepdims=True)
+            summed = jnp.dot(
+                far.astype(jnp.bfloat16), held[:, value], preferred_element_type=jnp.float32
+            ) + jnp.dot(near.astype(jnp.bfloat16), new[:, value], preferred_element_type=jnp.float32)
+            result = (summed / total).astype(jnp.bfloat16)
+            for head in range(GQA):
+                column = (group * GQA + head) * HD
+                out_ref[:, :, column : column + HD] = result[
+                    head * flat : (head + 1) * flat
+                ].reshape(steps, block_rows, HD)
+
+    page_spec = pl.BlockSpec((chunk, new_width), lambda i, p, n: (0, 0))
+    return pl.pallas_call(
+        body,
+        grid_spec=pltpu.PrefetchScalarGridSpec(
+            num_scalar_prefetch=2,
+            grid=(blocks,),
+            in_specs=[
+                pl.BlockSpec((steps, block_rows, width), lambda i, p, n: (0, i, 0)),
+                pl.BlockSpec((steps, block_rows, new_width), lambda i, p, n: (0, i, 0)),
+            ]
+            + [page_spec] * (4 * CHUNKS),
+            out_specs=pl.BlockSpec((steps, block_rows, width), lambda i, p, n: (0, i, 0)),
+            scratch_shapes=[pltpu.VMEM((tokens, new_width), jnp.bfloat16)],
+        ),
+        out_shape=jax.ShapeDtypeStruct(queries.shape, jnp.bfloat16),
+        compiler_params=compiler_params(),
+        name="attend",
+    )(places, lengths, queries, news, *[part for page in pages for part in page])
+
+
+def spread(flag, attention, own_weight, moved_weight):
+    steps, rows, features = attention.shape
+    columns = own_weight.shape[1]
+    tile = 256 if columns % 256 == 0 else columns
+    flat = attention.reshape(steps * rows, features)
+
+    def body(flag_ref, rows_ref, own_ref, moved_ref, keep_ref, send_ref):
+        own = jnp.dot(rows_ref[...], own_ref[...], preferred_element_type=jnp.float32)
+        moved = jnp.dot(rows_ref[...], moved_ref[...], preferred_element_type=jnp.float32)
+        keeps_own = flag_ref[0] == 1
+        keep_ref[...] = jnp.where(keeps_own, own, moved).astype(jnp.bfloat16)
+        send_ref[...] = jnp.where(keeps_own, moved, own).astype(jnp.bfloat16)
+
+    column_spec = pl.BlockSpec((features, tile), lambda i, f: (0, i))
+    out_spec = pl.BlockSpec((steps * rows, tile), lambda i, f: (0, i))
+    out_shape = jax.ShapeDtypeStruct((steps * rows, columns), jnp.bfloat16)
+    keep, send = pl.pallas_call(
+        body,
+        grid_spec=pltpu.PrefetchScalarGridSpec(
+            num_scalar_prefetch=1,
+            grid=(columns // tile,),
+            in_specs=[
+                pl.BlockSpec((steps * rows, features), lambda i, f: (0, 0)),
+                column_spec,
+                column_spec,
+            ],
+            out_specs=[out_spec, out_spec],
+        ),
+        out_shape=[out_shape, out_shape],
+        compiler_params=compiler_params(),
+        name="spread",
+    )(flag, flat, own_weight, moved_weight)
+    return keep.reshape(steps, rows, columns), send.reshape(steps, rows, columns)
+
+
+def added(*parts):
+    total = parts[0].astype(jnp.float32)
+    for part in parts[1:]:
+        total = total + part.astype(jnp.float32)
+    return total.astype(jnp.bfloat16)
+
+
+def inward_plan(
+    prompt_states,
+    prompt_lengths,
+    prompt_owner,
+    kv_weight,
+    sampler_prompts,
+    step_queries,
+    step_kv,
+    out_weight,
+):
+    group, plane, head = (lax.axis_index(name) for name in ("groups", "samp", "head"))
+    chip, core = head // 2, head % 2
+    steps = step_queries.shape[0]
+
+    def on_samp(value, pairs):
+        return lax.ppermute(value, "samp", pairs)
+
+    def on_head(value, pairs):
+        return lax.ppermute(value, "head", pairs)
+
+    end_prompts = on_samp(sampler_prompts, INWARD)
+    end_queries = on_samp(step_queries, INWARD)
+    end_news = on_samp(step_kv, INWARD)
+
+    def table(prompts):
+        slots = jnp.take(prompt_owner, prompts)
+        places = jnp.where(
+            slots == plane,
+            0,
+            jnp.where(slots == (plane ^ 1), 1, jnp.where(slots == 3 - plane, 2, 3)),
+        )
+        return places.astype(jnp.int32), jnp.take(prompt_lengths, prompts)
+
+    states = prompt_states[0]
+    sent, kept = project(states, kv_weight, head ^ 3, head ^ 2)
+    crossing = []
+    for at in range(CHUNKS):
+        crossing.append(on_head(added(kept[at], on_head(sent[at], CORE)), ACROSS_X))
+    sent, kept = project(states, kv_weight, head ^ 1, head)
+    own_page, end_page, far_page, far_end_page = [], [], [], []
+    for at in range(CHUNKS):
+        part = added(kept[at], on_head(sent[at], CORE), crossing[at])
+        own_page.append(part)
+        end_page.append(on_samp(part, INWARD))
+        far_page.append(on_samp(part, MIDDLE))
+        far_end_page.append(on_samp(end_page[at], MIDDLE))
+    pages = (own_page, end_page, far_page, far_end_page)
+
+    half = out_weight.shape[0] // 2
+    piece = half // PIECES
+    mine, other = [], []
+    for at in range(PIECES):
+        moving = lax.dynamic_slice_in_dim(out_weight, group * half + at * piece, piece, 0)
+        moving, _ = lax.optimization_barrier((moving, own_page[1]))
+        mine.append(on_samp(moving, INWARD))
+        other.append(lax.ppermute(mine[at], "groups", [(0, 1), (1, 0)]))
+    mine, other = jnp.concatenate(mine, axis=0), jnp.concatenate(other, axis=0)
+    moved_weight = jnp.where(
+        group == 0,
+        jnp.concatenate([mine, other], axis=0),
+        jnp.concatenate([other, mine], axis=0),
+    )
+
+    end_rows = attend(*table(end_prompts), end_queries, end_news, pages)
+    far_end_rows = on_samp(end_rows, MIDDLE)
+    own_rows = attend(*table(sampler_prompts), step_queries, step_kv, pages)
+    far_rows = on_samp(own_rows, MIDDLE)
+
+    flag = (core == plane % 2).astype(jnp.int32).reshape(1)
+
+    def summed(rows):
+        keep, send = spread(flag, rows, out_weight, moved_weight)
+        arrived = on_head(send, CORE)
+
+        def half_of(value, which):
+            return lax.dynamic_slice_in_dim(value, which * (steps // 2), steps // 2, 0)
+
+        leaving = added(half_of(keep, 1 - chip), half_of(arrived, 1 - chip))
+        return added(half_of(keep, chip), half_of(arrived, chip), on_head(leaving, ACROSS_X))
+
+    end_sum = summed(end_rows)
+    near_out = on_samp(end_sum, OUTWARD)
+    own_sum = summed(own_rows)
+    beyond_out = on_samp(summed(far_end_rows), BEYOND)
+    middle_out = on_samp(summed(far_rows), MIDDLE)
+
+    is_middle = jnp.logical_or(plane == 1, plane == 2)
+    near = jnp.where(is_middle, own_sum, near_out)
+    far = jnp.where(is_middle, middle_out, beyond_out)
+    near_side = chip == plane // 2
+    stays = jnp.where(near_side, near, far)
+    comes = on_head(jnp.where(near_side, far, near), ACROSS_X)
+    return jnp.where(
+        chip == 0,
+        jnp.concatenate([stays, comes], axis=0),
+        jnp.concatenate([comes, stays], axis=0),
+    )
+
+
 def solution(mesh):
+    line, width = mesh.shape["samp"], mesh.shape["head"]
+    paired = line == 4 and width == 4 and mesh.shape["groups"] == 2
+    on_device = inward_plan if paired else general_plan
+
     placed = (
         P(("groups", "samp"), None, "head"),
         P("groups"),

time: 425 us -> 240 us (0.56)
  waiting for transfers between devices: 328 us -> 87.6 us
  starting transfers between devices: 0.12 us -> 65.7 us
  Pallas kernels: 0 us -> 62.2 us
  matrix products: 41.9 us -> 0 us
  local copies, waits for them, and re-layouts: 26.5 us -> 4.45 us
  between operations: 17.2 us -> 0.69 us
  other arithmetic: 7.45 us -> 15.4 us
    all_gather x2 -> x0, waiting for transfers between devices: 251 us -> none  [the longest x1 193 us: on_device(): lax.all_gather(out_weight, 'samp', axis=1, tiled=True)]
    ppermute x0 -> x45, waiting for transfers between devices: none -> 87.6 us  [the longest x22 45.1 us: on_samp(): return lax.ppermute(value, 'samp', pairs)]
    reduce_scatter x2 -> x0, waiting for transfers between devices: 77 us -> none  [the longest x1 44.9 us: on_device(): lax.psum_scatter(lax.dot_general(kv_weight, states, (((0,), (1,)), ((), (...]
    ppermute x0 -> x45, starting transfers between devices: none -> 65.7 us  [the longest x22 51.7 us: on_samp(): return lax.ppermute(value, 'samp', pairs)]
    pallas_call x0 -> x8, Pallas kernels: none -> 62.2 us  [the longest x4 26.8 us: spread(): pl.pallas_call(body, grid_spec=pltpu.PrefetchScalarGridSpec(num_scalar_pr...]
    dot_general x8 -> x0, matrix products: 41.9 us -> none  [the longest x1 9.78 us: on_device(): lax.dot_general(kv_weight, states, (((0,), (1,)), ((), ())), preferred_el...]
    select_n x2 -> x8, other arithmetic: 0.01 us -> 7.96 us  [the longest x1 4.47 us: inward_plan(): jnp.where(group == 0, jnp.concatenate([mine, other], axis=0), jnp.concate...]
    convert_element_type x0 -> x15, other arithmetic: none -> 6.79 us  [added(): return total.astype(jnp.bfloat16)]
  transfers between devices with their start and end apart: 4 -> 45, of which waited for: 4 -> 11; matrix products, arithmetic and copies ran while one was open for 12% -> 7% of each run, Pallas kernels for 0% -> 26%
where the time goes in v1:
time: 240 us; the launch traced here: 236 us
  waiting for transfers between devices  87.6 us (36%)
  starting transfers between devices  65.7 us (27%)
  Pallas kernels  62.2 us (26%)
  other arithmetic  15.4 us (6%)
  local copies, waits for them, and re-layouts  4.45 us (2%)
    ppermute x22, starting transfers between devices, on_samp(): return lax.ppermute(value, 'samp', pairs)  51.7 us
    ppermute x22, waiting for transfers between devices, on_samp(): return lax.ppermute(value, 'samp', pairs)  45.1 us
    ppermute x21, waiting for transfers between devices, on_head(): return lax.ppermute(value, 'head', pairs)  42.5 us
    pallas_call x4, Pallas kernels, spread(): pl.pallas_call(body, grid_spec=pltpu.PrefetchScalarGridSpec(num_scalar_pr...  26.8 us
    pallas_call x2, Pallas kernels, attend(): pl.pallas_call(body, grid_spec=pltpu.PrefetchScalarGridSpec(num_scalar_pr...  19.3 us
    pallas_call x2, Pallas kernels, project(): pl.pallas_call(body, grid_spec=pltpu.PrefetchScalarGridSpec(num_scalar_pr...  16.1 us
    ppermute x21, starting transfers between devices, on_head(): return lax.ppermute(value, 'head', pairs)  11.9 us
    convert_element_type x15, other arithmetic, added(): return total.astype(jnp.bfloat16)  6.79 us
  transfers between devices with their start and end apart: 45, of which 11 were waited for; matrix products, arithmetic and copies ran while one was open for 7% of the time, Pallas kernels for 26%

profile of v1, /device:TPU:6, one launch (start us, length us, event | category | flops | bytes accessed | tf_op | source)
XLA Modules:
  0.0 236.0 jit_solution(4121975867711822838)
XLA Ops:
  0.0 3.6 %collective-permute-start.30 = (s32[2]{0:T(128)}, s32[2]{0:T(128)S(1)}, u32[]{:S(2)}, u32[]{:S(2)}) collective-permute-start(s32[2]{0:T(128)} %param.14), channel_id=1, source_target_pairs={{0,4},{12,8},{1,5},{13,9},{2,6},{14,10},{3,7},{15,11},{16,20},{28,... | collective-permute-start | bytes 32 | tf_op jit(solution)/shard_map/ppermute | solution.py:329
  3.6 0.7 pad_add_fusion
  4.3 8.1 %project.3 = (bf16[256,512]{1,0:T(8,128)(2,1)}, bf16[256,512]{1,0:T(8,128)(2,1)}, bf16[256,512]{1,0:T(8,128)(2,1)}, bf16[256,512]{1,0:T(8,128)(2,1)}, bf16[256,5...) custom-call(s32[2]{0:T(128)} %get-tuple-element.67.places, ...), custom_call_target="tpu_custom_call" | custom-call | tf_op jit(solution)/shard_map/project/pallas_call | solution.py:169
  13.5 8.0 %project.2 = (bf16[256,512]{1,0:T(8,128)(2,1)}, bf16[256,512]{1,0:T(8,128)(2,1)}, bf16[256,512]{1,0:T(8,128)(2,1)}, bf16[256,512]{1,0:T(8,128)(2,1)}, bf16[256,5...) custom-call(s32[2]{0:T(128)} %get-tuple-element.66.places, ...), custom_call_target="tpu_custom_call" | custom-call | tf_op jit(solution)/shard_map/project/pallas_call | solution.py:169
  21.7 1.1 add_convert_fusion.15
  23.3 1.0 add_convert_fusion.13
  24.4 0.6 collective-permute-start.5
  25.0 1.0 add_convert_fusion.11
  26.1 1.6 collective-permute-start.2
  28.5 5.1 %collective-permute-done.5 = bf16[256,512]{1,0:T(8,128)(2,1)S(1)} collective-permute-done((bf16[256,512]{1,0:T(8,128)(2,1)S(1)}, bf16[256,512]{1,0:T(8,128)(2,1)S(1)}, u32[]{:S(2)}, u32[]{:S(2)}) %collective-permute-start.5) | collective-permute-done | bytes 262176 | tf_op jit(solution)/shard_map/ppermute | solution.py:332
  34.3 2.2 collective-permute-start.24
  36.5 2.7 %collective-permute-done.2 = bf16[256,512]{1,0:T(8,128)(2,1)S(1)} collective-permute-done((bf16[256,512]{1,0:T(8,128)(2,1)S(1)}, bf16[256,512]{1,0:T(8,128)(2,1)S(1)}, u32[]{:S(2)}, u32[]{:S(2)}) %collective-permute-start.2) | collective-permute-done | bytes 262176 | tf_op jit(solution)/shard_map/ppermute | solution.py:332
  39.2 2.2 collective-permute-start.25
  41.6 0.7 collective-permute-start.16
  42.3 2.6 %collective-permute-done.8 = bf16[256,512]{1,0:T(8,128)(2,1)S(1)} collective-permute-done((bf16[256,512]{1,0:T(8,128)(2,1)S(1)}, bf16[256,512]{1,0:T(8,128)(2,1)S(1)}, u32[]{:S(2)}, u32[]{:S(2)}) %collective-permute-start.8) | collective-permute-done | bytes 262176 | tf_op jit(solution)/shard_map/ppermute | solution.py:332
  44.9 1.3 collective-permute-start.12
  46.2 3.5 %collective-permute-done.11 = bf16[256,512]{1,0:T(8,128)(2,1)S(1)} collective-permute-done((bf16[256,512]{1,0:T(8,128)(2,1)S(1)}, bf16[256,512]{1,0:T(8,128)(2,1)S(1)}, u32[]{:S(2)}, u32[]{:S(2)}) %collective-permute-start.11) | collective-permute-done | bytes 262176 | tf_op jit(solution)/shard_map/ppermute | solution.py:332
  49.6 0.7 collective-permute-start.17
  50.5 4.1 %collective-permute-start.13 = (bf16[256,512]{1,0:T(8,128)(2,1)S(1)}, bf16[256,512]{1,0:T(8,128)(2,1)S(1)}, u32[]{:S(2)}, u32[]{:S(2)}) collective-permute-start(bf16[256,512]{1,0:T(8,128)(2,1)S(1)} %add_convert_fusion.12.rest_1_), channel_id=1, source_target_pairs={{0,4},{12,8},{1,5},{13,9},{2,6},{14,10},{3,7},{15,11},{16,20},{28,... | collective-permute-start | bytes 786440 | tf_op jit(solution)/shard_map/ppermute | solution.py:329
  54.6 22.8 %collective-permute-done.12.rest_4_ = bf16[256,512]{1,0:T(8,128)(2,1)S(1)} collective-permute-done((bf16[256,512]{1,0:T(8,128)(2,1)S(1)}, bf16[256,512]{1,0:T(8,128)(2,1)S(1)}, u32[]{:S(2)}, u32[]{:S(2)}) %collective-permute-start.12) | collective-permute-done | bytes 262176 | tf_op jit(solution)/shard_map/ppermute | solution.py:329
  77.4 0.7 collective-permute-start.18
  78.1 7.2 %collective-permute-start.14 = (bf16[256,512]{1,0:T(8,128)(2,1)S(1)}, bf16[256,512]{1,0:T(8,128)(2,1)S(1)}, u32[]{:S(2)}, u32[]{:S(2)}) collective-permute-start(bf16[256,512]{1,0:T(8,128)(2,1)S(1)} %add_convert_fusion.10.rest_2_), channel_id=1, source_target_pairs={{0,4},{12,8},{1,5},{13,9},{2,6},{14,10},{3,7},{15,11},{16,20},{28,... | collective-permute-start | bytes 786440 | tf_op jit(solution)/shard_map/ppermute | solution.py:329
  85.5 0.7 collective-permute-start.19
  86.2 6.4 %collective-permute-start.15 = (bf16[256,512]{1,0:T(8,128)(2,1)S(1)}, bf16[256,512]{1,0:T(8,128)(2,1)S(1)}, u32[]{:S(2)}, u32[]{:S(2)}) collective-permute-start(bf16[256,512]{1,0:T(8,128)(2,1)S(1)} %add_convert_fusion.8.rest_3_), channel_id=1, source_target_pairs={{0,4},{12,8},{1,5},{13,9},{2,6},{14,10},{3,7},{15,11},{16,20},{28,... | collective-permute-start | bytes 786440 | tf_op jit(solution)/shard_map/ppermute | solution.py:329
  92.7 0.7 collective-permute-start.20
  94.0 1.5 collective-permute-start.27
  95.5 0.6 gather_fusion.1
  96.1 0.6 gather_fusion
  96.8 5.6 %collective-permute-start.31 = (bf16[4,64,1280]{2,1,0:T(8,128)(2,1)}, bf16[4,64,1280]{2,1,0:T(8,128)(2,1)}, u32[]{:S(2)}, u32[]{:S(2)}) collective-permute-start(bf16[4,64,1280]{2,1,0:T(8,128)(2,1)} %query_ref.1), channel_id=1, source_target_pairs={{0,4},{12,8},{1,5},{13,9},{2,6},{14,10},{3,7},{15,11},{16,20},{28,... | collective-permute-start | bytes 1966088 | tf_op jit(solution)/shard_map/ppermute | solution.py:329
  102.4 1.4 collective-permute-start.21
  103.8 1.4 collective-permute-start.22
  105.7 6.7 %collective-permute-start.32 = (bf16[4,64,512]{2,1,0:T(8,128)(2,1)}, bf16[4,64,512]{2,1,0:T(8,128)(2,1)}, u32[]{:S(2)}, u32[]{:S(2)}) collective-permute-start(bf16[4,64,512]{2,1,0:T(8,128)(2,1)} %new_ref.1), channel_id=1, source_target_pairs={{0,4},{12,8},{1,5},{13,9},{2,6},{14,10},{3,7},{15,11},{16,20},{28,... | collective-permute-start | bytes 786440 | tf_op jit(solution)/shard_map/ppermute | solution.py:329
  112.4 1.4 collective-permute-start.23
  113.8 0.6 gather_fusion.3
  114.4 0.6 gather_fusion.2
  115.0 0.6 broadcast_select_fusion.3
  115.8 9.7 %attend.2 = bf16[4,64,1280]{2,1,0:T(8,128)(2,1)} custom-call(s32[2]{0:T(128)} %get-tuple-element.65.places_ref, s32[2]{0:T(128)} %get-tuple-element.64.lengths_ref, bf16[4,64,1280]{2,1,0:T(8,128)(2,1)} %query_ref.1, bf16[4,64,512]{2,1,0:T(8,128)(2,1)} %new_ref.1, bf16[256,512]{1,0:T(8,128)(2,1)} %copy-done.4, bf16[256,512]{1,0:T(8,128)(2,1)} %copy-done.3, ...), custom_call_target="tpu_custom_call" | custom-call | tf_op jit(solution)/shard_map/attend/pallas_call | solution.py:253
  125.4 0.7 collective-permute-start.36
  126.1 9.7 %attend.3 = bf16[4,64,1280]{2,1,0:T(8,128)(2,1)} custom-call(s32[2]{0:T(128)} %get-tuple-element.63.places_ref, s32[2]{0:T(128)} %get-tuple-element.62.lengths_ref, bf16[4,64,1280]{2,1,0:T(8,128)(2,1)} %collective-permute-done.31.query_ref, bf16[4,64,512]{2,1,0:T(8,128)(2,1)} %collective-permute-done.32.new_ref, bf16[256,512]{1,0:T(8,128)(2,1)} %copy-done.4, ...), custom_call_target="tpu_custom_call" | custom-call | tf_op jit(solution)/shard_map/attend/pallas_call | solution.py:253
  135.8 0.9 collective-permute-start.40
  136.7 4.5 %maximum_select_fusion.moved_ref = bf16[1280,1280]{1,0:T(8,128)(2,1)} fusion(bf16[320,1280]{1,0:T(8,128)(2,1)} %collective-permute-done.27, bf16[320,1280]{1,0:T(8,128)(2,1)} %collective-permute-done.26, bf16[320,1280]{1,0:T(8,128)(2,1)} %collective-permute-done.25, bf16[320,1280]{1,0:T(8,128)(2,1)} %collective-permute-done.24, pred[]{:T(512)S(6)} %eq.62), kind=kLoop, calls=%fused_computation.4 | loop fusion | flops 27852800 | bytes 6553601 | tf_op jit(solution)/shard_map/jit(_where)/select_n | solution.py:371
  141.2 6.7 %spread.5 = (bf16[256,1280]{1,0:T(8,128)(2,1)}, bf16[256,1280]{1,0:T(8,128)(2,1)}) custom-call(s32[1]{0:T(128)} %bitcast.flag_ref, bf16[256,1280]{1,0:T(8,128)(2,1)} %bitcast.20, bf16[1280,1280]{1,0:T(8,128)(2,1)} %own_ref.7, bf16[1280,1280]{1,0:T(8,128)(2,1)} %maximum_select_fusion.moved_ref), custom_call_target="tpu_custom_call" | custom-call | tf_op jit(solution)/shard_map/spread/pallas_call | solution.py:288
  147.8 6.7 %spread.4 = (bf16[256,1280]{1,0:T(8,128)(2,1)}, bf16[256,1280]{1,0:T(8,128)(2,1)}) custom-call(s32[1]{0:T(128)} %bitcast.flag_ref, bf16[256,1280]{1,0:T(8,128)(2,1)} %bitcast.21, bf16[1280,1280]{1,0:T(8,128)(2,1)} %own_ref.7, bf16[1280,1280]{1,0:T(8,128)(2,1)} %maximum_select_fusion.moved_ref), custom_call_target="tpu_custom_call" | custom-call | tf_op jit(solution)/shard_map/spread/pallas_call | solution.py:288
  155.0 0.8 copy-done.17
  155.9 6.6 %spread.6 = (bf16[256,1280]{1,0:T(8,128)(2,1)}, bf16[256,1280]{1,0:T(8,128)(2,1)}) custom-call(s32[1]{0:T(128)} %bitcast.flag_ref, bf16[256,1280]{1,0:T(8,128)(2,1)} %bitcast.23, bf16[1280,1280]{1,0:T(8,128)(2,1)} %own_ref.7, bf16[1280,1280]{1,0:T(8,128)(2,1)} %maximum_select_fusion.moved_ref), custom_call_target="tpu_custom_call" | custom-call | tf_op jit(solution)/shard_map/spread/pallas_call | solution.py:288
  162.5 0.8 copy-done.16
  163.4 6.8 %spread.7 = (bf16[256,1280]{1,0:T(8,128)(2,1)}, bf16[256,1280]{1,0:T(8,128)(2,1)}) custom-call(s32[1]{0:T(128)} %bitcast.flag_ref, bf16[256,1280]{1,0:T(8,128)(2,1)} %bitcast.22, bf16[1280,1280]{1,0:T(8,128)(2,1)} %own_ref.7, bf16[1280,1280]{1,0:T(8,128)(2,1)} %maximum_select_fusion.moved_ref), custom_call_target="tpu_custom_call" | custom-call | tf_op jit(solution)/shard_map/spread/pallas_call | solution.py:288
  170.7 1.5 collective-permute-start.34
  172.3 0.8 add_convert_fusion.7
  173.7 1.5 collective-permute-start.38
  175.2 1.1 add_convert_fusion.1
  176.3 0.6 collective-permute-start.42
  176.9 4.4 %collective-permute-done.34 = bf16[2,64,1280]{2,1,0:T(8,128)(2,1)S(1)} collective-permute-done((bf16[2,64,1280]{2,1,0:T(8,128)(2,1)S(1)}, bf16[2,64,1280]{2,1,0:T(8,128)(2,1)S(1)}, u32[]{:S(2)}, u32[]{:S(2)}) %collective-permute-start.34) | collective-permute-done | bytes 327712 | tf_op jit(solution)/shard_map/ppermute | solution.py:332
  181.4 0.8 add_convert_fusion.4
  182.2 1.3 collective-permute-start.35
  183.5 11.9 %collective-permute-done.38 = bf16[2,64,1280]{2,1,0:T(8,128)(2,1)S(1)} collective-permute-done((bf16[2,64,1280]{2,1,0:T(8,128)(2,1)S(1)}, bf16[2,64,1280]{2,1,0:T(8,128)(2,1)S(1)}, u32[]{:S(2)}, u32[]{:S(2)}) %collective-permute-start.38) | collective-permute-done | bytes 327712 | tf_op jit(solution)/shard_map/ppermute | solution.py:332
  195.5 0.7 collective-permute-start.39
  196.2 5.3 %collective-permute-done.42 = bf16[2,64,1280]{2,1,0:T(8,128)(2,1)S(1)} collective-permute-done((bf16[2,64,1280]{2,1,0:T(8,128)(2,1)S(1)}, bf16[2,64,1280]{2,1,0:T(8,128)(2,1)S(1)}, u32[]{:S(2)}, u32[]{:S(2)}) %collective-permute-start.42) | collective-permute-done | bytes 327712 | tf_op jit(solution)/shard_map/ppermute | solution.py:332
  201.6 1.3 collective-permute-start.43
  203.3 21.8 %collective-permute-done.43 = bf16[2,64,1280]{2,1,0:T(8,128)(2,1)S(1)} collective-permute-done((bf16[2,64,1280]{2,1,0:T(8,128)(2,1)S(1)}, bf16[2,64,1280]{2,1,0:T(8,128)(2,1)S(1)}, u32[]{:S(2)}, u32[]{:S(2)}) %collective-permute-start.43) | collective-permute-done | bytes 327712 | tf_op jit(solution)/shard_map/ppermute | solution.py:329
  225.2 1.3 broadcast_select_fusion.2
  226.5 1.6 collective-permute-start.44
  228.1 7.0 %collective-permute-done.44 = bf16[2,64,1280]{2,1,0:T(8,128)(2,1)S(1)} collective-permute-done((bf16[2,64,1280]{2,1,0:T(8,128)(2,1)S(1)}, bf16[2,64,1280]{2,1,0:T(8,128)(2,1)S(1)}, u32[]{:S(2)}, u32[]{:S(2)}) %collective-permute-start.44) | collective-permute-done | bytes 327712 | tf_op jit(solution)/shard_map/ppermute | solution.py:332
  235.1 0.9 maximum_select_fusion.1
  (127 shorter events, 7.3 us)
Async XLA Ops:
  0.0 95.5 %copy-start = (s32[4]{0:T(128)S(1)}, s32[4]{0:T(128)}, u32[]{:S(2)}) copy-start(s32[4]{0:T(128)} %param.11) | copy-start | bytes 52
  0.0 26.0 %collective-permute-start.30 = (s32[2]{0:T(128)}, s32[2]{0:T(128)S(1)}, u32[]{:S(2)}, u32[]{:S(2)}) collective-permute-start(s32[2]{0:T(128)} %param.14), channel_id=1, source_target_pairs={{0,4},{12,8},{1,5},{13,9},{2,6},{14,10},{3,7},{15,11},{16,20},{28,... | collective-permute-start | bytes 32 | tf_op jit(solution)/shard_map/ppermute | solution.py:329
  12.4 9.3 %collective-permute-start.1 = (bf16[256,512]{1,0:T(8,128)(2,1)}, bf16[256,512]{1,0:T(8,128)(2,1)}, u32[]{:S(2)}, u32[]{:S(2)}) collective-permute-start(bf16[256,512]{1,0:T(8,128)(2,1)} %get-tuple-element.35), channel_id=1, source_target_pairs={{0,1},{1,0},{2,3},{3,2},{4,5},{5,4},{6,7},{7,6},{8,9},{9,8},{10,11... | collective-permute-start | bytes 786440 | tf_op jit(solution)/shard_map/ppermute | solution.py:332
  12.4 10.5 %collective-permute-start.4 = (bf16[256,512]{1,0:T(8,128)(2,1)}, bf16[256,512]{1,0:T(8,128)(2,1)}, u32[]{:S(2)}, u32[]{:S(2)}) collective-permute-start(bf16[256,512]{1,0:T(8,128)(2,1)} %get-tuple-element.39), channel_id=1, source_target_pairs={{0,1},{1,0},{2,3},{3,2},{4,5},{5,4},{6,7},{7,6},{8,9},{9,8},{10,11... | collective-permute-start | bytes 786440 | tf_op jit(solution)/shard_map/ppermute | solution.py:332
  12.9 11.5 %collective-permute-start.7 = (bf16[256,512]{1,0:T(8,128)(2,1)}, bf16[256,512]{1,0:T(8,128)(2,1)}, u32[]{:S(2)}, u32[]{:S(2)}) collective-permute-start(bf16[256,512]{1,0:T(8,128)(2,1)} %get-tuple-element.43), channel_id=1, source_target_pairs={{0,1},{1,0},{2,3},{3,2},{4,5},{5,4},{6,7},{7,6},{8,9},{9,8},{10,11... | collective-permute-start | bytes 786440 | tf_op jit(solution)/shard_map/ppermute | solution.py:332
  12.9 13.2 %collective-permute-start.10 = (bf16[256,512]{1,0:T(8,128)(2,1)}, bf16[256,512]{1,0:T(8,128)(2,1)S(1)}, u32[]{:S(2)}, u32[]{:S(2)}) collective-permute-start(bf16[256,512]{1,0:T(8,128)(2,1)} %get-tuple-element.47), channel_id=1, source_target_pairs={{0,1},{1,0},{2,3},{3,2},{4,5},{5,4},{6,7},{7,6},{8,9},{9,8},{10,11... | collective-permute-start | bytes 786440 | tf_op jit(solution)/shard_map/ppermute | solution.py:332
  13.5 14.1 %copy-start.22 = (bf16[256,512]{1,0:T(8,128)(2,1)S(1)}, bf16[256,512]{1,0:T(8,128)(2,1)}, u32[]{:S(2)}) copy-start(bf16[256,512]{1,0:T(8,128)(2,1)} %get-tuple-element.46) | copy-start | bytes 786436
  21.6 19.8 %copy-start.28 = (bf16[256,512]{1,0:T(8,128)(2,1)S(1)}, bf16[256,512]{1,0:T(8,128)(2,1)}, u32[]{:S(2)}) copy-start(bf16[256,512]{1,0:T(8,128)(2,1)} %get-tuple-element.32) | copy-start | bytes 786436
  21.6 28.7 %copy-start.27 = (bf16[256,512]{1,0:T(8,128)(2,1)S(1)}, bf16[256,512]{1,0:T(8,128)(2,1)}, u32[]{:S(2)}) copy-start(bf16[256,512]{1,0:T(8,128)(2,1)} %get-tuple-element.40) | copy-start | bytes 786436
  21.6 63.7 %copy-start.26 = (bf16[256,512]{1,0:T(8,128)(2,1)S(1)}, bf16[256,512]{1,0:T(8,128)(2,1)}, u32[]{:S(2)}) copy-start(bf16[256,512]{1,0:T(8,128)(2,1)} %get-tuple-element.44) | copy-start | bytes 786436
  21.6 6.1 %collective-permute-start = (bf16[256,512]{1,0:T(8,128)(2,1)}, bf16[256,512]{1,0:T(8,128)(2,1)S(1)}, u32[]{:S(2)}, u32[]{:S(2)}) collective-permute-start(bf16[256,512]{1,0:T(8,128)(2,1)} %get-tuple-element.33), channel_id=1, source_target_pairs={{0,1},{1,0},{2,3},{3,2},{4,5},{5,4},{6,7},{7,6},{8,9},{9,8},{10,11... | collective-permute-start | bytes 786440 | tf_op jit(solution)/shard_map/ppermute | solution.py:332
  22.9 5.1 %collective-permute-start.3 = (bf16[256,512]{1,0:T(8,128)(2,1)}, bf16[256,512]{1,0:T(8,128)(2,1)S(1)}, u32[]{:S(2)}, u32[]{:S(2)}) collective-permute-start(bf16[256,512]{1,0:T(8,128)(2,1)} %get-tuple-element.37), channel_id=1, source_target_pairs={{0,1},{1,0},{2,3},{3,2},{4,5},{5,4},{6,7},{7,6},{8,9},{9,8},{10,11... | collective-permute-start | bytes 786440 | tf_op jit(solution)/shard_map/ppermute | solution.py:332
  23.3 70.0 %copy-start.30 = (s32[2]{0:T(128)S(1)}, s32[2]{0:T(128)}, u32[]{:S(2)}) copy-start(s32[2]{0:T(128)} %param.14) | copy-start | bytes 28
  24.4 71.8 %copy-start.1 = (s32[4]{0:T(128)S(1)}, s32[4]{0:T(128)}, u32[]{:S(2)}) copy-start(s32[4]{0:T(128)} %param.12) | copy-start | bytes 52
  24.4 9.2 %collective-permute-start.5 = (bf16[256,512]{1,0:T(8,128)(2,1)S(1)}, bf16[256,512]{1,0:T(8,128)(2,1)S(1)}, u32[]{:S(2)}, u32[]{:S(2)}) collective-permute-start(bf16[256,512]{1,0:T(8,128)(2,1)S(1)} %add_convert_fusion.13), channel_id=1, source_target_pairs={{0,2},{2,0},{1,3},{3,1},{4,6},{6,4},{5,7},{7,5},{8,10},{10,8},{9,1... | collective-permute-start | bytes 786440 | tf_op jit(solution)/shard_map/ppermute | solution.py:332
  26.0 8.2 %collective-permute-start.6 = (bf16[256,512]{1,0:T(8,128)(2,1)}, bf16[256,512]{1,0:T(8,128)(2,1)S(1)}, u32[]{:S(2)}, u32[]{:S(2)}) collective-permute-start(bf16[256,512]{1,0:T(8,128)(2,1)} %get-tuple-element.41), channel_id=1, source_target_pairs={{0,1},{1,0},{2,3},{3,2},{4,5},{5,4},{6,7},{7,6},{8,9},{9,8},{10,11... | collective-permute-start | bytes 786440 | tf_op jit(solution)/shard_map/ppermute | solution.py:332
  26.1 13.1 %collective-permute-start.2 = (bf16[256,512]{1,0:T(8,128)(2,1)S(1)}, bf16[256,512]{1,0:T(8,128)(2,1)S(1)}, u32[]{:S(2)}, u32[]{:S(2)}) collective-permute-start(bf16[256,512]{1,0:T(8,128)(2,1)S(1)} %add_convert_fusion.15), channel_id=1, source_target_pairs={{0,2},{2,0},{1,3},{3,1},{4,6},{6,4},{5,7},{7,5},{8,10},{10,8},{9,1... | collective-permute-start | bytes 786440 | tf_op jit(solution)/shard_map/ppermute | solution.py:332
  27.8 13.8 %collective-permute-start.9 = (bf16[256,512]{1,0:T(8,128)(2,1)}, bf16[256,512]{1,0:T(8,128)(2,1)S(1)}, u32[]{:S(2)}, u32[]{:S(2)}) collective-permute-start(bf16[256,512]{1,0:T(8,128)(2,1)} %get-tuple-element.45), channel_id=1, source_target_pairs={{0,1},{1,0},{2,3},{3,2},{4,5},{5,4},{6,7},{7,6},{8,9},{9,8},{10,11... | collective-permute-start | bytes 786440 | tf_op jit(solution)/shard_map/ppermute | solution.py:332
  28.0 16.9 %collective-permute-start.8 = (bf16[256,512]{1,0:T(8,128)(2,1)S(1)}, bf16[256,512]{1,0:T(8,128)(2,1)S(1)}, u32[]{:S(2)}, u32[]{:S(2)}) collective-permute-start(bf16[256,512]{1,0:T(8,128)(2,1)S(1)} %add_convert_fusion.11), channel_id=1, source_target_pairs={{0,2},{2,0},{1,3},{3,1},{4,6},{6,4},{5,7},{7,5},{8,10},{10,8},{9,1... | collective-permute-start | bytes 786440 | tf_op jit(solution)/shard_map/ppermute | solution.py:332
  33.6 16.0 %collective-permute-start.11 = (bf16[256,512]{1,0:T(8,128)(2,1)S(1)}, bf16[256,512]{1,0:T(8,128)(2,1)S(1)}, u32[]{:S(2)}, u32[]{:S(2)}) collective-permute-start(bf16[256,512]{1,0:T(8,128)(2,1)S(1)} %add_convert_fusion.9), channel_id=1, source_target_pairs={{0,2},{2,0},{1,3},{3,1},{4,6},{6,4},{5,7},{7,5},{8,10},{10,8},{9,1... | collective-permute-start | bytes 786440 | tf_op jit(solution)/shard_map/ppermute | solution.py:332
  34.3 81.4 %copy-start.3 = (bf16[256,512]{1,0:T(8,128)(2,1)}, bf16[256,512]{1,0:T(8,128)(2,1)S(1)}, u32[]{:S(2)}) copy-start(bf16[256,512]{1,0:T(8,128)(2,1)S(1)} %add_convert_fusion.12.rest_1_) | copy-start | bytes 786436
  34.3 59.1 %collective-permute-start.24 = (bf16[320,1280]{1,0:T(8,128)(2,1)S(1)}, bf16[320,1280]{1,0:T(8,128)(2,1)}, u32[]{:S(2)}, u32[]{:S(2)}) collective-permute-start(bf16[320,1280]{1,0:T(8,128)(2,1)S(1)} %get-tuple-element.48), channel_id=1, source_target_pairs={{0,4},{12,8},{1,5},{13,9},{2,6},{14,10},{3,7},{15,11},{16,20},{28,... | collective-permute-start | bytes 2457608 | tf_op jit(solution)/shard_map/ppermute | solution.py:329
  39.2 54.7 %collective-permute-start.25 = (bf16[320,1280]{1,0:T(8,128)(2,1)S(1)}, bf16[320,1280]{1,0:T(8,128)(2,1)}, u32[]{:S(2)}, u32[]{:S(2)}) collective-permute-start(bf16[320,1280]{1,0:T(8,128)(2,1)S(1)} %get-tuple-element.49), channel_id=1, source_target_pairs={{0,4},{12,8},{1,5},{13,9},{2,6},{14,10},{3,7},{15,11},{16,20},{28,... | collective-permute-start | bytes 2457608 | tf_op jit(solution)/shard_map/ppermute | solution.py:329
  41.5 74.1 %copy-start.4 = (bf16[256,512]{1,0:T(8,128)(2,1)}, bf16[256,512]{1,0:T(8,128)(2,1)S(1)}, u32[]{:S(2)}) copy-start(bf16[256,512]{1,0:T(8,128)(2,1)S(1)} %add_convert_fusion.14.rest_0_) | copy-start | bytes 786436
  41.6 8.9 %collective-permute-start.16 = (bf16[256,512]{1,0:T(8,128)(2,1)S(1)}, bf16[256,512]{1,0:T(8,128)(2,1)S(1)}, u32[]{:S(2)}, u32[]{:S(2)}) collective-permute-start(bf16[256,512]{1,0:T(8,128)(2,1)S(1)} %add_convert_fusion.14.rest_0_), channel_id=1, source_target_pairs={{4,8},{8,4},{5,9},{9,5},{6,10},{10,6},{7,11},{11,7},{20,24},{24,20... | collective-permute-start | bytes 786440 | tf_op jit(solution)/shard_map/ppermute | solution.py:329
  44.9 32.6 %collective-permute-start.12 = (bf16[256,512]{1,0:T(8,128)(2,1)S(1)}, bf16[256,512]{1,0:T(8,128)(2,1)S(1)}, u32[]{:S(2)}, u32[]{:S(2)}) collective-permute-start(bf16[256,512]{1,0:T(8,128)(2,1)S(1)} %add_convert_fusion.14.rest_0_), channel_id=1, source_target_pairs={{0,4},{12,8},{1,5},{13,9},{2,6},{14,10},{3,7},{15,11},{16,20},{28,... | collective-permute-start | bytes 786440 | tf_op jit(solution)/shard_map/ppermute | solution.py:329
  49.6 28.5 %collective-permute-start.17 = (bf16[256,512]{1,0:T(8,128)(2,1)S(1)}, bf16[256,512]{1,0:T(8,128)(2,1)S(1)}, u32[]{:S(2)}, u32[]{:S(2)}) collective-permute-start(bf16[256,512]{1,0:T(8,128)(2,1)S(1)} %add_convert_fusion.12.rest_1_), channel_id=1, source_target_pairs={{4,8},{8,4},{5,9},{9,5},{6,10},{10,6},{7,11},{11,7},{20,24},{24,20... | collective-permute-start | bytes 786440 | tf_op jit(solution)/shard_map/ppermute | solution.py:329
  50.4 65.2 %copy-start.5 = (bf16[256,512]{1,0:T(8,128)(2,1)}, bf16[256,512]{1,0:T(8,128)(2,1)S(1)}, u32[]{:S(2)}) copy-start(bf16[256,512]{1,0:T(8,128)(2,1)S(1)} %add_convert_fusion.10.rest_2_) | copy-start | bytes 786436
  50.5 65.2 %copy-start.7 = (bf16[256,512]{1,0:T(8,128)(2,1)}, bf16[256,512]{1,0:T(8,128)(2,1)S(1)}, u32[]{:S(2)}) copy-start(bf16[256,512]{1,0:T(8,128)(2,1)S(1)} %collective-permute-done.16.rest_8_) | copy-start | bytes 786436
  50.5 35.0 %collective-permute-start.13 = (bf16[256,512]{1,0:T(8,128)(2,1)S(1)}, bf16[256,512]{1,0:T(8,128)(2,1)S(1)}, u32[]{:S(2)}, u32[]{:S(2)}) collective-permute-start(bf16[256,512]{1,0:T(8,128)(2,1)S(1)} %add_convert_fusion.12.rest_1_), channel_id=1, source_target_pairs={{0,4},{12,8},{1,5},{13,9},{2,6},{14,10},{3,7},{15,11},{16,20},{28,... | collective-permute-start | bytes 786440 | tf_op jit(solution)/shard_map/ppermute | solution.py:329
  77.4 38.2 %copy-start.8 = (bf16[256,512]{1,0:T(8,128)(2,1)}, bf16[256,512]{1,0:T(8,128)(2,1)S(1)}, u32[]{:S(2)}) copy-start(bf16[256,512]{1,0:T(8,128)(2,1)S(1)} %collective-permute-done.12.rest_4_) | copy-start | bytes 786436
  77.4 8.7 %collective-permute-start.18 = (bf16[256,512]{1,0:T(8,128)(2,1)S(1)}, bf16[256,512]{1,0:T(8,128)(2,1)S(1)}, u32[]{:S(2)}, u32[]{:S(2)}) collective-permute-start(bf16[256,512]{1,0:T(8,128)(2,1)S(1)} %add_convert_fusion.10.rest_2_), channel_id=1, source_target_pairs={{4,8},{8,4},{5,9},{9,5},{6,10},{10,6},{7,11},{11,7},{20,24},{24,20... | collective-permute-start | bytes 786440 | tf_op jit(solution)/shard_map/ppermute | solution.py:329
  78.1 37.6 %copy-start.9 = (bf16[256,512]{1,0:T(8,128)(2,1)}, bf16[256,512]{1,0:T(8,128)(2,1)S(1)}, u32[]{:S(2)}) copy-start(bf16[256,512]{1,0:T(8,128)(2,1)S(1)} %collective-permute-done.17.rest_9_) | copy-start | bytes 786436
  78.1 14.5 %collective-permute-start.14 = (bf16[256,512]{1,0:T(8,128)(2,1)S(1)}, bf16[256,512]{1,0:T(8,128)(2,1)S(1)}, u32[]{:S(2)}, u32[]{:S(2)}) collective-permute-start(bf16[256,512]{1,0:T(8,128)(2,1)S(1)} %add_convert_fusion.10.rest_2_), channel_id=1, source_target_pairs={{0,4},{12,8},{1,5},{13,9},{2,6},{14,10},{3,7},{15,11},{16,20},{28,... | collective-permute-start | bytes 786440 | tf_op jit(solution)/shard_map/ppermute | solution.py:329
  85.5 30.2 %copy-start.6 = (bf16[256,512]{1,0:T(8,128)(2,1)}, bf16[256,512]{1,0:T(8,128)(2,1)S(1)}, u32[]{:S(2)}) copy-start(bf16[256,512]{1,0:T(8,128)(2,1)S(1)} %add_convert_fusion.8.rest_3_) | copy-start | bytes 786436
  85.5 30.2 %copy-start.10 = (bf16[256,512]{1,0:T(8,128)(2,1)}, bf16[256,512]{1,0:T(8,128)(2,1)S(1)}, u32[]{:S(2)}) copy-start(bf16[256,512]{1,0:T(8,128)(2,1)S(1)} %collective-permute-done.13.rest_5_) | copy-start | bytes 786436
  85.5 11.3 %collective-permute-start.19 = (bf16[256,512]{1,0:T(8,128)(2,1)S(1)}, bf16[256,512]{1,0:T(8,128)(2,1)S(1)}, u32[]{:S(2)}, u32[]{:S(2)}) collective-permute-start(bf16[256,512]{1,0:T(8,128)(2,1)S(1)} %add_convert_fusion.8.rest_3_), channel_id=1, source_target_pairs={{4,8},{8,4},{5,9},{9,5},{6,10},{10,6},{7,11},{11,7},{20,24},{24,20... | collective-permute-start | bytes 786440 | tf_op jit(solution)/shard_map/ppermute | solution.py:329
  86.2 29.5 %copy-start.11 = (bf16[256,512]{1,0:T(8,128)(2,1)}, bf16[256,512]{1,0:T(8,128)(2,1)S(1)}, u32[]{:S(2)}) copy-start(bf16[256,512]{1,0:T(8,128)(2,1)S(1)} %collective-permute-done.18.rest_10_) | copy-start | bytes 786436
  86.2 16.2 %collective-permute-start.15 = (bf16[256,512]{1,0:T(8,128)(2,1)S(1)}, bf16[256,512]{1,0:T(8,128)(2,1)S(1)}, u32[]{:S(2)}, u32[]{:S(2)}) collective-permute-start(bf16[256,512]{1,0:T(8,128)(2,1)S(1)} %add_convert_fusion.8.rest_3_), channel_id=1, source_target_pairs={{0,4},{12,8},{1,5},{13,9},{2,6},{14,10},{3,7},{15,11},{16,20},{28,... | collective-permute-start | bytes 786440 | tf_op jit(solution)/shard_map/ppermute | solution.py:329
  92.7 23.0 %copy-start.12 = (bf16[256,512]{1,0:T(8,128)(2,1)}, bf16[256,512]{1,0:T(8,128)(2,1)S(1)}, u32[]{:S(2)}) copy-start(bf16[256,512]{1,0:T(8,128)(2,1)S(1)} %collective-permute-done.14.rest_6_) | copy-start | bytes 786436
  92.7 11.1 %collective-permute-start.20 = (bf16[256,512]{1,0:T(8,128)(2,1)S(1)}, bf16[256,512]{1,0:T(8,128)(2,1)S(1)}, u32[]{:S(2)}, u32[]{:S(2)}) collective-permute-start(bf16[256,512]{1,0:T(8,128)(2,1)S(1)} %collective-permute-done.12.rest_4_), channel_id=1, source_target_pairs={{4,8},{8,4},{5,9},{9,5},{6,10},{10,6},{7,11},{11,7},{20,24},{24,20... | collective-permute-start | bytes 786440 | tf_op jit(solution)/shard_map/ppermute | solution.py:329
  93.4 43.3 %collective-permute-start.26 = (bf16[320,1280]{1,0:T(8,128)(2,1)}, bf16[320,1280]{1,0:T(8,128)(2,1)}, u32[]{:S(2)}, u32[]{:S(2)}) collective-permute-start(bf16[320,1280]{1,0:T(8,128)(2,1)} %collective-permute-done.24), channel_id=1, source_target_pairs={{0,16},{16,0},{1,17},{17,1},{2,18},{18,2},{3,19},{19,3},{4,20},{20... | collective-permute-start | bytes 2457608 | tf_op jit(solution)/shard_map/ppermute | solution.py:369
  94.0 42.7 %collective-permute-start.27 = (bf16[320,1280]{1,0:T(8,128)(2,1)}, bf16[320,1280]{1,0:T(8,128)(2,1)}, u32[]{:S(2)}, u32[]{:S(2)}) collective-permute-start(bf16[320,1280]{1,0:T(8,128)(2,1)} %collective-permute-done.25), channel_id=1, source_target_pairs={{0,16},{16,0},{1,17},{17,1},{2,18},{18,2},{3,19},{19,3},{4,20},{20... | collective-permute-start | bytes 2457608 | tf_op jit(solution)/shard_map/ppermute | solution.py:369
  96.8 18.9 %copy-start.13 = (bf16[256,512]{1,0:T(8,128)(2,1)}, bf16[256,512]{1,0:T(8,128)(2,1)S(1)}, u32[]{:S(2)}) copy-start(bf16[256,512]{1,0:T(8,128)(2,1)S(1)} %collective-permute-done.19.rest_11_) | copy-start | bytes 786436
  96.8 29.3 %collective-permute-start.31 = (bf16[4,64,1280]{2,1,0:T(8,128)(2,1)}, bf16[4,64,1280]{2,1,0:T(8,128)(2,1)}, u32[]{:S(2)}, u32[]{:S(2)}) collective-permute-start(bf16[4,64,1280]{2,1,0:T(8,128)(2,1)} %query_ref.1), channel_id=1, source_target_pairs={{0,4},{12,8},{1,5},{13,9},{2,6},{14,10},{3,7},{15,11},{16,20},{28,... | collective-permute-start | bytes 1966088 | tf_op jit(solution)/shard_map/ppermute | solution.py:329
  102.4 3.3 %collective-permute-start.21 = (bf16[256,512]{1,0:T(8,128)(2,1)S(1)}, bf16[256,512]{1,0:T(8,128)(2,1)}, u32[]{:S(2)}, u32[]{:S(2)}) collective-permute-start(bf16[256,512]{1,0:T(8,128)(2,1)S(1)} %collective-permute-done.13.rest_5_), channel_id=1, source_target_pairs={{4,8},{8,4},{5,9},{9,5},{6,10},{10,6},{7,11},{11,7},{20,24},{24,20... | collective-permute-start | bytes 786440 | tf_op jit(solution)/shard_map/ppermute | solution.py:329
  103.8 8.6 %collective-permute-start.22 = (bf16[256,512]{1,0:T(8,128)(2,1)S(1)}, bf16[256,512]{1,0:T(8,128)(2,1)}, u32[]{:S(2)}, u32[]{:S(2)}) collective-permute-start(bf16[256,512]{1,0:T(8,128)(2,1)S(1)} %collective-permute-done.14.rest_6_), channel_id=1, source_target_pairs={{4,8},{8,4},{5,9},{9,5},{6,10},{10,6},{7,11},{11,7},{20,24},{24,20... | collective-permute-start | bytes 786440 | tf_op jit(solution)/shard_map/ppermute | solution.py:329
  105.7 20.4 %collective-permute-start.32 = (bf16[4,64,512]{2,1,0:T(8,128)(2,1)}, bf16[4,64,512]{2,1,0:T(8,128)(2,1)}, u32[]{:S(2)}, u32[]{:S(2)}) collective-permute-start(bf16[4,64,512]{2,1,0:T(8,128)(2,1)} %new_ref.1), channel_id=1, source_target_pairs={{0,4},{12,8},{1,5},{13,9},{2,6},{14,10},{3,7},{15,11},{16,20},{28,... | collective-permute-start | bytes 786440 | tf_op jit(solution)/shard_map/ppermute | solution.py:329
  112.4 3.2 %collective-permute-start.23 = (bf16[256,512]{1,0:T(8,128)(2,1)S(1)}, bf16[256,512]{1,0:T(8,128)(2,1)}, u32[]{:S(2)}, u32[]{:S(2)}) collective-permute-start(bf16[256,512]{1,0:T(8,128)(2,1)S(1)} %collective-permute-done.15.rest_7_), channel_id=1, source_target_pairs={{4,8},{8,4},{5,9},{9,5},{6,10},{10,6},{7,11},{11,7},{20,24},{24,20... | collective-permute-start | bytes 786440 | tf_op jit(solution)/shard_map/ppermute | solution.py:329
  125.4 29.6 %collective-permute-start.36 = (bf16[4,64,1280]{2,1,0:T(8,128)(2,1)}, bf16[4,64,1280]{2,1,0:T(8,128)(2,1)S(1)}, u32[]{:S(2)}, u32[]{:S(2)}) collective-permute-start(bf16[4,64,1280]{2,1,0:T(8,128)(2,1)} %attend.2), channel_id=1, source_target_pairs={{4,8},{8,4},{5,9},{9,5},{6,10},{10,6},{7,11},{11,7},{20,24},{24,20... | collective-permute-start | bytes 1966088 | tf_op jit(solution)/shard_map/ppermute | solution.py:329
  135.8 26.7 %collective-permute-start.40 = (bf16[4,64,1280]{2,1,0:T(8,128)(2,1)}, bf16[4,64,1280]{2,1,0:T(8,128)(2,1)S(1)}, u32[]{:S(2)}, u32[]{:S(2)}) collective-permute-start(bf16[4,64,1280]{2,1,0:T(8,128)(2,1)} %attend.3), channel_id=1, source_target_pairs={{4,8},{8,4},{5,9},{9,5},{6,10},{10,6},{7,11},{11,7},{20,24},{24,20... | collective-permute-start | bytes 1966088 | tf_op jit(solution)/shard_map/ppermute | solution.py:329
  147.8 22.8 %collective-permute-start.33 = (bf16[4,64,1280]{2,1,0:T(8,128)(2,1)}, bf16[4,64,1280]{2,1,0:T(8,128)(2,1)S(1)}, u32[]{:S(2)}, u32[]{:S(2)}) collective-permute-start(bf16[4,64,1280]{2,1,0:T(8,128)(2,1)} %bitcast.34), channel_id=1, source_target_pairs={{0,1},{1,0},{2,3},{3,2},{4,5},{5,4},{6,7},{7,6},{8,9},{9,8},{10,11... | collective-permute-start | bytes 1966088 | tf_op jit(solution)/shard_map/ppermute | solution.py:332
  154.5 17.7 %collective-permute-start.28 = (bf16[4,64,1280]{2,1,0:T(8,128)(2,1)}, bf16[4,64,1280]{2,1,0:T(8,128)(2,1)S(1)}, u32[]{:S(2)}, u32[]{:S(2)}) collective-permute-start(bf16[4,64,1280]{2,1,0:T(8,128)(2,1)} %bitcast.32), channel_id=1, source_target_pairs={{0,1},{1,0},{2,3},{3,2},{4,5},{5,4},{6,7},{7,6},{8,9},{9,8},{10,11... | collective-permute-start | bytes 1966088 | tf_op jit(solution)/shard_map/ppermute | solution.py:332
  162.5 11.1 %collective-permute-start.37 = (bf16[4,64,1280]{2,1,0:T(8,128)(2,1)}, bf16[4,64,1280]{2,1,0:T(8,128)(2,1)S(1)}, u32[]{:S(2)}, u32[]{:S(2)}) collective-permute-start(bf16[4,64,1280]{2,1,0:T(8,128)(2,1)} %bitcast.33), channel_id=1, source_target_pairs={{0,1},{1,0},{2,3},{3,2},{4,5},{5,4},{6,7},{7,6},{8,9},{9,8},{10,11... | collective-permute-start | bytes 1966088 | tf_op jit(solution)/shard_map/ppermute | solution.py:332
  170.1 5.1 %collective-permute-start.41 = (bf16[4,64,1280]{2,1,0:T(8,128)(2,1)}, bf16[4,64,1280]{2,1,0:T(8,128)(2,1)S(1)}, u32[]{:S(2)}, u32[]{:S(2)}) collective-permute-start(bf16[4,64,1280]{2,1,0:T(8,128)(2,1)} %bitcast.35), channel_id=1, source_target_pairs={{0,1},{1,0},{2,3},{3,2},{4,5},{5,4},{6,7},{7,6},{8,9},{9,8},{10,11... | collective-permute-start | bytes 1966088 | tf_op jit(solution)/shard_map/ppermute | solution.py:332
  170.6 30.9 %copy-start.20 = (bf16[256,1280]{1,0:T(8,128)(2,1)S(1)}, bf16[256,1280]{1,0:T(8,128)(2,1)}, u32[]{:S(2)}) copy-start(bf16[256,1280]{1,0:T(8,128)(2,1)} %get-tuple-element.56) | copy-start | bytes 1966084
  170.7 10.6 %collective-permute-start.34 = (bf16[2,64,1280]{2,1,0:T(8,128)(2,1)S(1)}, bf16[2,64,1280]{2,1,0:T(8,128)(2,1)S(1)}, u32[]{:S(2)}, u32[]{:S(2)}) collective-permute-start(bf16[2,64,1280]{2,1,0:T(8,128)(2,1)S(1)} %add_convert_fusion.5), channel_id=1, source_target_pairs={{0,2},{2,0},{1,3},{3,1},{4,6},{6,4},{5,7},{7,5},{8,10},{10,8},{9,1... | collective-permute-start | bytes 983048 | tf_op jit(solution)/shard_map/ppermute | solution.py:332
  173.1 29.9 %collective-permute-start.29 = (bf16[2,64,1280]{2,1,0:T(8,128)(2,1)}, bf16[2,64,1280]{2,1,0:T(8,128)(2,1)}, u32[]{:S(2)}, u32[]{:S(2)}) collective-permute-start(bf16[2,64,1280]{2,1,0:T(8,128)(2,1)} %add_convert_fusion.7), channel_id=1, source_target_pairs={{0,2},{2,0},{1,3},{3,1},{4,6},{6,4},{5,7},{7,5},{8,10},{10,8},{9,1... | collective-permute-start | bytes 983048 | tf_op jit(solution)/shard_map/ppermute | solution.py:332
  173.7 21.7 %collective-permute-start.38 = (bf16[2,64,1280]{2,1,0:T(8,128)(2,1)S(1)}, bf16[2,64,1280]{2,1,0:T(8,128)(2,1)S(1)}, u32[]{:S(2)}, u32[]{:S(2)}) collective-permute-start(bf16[2,64,1280]{2,1,0:T(8,128)(2,1)S(1)} %add_convert_fusion.3), channel_id=1, source_target_pairs={{0,2},{2,0},{1,3},{3,1},{4,6},{6,4},{5,7},{7,5},{8,10},{10,8},{9,1... | collective-permute-start | bytes 983048 | tf_op jit(solution)/shard_map/ppermute | solution.py:332
  176.3 25.2 %collective-permute-start.42 = (bf16[2,64,1280]{2,1,0:T(8,128)(2,1)S(1)}, bf16[2,64,1280]{2,1,0:T(8,128)(2,1)S(1)}, u32[]{:S(2)}, u32[]{:S(2)}) collective-permute-start(bf16[2,64,1280]{2,1,0:T(8,128)(2,1)S(1)} %add_convert_fusion.1), channel_id=1, source_target_pairs={{0,2},{2,0},{1,3},{3,1},{4,6},{6,4},{5,7},{7,5},{8,10},{10,8},{9,1... | collective-permute-start | bytes 983048 | tf_op jit(solution)/shard_map/ppermute | solution.py:332
  182.2 21.1 %collective-permute-start.35 = (bf16[2,64,1280]{2,1,0:T(8,128)(2,1)}, bf16[2,64,1280]{2,1,0:T(8,128)(2,1)}, u32[]{:S(2)}, u32[]{:S(2)}) collective-permute-start(bf16[2,64,1280]{2,1,0:T(8,128)(2,1)} %add_convert_fusion.4), channel_id=1, source_target_pairs={{4,0},{8,12},{5,1},{9,13},{6,2},{10,14},{7,3},{11,15},{20,16},{24,... | collective-permute-start | bytes 983048 | tf_op jit(solution)/shard_map/ppermute | solution.py:329
  195.5 7.8 %collective-permute-start.39 = (bf16[2,64,1280]{2,1,0:T(8,128)(2,1)S(1)}, bf16[2,64,1280]{2,1,0:T(8,128)(2,1)S(1)}, u32[]{:S(2)}, u32[]{:S(2)}) collective-permute-start(bf16[2,64,1280]{2,1,0:T(8,128)(2,1)S(1)} %add_convert_fusion.2), channel_id=1, source_target_pairs={{4,8},{8,4},{5,9},{9,5},{6,10},{10,6},{7,11},{11,7},{20,24},{24,20... | collective-permute-start | bytes 983048 | tf_op jit(solution)/shard_map/ppermute | solution.py:329
  201.6 23.5 %collective-permute-start.43 = (bf16[2,64,1280]{2,1,0:T(8,128)(2,1)S(1)}, bf16[2,64,1280]{2,1,0:T(8,128)(2,1)S(1)}, u32[]{:S(2)}, u32[]{:S(2)}) collective-permute-start(bf16[2,64,1280]{2,1,0:T(8,128)(2,1)S(1)} %add_convert_fusion), channel_id=1, source_target_pairs={{4,12},{8,0},{5,13},{9,1},{6,14},{10,2},{7,15},{11,3},{20,28},{24,... | collective-permute-start | bytes 983048 | tf_op jit(solution)/shard_map/ppermute | solution.py:329
  226.5 8.6 %collective-permute-start.44 = (bf16[2,64,1280]{2,1,0:T(8,128)(2,1)S(1)}, bf16[2,64,1280]{2,1,0:T(8,128)(2,1)S(1)}, u32[]{:S(2)}, u32[]{:S(2)}) collective-permute-start(bf16[2,64,1280]{2,1,0:T(8,128)(2,1)S(1)} %broadcast_select_fusion.1), channel_id=1, source_target_pairs={{0,2},{2,0},{1,3},{3,1},{4,6},{6,4},{5,7},{7,5},{8,10},{10,8},{9,1... | collective-permute-start | bytes 983048 | tf_op jit(solution)/shard_map/ppermute | solution.py:332
  (12 other events, 104.7 us)

commit v2 on v0

--- a/solution.py
+++ b/solution.py
@@ -3,6 +3,8 @@
 import jax
 import jax.numpy as jnp
 from jax import lax
+from jax.experimental import pallas as pl
+from jax.experimental.pallas import tpu as pltpu
 from jax.sharding import PartitionSpec as P
 
 HD = 128
@@ -40,7 +42,7 @@
     return (summed, peak_score, totals)
 
 
-def on_device(
+def general_plan(
     prompt_states,
     prompt_lengths,
     prompt_owner,
@@ -131,7 +133,424 @@
     return mixed.astype(jnp.bfloat16).reshape(step_count, row_total, mixed.shape[1])
 
 
+FIRST_VMEM = 60 * 1024 * 1024
+VMEM = 24 * 1024 * 1024
+
+CORE = [(0, 1), (1, 0), (2, 3), (3, 2)]
+ACROSS_X = [(0, 2), (2, 0), (1, 3), (3, 1)]
+INWARD = [(0, 1), (3, 2)]
+MIDDLE = [(1, 2), (2, 1)]
+
+
+def compiler_params(limit=VMEM):
+    return pltpu.CompilerParams(vmem_limit_bytes=limit)
+
+
+def small_cost():
+    return pl.CostEstimate(flops=64, bytes_accessed=64, transcendentals=0)
+
+
+def project(limit, here, states, weight, masks, cuts):
+    features, width = weight.shape[0], weight.shape[1] // 4
+    parts = [(low, high - low) for low, high in zip(cuts[:-1], cuts[1:])]
+
+    def body(here_ref, state_any, weight_any, *rest):
+        outs, (state, blocks, state_sems, block_sems) = rest[: 2 * len(parts)], rest[2 * len(parts) :]
+        fetches, blocks_in = [], []
+        for side in range(2):
+            place = here_ref[2] ^ masks[side]
+            columns = pl.ds(pl.multiple_of(place * width, width), width)
+            blocks_in.append(
+                pltpu.make_async_copy(
+                    weight_any.at[:, columns], blocks.at[side], block_sems.at[side]
+                )
+            )
+        for at, (low, rows) in enumerate(parts):
+            fetches.append(
+                pltpu.make_async_copy(
+                    state_any.at[low : low + rows], state.at[low : low + rows], state_sems.at[at]
+                )
+            )
+        blocks_in[0].start()
+        fetches[0].start()
+        blocks_in[1].start()
+        for fetch in fetches[1:]:
+            fetch.start()
+        for at, (low, rows) in enumerate(parts):
+            fetches[at].wait()
+            for side in range(2):
+                if at == 0:
+                    blocks_in[side].wait()
+                outs[side * len(parts) + at][...] = jnp.dot(
+                    state[low : low + rows], blocks[side], preferred_element_type=jnp.float32
+                ).astype(jnp.bfloat16)
+
+    in_any = pl.BlockSpec(memory_space=pl.ANY)
+    in_vmem = pl.BlockSpec(memory_space=pltpu.VMEM)
+    outs = pl.pallas_call(
+        body,
+        in_specs=[pl.BlockSpec(memory_space=pltpu.SMEM), in_any, in_any],
+        out_specs=[in_vmem] * (2 * len(parts)),
+        out_shape=[jax.ShapeDtypeStruct((rows, width), jnp.bfloat16) for _, rows in parts] * 2,
+        scratch_shapes=[
+            pltpu.VMEM(states.shape, jnp.bfloat16),
+            pltpu.VMEM((2, features, width), jnp.bfloat16),
+            pltpu.SemaphoreType.DMA((len(parts),)),
+            pltpu.SemaphoreType.DMA((2,)),
+        ],
+        compiler_params=compiler_params(limit),
+        cost_estimate=small_cost(),
+        name="project",
+    )(here, states, weight)
+    return outs[: len(parts)], outs[len(parts) :]
+
+
+def attend(here, prompts, owners, lengths, queries, news, pages):
+    steps, rows, width = queries.shape
+    blocks = prompts.shape[0]
+    block_rows = rows // blocks
+    new_width = news.shape[2]
+    groups = new_width // (2 * HD)
+    sizes = [part.shape[0] for part in pages[0]]
+    starts = [sum(sizes[:at]) for at in range(len(sizes))]
+    tokens = sum(sizes)
+    tiles = 4
+    chunk = tokens // tiles
+    flat = steps * block_rows
+    factor = math.log2(math.e) / math.sqrt(HD)
+
+    def body(here_ref, prompts_ref, owners_ref, lengths_ref, query_any, new_any, *rest):
+        page_refs, rest = rest[: 4 * len(sizes)], rest[4 * len(sizes) :]
+        out_ref, held, query_ref, new_ref, sems = rest
+        plane = here_ref[1]
+
+        def run(mine, used, length):
+            query = query_ref[...].reshape(flat, width)
+            new = new_ref[...].reshape(flat, new_width)
+            shape = (GQA * flat, flat)
+            asker = lax.broadcasted_iota(jnp.int32, shape, 0) % flat
+            holder = lax.broadcasted_iota(jnp.int32, shape, 1)
+            near_ok = jnp.logical_and(asker % block_rows == holder % block_rows, holder <= asker)
+            last = (GQA * flat, chunk)
+            last_ok = lax.broadcasted_iota(jnp.int32, last, 1) < length - (used - chunk)
+            for group in range(groups):
+                key = slice(2 * group * HD, (2 * group + 1) * HD)
+                value = slice((2 * group + 1) * HD, (2 * group + 2) * HD)
+                asked = jnp.concatenate(
+                    [
+                        query[:, (group * GQA + head) * HD : (group * GQA + head + 1) * HD]
+                        for head in range(GQA)
+                    ],
+                    axis=0,
+                )
+
+                def scores(keys):
+                    return lax.dot_general(
+                        asked, keys, (((1,), (1,)), ((), ())), preferred_element_type=jnp.float32
+                    )
+
+                parts = [
+                    scores(held[at * chunk : (at + 1) * chunk, key]) for at in range(used // chunk)
+                ]
+                parts[-1] = jnp.where(last_ok, parts[-1], masked_score)
+                parts.append(jnp.where(near_ok, scores(new[:, key]), masked_score))
+                peak = jnp.max(parts[0], axis=1, keepdims=True)
+                for part in parts[1:]:
+                    peak = jnp.maximum(peak, jnp.max(part, axis=1, keepdims=True))
+                total, summed = 0.0, 0.0
+                for at, part in enumerate(parts):
+                    weights = jnp.exp2((part - peak) * factor)
+                    total = total + jnp.sum(weights, axis=1, keepdims=True)
+                    values = (
+                        held[at * chunk : (at + 1) * chunk, value]
+                        if at < len(parts) - 1
+                        else new[:, value]
+                    )
+                    summed = summed + jnp.dot(
+                        weights.astype(jnp.bfloat16), values, preferred_element_type=jnp.float32
+                    )
+                result = (summed / total).astype(jnp.bfloat16)
+                for head in range(GQA):
+                    column = (group * GQA + head) * HD
+                    out_ref[:, mine, column : column + HD] = result[
+                        head * flat : (head + 1) * flat
+                    ].reshape(steps, block_rows, HD)
+
+        @pl.loop(0, blocks)
+        def _(block):
+            mine = pl.ds(pl.multiple_of(block * block_rows, block_rows), block_rows)
+            prompt = prompts_ref[block]
+            slot, length = owners_ref[prompt], lengths_ref[prompt]
+            fetch_query = pltpu.make_async_copy(query_any.at[:, mine], query_ref, sems.at[0])
+            fetch_new = pltpu.make_async_copy(new_any.at[:, mine], new_ref, sems.at[1])
+            fetch_query.start()
+            fetch_new.start()
+            for which, place in enumerate((plane, plane ^ 1, 3 - plane, (3 - plane) ^ 1)):
+
+                @pl.when(slot == place)
+                def _():
+                    fetches = [
+                        pltpu.make_async_copy(
+                            page_refs[which * len(sizes) + at],
+                            held.at[low : low + size],
+                            sems.at[2 + at],
+                        )
+                        for at, (low, size) in enumerate(zip(starts, sizes))
+                    ]
+                    for fetch in fetches:
+                        fetch.start()
+                    for fetch in fetches:
+                        fetch.wait()
+
+            fetch_query.wait()
+            fetch_new.wait()
+            for count in range(1, tiles + 1):
+                enough = length > (count - 1) * chunk
+                if count < tiles:
+                    enough = jnp.logical_and(enough, length <= count * chunk)
+
+                @pl.when(enough)
+                def _():
+                    run(mine, count * chunk, length)
+
+    in_vmem, in_smem, in_any = (
+        pl.BlockSpec(memory_space=space) for space in (pltpu.VMEM, pltpu.SMEM, pl.ANY)
+    )
+    return pl.pallas_call(
+        body,
+        in_specs=[in_smem] * 4 + [in_any] * (2 + 4 * len(sizes)),
+        out_specs=in_vmem,
+        out_shape=jax.ShapeDtypeStruct(queries.shape, jnp.bfloat16),
+        scratch_shapes=[
+            pltpu.VMEM((tokens, new_width), jnp.bfloat16),
+            pltpu.VMEM((steps, block_rows, width), jnp.bfloat16),
+            pltpu.VMEM((steps, block_rows, new_width), jnp.bfloat16),
+            pltpu.SemaphoreType.DMA((2 + len(sizes),)),
+        ],
+        compiler_params=compiler_params(),
+        cost_estimate=small_cost(),
+        name="attend",
+    )(here, prompts, owners, lengths, queries, news, *[part for page in pages for part in page])
+
+
+def spread(here, rows, own_weight, moved_weight):
+    steps, count, features = rows.shape
+    columns = own_weight.shape[1]
+    tile = 256 if columns % 256 == 0 else columns
+
+    def body(here_ref, row_ref, own_ref, moved_ref, keep_ref, send_ref):
+        taken = row_ref[...].reshape(steps * count, features)
+        keeps_own = (here_ref[1] ^ here_ref[2]) % 2 == 0
+        for column in range(0, columns, tile):
+            part = slice(column, column + tile)
+            own = jnp.dot(taken, own_ref[:, part], preferred_element_type=jnp.float32)
+            moved = jnp.dot(taken, moved_ref[:, part], preferred_element_type=jnp.float32)
+            keep = jnp.where(keeps_own, own, moved).astype(jnp.bfloat16)
+            send = jnp.where(keeps_own, moved, own).astype(jnp.bfloat16)
+            keep_ref[:, :, part] = keep.reshape(steps, count, tile)
+            send_ref[:, :, part] = send.reshape(steps, count, tile)
+
+    in_vmem = pl.BlockSpec(memory_space=pltpu.VMEM)
+    out_shape = jax.ShapeDtypeStruct((steps, count, columns), jnp.bfloat16)
+    return pl.pallas_call(
+        body,
+        in_specs=[pl.BlockSpec(memory_space=pltpu.SMEM)] + [in_vmem] * 3,
+        out_specs=[in_vmem, in_vmem],
+        out_shape=[out_shape, out_shape],
+        compiler_params=compiler_params(),
+        cost_estimate=small_cost(),
+        name="spread",
+    )(here, rows, own_weight, moved_weight)
+
+
+def run_small(body, name, here, operands, out_shape):
+    in_vmem = pl.BlockSpec(memory_space=pltpu.VMEM)
+    return pl.pallas_call(
+        body,
+        in_specs=[pl.BlockSpec(memory_space=pltpu.SMEM)] + [in_vmem] * len(operands),
+        out_specs=in_vmem,
+        out_shape=jax.ShapeDtypeStruct(out_shape, jnp.bfloat16),
+        compiler_params=compiler_params(),
+        cost_estimate=small_cost(),
+        name=name,
+    )(here, *operands)
+
+
+def added(here, *parts):
+    def body(_, *refs):
+        total = refs[0][...].astype(jnp.float32)
+        for ref in refs[1:-1]:
+            total = total + ref[...].astype(jnp.float32)
+        refs[-1][...] = total.astype(jnp.bfloat16)
+
+    return run_small(body, "added", here, parts, parts[0].shape)
+
+
+def added_half(here, mine, wide, *narrow):
+    half = wide[0].shape[0] // 2
+
+    def body(here_ref, *refs):
+        chip = here_ref[2] // 2
+        steps = pl.ds((chip if mine else 1 - chip) * half, half)
+        total = refs[0][steps].astype(jnp.float32)
+        for at, ref in enumerate(refs[1:-1], 1):
+            part = ref[steps] if at < len(wide) else ref[...]
+            total = total + part.astype(jnp.float32)
+        refs[-1][...] = total.astype(jnp.bfloat16)
+
+    shape = (half, *wide[0].shape[1:])
+    return run_small(body, "added_half", here, (*wide, *narrow), shape)
+
+
+def after(value, *others):
+    return lax.optimization_barrier((value, *others))[0]
+
+
+def sent_home(value, target):
+    same, turned = [], []
+    for source in (1, 2):
+        side = source // 2
+        for at in range(2):
+            goal = target(source) * 4 + 2 * side + at
+            same.append((source * 4 + 2 * side + at, goal))
+            turned.append((source * 4 + 2 * (1 - side) + at, goal))
+    return [lax.ppermute(value, ("samp", "head"), pairs) for pairs in (same, turned)]
+
+
+def across_home(value):
+    pairs = [
+        (source * 4 + 2 * (1 - source // 2) + at, source * 4 + 2 * (source // 2) + at)
+        for source in (1, 2)
+        for at in range(2)
+    ]
+    return lax.ppermute(value, ("samp", "head"), pairs)
+
+
+def inward_plan(
+    prompt_states,
+    prompt_lengths,
+    prompt_owner,
+    kv_weight,
+    sampler_prompts,
+    step_queries,
+    step_kv,
+    out_weight,
+):
+    group, plane, head = (lax.axis_index(name) for name in ("groups", "samp", "head"))
+    chip = head // 2
+    here = jnp.stack([group, plane, head]).astype(jnp.int32)
+
+    def on_samp(value, pairs):
+        return lax.ppermute(value, "samp", pairs)
+
+    def on_head(value, pairs):
+        return lax.ppermute(value, "head", pairs)
+
+    half = out_weight.shape[0] // 2
+    cut = half * 7 // 10
+
+    def weight_part(low, size, *others):
+        part = lax.dynamic_slice_in_dim(after(out_weight, *others), group * half + low, size, 0)
+        return on_samp(part, INWARD)
+
+    weight_first = weight_part(0, cut)
+    end_news = on_samp(step_kv, INWARD)
+
+    states = prompt_states[0]
+    tokens = states.shape[0]
+    cuts = [0, tokens * 3 // 8, tokens]
+    sent, kept = project(FIRST_VMEM, here, states, kv_weight, (3, 2), cuts)
+    leaving_first = added(here, kept[0], on_head(sent[0], CORE))
+    leaving_second = added(here, kept[1], after(on_head(sent[1], CORE), leaving_first))
+    crossed_first = on_head(leaving_first, ACROSS_X)
+    crossed_second = on_head(leaving_second, ACROSS_X)
+    sent, kept = project(
+        VMEM, here, after(states, leaving_first, leaving_second), kv_weight, (1, 0), cuts
+    )
+    sent = [on_head(value, CORE) for value in sent]
+    first = added(here, after(kept[0], end_news), sent[0], crossed_first)
+    end_first = on_samp(after(first, weight_first), INWARD)
+    far_first = on_samp(first, MIDDLE)
+    far_end_first = on_samp(end_first, MIDDLE)
+    second = added(here, kept[1], after(sent[1], far_first, far_end_first), crossed_second)
+    end_second = on_samp(second, INWARD)
+    far_second = on_samp(second, MIDDLE)
+    moved_first = lax.ppermute(weight_first, "groups", [(0, 1), (1, 0)])
+    far_end_second = on_samp(after(end_second, far_second, moved_first), MIDDLE)
+    pages = (
+        (first, second),
+        (end_first, end_second),
+        (far_first, far_second),
+        (far_end_first, far_end_second),
+    )
+    weight_second = weight_part(cut, half - cut, end_second)
+
+    def attended(prompts, queries, news):
+        return attend(here, prompts, prompt_owner, prompt_lengths, queries, news, pages)
+
+    end_prompts = on_samp(after(sampler_prompts, second), INWARD)
+    end_queries = on_samp(after(step_queries, weight_second), INWARD)
+    moved_second = lax.ppermute(weight_second, "groups", [(0, 1), (1, 0)])
+    mine = jnp.concatenate([weight_first, weight_second], axis=0)
+    other = jnp.concatenate([moved_first, moved_second], axis=0)
+    moved_weight = jnp.where(
+        group == 0,
+        jnp.concatenate([mine, other], axis=0),
+        jnp.concatenate([other, mine], axis=0),
+    )
+
+    def spread_out(rows):
+        keep, send = spread(here, rows, out_weight, moved_weight)
+        return keep, on_head(send, CORE)
+
+    own_rows = attended(sampler_prompts, after(step_queries, weight_second), step_kv)
+    far_own_rows = on_samp(own_rows, MIDDLE)
+    own_keep, own_arrived = spread_out(own_rows)
+    end_rows = attended(end_prompts, after(end_queries, own_keep), end_news)
+    far_end_rows = on_samp(end_rows, MIDDLE)
+    own_chip = added(here, own_keep, after(own_arrived, end_rows))
+    own_crossed = across_home(own_chip)
+    far_keep, far_arrived = spread_out(after(far_own_rows, own_chip))
+    end_keep, end_arrived = spread_out(after(end_rows, far_keep))
+    far_leaving = added_half(here, False, (far_keep, after(far_arrived, end_keep)))
+    far_crossed = on_head(far_leaving, ACROSS_X)
+    end_leaving = added_half(here, False, (end_keep, after(end_arrived, far_leaving)))
+    end_crossed = on_head(end_leaving, ACROSS_X)
+    own_home = added(here, own_chip, after(own_crossed, end_leaving))
+    beyond_keep, beyond_arrived = spread_out(after(far_end_rows, own_home))
+    beyond_leaving = added_half(here, False, (beyond_keep, beyond_arrived))
+    beyond_crossed = on_head(beyond_leaving, ACROSS_X)
+    far_sum = added_half(here, True, (far_keep, after(far_arrived, beyond_leaving)), far_crossed)
+    far_home = sent_home(far_sum, lambda at: 3 - at)
+    end_sum = added_half(here, True, (end_keep, after(end_arrived, far_sum)), end_crossed)
+    end_home = sent_home(end_sum, lambda at: at ^ 1)
+    beyond_sum = added_half(
+        here, True, (beyond_keep, after(beyond_arrived, *far_home)), beyond_crossed
+    )
+    beyond_home = sent_home(beyond_sum, lambda at: (3 - at) ^ 1)
+
+    is_middle = jnp.logical_or(plane == 1, plane == 2)
+    near_side = chip == plane // 2
+    straight, turned = (
+        jnp.where(is_middle, far_home[which], jnp.where(near_side, end_home[which], beyond_home[which]))
+        for which in range(2)
+    )
+    return jnp.where(
+        jnp.logical_and(is_middle, near_side),
+        own_home,
+        jnp.where(
+            chip == 0,
+            jnp.concatenate([straight, turned], axis=0),
+            jnp.concatenate([turned, straight], axis=0),
+        ),
+    )
+
+
 def solution(mesh):
+    line, width = mesh.shape["samp"], mesh.shape["head"]
+    paired = line == 4 and width == 4 and mesh.shape["groups"] == 2
+    on_device = inward_plan if paired else general_plan
+
     placed = (
         P(("groups", "samp"), None, "head"),
         P("groups"),

time: 425 us -> 228 us (0.54)
  the two profiles are of different devices: /device:TPU:6 before, /device:TPU:0 now
where the time goes in v2:
time: 228 us; the launch traced here: 227 us
  waiting for transfers between devices  99.1 us (43%)
  starting transfers between devices  65.1 us (29%)
  Pallas kernels  41 us (18%)
  local copies, waits for them, and re-layouts  15.7 us (7%)
  other arithmetic  5.11 us (2%)
    ppermute x13, starting transfers between devices, on_samp(): return lax.ppermute(value, 'samp', pairs)  49.6 us
    ppermute x6, waiting for transfers between devices, sent_home(): lax.ppermute(value, ('samp', 'head'), pairs)  43.6 us
    ppermute x13, waiting for transfers between devices, on_head(): return lax.ppermute(value, 'head', pairs)  25 us
    ppermute x13, waiting for transfers between devices, on_samp(): return lax.ppermute(value, 'samp', pairs)  22.1 us
    unnamed x54, local copies, waits for them, and re-layouts  13.4 us
    pallas_call x2, Pallas kernels, attend(): pl.pallas_call(body, in_specs=[in_smem] * 4 + [in_any] * (2 + 4 * len(siz...  11.2 us
    pallas_call x2, Pallas kernels, project(): pl.pallas_call(body, in_specs=[pl.BlockSpec(memory_space=pltpu.SMEM), in_...  11.1 us
    pallas_call x4, Pallas kernels, spread(): pl.pallas_call(body, in_specs=[pl.BlockSpec(memory_space=pltpu.SMEM)] + [...  9.73 us
  transfers between devices with their start and end apart: 35, of which 12 were waited for; matrix products, arithmetic and copies ran while one was open for 2% of the time, Pallas kernels for 15%

profile of v2, /device:TPU:0, one launch (start us, length us, event | category | flops | bytes accessed | tf_op | source)
XLA Modules:
  0.0 226.7 jit_solution(14946858362550835385)
XLA Ops:
  0.0 2.3 %constant_dynamic-slice_fusion.1 = bf16[448,1280]{1,0:T(8,128)(2,1)} fusion(bf16[1280,1280]{1,0:T(8,128)(2,1)} %own_ref.7, s32[]{:T(128)S(6)} %select_n.61), kind=kLoop, calls=%fused_computation.7 | loop fusion | bytes 2293764 | tf_op jit(solution)/shard_map/dynamic_slice | solution.py:453
  2.3 6.0 %collective-permute-start.7 = (bf16[448,1280]{1,0:T(8,128)(2,1)}, bf16[448,1280]{1,0:T(8,128)(2,1)}, u32[]{:S(2)}, u32[]{:S(2)}) collective-permute-start(bf16[448,1280]{1,0:T(8,128)(2,1)} %constant_dynamic-slice_fusion.1), channel_id=1, source_target_pairs={{0,4},{12,8},{1,5},{13,9},{2,6},{14,10},{3,7},{15,11},{16,20},{28,... | collective-permute-start | bytes 3440648 | tf_op jit(solution)/shard_map/ppermute | solution.py:444
  9.0 6.4 %project.2 = (bf16[384,512]{1,0:T(8,128)(2,1)}, bf16[640,512]{1,0:T(8,128)(2,1)}, bf16[384,512]{1,0:T(8,128)(2,1)}, bf16[640,512]{1,0:T(8,128)(2,1)}) custom-call(s32[3]{0:T(128)} %pad_add_fusion.here_ref._, bf16[1024,1280]{1,0:T(8,128)(2,1)} %bitcast.4, bf16[1280,2048]{1,0:T(8,128)(2,1)} %weight_any.3), custom_call_target="tpu_custom_call" | custom-call | flops 64 | bytes 64 | tf_op jit(solution)/shard_map/project/pallas_call | solution.py:190
  16.0 2.4 %collective-permute-done.refs_1_ = bf16[384,512]{1,0:T(8,128)(2,1)S(1)} collective-permute-done((bf16[384,512]{1,0:T(8,128)(2,1)}, bf16[384,512]{1,0:T(8,128)(2,1)S(1)}, u32[]{:S(2)}, u32[]{:S(2)}) %collective-permute-start) | collective-permute-done | bytes 393248 | tf_op jit(solution)/shard_map/ppermute | solution.py:447
  18.4 1.0 copy-done.19
  20.0 1.6 collective-permute-start.5
  21.5 1.1 copy-done.17
  22.6 0.7 added.7
  23.4 2.5 %copy-done.1 = bf16[1280,2048]{1,0:T(8,128)(2,1)S(1)} copy-done((bf16[1280,2048]{1,0:T(8,128)(2,1)S(1)}, bf16[1280,2048]{1,0:T(8,128)(2,1)}, u32[]{:S(2)}) %copy-start.1) | copy-done | bytes 5242904
  25.8 4.7 %project.3 = (bf16[384,512]{1,0:T(8,128)(2,1)S(1)}, bf16[640,512]{1,0:T(8,128)(2,1)S(1)}, bf16[384,512]{1,0:T(8,128)(2,1)S(1)}, bf16[640,512]{1,0:T(8,128)(2,1)S(1)}) custom-call(s32[3]{0:T(128)S(1)} %copy-done.23, bf16[1024,1280]{1,0:T(8,128)(2,1)S(1)} %bitcast.5, bf16[1280,2048]{1,0:T(8,128)(2,1)S(1)} %copy-done.1), custom_call_target="tpu_custom_call" | custom-call | flops 64 | bytes 64 | tf_op jit(solution)/shard_map/project/pallas_call | solution.py:190
  30.7 1.6 collective-permute-start.3
  32.2 6.3 %collective-permute-done.3.new_any = bf16[4,64,512]{2,1,0:T(8,128)(2,1)S(1)} collective-permute-done((bf16[4,64,512]{2,1,0:T(8,128)(2,1)S(1)}, bf16[4,64,512]{2,1,0:T(8,128)(2,1)S(1)}, u32[]{:S(2)}, u32[]{:S(2)}) %collective-permute-start.3) | collective-permute-done | bytes 262176 | tf_op jit(solution)/shard_map/ppermute | solution.py:444
  38.6 0.7 copy-done.21
  39.3 0.7 added.8.rest_0_
  40.0 4.4 %collective-permute-start.8 = (bf16[384,512]{1,0:T(8,128)(2,1)S(1)}, bf16[384,512]{1,0:T(8,128)(2,1)S(1)}, u32[]{:S(2)}, u32[]{:S(2)}) collective-permute-start(bf16[384,512]{1,0:T(8,128)(2,1)S(1)} %added.8.rest_0_), channel_id=1, source_target_pairs={{0,4},{12,8},{1,5},{13,9},{2,6},{14,10},{3,7},{15,11},{16,20},{28,... | collective-permute-start | bytes 1179656 | tf_op jit(solution)/shard_map/ppermute | solution.py:444
  45.8 0.7 copy-done.3
  46.5 6.2 %collective-permute-done.8.rest_2_ = bf16[384,512]{1,0:T(8,128)(2,1)S(1)} collective-permute-done((bf16[384,512]{1,0:T(8,128)(2,1)S(1)}, bf16[384,512]{1,0:T(8,128)(2,1)S(1)}, u32[]{:S(2)}, u32[]{:S(2)}) %collective-permute-start.8) | collective-permute-done | bytes 393248 | tf_op jit(solution)/shard_map/ppermute | solution.py:444
  53.4 0.7 copy-done.8
  54.1 0.7 copy-done.11
  54.9 0.7 copy-done.14
  55.6 6.0 %collective-permute-done.10.refs_2_ = bf16[640,512]{1,0:T(8,128)(2,1)S(1)} collective-permute-done((bf16[640,512]{1,0:T(8,128)(2,1)S(1)}, bf16[640,512]{1,0:T(8,128)(2,1)S(1)}, u32[]{:S(2)}, u32[]{:S(2)}) %collective-permute-start.10) | collective-permute-done | bytes 655392 | tf_op jit(solution)/shard_map/ppermute | solution.py:447
  61.6 1.6 added.9.rest_1_
  63.3 8.8 %collective-permute-start.11 = (bf16[640,512]{1,0:T(8,128)(2,1)}, bf16[640,512]{1,0:T(8,128)(2,1)}, u32[]{:S(2)}, u32[]{:S(2)}) collective-permute-start(bf16[640,512]{1,0:T(8,128)(2,1)} %added.9.rest_1_), channel_id=1, source_target_pairs={{0,4},{12,8},{1,5},{13,9},{2,6},{14,10},{3,7},{15,11},{16,20},{28,... | collective-permute-start | bytes 1966088 | tf_op jit(solution)/shard_map/ppermute | solution.py:444
  72.0 1.5 collective-permute-start.14
  73.6 1.5 collective-permute-start.13
  75.1 8.6 %collective-permute-done.11.rest_3_ = bf16[640,512]{1,0:T(8,128)(2,1)} collective-permute-done((bf16[640,512]{1,0:T(8,128)(2,1)}, bf16[640,512]{1,0:T(8,128)(2,1)}, u32[]{:S(2)}, u32[]{:S(2)}) %collective-permute-start.11) | collective-permute-done | bytes 655392 | tf_op jit(solution)/shard_map/ppermute | solution.py:444
  83.7 5.2 %collective-permute-start.12 = (bf16[192,1280]{1,0:T(8,128)(2,1)S(1)}, bf16[192,1280]{1,0:T(8,128)(2,1)}, u32[]{:S(2)}, u32[]{:S(2)}) collective-permute-start(bf16[192,1280]{1,0:T(8,128)(2,1)S(1)} %constant_dynamic-slice_fusion), channel_id=1, source_target_pairs={{0,4},{12,8},{1,5},{13,9},{2,6},{14,10},{3,7},{15,11},{16,20},{28,... | collective-permute-start | bytes 1474568 | tf_op jit(solution)/shard_map/ppermute | solution.py:444
  88.9 8.4 %collective-permute-done.14 = bf16[448,1280]{1,0:T(8,128)(2,1)} collective-permute-done((bf16[448,1280]{1,0:T(8,128)(2,1)}, bf16[448,1280]{1,0:T(8,128)(2,1)}, u32[]{:S(2)}, u32[]{:S(2)}) %collective-permute-start.14) | collective-permute-done | bytes 1146912 | tf_op jit(solution)/shard_map/ppermute | solution.py:478
  97.2 1.5 collective-permute-start.15
  98.7 1.5 collective-permute-start.16
  100.2 3.1 %collective-permute-start.19 = (bf16[4,64,1280]{2,1,0:T(8,128)(2,1)}, bf16[4,64,1280]{2,1,0:T(8,128)(2,1)S(1)}, u32[]{:S(2)}, u32[]{:S(2)}) collective-permute-start(bf16[4,64,1280]{2,1,0:T(8,128)(2,1)} %query_any), channel_id=1, source_target_pairs={{0,4},{12,8},{1,5},{13,9},{2,6},{14,10},{3,7},{15,11},{16,20},{28,... | collective-permute-start | bytes 1966088 | tf_op jit(solution)/shard_map/ppermute | solution.py:444
  103.4 1.0 copy-done.4
  104.4 1.0 copy-done.9
  105.4 1.0 copy-done.12
  106.3 1.0 copy-done.15
  107.3 1.1 copy-done.18
  108.4 5.6 %attend.2.row_ref = bf16[4,64,1280]{2,1,0:T(8,128)(2,1)S(1)} custom-call(s32[3]{0:T(128)S(1)} %copy-done.23, s32[2]{0:T(128)S(1)} %copy-done.26, s32[4]{0:T(128)S(1)} %copy-done.24, s32[4]{0:T(128)S(1)} %copy-done.25, bf16[4,64,1280]{2,1,0:T(8,128)(2,1)S(1)} %copy-done.18, bf16[4,64,512]{2,1,0:T(8,128)(2,1)S(1)} %copy-done.20, ...), custom_call_target="tpu_custom_call" | custom-call | flops 64 | bytes 64 | tf_op jit(solution)/shard_map/attend/pallas_call | solution.py:319
  114.0 3.4 %maximum_select_fusion.moved_ref = bf16[1280,1280]{1,0:T(8,128)(2,1)S(1)} fusion(bf16[192,1280]{1,0:T(8,128)(2,1)} %collective-permute-done.16, bf16[448,1280]{1,0:T(8,128)(2,1)} %collective-permute-done.14, bf16[192,1280]{1,0:T(8,128)(2,1)} %collective-permute-done.12, bf16[448,1280]{1,0:T(8,128)(2,1)} %collective-permute-done.7, pred[]{:T(512)S(6)} %eq.18), kind=kLoop, calls=%fused_computation | loop fusion | flops 27852800 | bytes 6553601 | tf_op jit(solution)/shard_map/jit(_where)/select_n | solution.py:496
  117.5 2.4 %spread.4 = (bf16[4,64,1280]{2,1,0:T(8,128)(2,1)S(1)}, bf16[4,64,1280]{2,1,0:T(8,128)(2,1)S(1)}) custom-call(s32[3]{0:T(128)S(1)} %copy-done.23, bf16[4,64,1280]{2,1,0:T(8,128)(2,1)S(1)} %attend.2.row_ref, bf16[1280,1280]{1,0:T(8,128)(2,1)S(1)} %copy-done, bf16[1280,1280]{1,0:T(8,128)(2,1)S(1)} %maximum_select_fusion.moved_ref), custom_call_target="tpu_custom_call" | custom-call | flops 64 | bytes 64 | tf_op jit(solution)/shard_map/spread/pallas_call | solution.py:355
  120.0 0.7 collective-permute-start.21
  120.7 14.5 %collective-permute-start.18 = (s32[2]{0:T(128)S(1)}, s32[2]{0:T(128)S(1)}, u32[]{:S(2)}, u32[]{:S(2)}) collective-permute-start(s32[2]{0:T(128)S(1)} %copy-done.26), channel_id=1, source_target_pairs={{0,4},{12,8},{1,5},{13,9},{2,6},{14,10},{3,7},{15,11},{16,20},{28,... | collective-permute-start | bytes 32 | tf_op jit(solution)/shard_map/ppermute | solution.py:444
  135.2 1.0 collective-permute-done.18.prompts_ref
  136.3 5.6 %attend.3.row_ref = bf16[4,64,1280]{2,1,0:T(8,128)(2,1)S(1)} custom-call(s32[3]{0:T(128)S(1)} %copy-done.23, s32[2]{0:T(128)S(1)} %collective-permute-done.18.prompts_ref, s32[4]{0:T(128)S(1)} %copy-done.24, s32[4]{0:T(128)S(1)} %copy-done.25, bf16[4,64,1280]{2,1,0:T(8,128)(2,1)S(1)} %collective-permute-done.19.query_any, ...), custom_call_target="tpu_custom_call" | custom-call | flops 64 | bytes 64 | tf_op jit(solution)/shard_map/attend/pallas_call | solution.py:319
  141.9 0.7 added.10.refs_0_
  142.6 2.4 %spread.5 = (bf16[4,64,1280]{2,1,0:T(8,128)(2,1)S(1)}, bf16[4,64,1280]{2,1,0:T(8,128)(2,1)S(1)}) custom-call(s32[3]{0:T(128)S(1)} %copy-done.23, bf16[4,64,1280]{2,1,0:T(8,128)(2,1)S(1)} %collective-permute-done.21.row_ref, bf16[1280,1280]{1,0:T(8,128)(2,1)S(1)} %copy-done, bf16[1280,1280]{1,0:T(8,128)(2,1)S(1)} %maximum_select_fusion.moved_ref), custom_call_target="tpu_custom_call" | custom-call | flops 64 | bytes 64 | tf_op jit(solution)/shard_map/spread/pallas_call | solution.py:355
  145.2 2.4 %spread.6 = (bf16[4,64,1280]{2,1,0:T(8,128)(2,1)S(1)}, bf16[4,64,1280]{2,1,0:T(8,128)(2,1)S(1)}) custom-call(s32[3]{0:T(128)S(1)} %copy-done.23, bf16[4,64,1280]{2,1,0:T(8,128)(2,1)S(1)} %attend.3.row_ref, bf16[1280,1280]{1,0:T(8,128)(2,1)S(1)} %copy-done, bf16[1280,1280]{1,0:T(8,128)(2,1)S(1)} %maximum_select_fusion.moved_ref), custom_call_target="tpu_custom_call" | custom-call | flops 64 | bytes 64 | tf_op jit(solution)/shard_map/spread/pallas_call | solution.py:355
  148.2 0.7 collective-permute-start.20
  148.9 1.0 collective-permute-start.24
  151.1 0.7 added.11
  151.9 2.4 %spread.7 = (bf16[4,64,1280]{2,1,0:T(8,128)(2,1)S(1)}, bf16[4,64,1280]{2,1,0:T(8,128)(2,1)S(1)}) custom-call(s32[3]{0:T(128)S(1)} %copy-done.23, bf16[4,64,1280]{2,1,0:T(8,128)(2,1)S(1)} %collective-permute-done.24.row_ref, bf16[1280,1280]{1,0:T(8,128)(2,1)S(1)} %copy-done, bf16[1280,1280]{1,0:T(8,128)(2,1)S(1)} %maximum_select_fusion.moved_ref), custom_call_target="tpu_custom_call" | custom-call | flops 64 | bytes 64 | tf_op jit(solution)/shard_map/spread/pallas_call | solution.py:355
  155.0 1.5 collective-permute-start.28
  157.1 7.8 %collective-permute-done.26.refs_2_ = bf16[2,64,1280]{2,1,0:T(8,128)(2,1)S(1)} collective-permute-done((bf16[2,64,1280]{2,1,0:T(8,128)(2,1)S(1)}, bf16[2,64,1280]{2,1,0:T(8,128)(2,1)S(1)}, u32[]{:S(2)}, u32[]{:S(2)}) %collective-permute-start.26) | collective-permute-done | bytes 327712 | tf_op jit(solution)/shard_map/ppermute | solution.py:447
  165.0 0.7 added_half.9
  165.7 0.8 collective-permute-start.27
  166.5 0.7 collective-permute-start.30
  167.8 4.2 %collective-permute-done.28.refs_2_ = bf16[2,64,1280]{2,1,0:T(8,128)(2,1)S(1)} collective-permute-done((bf16[2,64,1280]{2,1,0:T(8,128)(2,1)S(1)}, bf16[2,64,1280]{2,1,0:T(8,128)(2,1)S(1)}, u32[]{:S(2)}, u32[]{:S(2)}) %collective-permute-start.28) | collective-permute-done | bytes 327712 | tf_op jit(solution)/shard_map/ppermute | solution.py:447
  172.0 0.7 added_half.10
  172.7 1.3 collective-permute-start.29
  174.0 4.6 %collective-permute-done.31.refs_2_ = bf16[2,64,1280]{2,1,0:T(8,128)(2,1)S(1)} collective-permute-done((bf16[2,64,1280]{2,1,0:T(8,128)(2,1)S(1)}, bf16[2,64,1280]{2,1,0:T(8,128)(2,1)S(1)}, u32[]{:S(2)}, u32[]{:S(2)}) %collective-permute-start.31) | collective-permute-done | bytes 327712 | tf_op jit(solution)/shard_map/ppermute | solution.py:447
  179.2 0.7 collective-permute-start.32
  180.0 1.3 collective-permute-start.33
  182.0 22.0 %collective-permute-done.29 = bf16[2,64,1280]{2,1,0:T(8,128)(2,1)S(1)} collective-permute-done((bf16[2,64,1280]{2,1,0:T(8,128)(2,1)S(1)}, bf16[2,64,1280]{2,1,0:T(8,128)(2,1)S(1)}, u32[]{:S(2)}, u32[]{:S(2)}) %collective-permute-start.29) | collective-permute-done | bytes 327712 | tf_op jit(solution)/shard_map/ppermute | solution.py:417
  204.0 21.7 %collective-permute-done.33 = bf16[2,64,1280]{2,1,0:T(8,128)(2,1)S(1)} collective-permute-done((bf16[2,64,1280]{2,1,0:T(8,128)(2,1)S(1)}, bf16[2,64,1280]{2,1,0:T(8,128)(2,1)S(1)}, u32[]{:S(2)}, u32[]{:S(2)}) %collective-permute-start.33) | collective-permute-done | bytes 327712 | tf_op jit(solution)/shard_map/ppermute | solution.py:417
  225.7 1.0 fusion
  (87 shorter events, 9.4 us)
Async XLA Ops:
  2.3 37.7 %collective-permute-start.7 = (bf16[448,1280]{1,0:T(8,128)(2,1)}, bf16[448,1280]{1,0:T(8,128)(2,1)}, u32[]{:S(2)}, u32[]{:S(2)}) collective-permute-start(bf16[448,1280]{1,0:T(8,128)(2,1)} %constant_dynamic-slice_fusion.1), channel_id=1, source_target_pairs={{0,4},{12,8},{1,5},{13,9},{2,6},{14,10},{3,7},{15,11},{16,20},{28,... | collective-permute-start | bytes 3440648 | tf_op jit(solution)/shard_map/ppermute | solution.py:444
  9.0 9.4 %copy-start.23 = (s32[3]{0:T(128)S(1)}, s32[3]{0:T(128)}, u32[]{:S(2)}) copy-start(s32[3]{0:T(128)} %pad_add_fusion.here_ref._) | copy-start | bytes 40
  15.4 7.9 %copy-start.2 = (bf16[1,1024,1280]{2,1,0:T(8,128)(2,1)S(1)}, bf16[1,1024,1280]{2,1,0:T(8,128)(2,1)}, u32[]{:S(2)}) copy-start(bf16[1,1024,1280]{2,1,0:T(8,128)(2,1)} %param.8) | copy-start | bytes 7864324
  15.4 6.1 %collective-permute-start.1 = (bf16[640,512]{1,0:T(8,128)(2,1)}, bf16[640,512]{1,0:T(8,128)(2,1)S(1)}, u32[]{:S(2)}, u32[]{:S(2)}) collective-permute-start(bf16[640,512]{1,0:T(8,128)(2,1)} %get-tuple-element.44), channel_id=1, source_target_pairs={{0,1},{1,0},{2,3},{3,2},{4,5},{5,4},{6,7},{7,6},{8,9},{9,8},{10,11... | collective-permute-start | bytes 1966088 | tf_op jit(solution)/shard_map/ppermute | solution.py:447
  15.5 2.9 %collective-permute-start = (bf16[384,512]{1,0:T(8,128)(2,1)}, bf16[384,512]{1,0:T(8,128)(2,1)S(1)}, u32[]{:S(2)}, u32[]{:S(2)}) collective-permute-start(bf16[384,512]{1,0:T(8,128)(2,1)} %get-tuple-element.42), channel_id=1, source_target_pairs={{0,1},{1,0},{2,3},{3,2},{4,5},{5,4},{6,7},{7,6},{8,9},{9,8},{10,11... | collective-permute-start | bytes 1179656 | tf_op jit(solution)/shard_map/ppermute | solution.py:447
  18.3 1.0 copy-start.19
  20.0 19.3 %collective-permute-start.5 = (bf16[384,512]{1,0:T(8,128)(2,1)S(1)}, bf16[384,512]{1,0:T(8,128)(2,1)S(1)}, u32[]{:S(2)}, u32[]{:S(2)}) collective-permute-start(bf16[384,512]{1,0:T(8,128)(2,1)S(1)} %added.6), channel_id=1, source_target_pairs={{0,2},{2,0},{1,3},{3,1},{4,6},{6,4},{5,7},{7,5},{8,10},{10,8},{9,1... | collective-permute-start | bytes 1179656 | tf_op jit(solution)/shard_map/ppermute | solution.py:447
  21.5 1.1 copy-start.17
  23.3 2.5 %copy-start.1 = (bf16[1280,2048]{1,0:T(8,128)(2,1)S(1)}, bf16[1280,2048]{1,0:T(8,128)(2,1)}, u32[]{:S(2)}) copy-start(bf16[1280,2048]{1,0:T(8,128)(2,1)} %weight_any.3) | copy-start | bytes 15728644
  25.8 4.8 %copy-start.20 = (bf16[4,64,512]{2,1,0:T(8,128)(2,1)S(1)}, bf16[4,64,512]{2,1,0:T(8,128)(2,1)}, u32[]{:S(2)}) copy-start(bf16[4,64,512]{2,1,0:T(8,128)(2,1)} %new_any.1) | copy-start | bytes 786436
  30.5 53.1 %copy-start = (bf16[1280,1280]{1,0:T(8,128)(2,1)S(1)}, bf16[1280,1280]{1,0:T(8,128)(2,1)}, u32[]{:S(2)}) copy-start(bf16[1280,1280]{1,0:T(8,128)(2,1)} %own_ref.7) | copy-start | bytes 9830404
  30.5 72.8 %copy-start.24 = (s32[4]{0:T(128)S(1)}, s32[4]{0:T(128)}, u32[]{:S(2)}) copy-start(s32[4]{0:T(128)} %owners_ref.3) | copy-start | bytes 52
  30.6 72.8 %copy-start.25 = (s32[4]{0:T(128)S(1)}, s32[4]{0:T(128)}, u32[]{:S(2)}) copy-start(s32[4]{0:T(128)} %lengths_ref.3) | copy-start | bytes 52
  30.6 72.8 %copy-start.26 = (s32[2]{0:T(128)S(1)}, s32[2]{0:T(128)}, u32[]{:S(2)}) copy-start(s32[2]{0:T(128)} %prompts_ref.1) | copy-start | bytes 28
  30.6 8.7 %collective-permute-start.4 = (bf16[384,512]{1,0:T(8,128)(2,1)S(1)}, bf16[384,512]{1,0:T(8,128)(2,1)S(1)}, u32[]{:S(2)}, u32[]{:S(2)}) collective-permute-start(bf16[384,512]{1,0:T(8,128)(2,1)S(1)} %get-tuple-element.51), channel_id=1, source_target_pairs={{0,1},{1,0},{2,3},{3,2},{4,5},{5,4},{6,7},{7,6},{8,9},{9,8},{10,11... | collective-permute-start | bytes 1179656 | tf_op jit(solution)/shard_map/ppermute | solution.py:447
  30.7 7.9 %collective-permute-start.3 = (bf16[4,64,512]{2,1,0:T(8,128)(2,1)S(1)}, bf16[4,64,512]{2,1,0:T(8,128)(2,1)S(1)}, u32[]{:S(2)}, u32[]{:S(2)}) collective-permute-start(bf16[4,64,512]{2,1,0:T(8,128)(2,1)S(1)} %copy-done.20), channel_id=1, source_target_pairs={{0,4},{12,8},{1,5},{13,9},{2,6},{14,10},{3,7},{15,11},{16,20},{28,... | collective-permute-start | bytes 786440 | tf_op jit(solution)/shard_map/ppermute | solution.py:444
  38.6 0.7 copy-start.21
  40.0 12.7 %collective-permute-start.8 = (bf16[384,512]{1,0:T(8,128)(2,1)S(1)}, bf16[384,512]{1,0:T(8,128)(2,1)S(1)}, u32[]{:S(2)}, u32[]{:S(2)}) collective-permute-start(bf16[384,512]{1,0:T(8,128)(2,1)S(1)} %added.8.rest_0_), channel_id=1, source_target_pairs={{0,4},{12,8},{1,5},{13,9},{2,6},{14,10},{3,7},{15,11},{16,20},{28,... | collective-permute-start | bytes 1179656 | tf_op jit(solution)/shard_map/ppermute | solution.py:444
  44.4 9.7 %collective-permute-start.2 = (bf16[640,512]{1,0:T(8,128)(2,1)S(1)}, bf16[640,512]{1,0:T(8,128)(2,1)S(1)}, u32[]{:S(2)}, u32[]{:S(2)}) collective-permute-start(bf16[640,512]{1,0:T(8,128)(2,1)S(1)} %get-tuple-element.48), channel_id=1, source_target_pairs={{0,1},{1,0},{2,3},{3,2},{4,5},{5,4},{6,7},{7,6},{8,9},{9,8},{10,11... | collective-permute-start | bytes 1966088 | tf_op jit(solution)/shard_map/ppermute | solution.py:447
  44.5 17.1 %collective-permute-start.10 = (bf16[640,512]{1,0:T(8,128)(2,1)S(1)}, bf16[640,512]{1,0:T(8,128)(2,1)S(1)}, u32[]{:S(2)}, u32[]{:S(2)}) collective-permute-start(bf16[640,512]{1,0:T(8,128)(2,1)S(1)} %added.7), channel_id=1, source_target_pairs={{0,2},{2,0},{1,3},{3,1},{4,6},{6,4},{5,7},{7,5},{8,10},{10,8},{9,1... | collective-permute-start | bytes 1966088 | tf_op jit(solution)/shard_map/ppermute | solution.py:447
  45.1 9.0 %collective-permute-start.6 = (bf16[384,512]{1,0:T(8,128)(2,1)S(1)}, bf16[384,512]{1,0:T(8,128)(2,1)S(1)}, u32[]{:S(2)}, u32[]{:S(2)}) collective-permute-start(bf16[384,512]{1,0:T(8,128)(2,1)S(1)} %added.8.rest_0_), channel_id=1, source_target_pairs={{4,8},{8,4},{5,9},{9,5},{6,10},{10,6},{7,11},{11,7},{20,24},{24,20... | collective-permute-start | bytes 1179656 | tf_op jit(solution)/shard_map/ppermute | solution.py:444
  45.8 0.7 copy-start.3
  52.7 2.2 collective-permute-start.9
  53.4 0.8 copy-start.8
  54.1 0.8 copy-start.11
  54.9 0.7 copy-start.14
  63.3 20.4 %collective-permute-start.11 = (bf16[640,512]{1,0:T(8,128)(2,1)}, bf16[640,512]{1,0:T(8,128)(2,1)}, u32[]{:S(2)}, u32[]{:S(2)}) collective-permute-start(bf16[640,512]{1,0:T(8,128)(2,1)} %added.9.rest_1_), channel_id=1, source_target_pairs={{0,4},{12,8},{1,5},{13,9},{2,6},{14,10},{3,7},{15,11},{16,20},{28,... | collective-permute-start | bytes 1966088 | tf_op jit(solution)/shard_map/ppermute | solution.py:444
  72.0 25.2 %collective-permute-start.14 = (bf16[448,1280]{1,0:T(8,128)(2,1)}, bf16[448,1280]{1,0:T(8,128)(2,1)}, u32[]{:S(2)}, u32[]{:S(2)}) collective-permute-start(bf16[448,1280]{1,0:T(8,128)(2,1)} %collective-permute-done.7), channel_id=1, source_target_pairs={{0,16},{16,0},{1,17},{17,1},{2,18},{18,2},{3,19},{19,3},{4,20},{20... | collective-permute-start | bytes 3440648 | tf_op jit(solution)/shard_map/ppermute | solution.py:478
  73.6 23.7 %collective-permute-start.13 = (bf16[640,512]{1,0:T(8,128)(2,1)}, bf16[640,512]{1,0:T(8,128)(2,1)}, u32[]{:S(2)}, u32[]{:S(2)}) collective-permute-start(bf16[640,512]{1,0:T(8,128)(2,1)} %added.9.rest_1_), channel_id=1, source_target_pairs={{4,8},{8,4},{5,9},{9,5},{6,10},{10,6},{7,11},{11,7},{20,24},{24,20... | collective-permute-start | bytes 1966088 | tf_op jit(solution)/shard_map/ppermute | solution.py:444
  83.7 15.1 %collective-permute-start.12 = (bf16[192,1280]{1,0:T(8,128)(2,1)S(1)}, bf16[192,1280]{1,0:T(8,128)(2,1)}, u32[]{:S(2)}, u32[]{:S(2)}) collective-permute-start(bf16[192,1280]{1,0:T(8,128)(2,1)S(1)} %constant_dynamic-slice_fusion), channel_id=1, source_target_pairs={{0,4},{12,8},{1,5},{13,9},{2,6},{14,10},{3,7},{15,11},{16,20},{28,... | collective-permute-start | bytes 1474568 | tf_op jit(solution)/shard_map/ppermute | solution.py:444
  97.2 6.1 %collective-permute-start.15 = (bf16[640,512]{1,0:T(8,128)(2,1)}, bf16[640,512]{1,0:T(8,128)(2,1)}, u32[]{:S(2)}, u32[]{:S(2)}) collective-permute-start(bf16[640,512]{1,0:T(8,128)(2,1)} %collective-permute-done.11.rest_3_), channel_id=1, source_target_pairs={{4,8},{8,4},{5,9},{9,5},{6,10},{10,6},{7,11},{11,7},{20,24},{24,20... | collective-permute-start | bytes 1966088 | tf_op jit(solution)/shard_map/ppermute | solution.py:444
  98.7 15.3 %collective-permute-start.16 = (bf16[192,1280]{1,0:T(8,128)(2,1)}, bf16[192,1280]{1,0:T(8,128)(2,1)}, u32[]{:S(2)}, u32[]{:S(2)}) collective-permute-start(bf16[192,1280]{1,0:T(8,128)(2,1)} %collective-permute-done.12), channel_id=1, source_target_pairs={{0,16},{16,0},{1,17},{17,1},{2,18},{18,2},{3,19},{19,3},{4,20},{20... | collective-permute-start | bytes 1474568 | tf_op jit(solution)/shard_map/ppermute | solution.py:493
  100.2 35.0 %collective-permute-start.19 = (bf16[4,64,1280]{2,1,0:T(8,128)(2,1)}, bf16[4,64,1280]{2,1,0:T(8,128)(2,1)S(1)}, u32[]{:S(2)}, u32[]{:S(2)}) collective-permute-start(bf16[4,64,1280]{2,1,0:T(8,128)(2,1)} %query_any), channel_id=1, source_target_pairs={{0,4},{12,8},{1,5},{13,9},{2,6},{14,10},{3,7},{15,11},{16,20},{28,... | collective-permute-start | bytes 1966088 | tf_op jit(solution)/shard_map/ppermute | solution.py:444
  103.4 1.0 copy-start.4
  104.4 1.0 copy-start.9
  105.3 1.0 copy-start.12
  106.3 1.0 copy-start.15
  107.3 1.1 copy-start.18
  117.4 18.9 %copy-start.5 = (bf16[384,512]{1,0:T(8,128)(2,1)S(1)}, bf16[384,512]{1,0:T(8,128)(2,1)}, u32[]{:S(2)}) copy-start(bf16[384,512]{1,0:T(8,128)(2,1)} %copy-done.3) | copy-start | bytes 1179652
  117.4 18.9 %copy-start.10 = (bf16[384,512]{1,0:T(8,128)(2,1)S(1)}, bf16[384,512]{1,0:T(8,128)(2,1)}, u32[]{:S(2)}) copy-start(bf16[384,512]{1,0:T(8,128)(2,1)} %copy-done.8) | copy-start | bytes 1179652
  117.4 18.9 %copy-start.13 = (bf16[384,512]{1,0:T(8,128)(2,1)S(1)}, bf16[384,512]{1,0:T(8,128)(2,1)}, u32[]{:S(2)}) copy-start(bf16[384,512]{1,0:T(8,128)(2,1)} %copy-done.11) | copy-start | bytes 1179652
  117.4 18.9 %copy-start.16 = (bf16[384,512]{1,0:T(8,128)(2,1)S(1)}, bf16[384,512]{1,0:T(8,128)(2,1)}, u32[]{:S(2)}) copy-start(bf16[384,512]{1,0:T(8,128)(2,1)} %copy-done.14) | copy-start | bytes 1179652
  117.5 18.8 %copy-start.22 = (bf16[4,64,512]{2,1,0:T(8,128)(2,1)S(1)}, bf16[4,64,512]{2,1,0:T(8,128)(2,1)}, u32[]{:S(2)}) copy-start(bf16[4,64,512]{2,1,0:T(8,128)(2,1)} %copy-done.21) | copy-start | bytes 786436
  119.9 22.0 %collective-permute-start.17 = (bf16[4,64,1280]{2,1,0:T(8,128)(2,1)S(1)}, bf16[4,64,1280]{2,1,0:T(8,128)(2,1)S(1)}, u32[]{:S(2)}, u32[]{:S(2)}) collective-permute-start(bf16[4,64,1280]{2,1,0:T(8,128)(2,1)S(1)} %get-tuple-element.58), channel_id=1, source_target_pairs={{0,1},{1,0},{2,3},{3,2},{4,5},{5,4},{6,7},{7,6},{8,9},{9,8},{10,11... | collective-permute-start | bytes 1966088 | tf_op jit(solution)/shard_map/ppermute | solution.py:447
  120.0 22.7 %collective-permute-start.21 = (bf16[4,64,1280]{2,1,0:T(8,128)(2,1)S(1)}, bf16[4,64,1280]{2,1,0:T(8,128)(2,1)S(1)}, u32[]{:S(2)}, u32[]{:S(2)}) collective-permute-start(bf16[4,64,1280]{2,1,0:T(8,128)(2,1)S(1)} %attend.2.row_ref), channel_id=1, source_target_pairs={{4,8},{8,4},{5,9},{9,5},{6,10},{10,6},{7,11},{11,7},{20,24},{24,20... | collective-permute-start | bytes 1966088 | tf_op jit(solution)/shard_map/ppermute | solution.py:444
  120.7 15.6 %collective-permute-start.18 = (s32[2]{0:T(128)S(1)}, s32[2]{0:T(128)S(1)}, u32[]{:S(2)}, u32[]{:S(2)}) collective-permute-start(s32[2]{0:T(128)S(1)} %copy-done.26), channel_id=1, source_target_pairs={{0,4},{12,8},{1,5},{13,9},{2,6},{14,10},{3,7},{15,11},{16,20},{28,... | collective-permute-start | bytes 32 | tf_op jit(solution)/shard_map/ppermute | solution.py:444
  145.1 4.8 %collective-permute-start.23 = (bf16[4,64,1280]{2,1,0:T(8,128)(2,1)S(1)}, bf16[4,64,1280]{2,1,0:T(8,128)(2,1)S(1)}, u32[]{:S(2)}, u32[]{:S(2)}) collective-permute-start(bf16[4,64,1280]{2,1,0:T(8,128)(2,1)S(1)} %get-tuple-element.67), channel_id=1, source_target_pairs={{0,1},{1,0},{2,3},{3,2},{4,5},{5,4},{6,7},{7,6},{8,9},{9,8},{10,11... | collective-permute-start | bytes 1966088 | tf_op jit(solution)/shard_map/ppermute | solution.py:447
  147.6 2.9 %collective-permute-start.22 = (bf16[4,64,1280]{2,1,0:T(8,128)(2,1)S(1)}, bf16[4,64,1280]{2,1,0:T(8,128)(2,1)S(1)}, u32[]{:S(2)}, u32[]{:S(2)}) collective-permute-start(bf16[4,64,1280]{2,1,0:T(8,128)(2,1)S(1)} %get-tuple-element.66), channel_id=1, source_target_pairs={{0,1},{1,0},{2,3},{3,2},{4,5},{5,4},{6,7},{7,6},{8,9},{9,8},{10,11... | collective-permute-start | bytes 1966088 | tf_op jit(solution)/shard_map/ppermute | solution.py:447
  148.2 3.0 %collective-permute-start.20 = (bf16[4,64,1280]{2,1,0:T(8,128)(2,1)S(1)}, bf16[4,64,1280]{2,1,0:T(8,128)(2,1)S(1)}, u32[]{:S(2)}, u32[]{:S(2)}) collective-permute-start(bf16[4,64,1280]{2,1,0:T(8,128)(2,1)S(1)} %added.10.refs_0_), channel_id=1, source_target_pairs={{6,4},{7,5},{8,10},{9,11},{22,20},{23,21},{24,26},{25,27}} | collective-permute-start | bytes 1966088 | tf_op jit(solution)/shard_map/ppermute | solution.py:426
  148.9 3.0 %collective-permute-start.24 = (bf16[4,64,1280]{2,1,0:T(8,128)(2,1)S(1)}, bf16[4,64,1280]{2,1,0:T(8,128)(2,1)S(1)}, u32[]{:S(2)}, u32[]{:S(2)}) collective-permute-start(bf16[4,64,1280]{2,1,0:T(8,128)(2,1)S(1)} %attend.3.row_ref), channel_id=1, source_target_pairs={{4,8},{8,4},{5,9},{9,5},{6,10},{10,6},{7,11},{11,7},{20,24},{24,20... | collective-permute-start | bytes 1966088 | tf_op jit(solution)/shard_map/ppermute | solution.py:444
  151.8 2.5 %copy-start.6 = (bf16[4,64,1280]{2,1,0:T(8,128)(2,1)}, bf16[4,64,1280]{2,1,0:T(8,128)(2,1)S(1)}, u32[]{:S(2)}) copy-start(bf16[4,64,1280]{2,1,0:T(8,128)(2,1)S(1)} %added.11) | copy-start | bytes 1966084
  154.3 2.2 collective-permute-start.25
  154.4 10.6 %collective-permute-start.26 = (bf16[2,64,1280]{2,1,0:T(8,128)(2,1)S(1)}, bf16[2,64,1280]{2,1,0:T(8,128)(2,1)S(1)}, u32[]{:S(2)}, u32[]{:S(2)}) collective-permute-start(bf16[2,64,1280]{2,1,0:T(8,128)(2,1)S(1)} %added_half.6), channel_id=1, source_target_pairs={{0,2},{2,0},{1,3},{3,1},{4,6},{6,4},{5,7},{7,5},{8,10},{10,8},{9,1... | collective-permute-start | bytes 983048 | tf_op jit(solution)/shard_map/ppermute | solution.py:447
  155.0 17.0 %collective-permute-start.28 = (bf16[2,64,1280]{2,1,0:T(8,128)(2,1)S(1)}, bf16[2,64,1280]{2,1,0:T(8,128)(2,1)S(1)}, u32[]{:S(2)}, u32[]{:S(2)}) collective-permute-start(bf16[2,64,1280]{2,1,0:T(8,128)(2,1)S(1)} %added_half.7), channel_id=1, source_target_pairs={{0,2},{2,0},{1,3},{3,1},{4,6},{6,4},{5,7},{7,5},{8,10},{10,8},{9,1... | collective-permute-start | bytes 983048 | tf_op jit(solution)/shard_map/ppermute | solution.py:447
  165.7 60.0 %copy-start.7 = (bf16[4,64,1280]{2,1,0:T(8,128)(2,1)S(1)}, bf16[4,64,1280]{2,1,0:T(8,128)(2,1)}, u32[]{:S(2)}) copy-start(bf16[4,64,1280]{2,1,0:T(8,128)(2,1)} %copy-done.6) | copy-start | bytes 1966084
  165.7 8.3 %collective-permute-start.27 = (bf16[2,64,1280]{2,1,0:T(8,128)(2,1)S(1)}, bf16[2,64,1280]{2,1,0:T(8,128)(2,1)S(1)}, u32[]{:S(2)}, u32[]{:S(2)}) collective-permute-start(bf16[2,64,1280]{2,1,0:T(8,128)(2,1)S(1)} %added_half.9), channel_id=1, source_target_pairs={{4,8},{5,9},{10,6},{11,7},{20,24},{21,25},{26,22},{27,23}} | collective-permute-start | bytes 983048 | tf_op jit(solution)/shard_map/ppermute | solution.py:417
  166.5 7.5 %collective-permute-start.30 = (bf16[2,64,1280]{2,1,0:T(8,128)(2,1)S(1)}, bf16[2,64,1280]{2,1,0:T(8,128)(2,1)S(1)}, u32[]{:S(2)}, u32[]{:S(2)}) collective-permute-start(bf16[2,64,1280]{2,1,0:T(8,128)(2,1)S(1)} %added_half.9), channel_id=1, source_target_pairs={{6,8},{7,9},{8,6},{9,7},{22,24},{23,25},{24,22},{25,23}} | collective-permute-start | bytes 983048 | tf_op jit(solution)/shard_map/ppermute | solution.py:417
  167.2 11.4 %collective-permute-start.31 = (bf16[2,64,1280]{2,1,0:T(8,128)(2,1)S(1)}, bf16[2,64,1280]{2,1,0:T(8,128)(2,1)S(1)}, u32[]{:S(2)}, u32[]{:S(2)}) collective-permute-start(bf16[2,64,1280]{2,1,0:T(8,128)(2,1)S(1)} %added_half.8), channel_id=1, source_target_pairs={{0,2},{2,0},{1,3},{3,1},{4,6},{6,4},{5,7},{7,5},{8,10},{10,8},{9,1... | collective-permute-start | bytes 983048 | tf_op jit(solution)/shard_map/ppermute | solution.py:447
  172.7 31.2 %collective-permute-start.29 = (bf16[2,64,1280]{2,1,0:T(8,128)(2,1)S(1)}, bf16[2,64,1280]{2,1,0:T(8,128)(2,1)S(1)}, u32[]{:S(2)}, u32[]{:S(2)}) collective-permute-start(bf16[2,64,1280]{2,1,0:T(8,128)(2,1)S(1)} %added_half.10), channel_id=1, source_target_pairs={{4,0},{5,1},{10,14},{11,15},{20,16},{21,17},{26,30},{27,31}} | collective-permute-start | bytes 983048 | tf_op jit(solution)/shard_map/ppermute | solution.py:417
  179.2 24.7 %collective-permute-start.32 = (bf16[2,64,1280]{2,1,0:T(8,128)(2,1)S(1)}, bf16[2,64,1280]{2,1,0:T(8,128)(2,1)S(1)}, u32[]{:S(2)}, u32[]{:S(2)}) collective-permute-start(bf16[2,64,1280]{2,1,0:T(8,128)(2,1)S(1)} %added_half.11), channel_id=1, source_target_pairs={{4,12},{5,13},{10,2},{11,3},{20,28},{21,29},{26,18},{27,19}} | collective-permute-start | bytes 983048 | tf_op jit(solution)/shard_map/ppermute | solution.py:417
  180.0 45.7 %collective-permute-start.33 = (bf16[2,64,1280]{2,1,0:T(8,128)(2,1)S(1)}, bf16[2,64,1280]{2,1,0:T(8,128)(2,1)S(1)}, u32[]{:S(2)}, u32[]{:S(2)}) collective-permute-start(bf16[2,64,1280]{2,1,0:T(8,128)(2,1)S(1)} %added_half.10), channel_id=1, source_target_pairs={{6,0},{7,1},{8,14},{9,15},{22,16},{23,17},{24,30},{25,31}} | collective-permute-start | bytes 983048 | tf_op jit(solution)/shard_map/ppermute | solution.py:417
  181.3 44.4 %collective-permute-start.34 = (bf16[2,64,1280]{2,1,0:T(8,128)(2,1)S(1)}, bf16[2,64,1280]{2,1,0:T(8,128)(2,1)S(1)}, u32[]{:S(2)}, u32[]{:S(2)}) collective-permute-start(bf16[2,64,1280]{2,1,0:T(8,128)(2,1)S(1)} %added_half.11), channel_id=1, source_target_pairs={{6,12},{7,13},{8,2},{9,3},{22,28},{23,29},{24,18},{25,19}} | collective-permute-start | bytes 983048 | tf_op jit(solution)/shard_map/ppermute | solution.py:417

commit v3 on v2

--- a/solution.py
+++ b/solution.py
@@ -133,8 +133,8 @@
     return mixed.astype(jnp.bfloat16).reshape(step_count, row_total, mixed.shape[1])
 
 
-FIRST_VMEM = 60 * 1024 * 1024
 VMEM = 24 * 1024 * 1024
+LARGE_VMEM = 60 * 1024 * 1024
 
 CORE = [(0, 1), (1, 0), (2, 3), (3, 2)]
 ACROSS_X = [(0, 2), (2, 0), (1, 3), (3, 1)]
@@ -150,11 +150,11 @@
     return pl.CostEstimate(flops=64, bytes_accessed=64, transcendentals=0)
 
 
-def project(limit, here, states, weight, masks, cuts):
+def project(here, states, weight, masks, cuts):
     features, width = weight.shape[0], weight.shape[1] // 4
     parts = [(low, high - low) for low, high in zip(cuts[:-1], cuts[1:])]
 
-    def body(here_ref, state_any, weight_any, *rest):
+    def body(here_ref, state_hbm, weight_hbm, *rest):
         outs, (state, blocks, state_sems, block_sems) = rest[: 2 * len(parts)], rest[2 * len(parts) :]
         fetches, blocks_in = [], []
         for side in range(2):
@@ -162,13 +162,13 @@
             columns = pl.ds(pl.multiple_of(place * width, width), width)
             blocks_in.append(
                 pltpu.make_async_copy(
-                    weight_any.at[:, columns], blocks.at[side], block_sems.at[side]
+                    weight_hbm.at[:, columns], blocks.at[side], block_sems.at[side]
                 )
             )
         for at, (low, rows) in enumerate(parts):
             fetches.append(
                 pltpu.make_async_copy(
-                    state_any.at[low : low + rows], state.at[low : low + rows], state_sems.at[at]
+                    state_hbm.at[low : low + rows], state.at[low : low + rows], state_sems.at[at]
                 )
             )
         blocks_in[0].start()
@@ -185,11 +185,11 @@
                     state[low : low + rows], blocks[side], preferred_element_type=jnp.float32
                 ).astype(jnp.bfloat16)
 
-    in_any = pl.BlockSpec(memory_space=pl.ANY)
+    in_hbm = pl.BlockSpec(memory_space=pltpu.HBM)
     in_vmem = pl.BlockSpec(memory_space=pltpu.VMEM)
     outs = pl.pallas_call(
         body,
-        in_specs=[pl.BlockSpec(memory_space=pltpu.SMEM), in_any, in_any],
+        in_specs=[pl.BlockSpec(memory_space=pltpu.SMEM), in_hbm, in_hbm],
         out_specs=[in_vmem] * (2 * len(parts)),
         out_shape=[jax.ShapeDtypeStruct((rows, width), jnp.bfloat16) for _, rows in parts] * 2,
         scratch_shapes=[
@@ -198,33 +198,35 @@
             pltpu.SemaphoreType.DMA((len(parts),)),
             pltpu.SemaphoreType.DMA((2,)),
         ],
-        compiler_params=compiler_params(limit),
+        compiler_params=compiler_params(LARGE_VMEM),
         cost_estimate=small_cost(),
         name="project",
     )(here, states, weight)
     return outs[: len(parts)], outs[len(parts) :]
 
 
-def attend(here, prompts, owners, lengths, queries, news, pages):
-    steps, rows, width = queries.shape
+def attend(chosen, here, prompts, owners, lengths, queries, news, pages):
+    news, new_start = news
+    steps, rows, _ = queries.shape
     blocks = prompts.shape[0]
     block_rows = rows // blocks
-    new_width = news.shape[2]
+    new_width = pages[0][0].shape[1]
     groups = new_width // (2 * HD)
-    sizes = [part.shape[0] for part in pages[0]]
-    starts = [sum(sizes[:at]) for at in range(len(sizes))]
-    tokens = sum(sizes)
+    width = groups * GQA * HD
+    tokens = sum(part.shape[0] for part in pages[0])
+    most = max(len(page) for page in pages)
+    page_parts = [part for page in pages for part in page]
     tiles = 4
     chunk = tokens // tiles
     flat = steps * block_rows
     factor = math.log2(math.e) / math.sqrt(HD)
 
-    def body(here_ref, prompts_ref, owners_ref, lengths_ref, query_any, new_any, *rest):
-        page_refs, rest = rest[: 4 * len(sizes)], rest[4 * len(sizes) :]
+    def body(here_ref, prompts_ref, owners_ref, lengths_ref, query_hbm, new_hbm, *rest):
+        page_refs, rest = rest[: len(page_parts)], rest[len(page_parts) :]
         out_ref, held, query_ref, new_ref, sems = rest
         plane = here_ref[1]
 
-        def run(mine, used, length):
+        def run(written, used, length):
             query = query_ref[...].reshape(flat, width)
             new = new_ref[...].reshape(flat, new_width)
             shape = (GQA * flat, flat)
@@ -272,31 +274,34 @@
                 result = (summed / total).astype(jnp.bfloat16)
                 for head in range(GQA):
                     column = (group * GQA + head) * HD
-                    out_ref[:, mine, column : column + HD] = result[
+                    out_ref[:, written, column : column + HD] = result[
                         head * flat : (head + 1) * flat
                     ].reshape(steps, block_rows, HD)
 
-        @pl.loop(0, blocks)
+        @pl.loop(*chosen)
         def _(block):
             mine = pl.ds(pl.multiple_of(block * block_rows, block_rows), block_rows)
+            written = pl.ds(
+                pl.multiple_of((block - chosen[0]) * block_rows, block_rows), block_rows
+            )
             prompt = prompts_ref[block]
             slot, length = owners_ref[prompt], lengths_ref[prompt]
-            fetch_query = pltpu.make_async_copy(query_any.at[:, mine], query_ref, sems.at[0])
-            fetch_new = pltpu.make_async_copy(new_any.at[:, mine], new_ref, sems.at[1])
+            fetch_query = pltpu.make_async_copy(query_hbm.at[:, mine, :width], query_ref, sems.at[0])
+            fetch_new = pltpu.make_async_copy(new_hbm.at[:, mine, new_start : new_start + new_width], new_ref, sems.at[1])
             fetch_query.start()
             fetch_new.start()
-            for which, place in enumerate((plane, plane ^ 1, 3 - plane, (3 - plane) ^ 1)):
+            passed = 0
+            for page, place in zip(pages, (plane, plane ^ 1, 3 - plane, (3 - plane) ^ 1)):
+                refs = page_refs[passed : passed + len(page)]
+                passed += len(page)
 
                 @pl.when(slot == place)
                 def _():
-                    fetches = [
-                        pltpu.make_async_copy(
-                            page_refs[which * len(sizes) + at],
-                            held.at[low : low + size],
-                            sems.at[2 + at],
-                        )
-                        for at, (low, size) in enumerate(zip(starts, sizes))
-                    ]
+                    low, fetches = 0, []
+                    for at, ref in enumerate(refs):
+                        target = held.at[low : low + ref.shape[0]]
+                        fetches.append(pltpu.make_async_copy(ref, target, sems.at[2 + at]))
+                        low += ref.shape[0]
                     for fetch in fetches:
                         fetch.start()
                     for fetch in fetches:
@@ -311,65 +316,89 @@
 
                 @pl.when(enough)
                 def _():
-                    run(mine, count * chunk, length)
-
-    in_vmem, in_smem, in_any = (
-        pl.BlockSpec(memory_space=space) for space in (pltpu.VMEM, pltpu.SMEM, pl.ANY)
+                    run(written, count * chunk, length)
+
+    in_vmem, in_smem, in_hbm = (
+        pl.BlockSpec(memory_space=space) for space in (pltpu.VMEM, pltpu.SMEM, pltpu.HBM)
     )
     return pl.pallas_call(
         body,
-        in_specs=[in_smem] * 4 + [in_any] * (2 + 4 * len(sizes)),
+        in_specs=[in_smem] * 4 + [in_hbm] * (2 + len(page_parts)),
         out_specs=in_vmem,
-        out_shape=jax.ShapeDtypeStruct(queries.shape, jnp.bfloat16),
+        out_shape=jax.ShapeDtypeStruct(
+            (steps, (chosen[1] - chosen[0]) * block_rows, width), jnp.bfloat16
+        ),
         scratch_shapes=[
             pltpu.VMEM((tokens, new_width), jnp.bfloat16),
             pltpu.VMEM((steps, block_rows, width), jnp.bfloat16),
             pltpu.VMEM((steps, block_rows, new_width), jnp.bfloat16),
-            pltpu.SemaphoreType.DMA((2 + len(sizes),)),
+            pltpu.SemaphoreType.DMA((2 + most,)),
         ],
-        compiler_params=compiler_params(),
+        compiler_params=compiler_params(LARGE_VMEM),
         cost_estimate=small_cost(),
         name="attend",
-    )(here, prompts, owners, lengths, queries, news, *[part for page in pages for part in page])
-
-
-def spread(here, rows, own_weight, moved_weight):
-    steps, count, features = rows.shape
+    )(here, prompts, owners, lengths, queries, news, *page_parts)
+
+
+def spread(here, blocks, own_weight, moved_weights):
+    count, moved_count = len(blocks), len(moved_weights)
+    steps, _, features = blocks[0].shape
     columns = own_weight.shape[1]
     tile = 256 if columns % 256 == 0 else columns
-
-    def body(here_ref, row_ref, own_ref, moved_ref, keep_ref, send_ref):
-        taken = row_ref[...].reshape(steps * count, features)
+    ends = [0]
+    for block in blocks:
+        ends.append(ends[-1] + block.shape[1])
+    places = [slice(low, high) for low, high in zip(ends[:-1], ends[1:])]
+
+    def body(here_ref, *refs):
+        row_refs, own_ref, refs = refs[:count], refs[count], refs[count + 1 :]
+        moved_refs, (keep_ref, send_ref, taken_ref) = refs[:moved_count], refs[moved_count:]
+        for ref, place in zip(row_refs, places):
+            flat = slice(steps * place.start, steps * place.stop)
+            taken_ref[flat] = ref[...].reshape(flat.stop - flat.start, features)
+        taken = taken_ref[...]
+        pieces = []
+        for low, other, part in moved_weights:
+            start = (here_ref[0] ^ other) * (features // 2) + low
+            pieces.append(taken_ref[:, pl.ds(pl.multiple_of(start, 128), part.shape[0])])
         keeps_own = (here_ref[1] ^ here_ref[2]) % 2 == 0
         for column in range(0, columns, tile):
             part = slice(column, column + tile)
             own = jnp.dot(taken, own_ref[:, part], preferred_element_type=jnp.float32)
-            moved = jnp.dot(taken, moved_ref[:, part], preferred_element_type=jnp.float32)
+            moved = 0.0
+            for piece, moved_ref in zip(pieces, moved_refs):
+                moved = moved + jnp.dot(
+                    piece, moved_ref[:, part], preferred_element_type=jnp.float32
+                )
             keep = jnp.where(keeps_own, own, moved).astype(jnp.bfloat16)
             send = jnp.where(keeps_own, moved, own).astype(jnp.bfloat16)
-            keep_ref[:, :, part] = keep.reshape(steps, count, tile)
-            send_ref[:, :, part] = send.reshape(steps, count, tile)
+            for place in places:
+                flat = slice(steps * place.start, steps * place.stop)
+                shape = (steps, place.stop - place.start, tile)
+                keep_ref[:, place, part] = keep[flat].reshape(shape)
+                send_ref[:, place, part] = send[flat].reshape(shape)
 
     in_vmem = pl.BlockSpec(memory_space=pltpu.VMEM)
-    out_shape = jax.ShapeDtypeStruct((steps, count, columns), jnp.bfloat16)
+    out_shape = jax.ShapeDtypeStruct((steps, ends[-1], columns), jnp.bfloat16)
     return pl.pallas_call(
         body,
-        in_specs=[pl.BlockSpec(memory_space=pltpu.SMEM)] + [in_vmem] * 3,
+        in_specs=[pl.BlockSpec(memory_space=pltpu.SMEM)] + [in_vmem] * (count + 1 + moved_count),
         out_specs=[in_vmem, in_vmem],
         out_shape=[out_shape, out_shape],
+        scratch_shapes=[pltpu.VMEM((steps * ends[-1], features), jnp.bfloat16)],
         compiler_params=compiler_params(),
         cost_estimate=small_cost(),
         name="spread",
-    )(here, rows, own_weight, moved_weight)
-
-
-def run_small(body, name, here, operands, out_shape):
+    )(here, *blocks, own_weight, *[part for _, _, part in moved_weights])
+
+
+def run_small(body, name, here, operands, out_shape, outs=1):
     in_vmem = pl.BlockSpec(memory_space=pltpu.VMEM)
     return pl.pallas_call(
         body,
         in_specs=[pl.BlockSpec(memory_space=pltpu.SMEM)] + [in_vmem] * len(operands),
-        out_specs=in_vmem,
-        out_shape=jax.ShapeDtypeStruct(out_shape, jnp.bfloat16),
+        out_specs=[in_vmem] * outs,
+        out_shape=[jax.ShapeDtypeStruct(out_shape, jnp.bfloat16)] * outs,
         compiler_params=compiler_params(),
         cost_estimate=small_cost(),
         name=name,
@@ -383,38 +412,81 @@
             total = total + ref[...].astype(jnp.float32)
         refs[-1][...] = total.astype(jnp.bfloat16)
 
-    return run_small(body, "added", here, parts, parts[0].shape)
-
-
-def added_half(here, mine, wide, *narrow):
-    half = wide[0].shape[0] // 2
+    return run_small(body, "added", here, parts, parts[0].shape)[0]
+
+
+def stacked(here, *parts):
+    rows = [part.shape[0] for part in parts]
+
+    def body(_, *refs):
+        for at, ref in enumerate(refs[:-1]):
+            refs[-1][sum(rows[:at]) : sum(rows[: at + 1])] = ref[...]
+
+    return run_small(body, "stacked", here, parts, (sum(rows), *parts[0].shape[1:]))[0]
+
+
+def added_half(here, mine, wide, narrow=(), pieces=1):
+    steps, rows, columns = wide[0].shape
+    half, piece = steps // 2, rows // pieces
 
     def body(here_ref, *refs):
+        ins, outs = refs[:-pieces], refs[-pieces:]
         chip = here_ref[2] // 2
-        steps = pl.ds((chip if mine else 1 - chip) * half, half)
-        total = refs[0][steps].astype(jnp.float32)
-        for at, ref in enumerate(refs[1:-1], 1):
-            part = ref[steps] if at < len(wide) else ref[...]
+        taken = pl.ds((chip if mine else 1 - chip) * half, half)
+        total = ins[0][taken].astype(jnp.float32)
+        for at, ref in enumerate(ins[1:], 1):
+            part = ref[taken] if at < len(wide) else ref[...]
             total = total + part.astype(jnp.float32)
-        refs[-1][...] = total.astype(jnp.bfloat16)
-
-    shape = (half, *wide[0].shape[1:])
-    return run_small(body, "added_half", here, (*wide, *narrow), shape)
+        total = total.astype(jnp.bfloat16)
+        for at, out in enumerate(outs):
+            out[...] = total[:, at * piece : (at + 1) * piece]
+
+    outs = run_small(body, "added_half", here, (*wide, *narrow), (half, piece, columns), pieces)
+    return outs if pieces > 1 else outs[0]
+
+
+def added_halves(here, one, two, far_crossed, end_crossed):
+    steps, rows, columns = one.shape
+    half, piece = steps // 2, rows // 2
+
+    def body(here_ref, one_ref, two_ref, far_ref, end_ref, first_ref, second_ref):
+        chip = here_ref[2] // 2
+        taken = pl.ds(chip * half, half)
+        total = one_ref[taken].astype(jnp.float32) + two_ref[taken].astype(jnp.float32)
+        far = (total[:, :piece] + far_ref[...].astype(jnp.float32)).astype(jnp.bfloat16)
+        end = (total[:, piece:] + end_ref[...].astype(jnp.float32)).astype(jnp.bfloat16)
+        at_home = here_ref[1] // 2 == chip
+
+        @pl.when(at_home)
+        def _():
+            first_ref[...] = far
+            second_ref[...] = end
+
+        @pl.when(jnp.logical_not(at_home))
+        def _():
+            first_ref[...] = end
+            second_ref[...] = far
+
+    shape = (half, piece, columns)
+    return run_small(body, "added_halves", here, (one, two, far_crossed, end_crossed), shape, 2)
 
 
 def after(value, *others):
     return lax.optimization_barrier((value, *others))[0]
 
 
-def sent_home(value, target):
-    same, turned = [], []
+def home_pairs(target, turned):
+    pairs = []
     for source in (1, 2):
         side = source // 2
+        chip = 1 - side if turned else side
         for at in range(2):
-            goal = target(source) * 4 + 2 * side + at
-            same.append((source * 4 + 2 * side + at, goal))
-            turned.append((source * 4 + 2 * (1 - side) + at, goal))
-    return [lax.ppermute(value, ("samp", "head"), pairs) for pairs in (same, turned)]
+            pairs.append((source * 4 + 2 * chip + at, target(source) * 4 + 2 * side + at))
+    return pairs
+
+
+def sent_home(value, *pairs):
+    return lax.ppermute(value, ("samp", "head"), [pair for part in pairs for pair in part])
 
 
 def across_home(value):
@@ -446,95 +518,117 @@
     def on_head(value, pairs):
         return lax.ppermute(value, "head", pairs)
 
-    half = out_weight.shape[0] // 2
-    cut = half * 7 // 10
-
-    def weight_part(low, size, *others):
-        part = lax.dynamic_slice_in_dim(after(out_weight, *others), group * half + low, size, 0)
-        return on_samp(part, INWARD)
-
-    weight_first = weight_part(0, cut)
-    end_news = on_samp(step_kv, INWARD)
-
     states = prompt_states[0]
     tokens = states.shape[0]
     cuts = [0, tokens * 3 // 8, tokens]
-    sent, kept = project(FIRST_VMEM, here, states, kv_weight, (3, 2), cuts)
+    sent, kept = project(here, states, kv_weight, (3, 2), cuts)
+
+    half = out_weight.shape[0] // 2
+    weight_cuts = [0, half * 2 // 5, half * 3 // 5, half]
+
+    def weight_part(at, *others):
+        low, size = weight_cuts[at], weight_cuts[at + 1] - weight_cuts[at]
+        part = lax.dynamic_slice_in_dim(after(out_weight, *others), group * half + low, size, 0)
+        return on_samp(part, INWARD)
+
+    def swapped(part):
+        return lax.ppermute(part, "groups", [(0, 1), (1, 0)])
+
+    weight_0 = weight_part(0, sent[0])
     leaving_first = added(here, kept[0], on_head(sent[0], CORE))
     leaving_second = added(here, kept[1], after(on_head(sent[1], CORE), leaving_first))
     crossed_first = on_head(leaving_first, ACROSS_X)
     crossed_second = on_head(leaving_second, ACROSS_X)
     sent, kept = project(
-        VMEM, here, after(states, leaving_first, leaving_second), kv_weight, (1, 0), cuts
+        here, after(states, leaving_first, leaving_second), kv_weight, (1, 0), cuts
     )
     sent = [on_head(value, CORE) for value in sent]
-    first = added(here, after(kept[0], end_news), sent[0], crossed_first)
-    end_first = on_samp(after(first, weight_first), INWARD)
+    first = added(here, kept[0], sent[0], crossed_first)
+    end_first = on_samp(after(first, weight_0), INWARD)
     far_first = on_samp(first, MIDDLE)
-    far_end_first = on_samp(end_first, MIDDLE)
-    second = added(here, kept[1], after(sent[1], far_first, far_end_first), crossed_second)
+    second = added(here, kept[1], after(sent[1], far_first, end_first), crossed_second)
     end_second = on_samp(second, INWARD)
     far_second = on_samp(second, MIDDLE)
-    moved_first = lax.ppermute(weight_first, "groups", [(0, 1), (1, 0)])
-    far_end_second = on_samp(after(end_second, far_second, moved_first), MIDDLE)
-    pages = (
-        (first, second),
-        (end_first, end_second),
-        (far_first, far_second),
-        (far_end_first, far_end_second),
-    )
-    weight_second = weight_part(cut, half - cut, end_second)
-
-    def attended(prompts, queries, news):
-        return attend(here, prompts, prompt_owner, prompt_lengths, queries, news, pages)
-
+    end_page = stacked(here, end_first, end_second)
+    far_end_page = on_samp(after(end_page, far_second), MIDDLE)
+    pages = ((first, second), (end_page,), (far_first, far_second), (far_end_page,))
     end_prompts = on_samp(after(sampler_prompts, second), INWARD)
-    end_queries = on_samp(after(step_queries, weight_second), INWARD)
-    moved_second = lax.ppermute(weight_second, "groups", [(0, 1), (1, 0)])
-    mine = jnp.concatenate([weight_first, weight_second], axis=0)
-    other = jnp.concatenate([moved_first, moved_second], axis=0)
-    moved_weight = jnp.where(
-        group == 0,
-        jnp.concatenate([mine, other], axis=0),
-        jnp.concatenate([other, mine], axis=0),
-    )
-
-    def spread_out(rows):
-        keep, send = spread(here, rows, out_weight, moved_weight)
+    weight_1, weight_2 = (weight_part(at, end_second, end_prompts) for at in (1, 2))
+    asked = jnp.concatenate([after(step_queries, first), step_kv], axis=2)
+    end_asked = on_samp(after(asked, weight_1, weight_2), INWARD)
+    moved_0, moved_1, moved_2 = swapped(weight_0), swapped(weight_1), swapped(weight_2)
+    parts = ((weight_0, moved_0), (weight_1, moved_1), (weight_2, moved_2))
+    moved_weights = [
+        (low, side, part[side]) for side in range(2) for low, part in zip(weight_cuts, parts)
+    ]
+
+    def hopped(*values):
+        token = here
+        for value in values:
+            token = on_head(after(token, value), CORE)
+        return token
+
+    def attended(place, chosen, prompts, queries, news):
+        rows = attend(
+            chosen, place, prompts, prompt_owner, prompt_lengths, queries, news, pages
+        )
+        return rows, on_samp(rows, MIDDLE)
+
+    def spread_out(*blocks, place=here):
+        keep, send = spread(place, blocks, out_weight, moved_weights)
         return keep, on_head(send, CORE)
 
-    own_rows = attended(sampler_prompts, after(step_queries, weight_second), step_kv)
-    far_own_rows = on_samp(own_rows, MIDDLE)
-    own_keep, own_arrived = spread_out(own_rows)
-    end_rows = attended(end_prompts, after(end_queries, own_keep), end_news)
-    far_end_rows = on_samp(end_rows, MIDDLE)
-    own_chip = added(here, own_keep, after(own_arrived, end_rows))
+    blocks = sampler_prompts.shape[0]
+    own_rows, far_own_rows = attended(
+        here, (0, blocks), sampler_prompts, after(step_queries, moved_0), (step_kv, 0)
+    )
+    end_rows, far_end_rows = attended(
+        here,
+        (0, blocks),
+        end_prompts,
+        after(end_asked, own_rows),
+        (end_asked, step_queries.shape[2]),
+    )
+    both_keep, both_arrived = spread_out(far_own_rows, end_rows)
+    far_leaving, end_leaving = added_half(here, False, (both_keep, both_arrived), (), 2)
+    end_crossed = on_head(end_leaving, ACROSS_X)
+    far_crossed = on_head(far_leaving, ACROSS_X)
+    own_keep, own_arrived = spread_out(own_rows, place=hopped(end_leaving, end_leaving))
+    own_chip = added(here, own_keep, own_arrived)
     own_crossed = across_home(own_chip)
-    far_keep, far_arrived = spread_out(after(far_own_rows, own_chip))
-    end_keep, end_arrived = spread_out(after(end_rows, far_keep))
-    far_leaving = added_half(here, False, (far_keep, after(far_arrived, end_keep)))
-    far_crossed = on_head(far_leaving, ACROSS_X)
-    end_leaving = added_half(here, False, (end_keep, after(end_arrived, far_leaving)))
-    end_crossed = on_head(end_leaving, ACROSS_X)
-    own_home = added(here, own_chip, after(own_crossed, end_leaving))
-    beyond_keep, beyond_arrived = spread_out(after(far_end_rows, own_home))
+    beyond_keep, beyond_arrived = spread_out(
+        far_end_rows, place=hopped(far_end_rows, far_end_rows, own_chip, end_crossed)
+    )
     beyond_leaving = added_half(here, False, (beyond_keep, beyond_arrived))
     beyond_crossed = on_head(beyond_leaving, ACROSS_X)
-    far_sum = added_half(here, True, (far_keep, after(far_arrived, beyond_leaving)), far_crossed)
-    far_home = sent_home(far_sum, lambda at: 3 - at)
-    end_sum = added_half(here, True, (end_keep, after(end_arrived, far_sum)), end_crossed)
-    end_home = sent_home(end_sum, lambda at: at ^ 1)
+    first_sum, second_sum = added_halves(
+        hopped(beyond_leaving), both_keep, both_arrived, far_crossed, end_crossed
+    )
+
+    def far(at):
+        return 3 - at
+
+    def end(at):
+        return at ^ 1
+
+    def beyond(at):
+        return (3 - at) ^ 1
+
+    first_home = sent_home(first_sum, home_pairs(far, False), home_pairs(end, True))
+    second_home = sent_home(second_sum, home_pairs(far, True), home_pairs(end, False))
     beyond_sum = added_half(
-        here, True, (beyond_keep, after(beyond_arrived, *far_home)), beyond_crossed
-    )
-    beyond_home = sent_home(beyond_sum, lambda at: (3 - at) ^ 1)
+        hopped(beyond_crossed),
+        True,
+        (beyond_keep, after(beyond_arrived, first_home, second_home)),
+        (beyond_crossed,),
+    )
+    beyond_home = [sent_home(beyond_sum, home_pairs(beyond, turned)) for turned in (False, True)]
+    own_home = added(here, own_chip, after(own_crossed, beyond_sum))
 
     is_middle = jnp.logical_or(plane == 1, plane == 2)
     near_side = chip == plane // 2
-    straight, turned = (
-        jnp.where(is_middle, far_home[which], jnp.where(near_side, end_home[which], beyond_home[which]))
-        for which in range(2)
-    )
+    straight = jnp.where(is_middle, first_home, jnp.where(near_side, second_home, beyond_home[0]))
+    turned = jnp.where(is_middle, second_home, jnp.where(near_side, first_home, beyond_home[1]))
     return jnp.where(
         jnp.logical_and(is_middle, near_side),
         own_home,

time: 228 us -> 200 us (0.88)
  the two profiles are of different devices: /device:TPU:0 before, /device:TPU:6 now
where the time goes in v3:
time: 200 us; the launch traced here: 199 us
  waiting for transfers between devices  74.5 us (37%)
  Pallas kernels  57 us (28%)
  starting transfers between devices  52.9 us (26%)
  local copies, waits for them, and re-layouts  9.5 us (5%)
  other arithmetic  4.68 us (2%)
    ppermute x12, starting transfers between devices, on_samp(): return lax.ppermute(value, 'samp', pairs)  32.9 us
    ppermute x12, waiting for transfers between devices, on_samp(): return lax.ppermute(value, 'samp', pairs)  32.6 us
    ppermute x20, waiting for transfers between devices, on_head(): return lax.ppermute(value, 'head', pairs)  30.9 us
    pallas_call x2, Pallas kernels, attend(): pl.pallas_call(body, in_specs=[in_smem] * 4 + [in_hbm] * (2 + len(page_pa...  17.2 us
    pallas_call x11, Pallas kernels, run_small(): pl.pallas_call(body, in_specs=[pl.BlockSpec(memory_space=pltpu.SMEM)] + [...  13.4 us
    pallas_call x3, Pallas kernels, spread(): pl.pallas_call(body, in_specs=[pl.BlockSpec(memory_space=pltpu.SMEM)] + [...  13.3 us
    pallas_call x2, Pallas kernels, project(): pl.pallas_call(body, in_specs=[pl.BlockSpec(memory_space=pltpu.SMEM), in_...  13.1 us
    ppermute x20, starting transfers between devices, on_head(): return lax.ppermute(value, 'head', pairs)  12.8 us
  transfers between devices with their start and end apart: 40, of which 17 were waited for; matrix products, arithmetic and copies ran while one was open for 2% of the time, Pallas kernels for 20%

profile of v3, /device:TPU:6, one launch (start us, length us, event | category | flops | bytes accessed | tf_op | source)
XLA Modules:
  0.0 199.0 jit_solution(11096664511379633363)
XLA Ops:
  0.6 6.7 %project.2 = (bf16[384,512]{1,0:T(8,128)(2,1)}, bf16[640,512]{1,0:T(8,128)(2,1)}, bf16[384,512]{1,0:T(8,128)(2,1)}, bf16[640,512]{1,0:T(8,128)(2,1)}) custom-call(s32[3]{0:T(128)} %pad_add_fusion.here_ref._, bf16[1024,1280]{1,0:T(8,128)(2,1)} %bitcast.4, bf16[1280,2048]{1,0:T(8,128)(2,1)} %weight_hbm.3), custom_call_target="tpu_custom_call" | custom-call | flops 64 | bytes 64 | tf_op jit(solution)/shard_map/project/pallas_call | solution.py:190
  7.9 0.9 constant_dynamic-slice_fusion.2
  8.8 4.3 %collective-permute-start = (bf16[256,1280]{1,0:T(8,128)(2,1)}, bf16[256,1280]{1,0:T(8,128)(2,1)}, u32[]{:S(2)}, u32[]{:S(2)}) collective-permute-start(bf16[256,1280]{1,0:T(8,128)(2,1)} %constant_dynamic-slice_fusion.2), channel_id=1, source_target_pairs={{0,4},{12,8},{1,5},{13,9},{2,6},{14,10},{3,7},{15,11},{16,20},{28,... | collective-permute-start | bytes 1966088 | tf_op jit(solution)/shard_map/ppermute | solution.py:516
  13.2 1.0 copy-done.11
  14.2 1.9 added.6
  16.5 1.2 added.7
  17.8 0.9 copy-done.6
  18.7 6.4 %project.3 = (bf16[384,512]{1,0:T(8,128)(2,1)}, bf16[640,512]{1,0:T(8,128)(2,1)}, bf16[384,512]{1,0:T(8,128)(2,1)}, bf16[640,512]{1,0:T(8,128)(2,1)}) custom-call(s32[3]{0:T(128)} %pad_add_fusion.here_ref._, bf16[1024,1280]{1,0:T(8,128)(2,1)} %bitcast.5, bf16[1280,2048]{1,0:T(8,128)(2,1)} %weight_hbm.3), custom_call_target="tpu_custom_call" | custom-call | flops 64 | bytes 64 | tf_op jit(solution)/shard_map/project/pallas_call | solution.py:190
  25.7 1.5 collective-permute-start.9
  27.2 1.0 copy-done.12
  28.9 2.3 %collective-permute-start.8 = (bf16[384,512]{1,0:T(8,128)(2,1)S(1)}, bf16[384,512]{1,0:T(8,128)(2,1)S(1)}, u32[]{:S(2)}, u32[]{:S(2)}) collective-permute-start(bf16[384,512]{1,0:T(8,128)(2,1)S(1)} %added.8.rest_0_), channel_id=1, source_target_pairs={{0,4},{12,8},{1,5},{13,9},{2,6},{14,10},{3,7},{15,11},{16,20},{28,... | collective-permute-start | bytes 1179656 | tf_op jit(solution)/shard_map/ppermute | solution.py:516
  31.2 0.7 collective-permute-start.7
  32.0 7.1 %collective-permute-done.8.refs_0_ = bf16[384,512]{1,0:T(8,128)(2,1)S(1)} collective-permute-done((bf16[384,512]{1,0:T(8,128)(2,1)S(1)}, bf16[384,512]{1,0:T(8,128)(2,1)S(1)}, u32[]{:S(2)}, u32[]{:S(2)}) %collective-permute-start.8) | collective-permute-done | bytes 393248 | tf_op jit(solution)/shard_map/ppermute | solution.py:516
  39.1 0.8 copy-done.9
  39.8 2.8 %collective-permute-done.9.refs_2_ = bf16[640,512]{1,0:T(8,128)(2,1)S(1)} collective-permute-done((bf16[640,512]{1,0:T(8,128)(2,1)}, bf16[640,512]{1,0:T(8,128)(2,1)S(1)}, u32[]{:S(2)}, u32[]{:S(2)}) %collective-permute-start.9) | collective-permute-done | bytes 655392 | tf_op jit(solution)/shard_map/ppermute | solution.py:519
  42.6 1.1 copy-done.8
  43.7 1.6 added.9.rest_1_
  45.3 3.6 %collective-permute-start.10 = (bf16[640,512]{1,0:T(8,128)(2,1)}, bf16[640,512]{1,0:T(8,128)(2,1)}, u32[]{:S(2)}, u32[]{:S(2)}) collective-permute-start(bf16[640,512]{1,0:T(8,128)(2,1)} %added.9.rest_1_), channel_id=1, source_target_pairs={{0,4},{12,8},{1,5},{13,9},{2,6},{14,10},{3,7},{15,11},{16,20},{28,... | collective-permute-start | bytes 1966088 | tf_op jit(solution)/shard_map/ppermute | solution.py:516
  49.0 1.5 collective-permute-start.11
  50.5 2.4 %collective-permute-start.14 = (s32[2]{0:T(128)S(1)}, s32[2]{0:T(128)S(1)}, u32[]{:S(2)}, u32[]{:S(2)}) collective-permute-start(s32[2]{0:T(128)S(1)} %copy-done.19), channel_id=1, source_target_pairs={{0,4},{12,8},{1,5},{13,9},{2,6},{14,10},{3,7},{15,11},{16,20},{28,... | collective-permute-start | bytes 32 | tf_op jit(solution)/shard_map/ppermute | solution.py:516
  52.9 8.0 %collective-permute-done.10.refs_1_ = bf16[640,512]{1,0:T(8,128)(2,1)} collective-permute-done((bf16[640,512]{1,0:T(8,128)(2,1)}, bf16[640,512]{1,0:T(8,128)(2,1)}, u32[]{:S(2)}, u32[]{:S(2)}) %collective-permute-start.10) | collective-permute-done | bytes 655392 | tf_op jit(solution)/shard_map/ppermute | solution.py:516
  60.9 1.0 copy-done.10
  61.9 2.2 %stacked.1.rest_2_ = bf16[1024,512]{1,0:T(8,128)(2,1)} custom-call(s32[3]{0:T(128)S(1)} %copy-done.14, bf16[384,512]{1,0:T(8,128)(2,1)S(1)} %copy-done.10, bf16[640,512]{1,0:T(8,128)(2,1)} %collective-permute-done.10.refs_1_), custom_call_target="tpu_custom_call" | custom-call | flops 64 | bytes 64 | tf_op jit(solution)/shard_map/stacked/pallas_call | solution.py:397
  64.1 1.7 collective-permute-start.12
  65.7 0.9 constant_dynamic-slice_fusion
  66.6 7.1 %collective-permute-start.16 = (bf16[256,1280]{1,0:T(8,128)(2,1)}, bf16[256,1280]{1,0:T(8,128)(2,1)}, u32[]{:S(2)}, u32[]{:S(2)}) collective-permute-start(bf16[256,1280]{1,0:T(8,128)(2,1)} %constant_dynamic-slice_fusion), channel_id=1, source_target_pairs={{0,4},{12,8},{1,5},{13,9},{2,6},{14,10},{3,7},{15,11},{16,20},{28,... | collective-permute-start | bytes 1966088 | tf_op jit(solution)/shard_map/ppermute | solution.py:516
  74.2 1.3 collective-permute-start.15
  75.6 2.1 %pad_maximum_fusion = bf16[4,64,1792]{2,1,0:T(8,128)(2,1)} fusion(bf16[4,64,512]{2,1,0:T(8,128)(2,1)S(1)} %copy-done.17, bf16[4,64,1280]{2,1,0:T(8,128)(2,1)} %query_hbm), kind=kLoop, calls=%fused_computation | loop fusion | flops 1835008 | bytes 1835008 | tf_op jit(solution)/shard_map/concatenate | solution.py:557
  77.6 13.7 %collective-permute-done.15.refs_4_.refs_3_ = bf16[128,1280]{1,0:T(8,128)(2,1)S(1)} collective-permute-done((bf16[128,1280]{1,0:T(8,128)(2,1)S(1)}, bf16[128,1280]{1,0:T(8,128)(2,1)S(1)}, u32[]{:S(2)}, u32[]{:S(2)}) %collective-permute-start.15) | collective-permute-done | bytes 327712 | tf_op jit(solution)/shard_map/ppermute | solution.py:516
  91.3 5.3 %collective-permute-start.17 = (bf16[4,64,1792]{2,1,0:T(8,128)(2,1)}, bf16[4,64,1792]{2,1,0:T(8,128)(2,1)}, u32[]{:S(2)}, u32[]{:S(2)}) collective-permute-start(bf16[4,64,1792]{2,1,0:T(8,128)(2,1)} %pad_maximum_fusion), channel_id=1, source_target_pairs={{0,4},{12,8},{1,5},{13,9},{2,6},{14,10},{3,7},{15,11},{16,20},{28,... | collective-permute-start | bytes 2752520 | tf_op jit(solution)/shard_map/ppermute | solution.py:516
  96.7 0.8 copy-done.1
  98.0 7.2 %attend.2.refs_0_ = bf16[4,64,1280]{2,1,0:T(8,128)(2,1)} custom-call(s32[3]{0:T(128)} %pad_add_fusion.here_ref._, s32[2]{0:T(128)} %prompts_ref.1, s32[4]{0:T(128)} %owners_ref.3, s32[4]{0:T(128)} %lengths_ref.3, bf16[4,64,1280]{2,1,0:T(8,128)(2,1)} %query_hbm, bf16[4,64,512]{2,1,0:T(8,128)(2,1)} %new_hbm.1, bf16[384,512]{1,0:T(8,128)(2,1)} %copy-done.4, ...), custom_call_target="tpu_custom_call" | custom-call | flops 64 | bytes 64 | tf_op jit(solution)/shard_map/attend/pallas_call | solution.py:324
  105.3 1.6 collective-permute-start.13
  106.8 1.5 collective-permute-start.18
  108.4 3.7 %collective-permute-done.17.query_hbm.new_hbm = bf16[4,64,1792]{2,1,0:T(8,128)(2,1)} collective-permute-done((bf16[4,64,1792]{2,1,0:T(8,128)(2,1)}, bf16[4,64,1792]{2,1,0:T(8,128)(2,1)}, u32[]{:S(2)}, u32[]{:S(2)}) %collective-permute-start.17) | collective-permute-done | bytes 917536 | tf_op jit(solution)/shard_map/ppermute | solution.py:516
  112.1 9.9 %attend.3.refs_1_ = bf16[4,64,1280]{2,1,0:T(8,128)(2,1)} custom-call(s32[3]{0:T(128)} %pad_add_fusion.here_ref._, s32[2]{0:T(128)} %copy-done.18, s32[4]{0:T(128)} %owners_ref.3, s32[4]{0:T(128)} %lengths_ref.3, bf16[4,64,1792]{2,1,0:T(8,128)(2,1)} %collective-permute-done.17.query_hbm.new_hbm, ...), custom_call_target="tpu_custom_call" | custom-call | flops 64 | bytes 64 | tf_op jit(solution)/shard_map/attend/pallas_call | solution.py:324
  122.1 1.1 copy-done.2
  123.2 6.0 %spread.3 = (bf16[4,128,1280]{2,1,0:T(8,128)(2,1)S(1)}, bf16[4,128,1280]{2,1,0:T(8,128)(2,1)S(1)}) custom-call(s32[3]{0:T(128)S(1)} %copy-done.15, bf16[4,64,1280]{2,1,0:T(8,128)(2,1)} %collective-permute-done.13.refs_0_, bf16[4,64,1280]{2,1,0:T(8,128)(2,1)} %attend.3.refs_1_, bf16[1280,1280]{1,0:T(8,128)(2,1)S(1)} %copy-done, ...), custom_call_target="tpu_custom_call" | custom-call | flops 64 | bytes 64 | tf_op jit(solution)/shard_map/spread/pallas_call | solution.py:383
  129.3 1.1 collective-permute-start.25
  130.4 1.9 collective-permute-done.20.refs_1_.two_ref
  132.3 0.7 added_half.3
  133.2 1.0 collective-permute-done.21
  134.4 0.9 collective-permute-done.22.here_ref
  135.3 3.7 %spread.4 = (bf16[4,64,1280]{2,1,0:T(8,128)(2,1)S(1)}, bf16[4,64,1280]{2,1,0:T(8,128)(2,1)S(1)}) custom-call(s32[3]{0:T(128)S(1)} %collective-permute-done.22.here_ref, bf16[4,64,1280]{2,1,0:T(8,128)(2,1)S(1)} %copy-done.5, bf16[1280,1280]{1,0:T(8,128)(2,1)S(1)} %copy-done, bf16[256,1280]{1,0:T(8,128)(2,1)} %collective-permute-done.refs_3_.refs_2_, ...), custom_call_target="tpu_custom_call" | custom-call | flops 64 | bytes 64 | tf_op jit(solution)/shard_map/spread/pallas_call | solution.py:383
  139.3 4.5 %collective-permute-start.29 = (bf16[2,64,1280]{2,1,0:T(8,128)(2,1)S(1)}, bf16[2,64,1280]{2,1,0:T(8,128)(2,1)S(1)}, u32[]{:S(2)}, u32[]{:S(2)}) collective-permute-start(bf16[2,64,1280]{2,1,0:T(8,128)(2,1)S(1)} %get-tuple-element.67), channel_id=1, source_target_pairs={{0,2},{2,0},{1,3},{3,1},{4,6},{6,4},{5,7},{7,5},{8,10},{10,8},{9,1... | collective-permute-start | bytes 983048 | tf_op jit(solution)/shard_map/ppermute | solution.py:519
  143.8 1.1 collective-permute-done.26
  145.1 1.5 added.10.refs_0_
  146.9 5.0 %collective-permute-done.29.end_ref = bf16[2,64,1280]{2,1,0:T(8,128)(2,1)S(1)} collective-permute-done((bf16[2,64,1280]{2,1,0:T(8,128)(2,1)S(1)}, bf16[2,64,1280]{2,1,0:T(8,128)(2,1)S(1)}, u32[]{:S(2)}, u32[]{:S(2)}) %collective-permute-start.29) | collective-permute-done | bytes 327712 | tf_op jit(solution)/shard_map/ppermute | solution.py:519
  151.9 1.1 collective-permute-done.30.here_ref
  153.1 3.7 %spread.5 = (bf16[4,64,1280]{2,1,0:T(8,128)(2,1)S(1)}, bf16[4,64,1280]{2,1,0:T(8,128)(2,1)S(1)}) custom-call(s32[3]{0:T(128)S(1)} %collective-permute-done.30.here_ref, bf16[4,64,1280]{2,1,0:T(8,128)(2,1)S(1)} %collective-permute-done.25.refs_0_, bf16[1280,1280]{1,0:T(8,128)(2,1)S(1)} %copy-done, bf16[256,1280]{1,0:T(8,128)(2,1)} %collective-permute-done.refs_3_.refs_2_, ...), custom_call_target="tpu_custom_call" | custom-call | flops 64 | bytes 64 | tf_op jit(solution)/shard_map/spread/pallas_call | solution.py:383
  157.0 1.8 collective-permute-start.35
  159.5 1.8 collective-permute-start.32
  161.4 6.2 %collective-permute-done.35.far_ref = bf16[2,64,1280]{2,1,0:T(8,128)(2,1)S(1)} collective-permute-done((bf16[2,64,1280]{2,1,0:T(8,128)(2,1)S(1)}, bf16[2,64,1280]{2,1,0:T(8,128)(2,1)S(1)}, u32[]{:S(2)}, u32[]{:S(2)}) %collective-permute-start.35) | collective-permute-done | bytes 327712 | tf_op jit(solution)/shard_map/ppermute | solution.py:519
  167.6 1.0 added_halves.1
  169.9 0.7 collective-permute-start.24
  170.7 9.6 %collective-permute-done.32.refs_2_ = bf16[2,64,1280]{2,1,0:T(8,128)(2,1)S(1)} collective-permute-done((bf16[2,64,1280]{2,1,0:T(8,128)(2,1)S(1)}, bf16[2,64,1280]{2,1,0:T(8,128)(2,1)S(1)}, u32[]{:S(2)}, u32[]{:S(2)}) %collective-permute-start.32) | collective-permute-done | bytes 327712 | tf_op jit(solution)/shard_map/ppermute | solution.py:519
  180.3 1.1 collective-permute-done.33.here_ref
  182.0 1.3 collective-permute-start.38
  183.3 1.3 collective-permute-start.39
  184.7 1.2 added.11
  185.9 8.7 %collective-permute-done.38 = bf16[2,64,1280]{2,1,0:T(8,128)(2,1)S(1)} collective-permute-done((bf16[2,64,1280]{2,1,0:T(8,128)(2,1)S(1)}, bf16[2,64,1280]{2,1,0:T(8,128)(2,1)S(1)}, u32[]{:S(2)}, u32[]{:S(2)}) %collective-permute-start.38) | collective-permute-done | bytes 327712 | tf_op jit(solution)/shard_map/ppermute | solution.py:489
  194.7 2.3 %collective-permute-done.39 = bf16[2,64,1280]{2,1,0:T(8,128)(2,1)} collective-permute-done((bf16[2,64,1280]{2,1,0:T(8,128)(2,1)S(1)}, bf16[2,64,1280]{2,1,0:T(8,128)(2,1)}, u32[]{:S(2)}, u32[]{:S(2)}) %collective-permute-start.39) | collective-permute-done | bytes 327712 | tf_op jit(solution)/shard_map/ppermute | solution.py:489
  197.0 1.0 select_select_fusion.1
  198.0 1.0 fusion
  (81 shorter events, 8.5 us)
Async XLA Ops:
  0.6 7.3 %copy-start = (bf16[1280,1280]{1,0:T(8,128)(2,1)S(1)}, bf16[1280,1280]{1,0:T(8,128)(2,1)}, u32[]{:S(2)}) copy-start(bf16[1280,1280]{1,0:T(8,128)(2,1)} %refs_1_.3) | copy-start | bytes 9830404
  0.6 12.5 %copy-start.13 = (s32[3]{0:T(128)S(1)}, s32[3]{0:T(128)}, u32[]{:S(2)}) copy-start(s32[3]{0:T(128)} %pad_add_fusion.here_ref._) | copy-start | bytes 40
  7.3 9.2 %collective-permute-start.3 = (bf16[640,512]{1,0:T(8,128)(2,1)}, bf16[640,512]{1,0:T(8,128)(2,1)}, u32[]{:S(2)}, u32[]{:S(2)}) collective-permute-start(bf16[640,512]{1,0:T(8,128)(2,1)} %get-tuple-element.50), channel_id=1, source_target_pairs={{0,1},{1,0},{2,3},{3,2},{4,5},{5,4},{6,7},{7,6},{8,9},{9,8},{10,11... | collective-permute-start | bytes 1966088 | tf_op jit(solution)/shard_map/ppermute | solution.py:519
  7.4 5.7 %collective-permute-start.2 = (bf16[384,512]{1,0:T(8,128)(2,1)}, bf16[384,512]{1,0:T(8,128)(2,1)}, u32[]{:S(2)}, u32[]{:S(2)}) collective-permute-start(bf16[384,512]{1,0:T(8,128)(2,1)} %get-tuple-element.45), channel_id=1, source_target_pairs={{0,1},{1,0},{2,3},{3,2},{4,5},{5,4},{6,7},{7,6},{8,9},{9,8},{10,11... | collective-permute-start | bytes 1179656 | tf_op jit(solution)/shard_map/ppermute | solution.py:519
  7.9 8.6 %copy-start.7 = (bf16[640,512]{1,0:T(8,128)(2,1)S(1)}, bf16[640,512]{1,0:T(8,128)(2,1)}, u32[]{:S(2)}) copy-start(bf16[640,512]{1,0:T(8,128)(2,1)} %get-tuple-element.49.refs_0_) | copy-start | bytes 1966084
  8.8 20.1 %collective-permute-start = (bf16[256,1280]{1,0:T(8,128)(2,1)}, bf16[256,1280]{1,0:T(8,128)(2,1)}, u32[]{:S(2)}, u32[]{:S(2)}) collective-permute-start(bf16[256,1280]{1,0:T(8,128)(2,1)} %constant_dynamic-slice_fusion.2), channel_id=1, source_target_pairs={{0,4},{12,8},{1,5},{13,9},{2,6},{14,10},{3,7},{15,11},{16,20},{28,... | collective-permute-start | bytes 1966088 | tf_op jit(solution)/shard_map/ppermute | solution.py:516
  13.2 1.0 copy-start.11
  16.0 11.2 %collective-permute-start.5 = (bf16[384,512]{1,0:T(8,128)(2,1)}, bf16[384,512]{1,0:T(8,128)(2,1)S(1)}, u32[]{:S(2)}, u32[]{:S(2)}) collective-permute-start(bf16[384,512]{1,0:T(8,128)(2,1)} %added.6), channel_id=1, source_target_pairs={{0,2},{2,0},{1,3},{3,1},{4,6},{6,4},{5,7},{7,5},{8,10},{10,8},{9,1... | collective-permute-start | bytes 1179656 | tf_op jit(solution)/shard_map/ppermute | solution.py:519
  17.8 0.9 copy-start.6
  18.7 8.5 %copy-start.14 = (s32[3]{0:T(128)S(1)}, s32[3]{0:T(128)}, u32[]{:S(2)}) copy-start(s32[3]{0:T(128)} %pad_add_fusion.here_ref._) | copy-start | bytes 40
  25.1 25.4 %copy-start.19 = (s32[2]{0:T(128)S(1)}, s32[2]{0:T(128)}, u32[]{:S(2)}) copy-start(s32[2]{0:T(128)} %prompts_ref.1) | copy-start | bytes 28
  25.1 2.1 %collective-permute-start.4 = (bf16[384,512]{1,0:T(8,128)(2,1)}, bf16[384,512]{1,0:T(8,128)(2,1)S(1)}, u32[]{:S(2)}, u32[]{:S(2)}) collective-permute-start(bf16[384,512]{1,0:T(8,128)(2,1)} %get-tuple-element.54), channel_id=1, source_target_pairs={{0,1},{1,0},{2,3},{3,2},{4,5},{5,4},{6,7},{7,6},{8,9},{9,8},{10,11... | collective-permute-start | bytes 1179656 | tf_op jit(solution)/shard_map/ppermute | solution.py:519
  25.2 6.7 %collective-permute-start.6 = (bf16[640,512]{1,0:T(8,128)(2,1)}, bf16[640,512]{1,0:T(8,128)(2,1)S(1)}, u32[]{:S(2)}, u32[]{:S(2)}) collective-permute-start(bf16[640,512]{1,0:T(8,128)(2,1)} %get-tuple-element.56), channel_id=1, source_target_pairs={{0,1},{1,0},{2,3},{3,2},{4,5},{5,4},{6,7},{7,6},{8,9},{9,8},{10,11... | collective-permute-start | bytes 1966088 | tf_op jit(solution)/shard_map/ppermute | solution.py:519
  25.7 16.9 %collective-permute-start.9 = (bf16[640,512]{1,0:T(8,128)(2,1)}, bf16[640,512]{1,0:T(8,128)(2,1)S(1)}, u32[]{:S(2)}, u32[]{:S(2)}) collective-permute-start(bf16[640,512]{1,0:T(8,128)(2,1)} %copy-done.6), channel_id=1, source_target_pairs={{0,2},{2,0},{1,3},{3,1},{4,6},{6,4},{5,7},{7,5},{8,10},{10,8},{9,1... | collective-permute-start | bytes 1966088 | tf_op jit(solution)/shard_map/ppermute | solution.py:519
  27.2 1.0 copy-start.12
  28.9 2.4 %copy-start.4 = (bf16[384,512]{1,0:T(8,128)(2,1)}, bf16[384,512]{1,0:T(8,128)(2,1)S(1)}, u32[]{:S(2)}) copy-start(bf16[384,512]{1,0:T(8,128)(2,1)S(1)} %added.8.rest_0_) | copy-start | bytes 1179652
  28.9 10.2 %collective-permute-start.8 = (bf16[384,512]{1,0:T(8,128)(2,1)S(1)}, bf16[384,512]{1,0:T(8,128)(2,1)S(1)}, u32[]{:S(2)}, u32[]{:S(2)}) collective-permute-start(bf16[384,512]{1,0:T(8,128)(2,1)S(1)} %added.8.rest_0_), channel_id=1, source_target_pairs={{0,4},{12,8},{1,5},{13,9},{2,6},{14,10},{3,7},{15,11},{16,20},{28,... | collective-permute-start | bytes 1179656 | tf_op jit(solution)/shard_map/ppermute | solution.py:516
  31.2 8.6 %collective-permute-start.7 = (bf16[384,512]{1,0:T(8,128)(2,1)S(1)}, bf16[384,512]{1,0:T(8,128)(2,1)S(1)}, u32[]{:S(2)}, u32[]{:S(2)}) collective-permute-start(bf16[384,512]{1,0:T(8,128)(2,1)S(1)} %added.8.rest_0_), channel_id=1, source_target_pairs={{4,8},{8,4},{5,9},{9,5},{6,10},{10,6},{7,11},{11,7},{20,24},{24,20... | collective-permute-start | bytes 1179656 | tf_op jit(solution)/shard_map/ppermute | solution.py:516
  39.1 0.8 copy-start.9
  39.8 2.8 %copy-start.16 = (bf16[384,512]{1,0:T(8,128)(2,1)}, bf16[384,512]{1,0:T(8,128)(2,1)S(1)}, u32[]{:S(2)}) copy-start(bf16[384,512]{1,0:T(8,128)(2,1)S(1)} %collective-permute-done.7.rest_3_) | copy-start | bytes 1179652
  42.6 1.1 copy-start.8
  43.7 31.8 %copy-start.17 = (bf16[4,64,512]{2,1,0:T(8,128)(2,1)S(1)}, bf16[4,64,512]{2,1,0:T(8,128)(2,1)}, u32[]{:S(2)}) copy-start(bf16[4,64,512]{2,1,0:T(8,128)(2,1)} %new_hbm.1) | copy-start | bytes 786436
  45.3 15.6 %collective-permute-start.10 = (bf16[640,512]{1,0:T(8,128)(2,1)}, bf16[640,512]{1,0:T(8,128)(2,1)}, u32[]{:S(2)}, u32[]{:S(2)}) collective-permute-start(bf16[640,512]{1,0:T(8,128)(2,1)} %added.9.rest_1_), channel_id=1, source_target_pairs={{0,4},{12,8},{1,5},{13,9},{2,6},{14,10},{3,7},{15,11},{16,20},{28,... | collective-permute-start | bytes 1966088 | tf_op jit(solution)/shard_map/ppermute | solution.py:516
  49.0 15.1 %collective-permute-start.11 = (bf16[640,512]{1,0:T(8,128)(2,1)}, bf16[640,512]{1,0:T(8,128)(2,1)}, u32[]{:S(2)}, u32[]{:S(2)}) collective-permute-start(bf16[640,512]{1,0:T(8,128)(2,1)} %added.9.rest_1_), channel_id=1, source_target_pairs={{4,8},{8,4},{5,9},{9,5},{6,10},{10,6},{7,11},{11,7},{20,24},{24,20... | collective-permute-start | bytes 1966088 | tf_op jit(solution)/shard_map/ppermute | solution.py:516
  50.5 13.6 %collective-permute-start.14 = (s32[2]{0:T(128)S(1)}, s32[2]{0:T(128)S(1)}, u32[]{:S(2)}, u32[]{:S(2)}) collective-permute-start(s32[2]{0:T(128)S(1)} %copy-done.19), channel_id=1, source_target_pairs={{0,4},{12,8},{1,5},{13,9},{2,6},{14,10},{3,7},{15,11},{16,20},{28,... | collective-permute-start | bytes 32 | tf_op jit(solution)/shard_map/ppermute | solution.py:516
  60.9 1.0 copy-start.10
  64.1 41.2 %copy-start.18 = (s32[2]{0:T(128)}, s32[2]{0:T(128)S(1)}, u32[]{:S(2)}) copy-start(s32[2]{0:T(128)S(1)} %collective-permute-done.14.prompts_ref) | copy-start | bytes 28
  64.1 34.0 %collective-permute-start.12 = (bf16[1024,512]{1,0:T(8,128)(2,1)}, bf16[1024,512]{1,0:T(8,128)(2,1)}, u32[]{:S(2)}, u32[]{:S(2)}) collective-permute-start(bf16[1024,512]{1,0:T(8,128)(2,1)} %stacked.1.rest_2_), channel_id=1, source_target_pairs={{4,8},{8,4},{5,9},{9,5},{6,10},{10,6},{7,11},{11,7},{20,24},{24,20... | collective-permute-start | bytes 3145736 | tf_op jit(solution)/shard_map/ppermute | solution.py:516
  66.6 24.7 %collective-permute-start.16 = (bf16[256,1280]{1,0:T(8,128)(2,1)}, bf16[256,1280]{1,0:T(8,128)(2,1)}, u32[]{:S(2)}, u32[]{:S(2)}) collective-permute-start(bf16[256,1280]{1,0:T(8,128)(2,1)} %constant_dynamic-slice_fusion), channel_id=1, source_target_pairs={{0,4},{12,8},{1,5},{13,9},{2,6},{14,10},{3,7},{15,11},{16,20},{28,... | collective-permute-start | bytes 1966088 | tf_op jit(solution)/shard_map/ppermute | solution.py:516
  73.7 23.0 %collective-permute-start.1 = (bf16[256,1280]{1,0:T(8,128)(2,1)}, bf16[256,1280]{1,0:T(8,128)(2,1)S(1)}, u32[]{:S(2)}, u32[]{:S(2)}) collective-permute-start(bf16[256,1280]{1,0:T(8,128)(2,1)} %collective-permute-done.refs_3_.refs_2_), channel_id=1, source_target_pairs={{0,16},{16,0},{1,17},{17,1},{2,18},{18,2},{3,19},{19,3},{4,20},{20... | collective-permute-start | bytes 1966088 | tf_op jit(solution)/shard_map/ppermute | solution.py:535
  74.2 17.1 %collective-permute-start.15 = (bf16[128,1280]{1,0:T(8,128)(2,1)S(1)}, bf16[128,1280]{1,0:T(8,128)(2,1)S(1)}, u32[]{:S(2)}, u32[]{:S(2)}) collective-permute-start(bf16[128,1280]{1,0:T(8,128)(2,1)S(1)} %constant_dynamic-slice_fusion.1), channel_id=1, source_target_pairs={{0,4},{12,8},{1,5},{13,9},{2,6},{14,10},{3,7},{15,11},{16,20},{28,... | collective-permute-start | bytes 983048 | tf_op jit(solution)/shard_map/ppermute | solution.py:516
  91.3 20.7 %collective-permute-start.17 = (bf16[4,64,1792]{2,1,0:T(8,128)(2,1)}, bf16[4,64,1792]{2,1,0:T(8,128)(2,1)}, u32[]{:S(2)}, u32[]{:S(2)}) collective-permute-start(bf16[4,64,1792]{2,1,0:T(8,128)(2,1)} %pad_maximum_fusion), channel_id=1, source_target_pairs={{0,4},{12,8},{1,5},{13,9},{2,6},{14,10},{3,7},{15,11},{16,20},{28,... | collective-permute-start | bytes 2752520 | tf_op jit(solution)/shard_map/ppermute | solution.py:516
  96.7 0.8 copy-start.1
  97.5 24.5 %collective-permute-start.19 = (bf16[256,1280]{1,0:T(8,128)(2,1)}, bf16[256,1280]{1,0:T(8,128)(2,1)}, u32[]{:S(2)}, u32[]{:S(2)}) collective-permute-start(bf16[256,1280]{1,0:T(8,128)(2,1)} %collective-permute-done.16.refs_5_.refs_4_), channel_id=1, source_target_pairs={{0,16},{16,0},{1,17},{17,1},{2,18},{18,2},{3,19},{19,3},{4,20},{20... | collective-permute-start | bytes 1966088 | tf_op jit(solution)/shard_map/ppermute | solution.py:535
  105.3 16.8 %copy-start.15 = (s32[3]{0:T(128)S(1)}, s32[3]{0:T(128)}, u32[]{:S(2)}) copy-start(s32[3]{0:T(128)} %pad_add_fusion.here_ref._) | copy-start | bytes 40
  105.3 16.8 %collective-permute-start.13 = (bf16[4,64,1280]{2,1,0:T(8,128)(2,1)}, bf16[4,64,1280]{2,1,0:T(8,128)(2,1)}, u32[]{:S(2)}, u32[]{:S(2)}) collective-permute-start(bf16[4,64,1280]{2,1,0:T(8,128)(2,1)} %attend.2.refs_0_), channel_id=1, source_target_pairs={{4,8},{8,4},{5,9},{9,5},{6,10},{10,6},{7,11},{11,7},{20,24},{24,20... | collective-permute-start | bytes 1966088 | tf_op jit(solution)/shard_map/ppermute | solution.py:516
  106.8 15.2 %collective-permute-start.18 = (bf16[128,1280]{1,0:T(8,128)(2,1)S(1)}, bf16[128,1280]{1,0:T(8,128)(2,1)}, u32[]{:S(2)}, u32[]{:S(2)}) collective-permute-start(bf16[128,1280]{1,0:T(8,128)(2,1)S(1)} %collective-permute-done.15.refs_4_.refs_3_), channel_id=1, source_target_pairs={{0,16},{16,0},{1,17},{17,1},{2,18},{18,2},{3,19},{19,3},{4,20},{20... | collective-permute-start | bytes 983048 | tf_op jit(solution)/shard_map/ppermute | solution.py:535
  122.1 1.1 copy-start.2
  129.2 6.1 %copy-start.3 = (bf16[256,1280]{1,0:T(8,128)(2,1)S(1)}, bf16[256,1280]{1,0:T(8,128)(2,1)}, u32[]{:S(2)}) copy-start(bf16[256,1280]{1,0:T(8,128)(2,1)} %copy-done.1) | copy-start | bytes 1966084
  129.2 6.1 %copy-start.5 = (bf16[4,64,1280]{2,1,0:T(8,128)(2,1)S(1)}, bf16[4,64,1280]{2,1,0:T(8,128)(2,1)}, u32[]{:S(2)}) copy-start(bf16[4,64,1280]{2,1,0:T(8,128)(2,1)} %attend.2.refs_0_) | copy-start | bytes 1966084
  129.2 3.1 %collective-permute-start.20 = (bf16[4,128,1280]{2,1,0:T(8,128)(2,1)S(1)}, bf16[4,128,1280]{2,1,0:T(8,128)(2,1)S(1)}, u32[]{:S(2)}, u32[]{:S(2)}) collective-permute-start(bf16[4,128,1280]{2,1,0:T(8,128)(2,1)S(1)} %get-tuple-element.66), channel_id=1, source_target_pairs={{0,1},{1,0},{2,3},{3,2},{4,5},{5,4},{6,7},{7,6},{8,9},{9,8},{10,11... | collective-permute-start | bytes 3932168 | tf_op jit(solution)/shard_map/ppermute | solution.py:519
  129.3 14.5 %collective-permute-start.25 = (bf16[4,64,1280]{2,1,0:T(8,128)(2,1)}, bf16[4,64,1280]{2,1,0:T(8,128)(2,1)S(1)}, u32[]{:S(2)}, u32[]{:S(2)}) collective-permute-start(bf16[4,64,1280]{2,1,0:T(8,128)(2,1)} %attend.3.refs_1_), channel_id=1, source_target_pairs={{4,8},{8,4},{5,9},{9,5},{6,10},{10,6},{7,11},{11,7},{20,24},{24,20... | collective-permute-start | bytes 1966088 | tf_op jit(solution)/shard_map/ppermute | solution.py:516
  133.0 1.2 collective-permute-start.21
  134.2 1.1 collective-permute-start.22
  139.0 6.1 %collective-permute-start.23 = (bf16[4,64,1280]{2,1,0:T(8,128)(2,1)S(1)}, bf16[4,64,1280]{2,1,0:T(8,128)(2,1)S(1)}, u32[]{:S(2)}, u32[]{:S(2)}) collective-permute-start(bf16[4,64,1280]{2,1,0:T(8,128)(2,1)S(1)} %get-tuple-element.71), channel_id=1, source_target_pairs={{0,1},{1,0},{2,3},{3,2},{4,5},{5,4},{6,7},{7,6},{8,9},{9,8},{10,11... | collective-permute-start | bytes 1966088 | tf_op jit(solution)/shard_map/ppermute | solution.py:519
  139.3 12.7 %collective-permute-start.29 = (bf16[2,64,1280]{2,1,0:T(8,128)(2,1)S(1)}, bf16[2,64,1280]{2,1,0:T(8,128)(2,1)S(1)}, u32[]{:S(2)}, u32[]{:S(2)}) collective-permute-start(bf16[2,64,1280]{2,1,0:T(8,128)(2,1)S(1)} %get-tuple-element.67), channel_id=1, source_target_pairs={{0,2},{2,0},{1,3},{3,1},{4,6},{6,4},{5,7},{7,5},{8,10},{10,8},{9,1... | collective-permute-start | bytes 983048 | tf_op jit(solution)/shard_map/ppermute | solution.py:519
  143.8 1.1 collective-permute-start.26
  144.9 1.7 collective-permute-start.27
  146.6 5.3 %collective-permute-start.28 = (s32[3]{0:T(128)S(1)}, s32[3]{0:T(128)S(1)}, u32[]{:S(2)}, u32[]{:S(2)}) collective-permute-start(s32[3]{0:T(128)S(1)} %collective-permute-done.27), channel_id=1, source_target_pairs={{0,1},{1,0},{2,3},{3,2},{4,5},{5,4},{6,7},{7,6},{8,9},{9,8},{10,11... | collective-permute-start | bytes 44 | tf_op jit(solution)/shard_map/ppermute | solution.py:519
  151.9 1.1 collective-permute-start.30
  156.7 2.2 %collective-permute-start.31 = (bf16[4,64,1280]{2,1,0:T(8,128)(2,1)S(1)}, bf16[4,64,1280]{2,1,0:T(8,128)(2,1)S(1)}, u32[]{:S(2)}, u32[]{:S(2)}) collective-permute-start(bf16[4,64,1280]{2,1,0:T(8,128)(2,1)S(1)} %get-tuple-element.77), channel_id=1, source_target_pairs={{0,1},{1,0},{2,3},{3,2},{4,5},{5,4},{6,7},{7,6},{8,9},{9,8},{10,11... | collective-permute-start | bytes 1966088 | tf_op jit(solution)/shard_map/ppermute | solution.py:519
  157.0 10.5 %collective-permute-start.35 = (bf16[2,64,1280]{2,1,0:T(8,128)(2,1)S(1)}, bf16[2,64,1280]{2,1,0:T(8,128)(2,1)S(1)}, u32[]{:S(2)}, u32[]{:S(2)}) collective-permute-start(bf16[2,64,1280]{2,1,0:T(8,128)(2,1)S(1)} %get-tuple-element.80), channel_id=1, source_target_pairs={{0,2},{2,0},{1,3},{3,1},{4,6},{6,4},{5,7},{7,5},{8,10},{10,8},{9,1... | collective-permute-start | bytes 983048 | tf_op jit(solution)/shard_map/ppermute | solution.py:519
  159.5 20.7 %collective-permute-start.32 = (bf16[2,64,1280]{2,1,0:T(8,128)(2,1)S(1)}, bf16[2,64,1280]{2,1,0:T(8,128)(2,1)S(1)}, u32[]{:S(2)}, u32[]{:S(2)}) collective-permute-start(bf16[2,64,1280]{2,1,0:T(8,128)(2,1)S(1)} %added_half.4), channel_id=1, source_target_pairs={{0,2},{2,0},{1,3},{3,1},{4,6},{6,4},{5,7},{7,5},{8,10},{10,8},{9,1... | collective-permute-start | bytes 983048 | tf_op jit(solution)/shard_map/ppermute | solution.py:519
  161.4 6.2 %collective-permute-start.34 = (s32[3]{0:T(128)S(1)}, s32[3]{0:T(128)S(1)}, u32[]{:S(2)}, u32[]{:S(2)}) collective-permute-start(s32[3]{0:T(128)S(1)} %copy-done.15), channel_id=1, source_target_pairs={{0,1},{1,0},{2,3},{3,2},{4,5},{5,4},{6,7},{7,6},{8,9},{9,8},{10,11... | collective-permute-start | bytes 44 | tf_op jit(solution)/shard_map/ppermute | solution.py:519
  168.6 11.7 %collective-permute-start.36 = (bf16[2,64,1280]{2,1,0:T(8,128)(2,1)S(1)}, bf16[2,64,1280]{2,1,0:T(8,128)(2,1)S(1)}, u32[]{:S(2)}, u32[]{:S(2)}) collective-permute-start(bf16[2,64,1280]{2,1,0:T(8,128)(2,1)S(1)} %get-tuple-element.81), channel_id=1, source_target_pairs={{4,8},{5,9},{10,6},{11,7},{6,0},{7,1},{8,14},{9,15},{20,24},{21,25... | collective-permute-start | bytes 983048 | tf_op jit(solution)/shard_map/ppermute | solution.py:489
  169.3 11.0 %collective-permute-start.37 = (bf16[2,64,1280]{2,1,0:T(8,128)(2,1)S(1)}, bf16[2,64,1280]{2,1,0:T(8,128)(2,1)S(1)}, u32[]{:S(2)}, u32[]{:S(2)}) collective-permute-start(bf16[2,64,1280]{2,1,0:T(8,128)(2,1)S(1)} %get-tuple-element.82), channel_id=1, source_target_pairs={{6,8},{7,9},{8,6},{9,7},{4,0},{5,1},{10,14},{11,15},{22,24},{23,25... | collective-permute-start | bytes 983048 | tf_op jit(solution)/shard_map/ppermute | solution.py:489
  169.9 14.7 %collective-permute-start.24 = (bf16[4,64,1280]{2,1,0:T(8,128)(2,1)}, bf16[4,64,1280]{2,1,0:T(8,128)(2,1)S(1)}, u32[]{:S(2)}, u32[]{:S(2)}) collective-permute-start(bf16[4,64,1280]{2,1,0:T(8,128)(2,1)} %added.10.refs_0_), channel_id=1, source_target_pairs={{6,4},{7,5},{8,10},{9,11},{22,20},{23,21},{24,26},{25,27}} | collective-permute-start | bytes 1966088 | tf_op jit(solution)/shard_map/ppermute | solution.py:498
  180.2 1.1 collective-permute-start.33
  182.0 12.6 %collective-permute-start.38 = (bf16[2,64,1280]{2,1,0:T(8,128)(2,1)S(1)}, bf16[2,64,1280]{2,1,0:T(8,128)(2,1)S(1)}, u32[]{:S(2)}, u32[]{:S(2)}) collective-permute-start(bf16[2,64,1280]{2,1,0:T(8,128)(2,1)S(1)} %added_half.5), channel_id=1, source_target_pairs={{4,12},{5,13},{10,2},{11,3},{20,28},{21,29},{26,18},{27,19}} | collective-permute-start | bytes 983048 | tf_op jit(solution)/shard_map/ppermute | solution.py:489
  183.3 13.6 %collective-permute-start.39 = (bf16[2,64,1280]{2,1,0:T(8,128)(2,1)S(1)}, bf16[2,64,1280]{2,1,0:T(8,128)(2,1)}, u32[]{:S(2)}, u32[]{:S(2)}) collective-permute-start(bf16[2,64,1280]{2,1,0:T(8,128)(2,1)S(1)} %added_half.5), channel_id=1, source_target_pairs={{6,12},{7,13},{8,2},{9,3},{22,28},{23,29},{24,18},{25,19}} | collective-permute-start | bytes 983048 | tf_op jit(solution)/shard_map/ppermute | solution.py:489

commit v4 on v3

--- a/solution.py
+++ b/solution.py
@@ -214,7 +214,7 @@
     groups = new_width // (2 * HD)
     width = groups * GQA * HD
     tokens = sum(part.shape[0] for part in pages[0])
-    most = max(len(page) for page in pages)
+    count = chosen[1] - chosen[0]
     page_parts = [part for page in pages for part in page]
     tiles = 4
     chunk = tokens // tiles
@@ -226,9 +226,9 @@
         out_ref, held, query_ref, new_ref, sems = rest
         plane = here_ref[1]
 
-        def run(written, used, length):
-            query = query_ref[...].reshape(flat, width)
-            new = new_ref[...].reshape(flat, new_width)
+        def run(at, written, used, length):
+            query = query_ref[at].reshape(flat, width)
+            new = new_ref[at].reshape(flat, new_width)
             shape = (GQA * flat, flat)
             asker = lax.broadcasted_iota(jnp.int32, shape, 0) % flat
             holder = lax.broadcasted_iota(jnp.int32, shape, 1)
@@ -252,7 +252,8 @@
                     )
 
                 parts = [
-                    scores(held[at * chunk : (at + 1) * chunk, key]) for at in range(used // chunk)
+                    scores(held[at, tile * chunk : (tile + 1) * chunk, key])
+                    for tile in range(used // chunk)
                 ]
                 parts[-1] = jnp.where(last_ok, parts[-1], masked_score)
                 parts.append(jnp.where(near_ok, scores(new[:, key]), masked_score))
@@ -260,12 +261,12 @@
                 for part in parts[1:]:
                     peak = jnp.maximum(peak, jnp.max(part, axis=1, keepdims=True))
                 total, summed = 0.0, 0.0
-                for at, part in enumerate(parts):
+                for tile, part in enumerate(parts):
                     weights = jnp.exp2((part - peak) * factor)
                     total = total + jnp.sum(weights, axis=1, keepdims=True)
                     values = (
-                        held[at * chunk : (at + 1) * chunk, value]
-                        if at < len(parts) - 1
+                        held[at, tile * chunk : (tile + 1) * chunk, value]
+                        if tile < len(parts) - 1
                         else new[:, value]
                     )
                     summed = summed + jnp.dot(
@@ -278,45 +279,43 @@
                         head * flat : (head + 1) * flat
                     ].reshape(steps, block_rows, HD)
 
-        @pl.loop(*chosen)
-        def _(block):
-            mine = pl.ds(pl.multiple_of(block * block_rows, block_rows), block_rows)
-            written = pl.ds(
-                pl.multiple_of((block - chosen[0]) * block_rows, block_rows), block_rows
-            )
-            prompt = prompts_ref[block]
-            slot, length = owners_ref[prompt], lengths_ref[prompt]
-            fetch_query = pltpu.make_async_copy(query_hbm.at[:, mine, :width], query_ref, sems.at[0])
-            fetch_new = pltpu.make_async_copy(new_hbm.at[:, mine, new_start : new_start + new_width], new_ref, sems.at[1])
-            fetch_query.start()
-            fetch_new.start()
-            passed = 0
+        for block in range(*chosen):
+            at = block - chosen[0]
+            mine = slice(block * block_rows, (block + 1) * block_rows)
+            pltpu.make_async_copy(
+                query_hbm.at[:, mine, :width], query_ref.at[at], sems.at[0, at]
+            ).start()
+            pltpu.make_async_copy(
+                new_hbm.at[:, mine, new_start : new_start + new_width], new_ref.at[at], sems.at[1, at]
+            ).start()
+            slot, passed = owners_ref[prompts_ref[block]], 0
             for page, place in zip(pages, (plane, plane ^ 1, 3 - plane, (3 - plane) ^ 1)):
                 refs = page_refs[passed : passed + len(page)]
                 passed += len(page)
 
                 @pl.when(slot == place)
                 def _():
-                    low, fetches = 0, []
-                    for at, ref in enumerate(refs):
-                        target = held.at[low : low + ref.shape[0]]
-                        fetches.append(pltpu.make_async_copy(ref, target, sems.at[2 + at]))
+                    low = 0
+                    for ref in refs:
+                        target = held.at[at, low : low + ref.shape[0]]
+                        pltpu.make_async_copy(ref, target, sems.at[2, at]).start()
                         low += ref.shape[0]
-                    for fetch in fetches:
-                        fetch.start()
-                    for fetch in fetches:
-                        fetch.wait()
-
-            fetch_query.wait()
-            fetch_new.wait()
-            for count in range(1, tiles + 1):
-                enough = length > (count - 1) * chunk
-                if count < tiles:
-                    enough = jnp.logical_and(enough, length <= count * chunk)
+
+        @pl.loop(0, count)
+        def _(at):
+            written = pl.ds(pl.multiple_of(at * block_rows, block_rows), block_rows)
+            for kind, buffer in enumerate((query_ref, new_ref, held)):
+                whole = buffer.at[at]
+                pltpu.make_async_copy(whole, whole, sems.at[kind, at]).wait()
+            length = lengths_ref[prompts_ref[chosen[0] + at]]
+            for used in range(1, tiles + 1):
+                enough = length > (used - 1) * chunk
+                if used < tiles:
+                    enough = jnp.logical_and(enough, length <= used * chunk)
 
                 @pl.when(enough)
                 def _():
-                    run(written, count * chunk, length)
+                    run(at, written, used * chunk, length)
 
     in_vmem, in_smem, in_hbm = (
         pl.BlockSpec(memory_space=space) for space in (pltpu.VMEM, pltpu.SMEM, pltpu.HBM)
@@ -326,13 +325,13 @@
         in_specs=[in_smem] * 4 + [in_hbm] * (2 + len(page_parts)),
         out_specs=in_vmem,
         out_shape=jax.ShapeDtypeStruct(
-            (steps, (chosen[1] - chosen[0]) * block_rows, width), jnp.bfloat16
+            (steps, count * block_rows, width), jnp.bfloat16
         ),
         scratch_shapes=[
-            pltpu.VMEM((tokens, new_width), jnp.bfloat16),
-            pltpu.VMEM((steps, block_rows, width), jnp.bfloat16),
-            pltpu.VMEM((steps, block_rows, new_width), jnp.bfloat16),
-            pltpu.SemaphoreType.DMA((2 + most,)),
+            pltpu.VMEM((count, tokens, new_width), jnp.bfloat16),
+            pltpu.VMEM((count, steps, block_rows, width), jnp.bfloat16),
+            pltpu.VMEM((count, steps, block_rows, new_width), jnp.bfloat16),
+            pltpu.SemaphoreType.DMA((3, count)),
         ],
         compiler_params=compiler_params(LARGE_VMEM),
         cost_estimate=small_cost(),
@@ -352,7 +351,8 @@
 
     def body(here_ref, *refs):
         row_refs, own_ref, refs = refs[:count], refs[count], refs[count + 1 :]
-        moved_refs, (keep_ref, send_ref, taken_ref) = refs[:moved_count], refs[moved_count:]
+        moved_refs, refs = refs[:moved_count], refs[moved_count:]
+        keep_ref, send_refs, taken_ref = refs[0], refs[1:-1], refs[-1]
         for ref, place in zip(row_refs, places):
             flat = slice(steps * place.start, steps * place.stop)
             taken_ref[flat] = ref[...].reshape(flat.stop - flat.start, features)
@@ -372,89 +372,123 @@
                 )
             keep = jnp.where(keeps_own, own, moved).astype(jnp.bfloat16)
             send = jnp.where(keeps_own, moved, own).astype(jnp.bfloat16)
-            for place in places:
+            for place, send_ref in zip(places, send_refs):
                 flat = slice(steps * place.start, steps * place.stop)
                 shape = (steps, place.stop - place.start, tile)
                 keep_ref[:, place, part] = keep[flat].reshape(shape)
-                send_ref[:, place, part] = send[flat].reshape(shape)
+                send_ref[:, :, part] = send[flat].reshape(shape)
 
     in_vmem = pl.BlockSpec(memory_space=pltpu.VMEM)
-    out_shape = jax.ShapeDtypeStruct((steps, ends[-1], columns), jnp.bfloat16)
-    return pl.pallas_call(
+    out_rows = [ends[-1], *[block.shape[1] for block in blocks]]
+    keep, *sends = pl.pallas_call(
         body,
         in_specs=[pl.BlockSpec(memory_space=pltpu.SMEM)] + [in_vmem] * (count + 1 + moved_count),
-        out_specs=[in_vmem, in_vmem],
-        out_shape=[out_shape, out_shape],
+        out_specs=[in_vmem] * (1 + count),
+        out_shape=[jax.ShapeDtypeStruct((steps, rows, columns), jnp.bfloat16) for rows in out_rows],
         scratch_shapes=[pltpu.VMEM((steps * ends[-1], features), jnp.bfloat16)],
         compiler_params=compiler_params(),
         cost_estimate=small_cost(),
         name="spread",
     )(here, *blocks, own_weight, *[part for _, _, part in moved_weights])
-
-
-def run_small(body, name, here, operands, out_shape, outs=1):
+    return keep, sends
+
+
+def run_small(body, name, here, operands, out_shape, outs=1, limit=VMEM, waits_for=()):
     in_vmem = pl.BlockSpec(memory_space=pltpu.VMEM)
+
+    def whole(*refs):
+        body(*refs[: 1 + len(operands)], *refs[1 + len(operands) + len(waits_for) :])
+
     return pl.pallas_call(
-        body,
-        in_specs=[pl.BlockSpec(memory_space=pltpu.SMEM)] + [in_vmem] * len(operands),
+        whole,
+        in_specs=[pl.BlockSpec(memory_space=pltpu.SMEM)]
+        + [in_vmem] * len(operands)
+        + [pl.BlockSpec(memory_space=pltpu.HBM)] * len(waits_for),
         out_specs=[in_vmem] * outs,
         out_shape=[jax.ShapeDtypeStruct(out_shape, jnp.bfloat16)] * outs,
-        compiler_params=compiler_params(),
+        compiler_params=compiler_params(limit),
         cost_estimate=small_cost(),
         name=name,
-    )(here, *operands)
-
-
-def added(here, *parts):
+    )(here, *operands, *waits_for)
+
+
+def added(here, *parts, limit=VMEM):
     def body(_, *refs):
         total = refs[0][...].astype(jnp.float32)
         for ref in refs[1:-1]:
             total = total + ref[...].astype(jnp.float32)
         refs[-1][...] = total.astype(jnp.bfloat16)
 
-    return run_small(body, "added", here, parts, parts[0].shape)[0]
-
-
-def stacked(here, *parts):
+    return run_small(body, "added", here, parts, parts[0].shape, limit=limit)[0]
+
+
+def added_pieces(here, one, two, pieces, waits_for):
+    steps, rows, columns = one.shape
+    piece = rows // pieces
+
+    def body(_, one_ref, two_ref, *outs):
+        total = one_ref[...].astype(jnp.float32) + two_ref[...].astype(jnp.float32)
+        total = total.astype(jnp.bfloat16)
+        for at, out in enumerate(outs):
+            out[...] = total[:, at * piece : (at + 1) * piece]
+
+    shape = (steps, piece, columns)
+    return run_small(body, "added_pieces", here, (one, two), shape, pieces, waits_for=waits_for)
+
+
+def joined(here, ones, twos, waits_for):
+    steps, piece, columns = ones[0].shape
+    count = len(ones)
+
+    def body(_, *refs):
+        for at in range(count):
+            total = refs[at][...].astype(jnp.float32) + refs[count + at][...].astype(jnp.float32)
+            refs[-1][:, at * piece : (at + 1) * piece] = total.astype(jnp.bfloat16)
+
+    shape = (steps, count * piece, columns)
+    return run_small(body, "joined", here, (*ones, *twos), shape, waits_for=waits_for)[0]
+
+
+def stacked(here, *parts, waits_for):
     rows = [part.shape[0] for part in parts]
 
     def body(_, *refs):
         for at, ref in enumerate(refs[:-1]):
             refs[-1][sum(rows[:at]) : sum(rows[: at + 1])] = ref[...]
 
-    return run_small(body, "stacked", here, parts, (sum(rows), *parts[0].shape[1:]))[0]
-
-
-def added_half(here, mine, wide, narrow=(), pieces=1):
-    steps, rows, columns = wide[0].shape
-    half, piece = steps // 2, rows // pieces
-
-    def body(here_ref, *refs):
-        ins, outs = refs[:-pieces], refs[-pieces:]
+    shape = (sum(rows), *parts[0].shape[1:])
+    return run_small(body, "stacked", here, parts, shape, waits_for=waits_for)[0]
+
+
+def added_half(here, mine, keep, sends, crossed=None):
+    steps, rows, columns = keep.shape
+    half, count = steps // 2, len(sends)
+    ends = [sum(send.shape[1] for send in sends[:at]) for at in range(count + 1)]
+
+    def body(here_ref, keep_ref, *refs):
         chip = here_ref[2] // 2
         taken = pl.ds((chip if mine else 1 - chip) * half, half)
-        total = ins[0][taken].astype(jnp.float32)
-        for at, ref in enumerate(ins[1:], 1):
-            part = ref[taken] if at < len(wide) else ref[...]
-            total = total + part.astype(jnp.float32)
-        total = total.astype(jnp.bfloat16)
-        for at, out in enumerate(outs):
-            out[...] = total[:, at * piece : (at + 1) * piece]
-
-    outs = run_small(body, "added_half", here, (*wide, *narrow), (half, piece, columns), pieces)
-    return outs if pieces > 1 else outs[0]
-
-
-def added_halves(here, one, two, far_crossed, end_crossed):
-    steps, rows, columns = one.shape
+        for at in range(count):
+            place = slice(ends[at], ends[at + 1])
+            total = keep_ref[taken, place].astype(jnp.float32) + refs[at][taken].astype(jnp.float32)
+            if crossed is not None:
+                total = total + refs[count][:, place].astype(jnp.float32)
+            refs[-1][:, place] = total.astype(jnp.bfloat16)
+
+    operands = (keep, *sends) if crossed is None else (keep, *sends, crossed)
+    return run_small(body, "added_half", here, operands, (half, rows, columns))[0]
+
+
+def added_halves(here, keep, sends, crossed):
+    steps, rows, columns = keep.shape
     half, piece = steps // 2, rows // 2
 
-    def body(here_ref, one_ref, two_ref, far_ref, end_ref, first_ref, second_ref):
+    def body(here_ref, keep_ref, far_ref, end_ref, crossed_ref, first_ref, second_ref):
         chip = here_ref[2] // 2
         taken = pl.ds(chip * half, half)
-        total = one_ref[taken].astype(jnp.float32) + two_ref[taken].astype(jnp.float32)
-        far = (total[:, :piece] + far_ref[...].astype(jnp.float32)).astype(jnp.bfloat16)
-        end = (total[:, piece:] + end_ref[...].astype(jnp.float32)).astype(jnp.bfloat16)
+        total = keep_ref[taken].astype(jnp.float32) + crossed_ref[...].astype(jnp.float32)
+        far = (total[:, :piece] + far_ref[taken].astype(jnp.float32)).astype(jnp.bfloat16)
+        end = (total[:, piece:] + end_ref[taken].astype(jnp.float32)).astype(jnp.bfloat16)
         at_home = here_ref[1] // 2 == chip
 
         @pl.when(at_home)
@@ -468,7 +502,7 @@
             second_ref[...] = far
 
     shape = (half, piece, columns)
-    return run_small(body, "added_halves", here, (one, two, far_crossed, end_crossed), shape, 2)
+    return run_small(body, "added_halves", here, (keep, *sends, crossed), shape, 2)
 
 
 def after(value, *others):
@@ -518,55 +552,59 @@
     def on_head(value, pairs):
         return lax.ppermute(value, "head", pairs)
 
+    def hopped(*values):
+        token = here
+        for value in values:
+            token = on_head(after(token, *value), CORE)
+        return token
+
+    def beside(value, *others):
+        return on_head(after(value, *others), CORE)
+
     states = prompt_states[0]
     tokens = states.shape[0]
-    cuts = [0, tokens * 3 // 8, tokens]
+    cuts = [0, tokens * 7 // 16, tokens]
     sent, kept = project(here, states, kv_weight, (3, 2), cuts)
 
     half = out_weight.shape[0] // 2
-    weight_cuts = [0, half * 2 // 5, half * 3 // 5, half]
+    weight_cuts = [0, half * 2 // 5, half]
 
     def weight_part(at, *others):
         low, size = weight_cuts[at], weight_cuts[at + 1] - weight_cuts[at]
-        part = lax.dynamic_slice_in_dim(after(out_weight, *others), group * half + low, size, 0)
-        return on_samp(part, INWARD)
+        return lax.dynamic_slice_in_dim(after(out_weight, *others), group * half + low, size, 0)
 
     def swapped(part):
         return lax.ppermute(part, "groups", [(0, 1), (1, 0)])
 
-    weight_0 = weight_part(0, sent[0])
-    leaving_first = added(here, kept[0], on_head(sent[0], CORE))
-    leaving_second = added(here, kept[1], after(on_head(sent[1], CORE), leaving_first))
+    weight_0 = on_samp(weight_part(0, sent[0]), INWARD)
+    leaving_first = added(here, kept[0], on_head(sent[0], CORE), limit=LARGE_VMEM)
+    leaving_second = added(here, kept[1], after(on_head(sent[1], CORE), leaving_first), limit=LARGE_VMEM)
     crossed_first = on_head(leaving_first, ACROSS_X)
     crossed_second = on_head(leaving_second, ACROSS_X)
     sent, kept = project(
         here, after(states, leaving_first, leaving_second), kv_weight, (1, 0), cuts
     )
     sent = [on_head(value, CORE) for value in sent]
-    first = added(here, kept[0], sent[0], crossed_first)
+    first = added(hopped((crossed_first,)), kept[0], sent[0], crossed_first, limit=LARGE_VMEM)
     end_first = on_samp(after(first, weight_0), INWARD)
     far_first = on_samp(first, MIDDLE)
-    second = added(here, kept[1], after(sent[1], far_first, end_first), crossed_second)
+    second = added(hopped((crossed_second,)), kept[1], sent[1], crossed_second, limit=LARGE_VMEM)
     end_second = on_samp(second, INWARD)
     far_second = on_samp(second, MIDDLE)
-    end_page = stacked(here, end_first, end_second)
+    end_page = stacked(
+        here, end_first, end_second, waits_for=(beside(leaving_first, far_first, end_first),)
+    )
+    moved_0 = swapped(weight_0)
     far_end_page = on_samp(after(end_page, far_second), MIDDLE)
     pages = ((first, second), (end_page,), (far_first, far_second), (far_end_page,))
     end_prompts = on_samp(after(sampler_prompts, second), INWARD)
-    weight_1, weight_2 = (weight_part(at, end_second, end_prompts) for at in (1, 2))
+    weight_1 = on_samp(after(weight_part(1, first), end_second, end_prompts), INWARD)
     asked = jnp.concatenate([after(step_queries, first), step_kv], axis=2)
-    end_asked = on_samp(after(asked, weight_1, weight_2), INWARD)
-    moved_0, moved_1, moved_2 = swapped(weight_0), swapped(weight_1), swapped(weight_2)
-    parts = ((weight_0, moved_0), (weight_1, moved_1), (weight_2, moved_2))
+    end_asked = on_samp(after(asked, weight_1), INWARD)
+    parts = ((weight_0, moved_0), (weight_1, swapped(weight_1)))
     moved_weights = [
         (low, side, part[side]) for side in range(2) for low, part in zip(weight_cuts, parts)
     ]
-
-    def hopped(*values):
-        token = here
-        for value in values:
-            token = on_head(after(token, value), CORE)
-        return token
 
     def attended(place, chosen, prompts, queries, news):
         rows = attend(
@@ -575,8 +613,8 @@
         return rows, on_samp(rows, MIDDLE)
 
     def spread_out(*blocks, place=here):
-        keep, send = spread(place, blocks, out_weight, moved_weights)
-        return keep, on_head(send, CORE)
+        keep, sends = spread(place, blocks, out_weight, moved_weights)
+        return keep, [on_head(send, CORE) for send in sends]
 
     blocks = sampler_prompts.shape[0]
     own_rows, far_own_rows = attended(
@@ -590,20 +628,25 @@
         (end_asked, step_queries.shape[2]),
     )
     both_keep, both_arrived = spread_out(far_own_rows, end_rows)
-    far_leaving, end_leaving = added_half(here, False, (both_keep, both_arrived), (), 2)
-    end_crossed = on_head(end_leaving, ACROSS_X)
-    far_crossed = on_head(far_leaving, ACROSS_X)
-    own_keep, own_arrived = spread_out(own_rows, place=hopped(end_leaving, end_leaving))
-    own_chip = added(here, own_keep, own_arrived)
-    own_crossed = across_home(own_chip)
-    beyond_keep, beyond_arrived = spread_out(
-        far_end_rows, place=hopped(far_end_rows, far_end_rows, own_chip, end_crossed)
-    )
-    beyond_leaving = added_half(here, False, (beyond_keep, beyond_arrived))
+    own_keep, own_arrived = spread_out(after(own_rows, both_keep))
+    place = hopped((far_end_rows,), (far_end_rows,))
+    both_leaving = added_half(place, False, both_keep, both_arrived)
+    both_crossed = on_head(both_leaving, ACROSS_X)
+    beyond_keep, beyond_arrived = spread_out(after(far_end_rows, own_keep, both_leaving))
+    beyond_leaving = added_half(here, False, beyond_keep, beyond_arrived)
     beyond_crossed = on_head(beyond_leaving, ACROSS_X)
-    first_sum, second_sum = added_halves(
-        hopped(beyond_leaving), both_keep, both_arrived, far_crossed, end_crossed
-    )
+    own_chip = added_pieces(
+        here,
+        own_keep,
+        after(own_arrived[0], beyond_leaving),
+        2,
+        waits_for=(beside(own_rows, both_crossed),),
+    )
+    own_crossed = [
+        across_home(after(part, earlier))
+        for part, earlier in zip(own_chip, (both_crossed, beyond_crossed))
+    ]
+    first_sum, second_sum = added_halves(here, both_keep, both_arrived, both_crossed)
 
     def far(at):
         return 3 - at
@@ -617,13 +660,12 @@
     first_home = sent_home(first_sum, home_pairs(far, False), home_pairs(end, True))
     second_home = sent_home(second_sum, home_pairs(far, True), home_pairs(end, False))
     beyond_sum = added_half(
-        hopped(beyond_crossed),
-        True,
-        (beyond_keep, after(beyond_arrived, first_home, second_home)),
-        (beyond_crossed,),
+        here, True, beyond_keep, beyond_arrived, beyond_crossed
     )
     beyond_home = [sent_home(beyond_sum, home_pairs(beyond, turned)) for turned in (False, True)]
-    own_home = added(here, own_chip, after(own_crossed, beyond_sum))
+    own_home = joined(
+        here, own_chip, own_crossed, waits_for=(beside(own_keep, own_crossed[0]),)
+    )
 
     is_middle = jnp.logical_or(plane == 1, plane == 2)
     near_side = chip == plane // 2

time: 200 us -> 189 us (0.945)
  starting transfers between devices: 52.9 us -> 42.8 us
  local copies, waits for them, and re-layouts: 9.5 us -> 6.04 us
  waiting for transfers between devices: 74.5 us -> 77.3 us
    ppermute x4, waiting for transfers between devices: 11 us -> 22.4 us  [sent_home(): lax.ppermute(value, ('samp', 'head'), [pair for part in pairs for pair in...]
    ppermute x20 -> x19, waiting for transfers between devices: 30.9 us -> 23 us  [on_head(): return lax.ppermute(value, 'head', pairs)]
    ppermute x20 -> x19, starting transfers between devices: 12.8 us -> 7.72 us  [on_head(): return lax.ppermute(value, 'head', pairs)]
    ppermute x12 -> x11, starting transfers between devices: 32.9 us -> 28.7 us  [on_samp(): return lax.ppermute(value, 'samp', pairs)]
    pallas_call x2, Pallas kernels: 17.2 us -> 13.9 us  [attend(): pl.pallas_call(body, in_specs=[in_smem] * 4 + [in_hbm] * (2 + len(page_pa...]
    unnamed x40 -> x34, local copies, waits for them, and re-layouts: 7.66 us -> 5.1 us
    ppermute x12 -> x11, waiting for transfers between devices: 32.6 us -> 31.9 us  [on_samp(): return lax.ppermute(value, 'samp', pairs)]
  transfers between devices with their start and end apart: 40 -> 38, of which waited for: 17 -> 12; matrix products, arithmetic and copies ran while one was open for 2% -> 2% of each run, Pallas kernels for 20% -> 26%
where the time goes in v4:
time: 189 us; the launch traced here: 187 us
  waiting for transfers between devices  77.3 us (41%)
  Pallas kernels  56.8 us (30%)
  starting transfers between devices  42.8 us (23%)
  local copies, waits for them, and re-layouts  6.04 us (3%)
  other arithmetic  3.72 us (2%)
    ppermute x11, waiting for transfers between devices, on_samp(): return lax.ppermute(value, 'samp', pairs)  31.9 us
    ppermute x11, starting transfers between devices, on_samp(): return lax.ppermute(value, 'samp', pairs)  28.7 us
    ppermute x19, waiting for transfers between devices, on_head(): return lax.ppermute(value, 'head', pairs)  23 us
    ppermute x4, waiting for transfers between devices, sent_home(): lax.ppermute(value, ('samp', 'head'), [pair for part in pairs for pair in...  22.4 us
    pallas_call x11, Pallas kernels, run_small(): pl.pallas_call(whole, in_specs=[pl.BlockSpec(memory_space=pltpu.SMEM)] +...  15.3 us
    pallas_call x3, Pallas kernels, spread(): pl.pallas_call(body, in_specs=[pl.BlockSpec(memory_space=pltpu.SMEM)] + [...  14.5 us
    pallas_call x2, Pallas kernels, attend(): pl.pallas_call(body, in_specs=[in_smem] * 4 + [in_hbm] * (2 + len(page_pa...  13.9 us
    pallas_call x2, Pallas kernels, project(): pl.pallas_call(body, in_specs=[pl.BlockSpec(memory_space=pltpu.SMEM), in_...  13.2 us
  transfers between devices with their start and end apart: 38, of which 12 were waited for; matrix products, arithmetic and copies ran while one was open for 2% of the time, Pallas kernels for 26%

profile of v4, /device:TPU:6, one launch (start us, length us, event | category | flops | bytes accessed | tf_op | source)
XLA Modules:
  0.0 187.1 jit_solution(5040516897928066239)
XLA Ops:
  0.0 0.6 pad_add_fusion.here_ref.refs_0_
  0.6 6.7 %project.2 = (bf16[448,512]{1,0:T(8,128)(2,1)}, bf16[576,512]{1,0:T(8,128)(2,1)}, bf16[448,512]{1,0:T(8,128)(2,1)}, bf16[576,512]{1,0:T(8,128)(2,1)}) custom-call(s32[3]{0:T(128)} %pad_add_fusion.here_ref.refs_0_, bf16[1024,1280]{1,0:T(8,128)(2,1)} %bitcast.4, bf16[1280,2048]{1,0:T(8,128)(2,1)} %weight_hbm.3), custom_call_target="tpu_custom_call" | custom-call | flops 64 | bytes 64 | tf_op jit(solution)/shard_map/project/pallas_call | solution.py:190
  7.9 0.9 constant_dynamic-slice_fusion.1
  8.8 4.3 %collective-permute-start = (bf16[256,1280]{1,0:T(8,128)(2,1)}, bf16[256,1280]{1,0:T(8,128)(2,1)}, u32[]{:S(2)}, u32[]{:S(2)}) collective-permute-start(bf16[256,1280]{1,0:T(8,128)(2,1)} %constant_dynamic-slice_fusion.1), channel_id=1, source_target_pairs={{0,4},{12,8},{1,5},{13,9},{2,6},{14,10},{3,7},{15,11},{16,20},{28,... | collective-permute-start | bytes 1966088 | tf_op jit(solution)/shard_map/ppermute | solution.py:550
  13.1 2.1 %added.4 = bf16[448,512]{1,0:T(8,128)(2,1)} custom-call(s32[3]{0:T(128)} %pad_add_fusion.here_ref.refs_0_, bf16[448,512]{1,0:T(8,128)(2,1)} %get-tuple-element.51.refs_1_, bf16[448,512]{1,0:T(8,128)(2,1)} %collective-permute-done.2.refs_2_), custom_call_target="tpu_custom_call" | custom-call | flops 64 | bytes 64 | tf_op jit(solution)/shard_map/added/pallas_call | solution.py:402
  15.2 0.5 collective-permute-start.3
  15.7 2.2 %added.5 = bf16[576,512]{1,0:T(8,128)(2,1)} custom-call(s32[3]{0:T(128)} %pad_add_fusion.here_ref.refs_0_, bf16[576,512]{1,0:T(8,128)(2,1)} %get-tuple-element.53.refs_1_, bf16[576,512]{1,0:T(8,128)(2,1)} %collective-permute-done.5.refs_2_), custom_call_target="tpu_custom_call" | custom-call | flops 64 | bytes 64 | tf_op jit(solution)/shard_map/added/pallas_call | solution.py:402
  17.9 6.5 %project.3 = (bf16[448,512]{1,0:T(8,128)(2,1)}, bf16[576,512]{1,0:T(8,128)(2,1)}, bf16[448,512]{1,0:T(8,128)(2,1)}, bf16[576,512]{1,0:T(8,128)(2,1)}) custom-call(s32[3]{0:T(128)} %pad_add_fusion.here_ref.refs_0_, bf16[1024,1280]{1,0:T(8,128)(2,1)} %bitcast.5, bf16[1280,2048]{1,0:T(8,128)(2,1)} %weight_hbm.3), custom_call_target="tpu_custom_call" | custom-call | flops 64 | bytes 64 | tf_op jit(solution)/shard_map/project/pallas_call | solution.py:190
  24.5 1.6 collective-permute-start.7
  26.2 1.4 collective-permute-done.3.refs_3_
  27.6 1.1 collective-permute-done.4.refs_0_
  28.7 0.5 copy-done.15
  29.2 2.2 %added.6.rest_0_ = bf16[448,512]{1,0:T(8,128)(2,1)} custom-call(s32[3]{0:T(128)} %copy-done.15, bf16[448,512]{1,0:T(8,128)(2,1)} %get-tuple-element.57.refs_1_, bf16[448,512]{1,0:T(8,128)(2,1)} %collective-permute-done.6.refs_2_, bf16[448,512]{1,0:T(8,128)(2,1)} %copy-done.12), custom_call_target="tpu_custom_call" | custom-call | flops 64 | bytes 64 | tf_op jit(solution)/shard_map/added/pallas_call | solution.py:402
  31.5 2.2 %collective-permute-start.10 = (bf16[448,512]{1,0:T(8,128)(2,1)}, bf16[448,512]{1,0:T(8,128)(2,1)}, u32[]{:S(2)}, u32[]{:S(2)}) collective-permute-start(bf16[448,512]{1,0:T(8,128)(2,1)} %added.6.rest_0_), channel_id=1, source_target_pairs={{0,4},{12,8},{1,5},{13,9},{2,6},{14,10},{3,7},{15,11},{16,20},{28,... | collective-permute-start | bytes 1376264 | tf_op jit(solution)/shard_map/ppermute | solution.py:550
  33.7 1.5 collective-permute-start.12
  35.1 5.4 %collective-permute-done.7.refs_3_ = bf16[576,512]{1,0:T(8,128)(2,1)} collective-permute-done((bf16[576,512]{1,0:T(8,128)(2,1)}, bf16[576,512]{1,0:T(8,128)(2,1)}, u32[]{:S(2)}, u32[]{:S(2)}) %collective-permute-start.7) | collective-permute-done | bytes 589856 | tf_op jit(solution)/shard_map/ppermute | solution.py:553
  40.5 1.1 collective-permute-done.8.refs_0_
  41.6 0.5 copy-done.14
  42.2 2.5 %added.7.rest_1_ = bf16[576,512]{1,0:T(8,128)(2,1)} custom-call(s32[3]{0:T(128)} %copy-done.14, bf16[576,512]{1,0:T(8,128)(2,1)} %get-tuple-element.60.refs_1_, bf16[576,512]{1,0:T(8,128)(2,1)} %collective-permute-done.9.refs_2_, bf16[576,512]{1,0:T(8,128)(2,1)} %collective-permute-done.7.refs_3_), custom_call_target="tpu_custom_call" | custom-call | flops 64 | bytes 64 | tf_op jit(solution)/shard_map/added/pallas_call | solution.py:402
  44.7 2.2 %collective-permute-start.11 = (bf16[576,512]{1,0:T(8,128)(2,1)}, bf16[576,512]{1,0:T(8,128)(2,1)}, u32[]{:S(2)}, u32[]{:S(2)}) collective-permute-start(bf16[576,512]{1,0:T(8,128)(2,1)} %added.7.rest_1_), channel_id=1, source_target_pairs={{0,4},{12,8},{1,5},{13,9},{2,6},{14,10},{3,7},{15,11},{16,20},{28,... | collective-permute-start | bytes 1769480 | tf_op jit(solution)/shard_map/ppermute | solution.py:550
  46.9 0.8 collective-permute-start.14
  48.1 2.7 %collective-permute-start.17 = (s32[2]{0:T(128)S(1)}, s32[2]{0:T(128)S(1)}, u32[]{:S(2)}, u32[]{:S(2)}) collective-permute-start(s32[2]{0:T(128)S(1)} %copy-done.16), channel_id=1, source_target_pairs={{0,4},{12,8},{1,5},{13,9},{2,6},{14,10},{3,7},{15,11},{16,20},{28,... | collective-permute-start | bytes 32 | tf_op jit(solution)/shard_map/ppermute | solution.py:550
  50.9 8.8 %collective-permute-done.17.prompts_ref = s32[2]{0:T(128)S(1)} collective-permute-done((s32[2]{0:T(128)S(1)}, s32[2]{0:T(128)S(1)}, u32[]{:S(2)}, u32[]{:S(2)}) %collective-permute-start.17) | collective-permute-done | bytes 40 | tf_op jit(solution)/shard_map/ppermute | solution.py:550
  59.7 5.3 %collective-permute-start.18 = (bf16[384,1280]{1,0:T(8,128)(2,1)S(1)}, bf16[384,1280]{1,0:T(8,128)(2,1)}, u32[]{:S(2)}, u32[]{:S(2)}) collective-permute-start(bf16[384,1280]{1,0:T(8,128)(2,1)S(1)} %constant_dynamic-slice_fusion), channel_id=1, source_target_pairs={{0,4},{12,8},{1,5},{13,9},{2,6},{14,10},{3,7},{15,11},{16,20},{28,... | collective-permute-start | bytes 2949128 | tf_op jit(solution)/shard_map/ppermute | solution.py:550
  65.0 1.3 stacked.1.rest_2_
  66.3 1.0 copy-done.1
  67.3 1.6 collective-permute-start.15
  69.0 0.5 collective-permute-start.1
  69.5 15.4 %collective-permute-done.18.refs_4_.refs_3_ = bf16[384,1280]{1,0:T(8,128)(2,1)} collective-permute-done((bf16[384,1280]{1,0:T(8,128)(2,1)S(1)}, bf16[384,1280]{1,0:T(8,128)(2,1)}, u32[]{:S(2)}, u32[]{:S(2)}) %collective-permute-start.18) | collective-permute-done | bytes 983072 | tf_op jit(solution)/shard_map/ppermute | solution.py:550
  84.9 0.5 collective-permute-start.20
  85.4 1.0 pad_maximum_fusion
  86.4 5.4 %collective-permute-start.19 = (bf16[4,64,1792]{2,1,0:T(8,128)(2,1)}, bf16[4,64,1792]{2,1,0:T(8,128)(2,1)}, u32[]{:S(2)}, u32[]{:S(2)}) collective-permute-start(bf16[4,64,1792]{2,1,0:T(8,128)(2,1)} %pad_maximum_fusion), channel_id=1, source_target_pairs={{0,4},{12,8},{1,5},{13,9},{2,6},{14,10},{3,7},{15,11},{16,20},{28,... | collective-permute-start | bytes 2752520 | tf_op jit(solution)/shard_map/ppermute | solution.py:550
  91.9 0.8 copy-done.2
  92.7 7.5 %attend.2.refs_0_ = bf16[4,64,1280]{2,1,0:T(8,128)(2,1)} custom-call(s32[3]{0:T(128)} %pad_add_fusion.here_ref.refs_0_, s32[2]{0:T(128)} %prompts_ref.1, s32[4]{0:T(128)} %owners_ref.3, s32[4]{0:T(128)} %lengths_ref.3, bf16[4,64,1280]{2,1,0:T(8,128)(2,1)} %query_hbm, bf16[4,64,512]{2,1,0:T(8,128)(2,1)} %new_hbm.1, bf16[448,512]{1,0:T(8,128)(2,1)} %added.6.rest_0_, ...), custom_call_target="tpu_custom_call" | custom-call | flops 64 | bytes 64 | tf_op jit(solution)/shard_map/attend/pallas_call | solution.py:323
  100.3 1.6 collective-permute-start.16
  101.9 7.7 %collective-permute-done.19.query_hbm.new_hbm = bf16[4,64,1792]{2,1,0:T(8,128)(2,1)} collective-permute-done((bf16[4,64,1792]{2,1,0:T(8,128)(2,1)}, bf16[4,64,1792]{2,1,0:T(8,128)(2,1)}, u32[]{:S(2)}, u32[]{:S(2)}) %collective-permute-start.19) | collective-permute-done | bytes 917536 | tf_op jit(solution)/shard_map/ppermute | solution.py:550
  109.5 6.4 %attend.3.refs_1_ = bf16[4,64,1280]{2,1,0:T(8,128)(2,1)} custom-call(s32[3]{0:T(128)} %pad_add_fusion.here_ref.refs_0_, s32[2]{0:T(128)} %copy-done.13, s32[4]{0:T(128)} %owners_ref.3, s32[4]{0:T(128)} %lengths_ref.3, bf16[4,64,1792]{2,1,0:T(8,128)(2,1)} %collective-permute-done.19.query_hbm.new_hbm, ...), custom_call_target="tpu_custom_call" | custom-call | flops 64 | bytes 64 | tf_op jit(solution)/shard_map/attend/pallas_call | solution.py:323
  115.9 1.0 collective-permute-start.22
  116.9 1.1 copy-done.3
  118.0 1.1 copy-done.6
  119.1 5.9 %spread.3 = (bf16[4,128,1280]{2,1,0:T(8,128)(2,1)S(1)}, bf16[4,64,1280]{2,1,0:T(8,128)(2,1)S(1)}, bf16[4,64,1280]{2,1,0:T(8,128)(2,1)S(1)}) custom-call(s32[3]{0:T(128)S(1)} %copy-done.8, bf16[4,64,1280]{2,1,0:T(8,128)(2,1)} %collective-permute-done.16.refs_0_, bf16[4,64,1280]{2,1,0:T(8,128)(2,1)S(1)} %copy-done.6, bf16[1280,1280]{1,0:T(8,128)(2,1)S(1)} %copy-done, ...), custom_call_target="tpu_custom_call" | custom-call | flops 64 | bytes 64 | tf_op jit(solution)/shard_map/spread/pallas_call | solution.py:383
  125.7 2.4 %collective-permute-done.23 = s32[3]{0:T(128)S(1)} collective-permute-done((s32[3]{0:T(128)S(1)}, s32[3]{0:T(128)S(1)}, u32[]{:S(2)}, u32[]{:S(2)}) %collective-permute-start.23) | collective-permute-done | bytes 44 | tf_op jit(solution)/shard_map/ppermute | solution.py:553
  128.3 1.0 collective-permute-done.24.refs_0_
  129.3 0.7 added_half.3
  130.0 1.6 collective-permute-start.28
  131.6 4.7 %spread.4 = (bf16[4,64,1280]{2,1,0:T(8,128)(2,1)}, bf16[4,64,1280]{2,1,0:T(8,128)(2,1)S(1)}) custom-call(s32[3]{0:T(128)S(1)} %copy-done.8, bf16[4,64,1280]{2,1,0:T(8,128)(2,1)S(1)} %copy-done.5, bf16[1280,1280]{1,0:T(8,128)(2,1)S(1)} %copy-done, bf16[256,1280]{1,0:T(8,128)(2,1)} %collective-permute-done.refs_3_.refs_2_, ...), custom_call_target="tpu_custom_call" | custom-call | flops 64 | bytes 64 | tf_op jit(solution)/shard_map/spread/pallas_call | solution.py:383
  136.3 3.8 %spread.5 = (bf16[4,64,1280]{2,1,0:T(8,128)(2,1)S(1)}, bf16[4,64,1280]{2,1,0:T(8,128)(2,1)S(1)}) custom-call(s32[3]{0:T(128)S(1)} %copy-done.8, bf16[4,64,1280]{2,1,0:T(8,128)(2,1)S(1)} %collective-permute-done.22.refs_0_, bf16[1280,1280]{1,0:T(8,128)(2,1)S(1)} %copy-done, bf16[256,1280]{1,0:T(8,128)(2,1)} %collective-permute-done.refs_3_.refs_2_, ...), custom_call_target="tpu_custom_call" | custom-call | flops 64 | bytes 64 | tf_op jit(solution)/shard_map/spread/pallas_call | solution.py:383
  140.7 6.2 %collective-permute-done.28.refs_4_ = bf16[2,128,1280]{2,1,0:T(8,128)(2,1)S(1)} collective-permute-done((bf16[2,128,1280]{2,1,0:T(8,128)(2,1)S(1)}, bf16[2,128,1280]{2,1,0:T(8,128)(2,1)S(1)}, u32[]{:S(2)}, u32[]{:S(2)}) %collective-permute-start.28) | collective-permute-done | bytes 655392 | tf_op jit(solution)/shard_map/ppermute | solution.py:553
  146.9 0.6 added_half.4
  147.6 1.6 collective-permute-start.31
  149.1 1.2 added_pieces.1
  150.4 0.7 collective-permute-start.30
  151.1 1.0 added_halves.1
  152.1 0.7 collective-permute-start.34
  152.8 0.7 collective-permute-start.35
  153.5 4.3 %collective-permute-done.31.refs_3_ = bf16[2,64,1280]{2,1,0:T(8,128)(2,1)S(1)} collective-permute-done((bf16[2,64,1280]{2,1,0:T(8,128)(2,1)S(1)}, bf16[2,64,1280]{2,1,0:T(8,128)(2,1)S(1)}, u32[]{:S(2)}, u32[]{:S(2)}) %collective-permute-start.31) | collective-permute-done | bytes 327712 | tf_op jit(solution)/shard_map/ppermute | solution.py:553
  157.8 0.7 added_half.5
  158.4 1.3 collective-permute-start.37
  159.7 1.3 collective-permute-start.36
  161.2 0.7 collective-permute-start.32
  161.9 22.4 %collective-permute-done.37 = bf16[2,64,1280]{2,1,0:T(8,128)(2,1)} collective-permute-done((bf16[2,64,1280]{2,1,0:T(8,128)(2,1)S(1)}, bf16[2,64,1280]{2,1,0:T(8,128)(2,1)}, u32[]{:S(2)}, u32[]{:S(2)}) %collective-permute-start.37) | collective-permute-done | bytes 327712 | tf_op jit(solution)/shard_map/ppermute | solution.py:523
  184.3 1.2 select_select_fusion.1
  185.5 0.7 joined.1
  186.2 1.0 fusion
  (70 shorter events, 2.7 us)
Async XLA Ops:
  0.6 7.3 %copy-start = (bf16[1280,1280]{1,0:T(8,128)(2,1)S(1)}, bf16[1280,1280]{1,0:T(8,128)(2,1)}, u32[]{:S(2)}) copy-start(bf16[1280,1280]{1,0:T(8,128)(2,1)} %refs_1_.3) | copy-start | bytes 9830404
  7.3 8.4 %collective-permute-start.5 = (bf16[576,512]{1,0:T(8,128)(2,1)}, bf16[576,512]{1,0:T(8,128)(2,1)}, u32[]{:S(2)}, u32[]{:S(2)}) collective-permute-start(bf16[576,512]{1,0:T(8,128)(2,1)} %get-tuple-element.54), channel_id=1, source_target_pairs={{0,1},{1,0},{2,3},{3,2},{4,5},{5,4},{6,7},{7,6},{8,9},{9,8},{10,11... | collective-permute-start | bytes 1769480 | tf_op jit(solution)/shard_map/ppermute | solution.py:553
  7.4 5.7 %collective-permute-start.2 = (bf16[448,512]{1,0:T(8,128)(2,1)}, bf16[448,512]{1,0:T(8,128)(2,1)}, u32[]{:S(2)}, u32[]{:S(2)}) collective-permute-start(bf16[448,512]{1,0:T(8,128)(2,1)} %get-tuple-element.48), channel_id=1, source_target_pairs={{0,1},{1,0},{2,3},{3,2},{4,5},{5,4},{6,7},{7,6},{8,9},{9,8},{10,11... | collective-permute-start | bytes 1376264 | tf_op jit(solution)/shard_map/ppermute | solution.py:553
  8.8 22.7 %collective-permute-start = (bf16[256,1280]{1,0:T(8,128)(2,1)}, bf16[256,1280]{1,0:T(8,128)(2,1)}, u32[]{:S(2)}, u32[]{:S(2)}) collective-permute-start(bf16[256,1280]{1,0:T(8,128)(2,1)} %constant_dynamic-slice_fusion.1), channel_id=1, source_target_pairs={{0,4},{12,8},{1,5},{13,9},{2,6},{14,10},{3,7},{15,11},{16,20},{28,... | collective-permute-start | bytes 1966088 | tf_op jit(solution)/shard_map/ppermute | solution.py:550
  15.2 12.4 %collective-permute-start.3 = (bf16[448,512]{1,0:T(8,128)(2,1)}, bf16[448,512]{1,0:T(8,128)(2,1)S(1)}, u32[]{:S(2)}, u32[]{:S(2)}) collective-permute-start(bf16[448,512]{1,0:T(8,128)(2,1)} %added.4), channel_id=1, source_target_pairs={{0,2},{2,0},{1,3},{3,1},{4,6},{6,4},{5,7},{7,5},{8,10},{10,8},{9,1... | collective-permute-start | bytes 1376264 | tf_op jit(solution)/shard_map/ppermute | solution.py:553
  17.9 9.7 %copy-start.7 = (s32[3]{0:T(128)S(1)}, s32[3]{0:T(128)}, u32[]{:S(2)}) copy-start(s32[3]{0:T(128)} %pad_add_fusion.here_ref.refs_0_) | copy-start | bytes 40
  24.4 4.3 %collective-permute-start.6 = (bf16[448,512]{1,0:T(8,128)(2,1)}, bf16[448,512]{1,0:T(8,128)(2,1)}, u32[]{:S(2)}, u32[]{:S(2)}) collective-permute-start(bf16[448,512]{1,0:T(8,128)(2,1)} %get-tuple-element.58), channel_id=1, source_target_pairs={{0,1},{1,0},{2,3},{3,2},{4,5},{5,4},{6,7},{7,6},{8,9},{9,8},{10,11... | collective-permute-start | bytes 1376264 | tf_op jit(solution)/shard_map/ppermute | solution.py:553
  24.5 16.1 %collective-permute-start.7 = (bf16[576,512]{1,0:T(8,128)(2,1)}, bf16[576,512]{1,0:T(8,128)(2,1)}, u32[]{:S(2)}, u32[]{:S(2)}) collective-permute-start(bf16[576,512]{1,0:T(8,128)(2,1)} %added.5), channel_id=1, source_target_pairs={{0,2},{2,0},{1,3},{3,1},{4,6},{6,4},{5,7},{7,5},{8,10},{10,8},{9,1... | collective-permute-start | bytes 1769480 | tf_op jit(solution)/shard_map/ppermute | solution.py:553
  26.0 14.5 %collective-permute-start.9 = (bf16[576,512]{1,0:T(8,128)(2,1)}, bf16[576,512]{1,0:T(8,128)(2,1)}, u32[]{:S(2)}, u32[]{:S(2)}) collective-permute-start(bf16[576,512]{1,0:T(8,128)(2,1)} %get-tuple-element.61), channel_id=1, source_target_pairs={{0,1},{1,0},{2,3},{3,2},{4,5},{5,4},{6,7},{7,6},{8,9},{9,8},{10,11... | collective-permute-start | bytes 1769480 | tf_op jit(solution)/shard_map/ppermute | solution.py:553
  27.6 1.1 copy-start.12
  27.6 1.1 collective-permute-start.4
  28.7 0.5 copy-start.15
  31.5 16.7 %copy-start.16 = (s32[2]{0:T(128)S(1)}, s32[2]{0:T(128)}, u32[]{:S(2)}) copy-start(s32[2]{0:T(128)} %prompts_ref.1) | copy-start | bytes 28
  31.5 16.3 %collective-permute-start.10 = (bf16[448,512]{1,0:T(8,128)(2,1)}, bf16[448,512]{1,0:T(8,128)(2,1)}, u32[]{:S(2)}, u32[]{:S(2)}) collective-permute-start(bf16[448,512]{1,0:T(8,128)(2,1)} %added.6.rest_0_), channel_id=1, source_target_pairs={{0,4},{12,8},{1,5},{13,9},{2,6},{14,10},{3,7},{15,11},{16,20},{28,... | collective-permute-start | bytes 1376264 | tf_op jit(solution)/shard_map/ppermute | solution.py:550
  33.7 14.1 %collective-permute-start.12 = (bf16[448,512]{1,0:T(8,128)(2,1)}, bf16[448,512]{1,0:T(8,128)(2,1)}, u32[]{:S(2)}, u32[]{:S(2)}) collective-permute-start(bf16[448,512]{1,0:T(8,128)(2,1)} %added.6.rest_0_), channel_id=1, source_target_pairs={{4,8},{8,4},{5,9},{9,5},{6,10},{10,6},{7,11},{11,7},{20,24},{24,20... | collective-permute-start | bytes 1376264 | tf_op jit(solution)/shard_map/ppermute | solution.py:550
  40.5 1.1 collective-permute-start.8
  41.6 0.5 copy-start.14
  44.7 40.7 %copy-start.11 = (bf16[4,64,512]{2,1,0:T(8,128)(2,1)S(1)}, bf16[4,64,512]{2,1,0:T(8,128)(2,1)}, u32[]{:S(2)}) copy-start(bf16[4,64,512]{2,1,0:T(8,128)(2,1)} %new_hbm.1) | copy-start | bytes 786436
  44.7 15.0 %collective-permute-start.11 = (bf16[576,512]{1,0:T(8,128)(2,1)}, bf16[576,512]{1,0:T(8,128)(2,1)}, u32[]{:S(2)}, u32[]{:S(2)}) collective-permute-start(bf16[576,512]{1,0:T(8,128)(2,1)} %added.7.rest_1_), channel_id=1, source_target_pairs={{0,4},{12,8},{1,5},{13,9},{2,6},{14,10},{3,7},{15,11},{16,20},{28,... | collective-permute-start | bytes 1769480 | tf_op jit(solution)/shard_map/ppermute | solution.py:550
  46.9 38.5 %copy-start.9 = (bf16[4,64,1280]{2,1,0:T(8,128)(2,1)S(1)}, bf16[4,64,1280]{2,1,0:T(8,128)(2,1)}, u32[]{:S(2)}) copy-start(bf16[4,64,1280]{2,1,0:T(8,128)(2,1)} %query_hbm) | copy-start | bytes 1966084
  46.9 19.4 %collective-permute-start.14 = (bf16[576,512]{1,0:T(8,128)(2,1)}, bf16[576,512]{1,0:T(8,128)(2,1)S(1)}, u32[]{:S(2)}, u32[]{:S(2)}) collective-permute-start(bf16[576,512]{1,0:T(8,128)(2,1)} %added.7.rest_1_), channel_id=1, source_target_pairs={{4,8},{8,4},{5,9},{9,5},{6,10},{10,6},{7,11},{11,7},{20,24},{24,20... | collective-permute-start | bytes 1769480 | tf_op jit(solution)/shard_map/ppermute | solution.py:550
  47.8 17.2 %collective-permute-start.13 = (bf16[448,512]{1,0:T(8,128)(2,1)}, bf16[448,512]{1,0:T(8,128)(2,1)S(1)}, u32[]{:S(2)}, u32[]{:S(2)}) collective-permute-start(bf16[448,512]{1,0:T(8,128)(2,1)} %added.4), channel_id=1, source_target_pairs={{0,1},{1,0},{2,3},{3,2},{4,5},{5,4},{6,7},{7,6},{8,9},{9,8},{10,11... | collective-permute-start | bytes 1376264 | tf_op jit(solution)/shard_map/ppermute | solution.py:553
  48.1 11.5 %collective-permute-start.17 = (s32[2]{0:T(128)S(1)}, s32[2]{0:T(128)S(1)}, u32[]{:S(2)}, u32[]{:S(2)}) collective-permute-start(s32[2]{0:T(128)S(1)} %copy-done.16), channel_id=1, source_target_pairs={{0,4},{12,8},{1,5},{13,9},{2,6},{14,10},{3,7},{15,11},{16,20},{28,... | collective-permute-start | bytes 32 | tf_op jit(solution)/shard_map/ppermute | solution.py:550
  59.7 40.6 %copy-start.13 = (s32[2]{0:T(128)}, s32[2]{0:T(128)S(1)}, u32[]{:S(2)}) copy-start(s32[2]{0:T(128)S(1)} %collective-permute-done.17.prompts_ref) | copy-start | bytes 28
  59.7 25.2 %collective-permute-start.18 = (bf16[384,1280]{1,0:T(8,128)(2,1)S(1)}, bf16[384,1280]{1,0:T(8,128)(2,1)}, u32[]{:S(2)}, u32[]{:S(2)}) collective-permute-start(bf16[384,1280]{1,0:T(8,128)(2,1)S(1)} %constant_dynamic-slice_fusion), channel_id=1, source_target_pairs={{0,4},{12,8},{1,5},{13,9},{2,6},{14,10},{3,7},{15,11},{16,20},{28,... | collective-permute-start | bytes 2949128 | tf_op jit(solution)/shard_map/ppermute | solution.py:550
  66.3 1.0 copy-start.1
  67.3 24.5 %copy-start.10 = (bf16[576,512]{1,0:T(8,128)(2,1)}, bf16[576,512]{1,0:T(8,128)(2,1)S(1)}, u32[]{:S(2)}) copy-start(bf16[576,512]{1,0:T(8,128)(2,1)S(1)} %collective-permute-done.14.rest_4_) | copy-start | bytes 1769476
  67.3 25.4 %collective-permute-start.15 = (bf16[1024,512]{1,0:T(8,128)(2,1)S(1)}, bf16[1024,512]{1,0:T(8,128)(2,1)}, u32[]{:S(2)}, u32[]{:S(2)}) collective-permute-start(bf16[1024,512]{1,0:T(8,128)(2,1)S(1)} %stacked.1.rest_2_), channel_id=1, source_target_pairs={{4,8},{8,4},{5,9},{9,5},{6,10},{10,6},{7,11},{11,7},{20,24},{24,20... | collective-permute-start | bytes 3145736 | tf_op jit(solution)/shard_map/ppermute | solution.py:550
  69.0 22.9 %collective-permute-start.1 = (bf16[256,1280]{1,0:T(8,128)(2,1)}, bf16[256,1280]{1,0:T(8,128)(2,1)S(1)}, u32[]{:S(2)}, u32[]{:S(2)}) collective-permute-start(bf16[256,1280]{1,0:T(8,128)(2,1)} %collective-permute-done.refs_3_.refs_2_), channel_id=1, source_target_pairs={{0,16},{16,0},{1,17},{17,1},{2,18},{18,2},{3,19},{19,3},{4,20},{20... | collective-permute-start | bytes 1966088 | tf_op jit(solution)/shard_map/ppermute | solution.py:577
  84.9 32.0 %collective-permute-start.20 = (bf16[384,1280]{1,0:T(8,128)(2,1)}, bf16[384,1280]{1,0:T(8,128)(2,1)}, u32[]{:S(2)}, u32[]{:S(2)}) collective-permute-start(bf16[384,1280]{1,0:T(8,128)(2,1)} %collective-permute-done.18.refs_4_.refs_3_), channel_id=1, source_target_pairs={{0,16},{16,0},{1,17},{17,1},{2,18},{18,2},{3,19},{19,3},{4,20},{20... | collective-permute-start | bytes 2949128 | tf_op jit(solution)/shard_map/ppermute | solution.py:577
  86.4 23.1 %collective-permute-start.19 = (bf16[4,64,1792]{2,1,0:T(8,128)(2,1)}, bf16[4,64,1792]{2,1,0:T(8,128)(2,1)}, u32[]{:S(2)}, u32[]{:S(2)}) collective-permute-start(bf16[4,64,1792]{2,1,0:T(8,128)(2,1)} %pad_maximum_fusion), channel_id=1, source_target_pairs={{0,4},{12,8},{1,5},{13,9},{2,6},{14,10},{3,7},{15,11},{16,20},{28,... | collective-permute-start | bytes 2752520 | tf_op jit(solution)/shard_map/ppermute | solution.py:550
  91.9 0.8 copy-start.2
  100.3 16.7 %copy-start.8 = (s32[3]{0:T(128)S(1)}, s32[3]{0:T(128)}, u32[]{:S(2)}) copy-start(s32[3]{0:T(128)} %pad_add_fusion.here_ref.refs_0_) | copy-start | bytes 40
  100.3 16.6 %collective-permute-start.16 = (bf16[4,64,1280]{2,1,0:T(8,128)(2,1)}, bf16[4,64,1280]{2,1,0:T(8,128)(2,1)}, u32[]{:S(2)}, u32[]{:S(2)}) collective-permute-start(bf16[4,64,1280]{2,1,0:T(8,128)(2,1)} %attend.2.refs_0_), channel_id=1, source_target_pairs={{4,8},{8,4},{5,9},{9,5},{6,10},{10,6},{7,11},{11,7},{20,24},{24,20... | collective-permute-start | bytes 1966088 | tf_op jit(solution)/shard_map/ppermute | solution.py:550
  115.9 9.7 %collective-permute-start.22 = (bf16[4,64,1280]{2,1,0:T(8,128)(2,1)}, bf16[4,64,1280]{2,1,0:T(8,128)(2,1)S(1)}, u32[]{:S(2)}, u32[]{:S(2)}) collective-permute-start(bf16[4,64,1280]{2,1,0:T(8,128)(2,1)} %attend.3.refs_1_), channel_id=1, source_target_pairs={{4,8},{8,4},{5,9},{9,5},{6,10},{10,6},{7,11},{11,7},{20,24},{24,20... | collective-permute-start | bytes 1966088 | tf_op jit(solution)/shard_map/ppermute | solution.py:550
  116.9 1.1 copy-start.3
  118.0 1.1 copy-start.6
  125.0 6.5 %copy-start.4 = (bf16[256,1280]{1,0:T(8,128)(2,1)S(1)}, bf16[256,1280]{1,0:T(8,128)(2,1)}, u32[]{:S(2)}) copy-start(bf16[256,1280]{1,0:T(8,128)(2,1)} %copy-done.2) | copy-start | bytes 1966084
  125.1 6.5 %copy-start.5 = (bf16[4,64,1280]{2,1,0:T(8,128)(2,1)S(1)}, bf16[4,64,1280]{2,1,0:T(8,128)(2,1)}, u32[]{:S(2)}) copy-start(bf16[4,64,1280]{2,1,0:T(8,128)(2,1)} %attend.2.refs_0_) | copy-start | bytes 1966084
  125.1 4.2 %collective-permute-start.25 = (bf16[4,64,1280]{2,1,0:T(8,128)(2,1)S(1)}, bf16[4,64,1280]{2,1,0:T(8,128)(2,1)S(1)}, u32[]{:S(2)}, u32[]{:S(2)}) collective-permute-start(bf16[4,64,1280]{2,1,0:T(8,128)(2,1)S(1)} %get-tuple-element.77), channel_id=1, source_target_pairs={{0,1},{1,0},{2,3},{3,2},{4,5},{5,4},{6,7},{7,6},{8,9},{9,8},{10,11... | collective-permute-start | bytes 1966088 | tf_op jit(solution)/shard_map/ppermute | solution.py:553
  125.1 4.2 %collective-permute-start.26 = (bf16[4,64,1280]{2,1,0:T(8,128)(2,1)S(1)}, bf16[4,64,1280]{2,1,0:T(8,128)(2,1)S(1)}, u32[]{:S(2)}, u32[]{:S(2)}) collective-permute-start(bf16[4,64,1280]{2,1,0:T(8,128)(2,1)S(1)} %get-tuple-element.78), channel_id=1, source_target_pairs={{0,1},{1,0},{2,3},{3,2},{4,5},{5,4},{6,7},{7,6},{8,9},{9,8},{10,11... | collective-permute-start | bytes 1966088 | tf_op jit(solution)/shard_map/ppermute | solution.py:553
  125.6 2.5 %collective-permute-start.23 = (s32[3]{0:T(128)S(1)}, s32[3]{0:T(128)S(1)}, u32[]{:S(2)}, u32[]{:S(2)}) collective-permute-start(s32[3]{0:T(128)S(1)} %copy-done.8), channel_id=1, source_target_pairs={{0,1},{1,0},{2,3},{3,2},{4,5},{5,4},{6,7},{7,6},{8,9},{9,8},{10,11... | collective-permute-start | bytes 44 | tf_op jit(solution)/shard_map/ppermute | solution.py:553
  128.2 1.1 collective-permute-start.24
  130.0 16.9 %collective-permute-start.28 = (bf16[2,128,1280]{2,1,0:T(8,128)(2,1)S(1)}, bf16[2,128,1280]{2,1,0:T(8,128)(2,1)S(1)}, u32[]{:S(2)}, u32[]{:S(2)}) collective-permute-start(bf16[2,128,1280]{2,1,0:T(8,128)(2,1)S(1)} %added_half.3), channel_id=1, source_target_pairs={{0,2},{2,0},{1,3},{3,1},{4,6},{6,4},{5,7},{7,5},{8,10},{10,8},{9,1... | collective-permute-start | bytes 1966088 | tf_op jit(solution)/shard_map/ppermute | solution.py:553
  140.1 6.8 %collective-permute-start.27 = (bf16[4,64,1280]{2,1,0:T(8,128)(2,1)S(1)}, bf16[4,64,1280]{2,1,0:T(8,128)(2,1)S(1)}, u32[]{:S(2)}, u32[]{:S(2)}) collective-permute-start(bf16[4,64,1280]{2,1,0:T(8,128)(2,1)S(1)} %get-tuple-element.81), channel_id=1, source_target_pairs={{0,1},{1,0},{2,3},{3,2},{4,5},{5,4},{6,7},{7,6},{8,9},{9,8},{10,11... | collective-permute-start | bytes 1966088 | tf_op jit(solution)/shard_map/ppermute | solution.py:553
  140.2 8.9 %collective-permute-start.21 = (bf16[4,64,1280]{2,1,0:T(8,128)(2,1)S(1)}, bf16[4,64,1280]{2,1,0:T(8,128)(2,1)S(1)}, u32[]{:S(2)}, u32[]{:S(2)}) collective-permute-start(bf16[4,64,1280]{2,1,0:T(8,128)(2,1)S(1)} %get-tuple-element.74), channel_id=1, source_target_pairs={{0,1},{1,0},{2,3},{3,2},{4,5},{5,4},{6,7},{7,6},{8,9},{9,8},{10,11... | collective-permute-start | bytes 1966088 | tf_op jit(solution)/shard_map/ppermute | solution.py:553
  146.9 2.2 %collective-permute-start.29 = (bf16[4,64,1280]{2,1,0:T(8,128)(2,1)S(1)}, bf16[4,64,1280]{2,1,0:T(8,128)(2,1)S(1)}, u32[]{:S(2)}, u32[]{:S(2)}) collective-permute-start(bf16[4,64,1280]{2,1,0:T(8,128)(2,1)S(1)} %copy-done.5), channel_id=1, source_target_pairs={{0,1},{1,0},{2,3},{3,2},{4,5},{5,4},{6,7},{7,6},{8,9},{9,8},{10,11... | collective-permute-start | bytes 1966088 | tf_op jit(solution)/shard_map/ppermute | solution.py:553
  147.6 10.2 %collective-permute-start.31 = (bf16[2,64,1280]{2,1,0:T(8,128)(2,1)S(1)}, bf16[2,64,1280]{2,1,0:T(8,128)(2,1)S(1)}, u32[]{:S(2)}, u32[]{:S(2)}) collective-permute-start(bf16[2,64,1280]{2,1,0:T(8,128)(2,1)S(1)} %added_half.4), channel_id=1, source_target_pairs={{0,2},{2,0},{1,3},{3,1},{4,6},{6,4},{5,7},{7,5},{8,10},{10,8},{9,1... | collective-permute-start | bytes 983048 | tf_op jit(solution)/shard_map/ppermute | solution.py:553
  150.4 10.6 %collective-permute-start.30 = (bf16[4,32,1280]{2,1,0:T(8,128)(2,1)S(1)}, bf16[4,32,1280]{2,1,0:T(8,128)(2,1)S(1)}, u32[]{:S(2)}, u32[]{:S(2)}) collective-permute-start(bf16[4,32,1280]{2,1,0:T(8,128)(2,1)S(1)} %get-tuple-element.86.refs_1_), channel_id=1, source_target_pairs={{6,4},{7,5},{8,10},{9,11},{22,20},{23,21},{24,26},{25,27}} | collective-permute-start | bytes 983048 | tf_op jit(solution)/shard_map/ppermute | solution.py:532
  152.1 9.1 %collective-permute-start.34 = (bf16[2,64,1280]{2,1,0:T(8,128)(2,1)S(1)}, bf16[2,64,1280]{2,1,0:T(8,128)(2,1)S(1)}, u32[]{:S(2)}, u32[]{:S(2)}) collective-permute-start(bf16[2,64,1280]{2,1,0:T(8,128)(2,1)S(1)} %get-tuple-element.89), channel_id=1, source_target_pairs={{4,8},{5,9},{10,6},{11,7},{6,0},{7,1},{8,14},{9,15},{20,24},{21,25... | collective-permute-start | bytes 983048 | tf_op jit(solution)/shard_map/ppermute | solution.py:523
  152.8 9.1 %collective-permute-start.35 = (bf16[2,64,1280]{2,1,0:T(8,128)(2,1)S(1)}, bf16[2,64,1280]{2,1,0:T(8,128)(2,1)S(1)}, u32[]{:S(2)}, u32[]{:S(2)}) collective-permute-start(bf16[2,64,1280]{2,1,0:T(8,128)(2,1)S(1)} %get-tuple-element.90), channel_id=1, source_target_pairs={{6,8},{7,9},{8,6},{9,7},{4,0},{5,1},{10,14},{11,15},{22,24},{23,25... | collective-permute-start | bytes 983048 | tf_op jit(solution)/shard_map/ppermute | solution.py:523
  158.4 25.8 %collective-permute-start.37 = (bf16[2,64,1280]{2,1,0:T(8,128)(2,1)S(1)}, bf16[2,64,1280]{2,1,0:T(8,128)(2,1)}, u32[]{:S(2)}, u32[]{:S(2)}) collective-permute-start(bf16[2,64,1280]{2,1,0:T(8,128)(2,1)S(1)} %added_half.5), channel_id=1, source_target_pairs={{6,12},{7,13},{8,2},{9,3},{22,28},{23,29},{24,18},{25,19}} | collective-permute-start | bytes 983048 | tf_op jit(solution)/shard_map/ppermute | solution.py:523
  159.7 24.5 %collective-permute-start.36 = (bf16[2,64,1280]{2,1,0:T(8,128)(2,1)S(1)}, bf16[2,64,1280]{2,1,0:T(8,128)(2,1)}, u32[]{:S(2)}, u32[]{:S(2)}) collective-permute-start(bf16[2,64,1280]{2,1,0:T(8,128)(2,1)S(1)} %added_half.5), channel_id=1, source_target_pairs={{4,12},{5,13},{10,2},{11,3},{20,28},{21,29},{26,18},{27,19}} | collective-permute-start | bytes 983048 | tf_op jit(solution)/shard_map/ppermute | solution.py:523
  161.0 24.4 %collective-permute-start.33 = (bf16[4,64,1280]{2,1,0:T(8,128)(2,1)}, bf16[4,64,1280]{2,1,0:T(8,128)(2,1)S(1)}, u32[]{:S(2)}, u32[]{:S(2)}) collective-permute-start(bf16[4,64,1280]{2,1,0:T(8,128)(2,1)} %get-tuple-element.88.refs_1_), channel_id=1, source_target_pairs={{0,1},{1,0},{2,3},{3,2},{4,5},{5,4},{6,7},{7,6},{8,9},{9,8},{10,11... | collective-permute-start | bytes 1966088 | tf_op jit(solution)/shard_map/ppermute | solution.py:553
  161.2 24.3 %collective-permute-start.32 = (bf16[4,32,1280]{2,1,0:T(8,128)(2,1)S(1)}, bf16[4,32,1280]{2,1,0:T(8,128)(2,1)S(1)}, u32[]{:S(2)}, u32[]{:S(2)}) collective-permute-start(bf16[4,32,1280]{2,1,0:T(8,128)(2,1)S(1)} %get-tuple-element.87.refs_2_), channel_id=1, source_target_pairs={{6,4},{7,5},{8,10},{9,11},{22,20},{23,21},{24,26},{25,27}} | collective-permute-start | bytes 983048 | tf_op jit(solution)/shard_map/ppermute | solution.py:532

commit v5 on v4

--- a/solution.py
+++ b/solution.py
@@ -333,13 +333,13 @@
             pltpu.VMEM((count, steps, block_rows, new_width), jnp.bfloat16),
             pltpu.SemaphoreType.DMA((3, count)),
         ],
-        compiler_params=compiler_params(LARGE_VMEM),
+        compiler_params=compiler_params(40 * 1024 * 1024),
         cost_estimate=small_cost(),
         name="attend",
     )(here, prompts, owners, lengths, queries, news, *page_parts)
 
 
-def spread(here, blocks, own_weight, moved_weights):
+def spread(here, blocks, own_weight, moved_weights, waits_for):
     count, moved_count = len(blocks), len(moved_weights)
     steps, _, features = blocks[0].shape
     columns = own_weight.shape[1]
@@ -351,7 +351,7 @@
 
     def body(here_ref, *refs):
         row_refs, own_ref, refs = refs[:count], refs[count], refs[count + 1 :]
-        moved_refs, refs = refs[:moved_count], refs[moved_count:]
+        moved_refs, refs = refs[:moved_count], refs[moved_count + len(waits_for) :]
         keep_ref, send_refs, taken_ref = refs[0], refs[1:-1], refs[-1]
         for ref, place in zip(row_refs, places):
             flat = slice(steps * place.start, steps * place.stop)
@@ -382,14 +382,15 @@
     out_rows = [ends[-1], *[block.shape[1] for block in blocks]]
     keep, *sends = pl.pallas_call(
         body,
-        in_specs=[pl.BlockSpec(memory_space=pltpu.SMEM)] + [in_vmem] * (count + 1 + moved_count),
+        in_specs=[pl.BlockSpec(memory_space=pltpu.SMEM)] + [in_vmem] * (count + 1 + moved_count)
+        + [pl.BlockSpec(memory_space=pltpu.HBM)] * len(waits_for),
         out_specs=[in_vmem] * (1 + count),
         out_shape=[jax.ShapeDtypeStruct((steps, rows, columns), jnp.bfloat16) for rows in out_rows],
         scratch_shapes=[pltpu.VMEM((steps * ends[-1], features), jnp.bfloat16)],
         compiler_params=compiler_params(),
         cost_estimate=small_cost(),
         name="spread",
-    )(here, *blocks, own_weight, *[part for _, _, part in moved_weights])
+    )(here, *blocks, own_weight, *[part for _, _, part in moved_weights], *waits_for)
     return keep, sends
 
 
@@ -612,8 +613,8 @@
         )
         return rows, on_samp(rows, MIDDLE)
 
-    def spread_out(*blocks, place=here):
-        keep, sends = spread(place, blocks, out_weight, moved_weights)
+    def spread_out(*blocks, waits_for=()):
+        keep, sends = spread(here, blocks, out_weight, moved_weights, waits_for)
         return keep, [on_head(send, CORE) for send in sends]
 
     blocks = sampler_prompts.shape[0]
@@ -629,10 +630,12 @@
     )
     both_keep, both_arrived = spread_out(far_own_rows, end_rows)
     own_keep, own_arrived = spread_out(after(own_rows, both_keep))
-    place = hopped((far_end_rows,), (far_end_rows,))
-    both_leaving = added_half(place, False, both_keep, both_arrived)
+    both_leaving = added_half(here, False, both_keep, both_arrived)
     both_crossed = on_head(both_leaving, ACROSS_X)
-    beyond_keep, beyond_arrived = spread_out(after(far_end_rows, own_keep, both_leaving))
+    beyond_keep, beyond_arrived = spread_out(
+        after(far_end_rows, own_keep, both_leaving),
+        waits_for=(beside(own_keep, far_end_rows),),
+    )
     beyond_leaving = added_half(here, False, beyond_keep, beyond_arrived)
     beyond_crossed = on_head(beyond_leaving, ACROSS_X)
     own_chip = added_pieces(

time: 189 us -> 184 us (0.974)
  waiting for transfers between devices: 77.3 us -> 88.4 us
  Pallas kernels: 56.8 us -> 49.5 us
  local copies, waits for them, and re-layouts: 6.04 us -> 2.09 us
  starting transfers between devices: 42.8 us -> 39.2 us
    ppermute x11, waiting for transfers between devices: 31.9 us -> 39.3 us  [on_samp(): return lax.ppermute(value, 'samp', pairs)]
    pallas_call x2, Pallas kernels: 13.9 us -> 8.57 us  [attend(): pl.pallas_call(body, in_specs=[in_smem] * 4 + [in_hbm] * (2 + len(page_pa...]
    unnamed x34 -> x24, local copies, waits for them, and re-layouts: 5.1 us -> 1.15 us
    ppermute x11, starting transfers between devices: 28.7 us -> 25.2 us  [on_samp(): return lax.ppermute(value, 'samp', pairs)]
    ppermute x19 -> x18, waiting for transfers between devices: 23 us -> 25.1 us  [on_head(): return lax.ppermute(value, 'head', pairs)]
    pallas_call x3, Pallas kernels: 14.5 us -> 12.5 us  [spread(): pl.pallas_call(body, in_specs=[pl.BlockSpec(memory_space=pltpu.SMEM)] + [...]
    ppermute x19 -> x18, starting transfers between devices: 7.72 us -> 7.58 us  [on_head(): return lax.ppermute(value, 'head', pairs)]
  transfers between devices with their start and end apart: 38 -> 37, of which waited for: 12 -> 10; matrix products, arithmetic and copies ran while one was open for 2% -> 1% of each run, Pallas kernels for 26% -> 23%
where the time goes in v5:
time: 184 us; the launch traced here: 182 us
  waiting for transfers between devices  88.4 us (48%)
  Pallas kernels  49.5 us (27%)
  starting transfers between devices  39.2 us (21%)
  other arithmetic  2.86 us (2%)
  local copies, waits for them, and re-layouts  2.09 us (1%)
    ppermute x11, waiting for transfers between devices, on_samp(): return lax.ppermute(value, 'samp', pairs)  39.3 us
    ppermute x11, starting transfers between devices, on_samp(): return lax.ppermute(value, 'samp', pairs)  25.2 us
    ppermute x18, waiting for transfers between devices, on_head(): return lax.ppermute(value, 'head', pairs)  25.1 us
    ppermute x4, waiting for transfers between devices, sent_home(): lax.ppermute(value, ('samp', 'head'), [pair for part in pairs for pair in...  24 us
    pallas_call x11, Pallas kernels, run_small(): pl.pallas_call(whole, in_specs=[pl.BlockSpec(memory_space=pltpu.SMEM)] +...  15.2 us
    pallas_call x2, Pallas kernels, project(): pl.pallas_call(body, in_specs=[pl.BlockSpec(memory_space=pltpu.SMEM), in_...  13.2 us
    pallas_call x3, Pallas kernels, spread(): pl.pallas_call(body, in_specs=[pl.BlockSpec(memory_space=pltpu.SMEM)] + [...  12.5 us
    pallas_call x2, Pallas kernels, attend(): pl.pallas_call(body, in_specs=[in_smem] * 4 + [in_hbm] * (2 + len(page_pa...  8.57 us
  transfers between devices with their start and end apart: 37, of which 10 were waited for; matrix products, arithmetic and copies ran while one was open for 1% of the time, Pallas kernels for 23%

profile of v5, /device:TPU:6, one launch (start us, length us, event | category | flops | bytes accessed | tf_op | source)
XLA Modules:
  0.0 182.4 jit_solution(15261018867993854281)
XLA Ops:
  0.0 0.7 pad_add_fusion.here_ref.refs_0_
  0.7 6.7 %project.2 = (bf16[448,512]{1,0:T(8,128)(2,1)}, bf16[576,512]{1,0:T(8,128)(2,1)}, bf16[448,512]{1,0:T(8,128)(2,1)}, bf16[576,512]{1,0:T(8,128)(2,1)}) custom-call(s32[3]{0:T(128)} %pad_add_fusion.here_ref.refs_0_, bf16[1024,1280]{1,0:T(8,128)(2,1)} %bitcast.4, bf16[1280,2048]{1,0:T(8,128)(2,1)} %weight_hbm.3), custom_call_target="tpu_custom_call" | custom-call | flops 64 | bytes 64 | tf_op jit(solution)/shard_map/project/pallas_call | solution.py:190
  7.5 0.5 collective-permute-start.2
  8.0 0.9 constant_dynamic-slice_fusion.1
  8.9 4.3 %collective-permute-start = (bf16[256,1280]{1,0:T(8,128)(2,1)}, bf16[256,1280]{1,0:T(8,128)(2,1)}, u32[]{:S(2)}, u32[]{:S(2)}) collective-permute-start(bf16[256,1280]{1,0:T(8,128)(2,1)} %constant_dynamic-slice_fusion.1), channel_id=1, source_target_pairs={{0,4},{12,8},{1,5},{13,9},{2,6},{14,10},{3,7},{15,11},{16,20},{28,... | collective-permute-start | bytes 1966088 | tf_op jit(solution)/shard_map/ppermute | solution.py:551
  13.2 2.1 %added.4 = bf16[448,512]{1,0:T(8,128)(2,1)} custom-call(s32[3]{0:T(128)} %pad_add_fusion.here_ref.refs_0_, bf16[448,512]{1,0:T(8,128)(2,1)} %get-tuple-element.50.refs_1_, bf16[448,512]{1,0:T(8,128)(2,1)} %collective-permute-done.2.refs_2_), custom_call_target="tpu_custom_call" | custom-call | flops 64 | bytes 64 | tf_op jit(solution)/shard_map/added/pallas_call | solution.py:403
  15.3 0.5 collective-permute-start.3
  15.8 2.2 %added.5 = bf16[576,512]{1,0:T(8,128)(2,1)} custom-call(s32[3]{0:T(128)} %pad_add_fusion.here_ref.refs_0_, bf16[576,512]{1,0:T(8,128)(2,1)} %get-tuple-element.52.refs_1_, bf16[576,512]{1,0:T(8,128)(2,1)} %collective-permute-done.5.refs_2_), custom_call_target="tpu_custom_call" | custom-call | flops 64 | bytes 64 | tf_op jit(solution)/shard_map/added/pallas_call | solution.py:403
  18.0 6.5 %project.3 = (bf16[448,512]{1,0:T(8,128)(2,1)}, bf16[576,512]{1,0:T(8,128)(2,1)}, bf16[448,512]{1,0:T(8,128)(2,1)}, bf16[576,512]{1,0:T(8,128)(2,1)}) custom-call(s32[3]{0:T(128)} %pad_add_fusion.here_ref.refs_0_, bf16[1024,1280]{1,0:T(8,128)(2,1)} %bitcast.5, bf16[1280,2048]{1,0:T(8,128)(2,1)} %weight_hbm.3), custom_call_target="tpu_custom_call" | custom-call | flops 64 | bytes 64 | tf_op jit(solution)/shard_map/project/pallas_call | solution.py:190
  24.6 1.6 collective-permute-start.7
  26.1 0.2 collective-permute-start.9
  26.3 1.4 collective-permute-done.3.refs_3_
  27.7 1.1 collective-permute-done.4.refs_0_
  28.8 0.5 copy-done.11
  29.3 2.2 %added.6.rest_0_ = bf16[448,512]{1,0:T(8,128)(2,1)} custom-call(s32[3]{0:T(128)} %copy-done.11, bf16[448,512]{1,0:T(8,128)(2,1)} %get-tuple-element.56.refs_1_, bf16[448,512]{1,0:T(8,128)(2,1)} %collective-permute-done.6.refs_2_, bf16[448,512]{1,0:T(8,128)(2,1)} %copy-done.9), custom_call_target="tpu_custom_call" | custom-call | flops 64 | bytes 64 | tf_op jit(solution)/shard_map/added/pallas_call | solution.py:403
  31.6 2.2 %collective-permute-start.10 = (bf16[448,512]{1,0:T(8,128)(2,1)}, bf16[448,512]{1,0:T(8,128)(2,1)}, u32[]{:S(2)}, u32[]{:S(2)}) collective-permute-start(bf16[448,512]{1,0:T(8,128)(2,1)} %added.6.rest_0_), channel_id=1, source_target_pairs={{0,4},{12,8},{1,5},{13,9},{2,6},{14,10},{3,7},{15,11},{16,20},{28,... | collective-permute-start | bytes 1376264 | tf_op jit(solution)/shard_map/ppermute | solution.py:551
  33.8 1.5 collective-permute-start.12
  35.2 5.4 %collective-permute-done.7.refs_3_ = bf16[576,512]{1,0:T(8,128)(2,1)} collective-permute-done((bf16[576,512]{1,0:T(8,128)(2,1)}, bf16[576,512]{1,0:T(8,128)(2,1)}, u32[]{:S(2)}, u32[]{:S(2)}) %collective-permute-start.7) | collective-permute-done | bytes 589856 | tf_op jit(solution)/shard_map/ppermute | solution.py:554
  40.6 1.1 collective-permute-done.8.refs_0_
  41.7 0.6 copy-done.10
  42.3 2.5 %added.7.rest_1_ = bf16[576,512]{1,0:T(8,128)(2,1)} custom-call(s32[3]{0:T(128)} %copy-done.10, bf16[576,512]{1,0:T(8,128)(2,1)} %get-tuple-element.59.refs_1_, bf16[576,512]{1,0:T(8,128)(2,1)} %collective-permute-done.9.refs_2_, bf16[576,512]{1,0:T(8,128)(2,1)} %collective-permute-done.7.refs_3_), custom_call_target="tpu_custom_call" | custom-call | flops 64 | bytes 64 | tf_op jit(solution)/shard_map/added/pallas_call | solution.py:403
  44.8 2.2 %collective-permute-start.11 = (bf16[576,512]{1,0:T(8,128)(2,1)}, bf16[576,512]{1,0:T(8,128)(2,1)}, u32[]{:S(2)}, u32[]{:S(2)}) collective-permute-start(bf16[576,512]{1,0:T(8,128)(2,1)} %added.7.rest_1_), channel_id=1, source_target_pairs={{0,4},{12,8},{1,5},{13,9},{2,6},{14,10},{3,7},{15,11},{16,20},{28,... | collective-permute-start | bytes 1769480 | tf_op jit(solution)/shard_map/ppermute | solution.py:551
  47.0 0.8 collective-permute-start.14
  47.9 0.3 collective-permute-start.13
  48.3 2.9 %collective-permute-start.17 = (s32[2]{0:T(128)S(1)}, s32[2]{0:T(128)S(1)}, u32[]{:S(2)}, u32[]{:S(2)}) collective-permute-start(s32[2]{0:T(128)S(1)} %copy-done.8), channel_id=1, source_target_pairs={{0,4},{12,8},{1,5},{13,9},{2,6},{14,10},{3,7},{15,11},{16,20},{28,... | collective-permute-start | bytes 32 | tf_op jit(solution)/shard_map/ppermute | solution.py:551
  51.1 8.6 %collective-permute-done.17.prompts_ref = s32[2]{0:T(128)S(1)} collective-permute-done((s32[2]{0:T(128)S(1)}, s32[2]{0:T(128)S(1)}, u32[]{:S(2)}, u32[]{:S(2)}) %collective-permute-start.17) | collective-permute-done | bytes 40 | tf_op jit(solution)/shard_map/ppermute | solution.py:551
  59.7 4.4 %collective-permute-start.18 = (bf16[384,1280]{1,0:T(8,128)(2,1)S(1)}, bf16[384,1280]{1,0:T(8,128)(2,1)S(1)}, u32[]{:S(2)}, u32[]{:S(2)}) collective-permute-start(bf16[384,1280]{1,0:T(8,128)(2,1)S(1)} %constant_dynamic-slice_fusion), channel_id=1, source_target_pairs={{0,4},{12,8},{1,5},{13,9},{2,6},{14,10},{3,7},{15,11},{16,20},{28,... | collective-permute-start | bytes 2949128 | tf_op jit(solution)/shard_map/ppermute | solution.py:551
  64.2 1.3 stacked.1.rest_2_
  65.5 0.7 collective-permute-start.15
  66.2 0.6 collective-permute-start.1
  66.9 18.1 %collective-permute-done.18.refs_4_.refs_3_ = bf16[384,1280]{1,0:T(8,128)(2,1)S(1)} collective-permute-done((bf16[384,1280]{1,0:T(8,128)(2,1)S(1)}, bf16[384,1280]{1,0:T(8,128)(2,1)S(1)}, u32[]{:S(2)}, u32[]{:S(2)}) %collective-permute-start.18) | collective-permute-done | bytes 983072 | tf_op jit(solution)/shard_map/ppermute | solution.py:551
  85.0 4.4 %collective-permute-start.19 = (bf16[4,64,1792]{2,1,0:T(8,128)(2,1)S(1)}, bf16[4,64,1792]{2,1,0:T(8,128)(2,1)S(1)}, u32[]{:S(2)}, u32[]{:S(2)}) collective-permute-start(bf16[4,64,1792]{2,1,0:T(8,128)(2,1)S(1)} %pad_maximum_fusion), channel_id=1, source_target_pairs={{0,4},{12,8},{1,5},{13,9},{2,6},{14,10},{3,7},{15,11},{16,20},{28,... | collective-permute-start | bytes 2752520 | tf_op jit(solution)/shard_map/ppermute | solution.py:551
  89.4 0.6 collective-permute-start.20
  90.0 4.6 %attend.2.refs_0_ = bf16[4,64,1280]{2,1,0:T(8,128)(2,1)S(1)} custom-call(s32[3]{0:T(128)S(1)} %copy-done.5, s32[2]{0:T(128)S(1)} %copy-done.8, s32[4]{0:T(128)S(1)} %copy-done.6, s32[4]{0:T(128)S(1)} %copy-done.7, bf16[4,64,1280]{2,1,0:T(8,128)(2,1)S(1)} %copy-done.3, bf16[4,64,512]{2,1,0:T(8,128)(2,1)S(1)} %copy-done.4, bf16[448,512]{1,0:T(8,128)(2,1)S(1)} %copy-done.2, ...), custom_call_target="tpu_custom_call" | custom-call | flops 64 | bytes 64 | tf_op jit(solution)/shard_map/attend/pallas_call | solution.py:323
  94.7 0.7 collective-permute-start.16
  95.4 12.6 %collective-permute-done.19.query_hbm.new_hbm = bf16[4,64,1792]{2,1,0:T(8,128)(2,1)S(1)} collective-permute-done((bf16[4,64,1792]{2,1,0:T(8,128)(2,1)S(1)}, bf16[4,64,1792]{2,1,0:T(8,128)(2,1)S(1)}, u32[]{:S(2)}, u32[]{:S(2)}) %collective-permute-start.19) | collective-permute-done | bytes 917536 | tf_op jit(solution)/shard_map/ppermute | solution.py:551
  107.9 4.0 %attend.3.refs_1_ = bf16[4,64,1280]{2,1,0:T(8,128)(2,1)S(1)} custom-call(s32[3]{0:T(128)S(1)} %copy-done.5, s32[2]{0:T(128)S(1)} %collective-permute-done.17.prompts_ref, s32[4]{0:T(128)S(1)} %copy-done.6, s32[4]{0:T(128)S(1)} %copy-done.7, bf16[4,64,1792]{2,1,0:T(8,128)(2,1)S(1)} %collective-permute-done.19.query_hbm.new_hbm, ...), custom_call_target="tpu_custom_call" | custom-call | flops 64 | bytes 64 | tf_op jit(solution)/shard_map/attend/pallas_call | solution.py:323
  111.9 1.0 collective-permute-start.22
  112.9 5.1 %spread.3 = (bf16[4,128,1280]{2,1,0:T(8,128)(2,1)S(1)}, bf16[4,64,1280]{2,1,0:T(8,128)(2,1)S(1)}, bf16[4,64,1280]{2,1,0:T(8,128)(2,1)S(1)}) custom-call(s32[3]{0:T(128)S(1)} %copy-done.5, bf16[4,64,1280]{2,1,0:T(8,128)(2,1)S(1)} %collective-permute-done.16.refs_0_, bf16[4,64,1280]{2,1,0:T(8,128)(2,1)S(1)} %attend.3.refs_1_, bf16[1280,1280]{1,0:T(8,128)(2,1)S(1)} %copy-done, ...), custom_call_target="tpu_custom_call" | custom-call | flops 64 | bytes 64 | tf_op jit(solution)/shard_map/spread/pallas_call | solution.py:383
  118.1 0.5 collective-permute-start.24
  118.6 4.1 %spread.4 = (bf16[4,64,1280]{2,1,0:T(8,128)(2,1)}, bf16[4,64,1280]{2,1,0:T(8,128)(2,1)S(1)}) custom-call(s32[3]{0:T(128)S(1)} %copy-done.5, bf16[4,64,1280]{2,1,0:T(8,128)(2,1)S(1)} %attend.2.refs_0_, bf16[1280,1280]{1,0:T(8,128)(2,1)S(1)} %copy-done, bf16[256,1280]{1,0:T(8,128)(2,1)} %collective-permute-done.refs_3_.refs_2_, ...), custom_call_target="tpu_custom_call" | custom-call | flops 64 | bytes 64 | tf_op jit(solution)/shard_map/spread/pallas_call | solution.py:383
  122.7 0.1 collective-permute-start.25
  122.8 0.7 added_half.3
  123.5 1.6 collective-permute-start.27
  125.1 3.2 %spread.5 = (bf16[4,64,1280]{2,1,0:T(8,128)(2,1)S(1)}, bf16[4,64,1280]{2,1,0:T(8,128)(2,1)S(1)}) custom-call(s32[3]{0:T(128)S(1)} %copy-done.5, bf16[4,64,1280]{2,1,0:T(8,128)(2,1)S(1)} %collective-permute-done.22.refs_0_, bf16[1280,1280]{1,0:T(8,128)(2,1)S(1)} %copy-done, bf16[256,1280]{1,0:T(8,128)(2,1)} %collective-permute-done.refs_3_.refs_2_, ...), custom_call_target="tpu_custom_call" | custom-call | flops 64 | bytes 64 | tf_op jit(solution)/shard_map/spread/pallas_call | solution.py:383
  128.3 0.2 collective-permute-start.26
  128.5 0.3 collective-permute-start.21
  128.9 11.8 %collective-permute-done.27.refs_4_ = bf16[2,128,1280]{2,1,0:T(8,128)(2,1)S(1)} collective-permute-done((bf16[2,128,1280]{2,1,0:T(8,128)(2,1)S(1)}, bf16[2,128,1280]{2,1,0:T(8,128)(2,1)S(1)}, u32[]{:S(2)}, u32[]{:S(2)}) %collective-permute-start.27) | collective-permute-done | bytes 655392 | tf_op jit(solution)/shard_map/ppermute | solution.py:554
  140.7 0.6 added_half.4
  141.3 1.6 collective-permute-start.30
  142.9 1.3 added_pieces.1
  144.2 0.7 collective-permute-start.29
  144.9 1.0 added_halves.1
  145.9 0.7 collective-permute-start.33
  146.6 0.7 collective-permute-start.34
  147.3 4.2 %collective-permute-done.30.refs_3_ = bf16[2,64,1280]{2,1,0:T(8,128)(2,1)S(1)} collective-permute-done((bf16[2,64,1280]{2,1,0:T(8,128)(2,1)S(1)}, bf16[2,64,1280]{2,1,0:T(8,128)(2,1)S(1)}, u32[]{:S(2)}, u32[]{:S(2)}) %collective-permute-start.30) | collective-permute-done | bytes 327712 | tf_op jit(solution)/shard_map/ppermute | solution.py:554
  151.5 0.7 added_half.5
  152.2 1.3 collective-permute-start.36
  153.5 1.3 collective-permute-start.35
  154.9 0.7 collective-permute-start.31
  155.6 24.0 %collective-permute-done.36 = bf16[2,64,1280]{2,1,0:T(8,128)(2,1)} collective-permute-done((bf16[2,64,1280]{2,1,0:T(8,128)(2,1)S(1)}, bf16[2,64,1280]{2,1,0:T(8,128)(2,1)}, u32[]{:S(2)}, u32[]{:S(2)}) %collective-permute-start.36) | collective-permute-done | bytes 327712 | tf_op jit(solution)/shard_map/ppermute | solution.py:524
  179.6 1.2 select_select_fusion.1
  180.8 0.7 joined.1
  181.5 1.0 fusion
  (58 shorter events, 0.5 us)
Async XLA Ops:
  0.7 7.3 %copy-start = (bf16[1280,1280]{1,0:T(8,128)(2,1)S(1)}, bf16[1280,1280]{1,0:T(8,128)(2,1)}, u32[]{:S(2)}) copy-start(bf16[1280,1280]{1,0:T(8,128)(2,1)} %refs_1_.3) | copy-start | bytes 9830404
  7.4 8.4 %collective-permute-start.5 = (bf16[576,512]{1,0:T(8,128)(2,1)}, bf16[576,512]{1,0:T(8,128)(2,1)}, u32[]{:S(2)}, u32[]{:S(2)}) collective-permute-start(bf16[576,512]{1,0:T(8,128)(2,1)} %get-tuple-element.53), channel_id=1, source_target_pairs={{0,1},{1,0},{2,3},{3,2},{4,5},{5,4},{6,7},{7,6},{8,9},{9,8},{10,11... | collective-permute-start | bytes 1769480 | tf_op jit(solution)/shard_map/ppermute | solution.py:554
  7.5 5.7 %collective-permute-start.2 = (bf16[448,512]{1,0:T(8,128)(2,1)}, bf16[448,512]{1,0:T(8,128)(2,1)}, u32[]{:S(2)}, u32[]{:S(2)}) collective-permute-start(bf16[448,512]{1,0:T(8,128)(2,1)} %get-tuple-element.47), channel_id=1, source_target_pairs={{0,1},{1,0},{2,3},{3,2},{4,5},{5,4},{6,7},{7,6},{8,9},{9,8},{10,11... | collective-permute-start | bytes 1376264 | tf_op jit(solution)/shard_map/ppermute | solution.py:554
  8.9 22.7 %collective-permute-start = (bf16[256,1280]{1,0:T(8,128)(2,1)}, bf16[256,1280]{1,0:T(8,128)(2,1)}, u32[]{:S(2)}, u32[]{:S(2)}) collective-permute-start(bf16[256,1280]{1,0:T(8,128)(2,1)} %constant_dynamic-slice_fusion.1), channel_id=1, source_target_pairs={{0,4},{12,8},{1,5},{13,9},{2,6},{14,10},{3,7},{15,11},{16,20},{28,... | collective-permute-start | bytes 1966088 | tf_op jit(solution)/shard_map/ppermute | solution.py:551
  15.3 12.4 %collective-permute-start.3 = (bf16[448,512]{1,0:T(8,128)(2,1)}, bf16[448,512]{1,0:T(8,128)(2,1)S(1)}, u32[]{:S(2)}, u32[]{:S(2)}) collective-permute-start(bf16[448,512]{1,0:T(8,128)(2,1)} %added.4), channel_id=1, source_target_pairs={{0,2},{2,0},{1,3},{3,1},{4,6},{6,4},{5,7},{7,5},{8,10},{10,8},{9,1... | collective-permute-start | bytes 1376264 | tf_op jit(solution)/shard_map/ppermute | solution.py:554
  18.0 9.7 %copy-start.5 = (s32[3]{0:T(128)S(1)}, s32[3]{0:T(128)}, u32[]{:S(2)}) copy-start(s32[3]{0:T(128)} %pad_add_fusion.here_ref.refs_0_) | copy-start | bytes 40
  24.5 4.4 %collective-permute-start.6 = (bf16[448,512]{1,0:T(8,128)(2,1)}, bf16[448,512]{1,0:T(8,128)(2,1)}, u32[]{:S(2)}, u32[]{:S(2)}) collective-permute-start(bf16[448,512]{1,0:T(8,128)(2,1)} %get-tuple-element.57), channel_id=1, source_target_pairs={{0,1},{1,0},{2,3},{3,2},{4,5},{5,4},{6,7},{7,6},{8,9},{9,8},{10,11... | collective-permute-start | bytes 1376264 | tf_op jit(solution)/shard_map/ppermute | solution.py:554
  24.6 16.1 %collective-permute-start.7 = (bf16[576,512]{1,0:T(8,128)(2,1)}, bf16[576,512]{1,0:T(8,128)(2,1)}, u32[]{:S(2)}, u32[]{:S(2)}) collective-permute-start(bf16[576,512]{1,0:T(8,128)(2,1)} %added.5), channel_id=1, source_target_pairs={{0,2},{2,0},{1,3},{3,1},{4,6},{6,4},{5,7},{7,5},{8,10},{10,8},{9,1... | collective-permute-start | bytes 1769480 | tf_op jit(solution)/shard_map/ppermute | solution.py:554
  26.1 14.5 %collective-permute-start.9 = (bf16[576,512]{1,0:T(8,128)(2,1)}, bf16[576,512]{1,0:T(8,128)(2,1)}, u32[]{:S(2)}, u32[]{:S(2)}) collective-permute-start(bf16[576,512]{1,0:T(8,128)(2,1)} %get-tuple-element.60), channel_id=1, source_target_pairs={{0,1},{1,0},{2,3},{3,2},{4,5},{5,4},{6,7},{7,6},{8,9},{9,8},{10,11... | collective-permute-start | bytes 1769480 | tf_op jit(solution)/shard_map/ppermute | solution.py:554
  27.7 1.1 copy-start.9
  27.7 1.1 collective-permute-start.4
  28.8 0.5 copy-start.11
  31.6 16.6 %copy-start.8 = (s32[2]{0:T(128)S(1)}, s32[2]{0:T(128)}, u32[]{:S(2)}) copy-start(s32[2]{0:T(128)} %prompts_ref.1) | copy-start | bytes 28
  31.6 16.3 %collective-permute-start.10 = (bf16[448,512]{1,0:T(8,128)(2,1)}, bf16[448,512]{1,0:T(8,128)(2,1)}, u32[]{:S(2)}, u32[]{:S(2)}) collective-permute-start(bf16[448,512]{1,0:T(8,128)(2,1)} %added.6.rest_0_), channel_id=1, source_target_pairs={{0,4},{12,8},{1,5},{13,9},{2,6},{14,10},{3,7},{15,11},{16,20},{28,... | collective-permute-start | bytes 1376264 | tf_op jit(solution)/shard_map/ppermute | solution.py:551
  33.8 14.1 %collective-permute-start.12 = (bf16[448,512]{1,0:T(8,128)(2,1)}, bf16[448,512]{1,0:T(8,128)(2,1)}, u32[]{:S(2)}, u32[]{:S(2)}) collective-permute-start(bf16[448,512]{1,0:T(8,128)(2,1)} %added.6.rest_0_), channel_id=1, source_target_pairs={{4,8},{8,4},{5,9},{9,5},{6,10},{10,6},{7,11},{11,7},{20,24},{24,20... | collective-permute-start | bytes 1376264 | tf_op jit(solution)/shard_map/ppermute | solution.py:551
  40.6 1.1 collective-permute-start.8
  41.7 0.6 copy-start.10
  44.8 22.0 %copy-start.4 = (bf16[4,64,512]{2,1,0:T(8,128)(2,1)S(1)}, bf16[4,64,512]{2,1,0:T(8,128)(2,1)}, u32[]{:S(2)}) copy-start(bf16[4,64,512]{2,1,0:T(8,128)(2,1)} %new_hbm.1) | copy-start | bytes 786436
  44.8 15.0 %collective-permute-start.11 = (bf16[576,512]{1,0:T(8,128)(2,1)}, bf16[576,512]{1,0:T(8,128)(2,1)}, u32[]{:S(2)}, u32[]{:S(2)}) collective-permute-start(bf16[576,512]{1,0:T(8,128)(2,1)} %added.7.rest_1_), channel_id=1, source_target_pairs={{0,4},{12,8},{1,5},{13,9},{2,6},{14,10},{3,7},{15,11},{16,20},{28,... | collective-permute-start | bytes 1769480 | tf_op jit(solution)/shard_map/ppermute | solution.py:551
  47.0 19.8 %copy-start.3 = (bf16[4,64,1280]{2,1,0:T(8,128)(2,1)S(1)}, bf16[4,64,1280]{2,1,0:T(8,128)(2,1)}, u32[]{:S(2)}) copy-start(bf16[4,64,1280]{2,1,0:T(8,128)(2,1)} %query_hbm) | copy-start | bytes 1966084
  47.0 18.5 %collective-permute-start.14 = (bf16[576,512]{1,0:T(8,128)(2,1)}, bf16[576,512]{1,0:T(8,128)(2,1)S(1)}, u32[]{:S(2)}, u32[]{:S(2)}) collective-permute-start(bf16[576,512]{1,0:T(8,128)(2,1)} %added.7.rest_1_), channel_id=1, source_target_pairs={{4,8},{8,4},{5,9},{9,5},{6,10},{10,6},{7,11},{11,7},{20,24},{24,20... | collective-permute-start | bytes 1769480 | tf_op jit(solution)/shard_map/ppermute | solution.py:551
  47.9 16.3 %collective-permute-start.13 = (bf16[448,512]{1,0:T(8,128)(2,1)}, bf16[448,512]{1,0:T(8,128)(2,1)S(1)}, u32[]{:S(2)}, u32[]{:S(2)}) collective-permute-start(bf16[448,512]{1,0:T(8,128)(2,1)} %added.4), channel_id=1, source_target_pairs={{0,1},{1,0},{2,3},{3,2},{4,5},{5,4},{6,7},{7,6},{8,9},{9,8},{10,11... | collective-permute-start | bytes 1376264 | tf_op jit(solution)/shard_map/ppermute | solution.py:554
  48.2 41.8 %copy-start.1 = (bf16[576,512]{1,0:T(8,128)(2,1)S(1)}, bf16[576,512]{1,0:T(8,128)(2,1)}, u32[]{:S(2)}) copy-start(bf16[576,512]{1,0:T(8,128)(2,1)} %added.7.rest_1_) | copy-start | bytes 1769476
  48.2 41.8 %copy-start.2 = (bf16[448,512]{1,0:T(8,128)(2,1)S(1)}, bf16[448,512]{1,0:T(8,128)(2,1)}, u32[]{:S(2)}) copy-start(bf16[448,512]{1,0:T(8,128)(2,1)} %added.6.rest_0_) | copy-start | bytes 1376260
  48.2 41.8 %copy-start.6 = (s32[4]{0:T(128)S(1)}, s32[4]{0:T(128)}, u32[]{:S(2)}) copy-start(s32[4]{0:T(128)} %owners_ref.3) | copy-start | bytes 52
  48.2 41.8 %copy-start.7 = (s32[4]{0:T(128)S(1)}, s32[4]{0:T(128)}, u32[]{:S(2)}) copy-start(s32[4]{0:T(128)} %lengths_ref.3) | copy-start | bytes 52
  48.3 11.5 %collective-permute-start.17 = (s32[2]{0:T(128)S(1)}, s32[2]{0:T(128)S(1)}, u32[]{:S(2)}, u32[]{:S(2)}) collective-permute-start(s32[2]{0:T(128)S(1)} %copy-done.8), channel_id=1, source_target_pairs={{0,4},{12,8},{1,5},{13,9},{2,6},{14,10},{3,7},{15,11},{16,20},{28,... | collective-permute-start | bytes 32 | tf_op jit(solution)/shard_map/ppermute | solution.py:551
  59.7 25.2 %collective-permute-start.18 = (bf16[384,1280]{1,0:T(8,128)(2,1)S(1)}, bf16[384,1280]{1,0:T(8,128)(2,1)S(1)}, u32[]{:S(2)}, u32[]{:S(2)}) collective-permute-start(bf16[384,1280]{1,0:T(8,128)(2,1)S(1)} %constant_dynamic-slice_fusion), channel_id=1, source_target_pairs={{0,4},{12,8},{1,5},{13,9},{2,6},{14,10},{3,7},{15,11},{16,20},{28,... | collective-permute-start | bytes 2949128 | tf_op jit(solution)/shard_map/ppermute | solution.py:551
  65.5 24.5 %collective-permute-start.15 = (bf16[1024,512]{1,0:T(8,128)(2,1)S(1)}, bf16[1024,512]{1,0:T(8,128)(2,1)S(1)}, u32[]{:S(2)}, u32[]{:S(2)}) collective-permute-start(bf16[1024,512]{1,0:T(8,128)(2,1)S(1)} %stacked.1.rest_2_), channel_id=1, source_target_pairs={{4,8},{8,4},{5,9},{9,5},{6,10},{10,6},{7,11},{11,7},{20,24},{24,20... | collective-permute-start | bytes 3145736 | tf_op jit(solution)/shard_map/ppermute | solution.py:551
  66.2 23.8 %collective-permute-start.1 = (bf16[256,1280]{1,0:T(8,128)(2,1)}, bf16[256,1280]{1,0:T(8,128)(2,1)S(1)}, u32[]{:S(2)}, u32[]{:S(2)}) collective-permute-start(bf16[256,1280]{1,0:T(8,128)(2,1)} %collective-permute-done.refs_3_.refs_2_), channel_id=1, source_target_pairs={{0,16},{16,0},{1,17},{17,1},{2,18},{18,2},{3,19},{19,3},{4,20},{20... | collective-permute-start | bytes 1966088 | tf_op jit(solution)/shard_map/ppermute | solution.py:578
  85.0 23.0 %collective-permute-start.19 = (bf16[4,64,1792]{2,1,0:T(8,128)(2,1)S(1)}, bf16[4,64,1792]{2,1,0:T(8,128)(2,1)S(1)}, u32[]{:S(2)}, u32[]{:S(2)}) collective-permute-start(bf16[4,64,1792]{2,1,0:T(8,128)(2,1)S(1)} %pad_maximum_fusion), channel_id=1, source_target_pairs={{0,4},{12,8},{1,5},{13,9},{2,6},{14,10},{3,7},{15,11},{16,20},{28,... | collective-permute-start | bytes 2752520 | tf_op jit(solution)/shard_map/ppermute | solution.py:551
  89.4 23.5 %collective-permute-start.20 = (bf16[384,1280]{1,0:T(8,128)(2,1)S(1)}, bf16[384,1280]{1,0:T(8,128)(2,1)S(1)}, u32[]{:S(2)}, u32[]{:S(2)}) collective-permute-start(bf16[384,1280]{1,0:T(8,128)(2,1)S(1)} %collective-permute-done.18.refs_4_.refs_3_), channel_id=1, source_target_pairs={{0,16},{16,0},{1,17},{17,1},{2,18},{18,2},{3,19},{19,3},{4,20},{20... | collective-permute-start | bytes 2949128 | tf_op jit(solution)/shard_map/ppermute | solution.py:578
  94.7 18.2 %collective-permute-start.16 = (bf16[4,64,1280]{2,1,0:T(8,128)(2,1)S(1)}, bf16[4,64,1280]{2,1,0:T(8,128)(2,1)S(1)}, u32[]{:S(2)}, u32[]{:S(2)}) collective-permute-start(bf16[4,64,1280]{2,1,0:T(8,128)(2,1)S(1)} %attend.2.refs_0_), channel_id=1, source_target_pairs={{4,8},{8,4},{5,9},{9,5},{6,10},{10,6},{7,11},{11,7},{20,24},{24,20... | collective-permute-start | bytes 1966088 | tf_op jit(solution)/shard_map/ppermute | solution.py:551
  111.9 10.8 %collective-permute-start.22 = (bf16[4,64,1280]{2,1,0:T(8,128)(2,1)S(1)}, bf16[4,64,1280]{2,1,0:T(8,128)(2,1)S(1)}, u32[]{:S(2)}, u32[]{:S(2)}) collective-permute-start(bf16[4,64,1280]{2,1,0:T(8,128)(2,1)S(1)} %attend.3.refs_1_), channel_id=1, source_target_pairs={{4,8},{8,4},{5,9},{9,5},{6,10},{10,6},{7,11},{11,7},{20,24},{24,20... | collective-permute-start | bytes 1966088 | tf_op jit(solution)/shard_map/ppermute | solution.py:551
  118.1 4.7 %collective-permute-start.23 = (bf16[4,64,1280]{2,1,0:T(8,128)(2,1)S(1)}, bf16[4,64,1280]{2,1,0:T(8,128)(2,1)S(1)}, u32[]{:S(2)}, u32[]{:S(2)}) collective-permute-start(bf16[4,64,1280]{2,1,0:T(8,128)(2,1)S(1)} %get-tuple-element.74), channel_id=1, source_target_pairs={{0,1},{1,0},{2,3},{3,2},{4,5},{5,4},{6,7},{7,6},{8,9},{9,8},{10,11... | collective-permute-start | bytes 1966088 | tf_op jit(solution)/shard_map/ppermute | solution.py:554
  118.1 4.7 %collective-permute-start.24 = (bf16[4,64,1280]{2,1,0:T(8,128)(2,1)S(1)}, bf16[4,64,1280]{2,1,0:T(8,128)(2,1)S(1)}, u32[]{:S(2)}, u32[]{:S(2)}) collective-permute-start(bf16[4,64,1280]{2,1,0:T(8,128)(2,1)S(1)} %get-tuple-element.75), channel_id=1, source_target_pairs={{0,1},{1,0},{2,3},{3,2},{4,5},{5,4},{6,7},{7,6},{8,9},{9,8},{10,11... | collective-permute-start | bytes 1966088 | tf_op jit(solution)/shard_map/ppermute | solution.py:554
  122.7 2.4 %collective-permute-start.25 = (bf16[4,64,1280]{2,1,0:T(8,128)(2,1)}, bf16[4,64,1280]{2,1,0:T(8,128)(2,1)S(1)}, u32[]{:S(2)}, u32[]{:S(2)}) collective-permute-start(bf16[4,64,1280]{2,1,0:T(8,128)(2,1)} %get-tuple-element.86.refs_1_), channel_id=1, source_target_pairs={{0,1},{1,0},{2,3},{3,2},{4,5},{5,4},{6,7},{7,6},{8,9},{9,8},{10,11... | collective-permute-start | bytes 1966088 | tf_op jit(solution)/shard_map/ppermute | solution.py:554
  123.5 17.1 %collective-permute-start.27 = (bf16[2,128,1280]{2,1,0:T(8,128)(2,1)S(1)}, bf16[2,128,1280]{2,1,0:T(8,128)(2,1)S(1)}, u32[]{:S(2)}, u32[]{:S(2)}) collective-permute-start(bf16[2,128,1280]{2,1,0:T(8,128)(2,1)S(1)} %added_half.3), channel_id=1, source_target_pairs={{0,2},{2,0},{1,3},{3,1},{4,6},{6,4},{5,7},{7,5},{8,10},{10,8},{9,1... | collective-permute-start | bytes 1966088 | tf_op jit(solution)/shard_map/ppermute | solution.py:554
  128.3 12.4 %collective-permute-start.26 = (bf16[4,64,1280]{2,1,0:T(8,128)(2,1)S(1)}, bf16[4,64,1280]{2,1,0:T(8,128)(2,1)S(1)}, u32[]{:S(2)}, u32[]{:S(2)}) collective-permute-start(bf16[4,64,1280]{2,1,0:T(8,128)(2,1)S(1)} %get-tuple-element.79), channel_id=1, source_target_pairs={{0,1},{1,0},{2,3},{3,2},{4,5},{5,4},{6,7},{7,6},{8,9},{9,8},{10,11... | collective-permute-start | bytes 1966088 | tf_op jit(solution)/shard_map/ppermute | solution.py:554
  128.5 14.3 %collective-permute-start.21 = (bf16[4,64,1280]{2,1,0:T(8,128)(2,1)S(1)}, bf16[4,64,1280]{2,1,0:T(8,128)(2,1)S(1)}, u32[]{:S(2)}, u32[]{:S(2)}) collective-permute-start(bf16[4,64,1280]{2,1,0:T(8,128)(2,1)S(1)} %get-tuple-element.73), channel_id=1, source_target_pairs={{0,1},{1,0},{2,3},{3,2},{4,5},{5,4},{6,7},{7,6},{8,9},{9,8},{10,11... | collective-permute-start | bytes 1966088 | tf_op jit(solution)/shard_map/ppermute | solution.py:554
  140.7 2.2 %collective-permute-start.28 = (bf16[4,64,1280]{2,1,0:T(8,128)(2,1)S(1)}, bf16[4,64,1280]{2,1,0:T(8,128)(2,1)S(1)}, u32[]{:S(2)}, u32[]{:S(2)}) collective-permute-start(bf16[4,64,1280]{2,1,0:T(8,128)(2,1)S(1)} %attend.2.refs_0_), channel_id=1, source_target_pairs={{0,1},{1,0},{2,3},{3,2},{4,5},{5,4},{6,7},{7,6},{8,9},{9,8},{10,11... | collective-permute-start | bytes 1966088 | tf_op jit(solution)/shard_map/ppermute | solution.py:554
  141.3 10.2 %collective-permute-start.30 = (bf16[2,64,1280]{2,1,0:T(8,128)(2,1)S(1)}, bf16[2,64,1280]{2,1,0:T(8,128)(2,1)S(1)}, u32[]{:S(2)}, u32[]{:S(2)}) collective-permute-start(bf16[2,64,1280]{2,1,0:T(8,128)(2,1)S(1)} %added_half.4), channel_id=1, source_target_pairs={{0,2},{2,0},{1,3},{3,1},{4,6},{6,4},{5,7},{7,5},{8,10},{10,8},{9,1... | collective-permute-start | bytes 983048 | tf_op jit(solution)/shard_map/ppermute | solution.py:554
  144.2 10.6 %collective-permute-start.29 = (bf16[4,32,1280]{2,1,0:T(8,128)(2,1)S(1)}, bf16[4,32,1280]{2,1,0:T(8,128)(2,1)S(1)}, u32[]{:S(2)}, u32[]{:S(2)}) collective-permute-start(bf16[4,32,1280]{2,1,0:T(8,128)(2,1)S(1)} %get-tuple-element.84.refs_1_), channel_id=1, source_target_pairs={{6,4},{7,5},{8,10},{9,11},{22,20},{23,21},{24,26},{25,27}} | collective-permute-start | bytes 983048 | tf_op jit(solution)/shard_map/ppermute | solution.py:533
  145.9 9.0 %collective-permute-start.33 = (bf16[2,64,1280]{2,1,0:T(8,128)(2,1)S(1)}, bf16[2,64,1280]{2,1,0:T(8,128)(2,1)S(1)}, u32[]{:S(2)}, u32[]{:S(2)}) collective-permute-start(bf16[2,64,1280]{2,1,0:T(8,128)(2,1)S(1)} %get-tuple-element.87), channel_id=1, source_target_pairs={{4,8},{5,9},{10,6},{11,7},{6,0},{7,1},{8,14},{9,15},{20,24},{21,25... | collective-permute-start | bytes 983048 | tf_op jit(solution)/shard_map/ppermute | solution.py:524
  146.6 9.0 %collective-permute-start.34 = (bf16[2,64,1280]{2,1,0:T(8,128)(2,1)S(1)}, bf16[2,64,1280]{2,1,0:T(8,128)(2,1)S(1)}, u32[]{:S(2)}, u32[]{:S(2)}) collective-permute-start(bf16[2,64,1280]{2,1,0:T(8,128)(2,1)S(1)} %get-tuple-element.88), channel_id=1, source_target_pairs={{6,8},{7,9},{8,6},{9,7},{4,0},{5,1},{10,14},{11,15},{22,24},{23,25... | collective-permute-start | bytes 983048 | tf_op jit(solution)/shard_map/ppermute | solution.py:524
  152.2 27.4 %collective-permute-start.36 = (bf16[2,64,1280]{2,1,0:T(8,128)(2,1)S(1)}, bf16[2,64,1280]{2,1,0:T(8,128)(2,1)}, u32[]{:S(2)}, u32[]{:S(2)}) collective-permute-start(bf16[2,64,1280]{2,1,0:T(8,128)(2,1)S(1)} %added_half.5), channel_id=1, source_target_pairs={{6,12},{7,13},{8,2},{9,3},{22,28},{23,29},{24,18},{25,19}} | collective-permute-start | bytes 983048 | tf_op jit(solution)/shard_map/ppermute | solution.py:524
  153.5 26.1 %collective-permute-start.35 = (bf16[2,64,1280]{2,1,0:T(8,128)(2,1)S(1)}, bf16[2,64,1280]{2,1,0:T(8,128)(2,1)}, u32[]{:S(2)}, u32[]{:S(2)}) collective-permute-start(bf16[2,64,1280]{2,1,0:T(8,128)(2,1)S(1)} %added_half.5), channel_id=1, source_target_pairs={{4,12},{5,13},{10,2},{11,3},{20,28},{21,29},{26,18},{27,19}} | collective-permute-start | bytes 983048 | tf_op jit(solution)/shard_map/ppermute | solution.py:524
  154.8 26.0 %collective-permute-start.32 = (bf16[4,64,1280]{2,1,0:T(8,128)(2,1)}, bf16[4,64,1280]{2,1,0:T(8,128)(2,1)S(1)}, u32[]{:S(2)}, u32[]{:S(2)}) collective-permute-start(bf16[4,64,1280]{2,1,0:T(8,128)(2,1)} %get-tuple-element.86.refs_1_), channel_id=1, source_target_pairs={{0,1},{1,0},{2,3},{3,2},{4,5},{5,4},{6,7},{7,6},{8,9},{9,8},{10,11... | collective-permute-start | bytes 1966088 | tf_op jit(solution)/shard_map/ppermute | solution.py:554
  154.9 25.8 %collective-permute-start.31 = (bf16[4,32,1280]{2,1,0:T(8,128)(2,1)S(1)}, bf16[4,32,1280]{2,1,0:T(8,128)(2,1)S(1)}, u32[]{:S(2)}, u32[]{:S(2)}) collective-permute-start(bf16[4,32,1280]{2,1,0:T(8,128)(2,1)S(1)} %get-tuple-element.85.refs_2_), channel_id=1, source_target_pairs={{6,4},{7,5},{8,10},{9,11},{22,20},{23,21},{24,26},{25,27}} | collective-permute-start | bytes 983048 | tf_op jit(solution)/shard_map/ppermute | solution.py:533

commit v6 on v5

--- a/solution.py
+++ b/solution.py
@@ -578,18 +578,18 @@
         return lax.ppermute(part, "groups", [(0, 1), (1, 0)])
 
     weight_0 = on_samp(weight_part(0, sent[0]), INWARD)
-    leaving_first = added(here, kept[0], on_head(sent[0], CORE), limit=LARGE_VMEM)
-    leaving_second = added(here, kept[1], after(on_head(sent[1], CORE), leaving_first), limit=LARGE_VMEM)
+    leaving_first = added(here, kept[0], on_head(sent[0], CORE), limit=32 * 1024 * 1024)
+    leaving_second = added(here, kept[1], after(on_head(sent[1], CORE), leaving_first), limit=32 * 1024 * 1024)
     crossed_first = on_head(leaving_first, ACROSS_X)
     crossed_second = on_head(leaving_second, ACROSS_X)
     sent, kept = project(
         here, after(states, leaving_first, leaving_second), kv_weight, (1, 0), cuts
     )
     sent = [on_head(value, CORE) for value in sent]
-    first = added(hopped((crossed_first,)), kept[0], sent[0], crossed_first, limit=LARGE_VMEM)
+    first = added(hopped((crossed_first,)), kept[0], sent[0], crossed_first, limit=32 * 1024 * 1024)
     end_first = on_samp(after(first, weight_0), INWARD)
     far_first = on_samp(first, MIDDLE)
-    second = added(hopped((crossed_second,)), kept[1], sent[1], crossed_second, limit=LARGE_VMEM)
+    second = added(here, kept[1], sent[1], crossed_second, limit=32 * 1024 * 1024)
     end_second = on_samp(second, INWARD)
     far_second = on_samp(second, MIDDLE)
     end_page = stacked(

time: 184 us -> 178 us (0.967)
  waiting for transfers between devices: 88.4 us -> 80.4 us
  local copies, waits for them, and re-layouts: 2.09 us -> 4.91 us
    ppermute x4, waiting for transfers between devices: 24 us -> 19.8 us  [sent_home(): lax.ppermute(value, ('samp', 'head'), [pair for part in pairs for pair in...]
    pallas_call x2, Pallas kernels: 8.57 us -> 12.1 us  [attend(): pl.pallas_call(body, in_specs=[in_smem] * 4 + [in_hbm] * (2 + len(page_pa...]
    pallas_call x11, Pallas kernels: 15.2 us -> 12.3 us  [run_small(): pl.pallas_call(whole, in_specs=[pl.BlockSpec(memory_space=pltpu.SMEM)] +...]
    unnamed x24 -> x28, local copies, waits for them, and re-layouts: 1.15 us -> 3.96 us
    ppermute x11, waiting for transfers between devices: 39.3 us -> 37.1 us  [on_samp(): return lax.ppermute(value, 'samp', pairs)]
    ppermute x18 -> x17, waiting for transfers between devices: 25.1 us -> 23.6 us  [on_head(): return lax.ppermute(value, 'head', pairs)]
    ppermute x18 -> x17, starting transfers between devices: 7.58 us -> 7.44 us  [on_head(): return lax.ppermute(value, 'head', pairs)]
  transfers between devices with their start and end apart: 37 -> 36, of which waited for: 10 -> 9; matrix products, arithmetic and copies ran while one was open for 1% -> 1% of each run, Pallas kernels for 23% -> 24%
where the time goes in v6:
time: 178 us
  waiting for transfers between devices  80.4 us (45%)
  Pallas kernels  50.1 us (28%)
  starting transfers between devices  39.1 us (22%)
  local copies, waits for them, and re-layouts  4.91 us (3%)
  other arithmetic  2.81 us (2%)
    ppermute x11, waiting for transfers between devices, on_samp(): return lax.ppermute(value, 'samp', pairs)  37.1 us
    ppermute x11, starting transfers between devices, on_samp(): return lax.ppermute(value, 'samp', pairs)  25.2 us
    ppermute x17, waiting for transfers between devices, on_head(): return lax.ppermute(value, 'head', pairs)  23.6 us
    ppermute x4, waiting for transfers between devices, sent_home(): lax.ppermute(value, ('samp', 'head'), [pair for part in pairs for pair in...  19.8 us
    pallas_call x2, Pallas kernels, project(): pl.pallas_call(body, in_specs=[pl.BlockSpec(memory_space=pltpu.SMEM), in_...  13.2 us
    pallas_call x3, Pallas kernels, spread(): pl.pallas_call(body, in_specs=[pl.BlockSpec(memory_space=pltpu.SMEM)] + [...  12.5 us
    pallas_call x11, Pallas kernels, run_small(): pl.pallas_call(whole, in_specs=[pl.BlockSpec(memory_space=pltpu.SMEM)] +...  12.3 us
    pallas_call x2, Pallas kernels, attend(): pl.pallas_call(body, in_specs=[in_smem] * 4 + [in_hbm] * (2 + len(page_pa...  12.1 us
  transfers between devices with their start and end apart: 36, of which 9 were waited for; matrix products, arithmetic and copies ran while one was open for 1% of the time, Pallas kernels for 24%

profile of v6, /device:TPU:6, one launch (start us, length us, event | category | flops | bytes accessed | tf_op | source)
XLA Modules:
  0.0 177.7 jit_solution(4454412309652580223)
XLA Ops:
  0.0 0.6 pad_add_fusion.here_ref.refs_0_
  0.6 6.7 %project.2 = (bf16[448,512]{1,0:T(8,128)(2,1)}, bf16[576,512]{1,0:T(8,128)(2,1)}, bf16[448,512]{1,0:T(8,128)(2,1)}, bf16[576,512]{1,0:T(8,128)(2,1)}) custom-call(s32[3]{0:T(128)} %pad_add_fusion.here_ref.refs_0_, bf16[1024,1280]{1,0:T(8,128)(2,1)} %bitcast.4, bf16[1280,2048]{1,0:T(8,128)(2,1)} %weight_hbm.3), custom_call_target="tpu_custom_call" | custom-call | flops 64 | bytes 64 | tf_op jit(solution)/shard_map/project/pallas_call | solution.py:190
  7.4 0.5 collective-permute-start.2
  7.9 0.9 constant_dynamic-slice_fusion.1
  8.8 4.3 %collective-permute-start = (bf16[256,1280]{1,0:T(8,128)(2,1)}, bf16[256,1280]{1,0:T(8,128)(2,1)}, u32[]{:S(2)}, u32[]{:S(2)}) collective-permute-start(bf16[256,1280]{1,0:T(8,128)(2,1)} %constant_dynamic-slice_fusion.1), channel_id=1, source_target_pairs={{0,4},{12,8},{1,5},{13,9},{2,6},{14,10},{3,7},{15,11},{16,20},{28,... | collective-permute-start | bytes 1966088 | tf_op jit(solution)/shard_map/ppermute | solution.py:551
  13.1 1.0 copy-done.7
  14.2 1.2 added.4
  15.4 0.6 collective-permute-start.3
  16.0 1.3 added.5
  17.2 0.8 copy-done.4
  18.0 6.5 %project.3 = (bf16[448,512]{1,0:T(8,128)(2,1)}, bf16[576,512]{1,0:T(8,128)(2,1)}, bf16[448,512]{1,0:T(8,128)(2,1)}, bf16[576,512]{1,0:T(8,128)(2,1)}) custom-call(s32[3]{0:T(128)} %pad_add_fusion.here_ref.refs_0_, bf16[1024,1280]{1,0:T(8,128)(2,1)} %bitcast.5, bf16[1280,2048]{1,0:T(8,128)(2,1)} %weight_hbm.3), custom_call_target="tpu_custom_call" | custom-call | flops 64 | bytes 64 | tf_op jit(solution)/shard_map/project/pallas_call | solution.py:190
  24.6 1.6 collective-permute-start.8
  26.2 0.2 collective-permute-start.7
  26.3 1.4 collective-permute-done.3.refs_3_
  27.8 1.1 collective-permute-done.4.refs_0_
  28.9 1.0 copy-done.8
  29.9 2.0 %added.6.rest_0_ = bf16[448,512]{1,0:T(8,128)(2,1)} custom-call(s32[3]{0:T(128)S(1)} %collective-permute-done.4.refs_0_, bf16[448,512]{1,0:T(8,128)(2,1)S(1)} %copy-done.8, bf16[448,512]{1,0:T(8,128)(2,1)S(1)} %collective-permute-done.6.refs_2_, bf16[448,512]{1,0:T(8,128)(2,1)} %collective-permute-done.3.refs_3_), custom_call_target="tpu_custom_call" | custom-call | flops 64 | bytes 64 | tf_op jit(solution)/shard_map/added/pallas_call | solution.py:403
  31.9 2.2 %collective-permute-start.9 = (bf16[448,512]{1,0:T(8,128)(2,1)}, bf16[448,512]{1,0:T(8,128)(2,1)}, u32[]{:S(2)}, u32[]{:S(2)}) collective-permute-start(bf16[448,512]{1,0:T(8,128)(2,1)} %added.6.rest_0_), channel_id=1, source_target_pairs={{0,4},{12,8},{1,5},{13,9},{2,6},{14,10},{3,7},{15,11},{16,20},{28,... | collective-permute-start | bytes 1376264 | tf_op jit(solution)/shard_map/ppermute | solution.py:551
  34.1 1.4 collective-permute-start.11
  35.5 5.0 %collective-permute-done.8.refs_3_ = bf16[576,512]{1,0:T(8,128)(2,1)S(1)} collective-permute-done((bf16[576,512]{1,0:T(8,128)(2,1)}, bf16[576,512]{1,0:T(8,128)(2,1)S(1)}, u32[]{:S(2)}, u32[]{:S(2)}) %collective-permute-start.8) | collective-permute-done | bytes 589856 | tf_op jit(solution)/shard_map/ppermute | solution.py:554
  40.6 1.1 copy-done.3
  41.6 1.6 added.7.rest_1_
  43.2 2.2 %collective-permute-start.10 = (bf16[576,512]{1,0:T(8,128)(2,1)}, bf16[576,512]{1,0:T(8,128)(2,1)}, u32[]{:S(2)}, u32[]{:S(2)}) collective-permute-start(bf16[576,512]{1,0:T(8,128)(2,1)} %added.7.rest_1_), channel_id=1, source_target_pairs={{0,4},{12,8},{1,5},{13,9},{2,6},{14,10},{3,7},{15,11},{16,20},{28,... | collective-permute-start | bytes 1769480 | tf_op jit(solution)/shard_map/ppermute | solution.py:551
  45.4 0.8 collective-permute-start.13
  46.5 2.9 %collective-permute-start.16 = (s32[2]{0:T(128)S(1)}, s32[2]{0:T(128)S(1)}, u32[]{:S(2)}, u32[]{:S(2)}) collective-permute-start(s32[2]{0:T(128)S(1)} %copy-done.13), channel_id=1, source_target_pairs={{0,4},{12,8},{1,5},{13,9},{2,6},{14,10},{3,7},{15,11},{16,20},{28,... | collective-permute-start | bytes 32 | tf_op jit(solution)/shard_map/ppermute | solution.py:551
  49.4 8.3 %collective-permute-done.16.prompts_ref = s32[2]{0:T(128)S(1)} collective-permute-done((s32[2]{0:T(128)S(1)}, s32[2]{0:T(128)S(1)}, u32[]{:S(2)}, u32[]{:S(2)}) %collective-permute-start.16) | collective-permute-done | bytes 40 | tf_op jit(solution)/shard_map/ppermute | solution.py:551
  57.6 4.4 %collective-permute-start.17 = (bf16[384,1280]{1,0:T(8,128)(2,1)S(1)}, bf16[384,1280]{1,0:T(8,128)(2,1)S(1)}, u32[]{:S(2)}, u32[]{:S(2)}) collective-permute-start(bf16[384,1280]{1,0:T(8,128)(2,1)S(1)} %constant_dynamic-slice_fusion), channel_id=1, source_target_pairs={{0,4},{12,8},{1,5},{13,9},{2,6},{14,10},{3,7},{15,11},{16,20},{28,... | collective-permute-start | bytes 2949128 | tf_op jit(solution)/shard_map/ppermute | solution.py:551
  62.1 1.3 stacked.1.rest_2_
  63.4 0.7 collective-permute-start.14
  64.1 0.6 collective-permute-start.1
  64.8 17.5 %collective-permute-done.17.refs_4_.refs_3_ = bf16[384,1280]{1,0:T(8,128)(2,1)S(1)} collective-permute-done((bf16[384,1280]{1,0:T(8,128)(2,1)S(1)}, bf16[384,1280]{1,0:T(8,128)(2,1)S(1)}, u32[]{:S(2)}, u32[]{:S(2)}) %collective-permute-start.17) | collective-permute-done | bytes 983072 | tf_op jit(solution)/shard_map/ppermute | solution.py:551
  82.2 4.4 %collective-permute-start.18 = (bf16[4,64,1792]{2,1,0:T(8,128)(2,1)S(1)}, bf16[4,64,1792]{2,1,0:T(8,128)(2,1)S(1)}, u32[]{:S(2)}, u32[]{:S(2)}) collective-permute-start(bf16[4,64,1792]{2,1,0:T(8,128)(2,1)S(1)} %pad_maximum_fusion), channel_id=1, source_target_pairs={{0,4},{12,8},{1,5},{13,9},{2,6},{14,10},{3,7},{15,11},{16,20},{28,... | collective-permute-start | bytes 2752520 | tf_op jit(solution)/shard_map/ppermute | solution.py:551
  86.7 0.6 collective-permute-start.19
  87.3 5.2 %attend.2.refs_0_ = bf16[4,64,1280]{2,1,0:T(8,128)(2,1)S(1)} custom-call(s32[3]{0:T(128)S(1)} %copy-done.10, s32[2]{0:T(128)S(1)} %copy-done.13, s32[4]{0:T(128)S(1)} %copy-done.11, s32[4]{0:T(128)S(1)} %copy-done.12, bf16[4,64,1280]{2,1,0:T(8,128)(2,1)S(1)} %copy-done.1, bf16[4,64,512]{2,1,0:T(8,128)(2,1)S(1)} %copy-done.2, bf16[448,512]{1,0:T(8,128)(2,1)} %added.6.rest_0_, ...), custom_call_target="tpu_custom_call" | custom-call | flops 64 | bytes 64 | tf_op jit(solution)/shard_map/attend/pallas_call | solution.py:323
  92.5 0.7 collective-permute-start.15
  93.2 11.3 %collective-permute-done.18.query_hbm.new_hbm = bf16[4,64,1792]{2,1,0:T(8,128)(2,1)S(1)} collective-permute-done((bf16[4,64,1792]{2,1,0:T(8,128)(2,1)S(1)}, bf16[4,64,1792]{2,1,0:T(8,128)(2,1)S(1)}, u32[]{:S(2)}, u32[]{:S(2)}) %collective-permute-start.18) | collective-permute-done | bytes 917536 | tf_op jit(solution)/shard_map/ppermute | solution.py:551
  104.5 6.9 %attend.3.refs_1_ = bf16[4,64,1280]{2,1,0:T(8,128)(2,1)S(1)} custom-call(s32[3]{0:T(128)S(1)} %copy-done.10, s32[2]{0:T(128)S(1)} %collective-permute-done.16.prompts_ref, s32[4]{0:T(128)S(1)} %copy-done.11, s32[4]{0:T(128)S(1)} %copy-done.12, bf16[4,64,1792]{2,1,0:T(8,128)(2,1)S(1)} %collective-permute-done.18.query_hbm.new_hbm, ...), custom_call_target="tpu_custom_call" | custom-call | flops 64 | bytes 64 | tf_op jit(solution)/shard_map/attend/pallas_call | solution.py:323
  111.4 1.0 collective-permute-start.21
  112.4 5.1 %spread.3 = (bf16[4,128,1280]{2,1,0:T(8,128)(2,1)S(1)}, bf16[4,64,1280]{2,1,0:T(8,128)(2,1)S(1)}, bf16[4,64,1280]{2,1,0:T(8,128)(2,1)S(1)}) custom-call(s32[3]{0:T(128)S(1)} %copy-done.10, bf16[4,64,1280]{2,1,0:T(8,128)(2,1)S(1)} %collective-permute-done.15.refs_0_, bf16[4,64,1280]{2,1,0:T(8,128)(2,1)S(1)} %attend.3.refs_1_, bf16[1280,1280]{1,0:T(8,128)(2,1)S(1)} %copy-done, ...), custom_call_target="tpu_custom_call" | custom-call | flops 64 | bytes 64 | tf_op jit(solution)/shard_map/spread/pallas_call | solution.py:383
  117.7 0.5 collective-permute-start.23
  118.2 4.1 %spread.4 = (bf16[4,64,1280]{2,1,0:T(8,128)(2,1)}, bf16[4,64,1280]{2,1,0:T(8,128)(2,1)S(1)}) custom-call(s32[3]{0:T(128)S(1)} %copy-done.10, bf16[4,64,1280]{2,1,0:T(8,128)(2,1)S(1)} %attend.2.refs_0_, bf16[1280,1280]{1,0:T(8,128)(2,1)S(1)} %copy-done, bf16[256,1280]{1,0:T(8,128)(2,1)} %collective-permute-done.refs_3_.refs_2_, ...), custom_call_target="tpu_custom_call" | custom-call | flops 64 | bytes 64 | tf_op jit(solution)/shard_map/spread/pallas_call | solution.py:383
  122.2 0.1 collective-permute-start.24
  122.3 0.7 added_half.3
  123.0 1.6 collective-permute-start.26
  124.6 3.2 %spread.5 = (bf16[4,64,1280]{2,1,0:T(8,128)(2,1)S(1)}, bf16[4,64,1280]{2,1,0:T(8,128)(2,1)S(1)}) custom-call(s32[3]{0:T(128)S(1)} %copy-done.10, bf16[4,64,1280]{2,1,0:T(8,128)(2,1)S(1)} %collective-permute-done.21.refs_0_, bf16[1280,1280]{1,0:T(8,128)(2,1)S(1)} %copy-done, bf16[256,1280]{1,0:T(8,128)(2,1)} %collective-permute-done.refs_3_.refs_2_, ...), custom_call_target="tpu_custom_call" | custom-call | flops 64 | bytes 64 | tf_op jit(solution)/shard_map/spread/pallas_call | solution.py:383
  127.8 0.2 collective-permute-start.25
  128.1 0.3 collective-permute-start.20
  128.4 11.8 %collective-permute-done.26.refs_4_ = bf16[2,128,1280]{2,1,0:T(8,128)(2,1)S(1)} collective-permute-done((bf16[2,128,1280]{2,1,0:T(8,128)(2,1)S(1)}, bf16[2,128,1280]{2,1,0:T(8,128)(2,1)S(1)}, u32[]{:S(2)}, u32[]{:S(2)}) %collective-permute-start.26) | collective-permute-done | bytes 655392 | tf_op jit(solution)/shard_map/ppermute | solution.py:554
  140.2 0.6 added_half.4
  140.8 1.6 collective-permute-start.29
  142.4 1.3 added_pieces.1
  143.7 0.7 collective-permute-start.28
  144.4 1.0 added_halves.1
  145.4 0.7 collective-permute-start.32
  146.1 0.7 collective-permute-start.33
  146.8 4.2 %collective-permute-done.29.refs_3_ = bf16[2,64,1280]{2,1,0:T(8,128)(2,1)S(1)} collective-permute-done((bf16[2,64,1280]{2,1,0:T(8,128)(2,1)S(1)}, bf16[2,64,1280]{2,1,0:T(8,128)(2,1)S(1)}, u32[]{:S(2)}, u32[]{:S(2)}) %collective-permute-start.29) | collective-permute-done | bytes 327712 | tf_op jit(solution)/shard_map/ppermute | solution.py:554
  151.0 0.7 added_half.5
  151.7 1.3 collective-permute-start.35
  153.0 1.3 collective-permute-start.34
  154.4 0.7 collective-permute-start.30
  155.1 19.8 %collective-permute-done.35 = bf16[2,64,1280]{2,1,0:T(8,128)(2,1)} collective-permute-done((bf16[2,64,1280]{2,1,0:T(8,128)(2,1)S(1)}, bf16[2,64,1280]{2,1,0:T(8,128)(2,1)}, u32[]{:S(2)}, u32[]{:S(2)}) %collective-permute-start.35) | collective-permute-done | bytes 327712 | tf_op jit(solution)/shard_map/ppermute | solution.py:524
  174.9 1.2 select_select_fusion.1
  176.1 0.7 joined.1
  176.8 1.0 fusion
  (60 shorter events, 0.6 us)
Async XLA Ops:
  0.6 7.3 %copy-start = (bf16[1280,1280]{1,0:T(8,128)(2,1)S(1)}, bf16[1280,1280]{1,0:T(8,128)(2,1)}, u32[]{:S(2)}) copy-start(bf16[1280,1280]{1,0:T(8,128)(2,1)} %refs_1_.3) | copy-start | bytes 9830404
  0.6 12.5 %copy-start.9 = (s32[3]{0:T(128)S(1)}, s32[3]{0:T(128)}, u32[]{:S(2)}) copy-start(s32[3]{0:T(128)} %pad_add_fusion.here_ref.refs_0_) | copy-start | bytes 40
  7.3 8.6 %collective-permute-start.5 = (bf16[576,512]{1,0:T(8,128)(2,1)}, bf16[576,512]{1,0:T(8,128)(2,1)}, u32[]{:S(2)}, u32[]{:S(2)}) collective-permute-start(bf16[576,512]{1,0:T(8,128)(2,1)} %get-tuple-element.52), channel_id=1, source_target_pairs={{0,1},{1,0},{2,3},{3,2},{4,5},{5,4},{6,7},{7,6},{8,9},{9,8},{10,11... | collective-permute-start | bytes 1769480 | tf_op jit(solution)/shard_map/ppermute | solution.py:554
  7.4 5.7 %collective-permute-start.2 = (bf16[448,512]{1,0:T(8,128)(2,1)}, bf16[448,512]{1,0:T(8,128)(2,1)}, u32[]{:S(2)}, u32[]{:S(2)}) collective-permute-start(bf16[448,512]{1,0:T(8,128)(2,1)} %get-tuple-element.46), channel_id=1, source_target_pairs={{0,1},{1,0},{2,3},{3,2},{4,5},{5,4},{6,7},{7,6},{8,9},{9,8},{10,11... | collective-permute-start | bytes 1376264 | tf_op jit(solution)/shard_map/ppermute | solution.py:554
  7.9 8.0 %copy-start.5 = (bf16[576,512]{1,0:T(8,128)(2,1)S(1)}, bf16[576,512]{1,0:T(8,128)(2,1)}, u32[]{:S(2)}) copy-start(bf16[576,512]{1,0:T(8,128)(2,1)} %get-tuple-element.51.refs_1_) | copy-start | bytes 1769476
  8.8 23.1 %collective-permute-start = (bf16[256,1280]{1,0:T(8,128)(2,1)}, bf16[256,1280]{1,0:T(8,128)(2,1)}, u32[]{:S(2)}, u32[]{:S(2)}) collective-permute-start(bf16[256,1280]{1,0:T(8,128)(2,1)} %constant_dynamic-slice_fusion.1), channel_id=1, source_target_pairs={{0,4},{12,8},{1,5},{13,9},{2,6},{14,10},{3,7},{15,11},{16,20},{28,... | collective-permute-start | bytes 1966088 | tf_op jit(solution)/shard_map/ppermute | solution.py:551
  13.1 1.0 copy-start.7
  15.3 9.2 %copy-start.6 = (bf16[448,512]{1,0:T(8,128)(2,1)}, bf16[448,512]{1,0:T(8,128)(2,1)S(1)}, u32[]{:S(2)}) copy-start(bf16[448,512]{1,0:T(8,128)(2,1)S(1)} %added.4) | copy-start | bytes 1376260
  15.4 12.4 %collective-permute-start.3 = (bf16[448,512]{1,0:T(8,128)(2,1)S(1)}, bf16[448,512]{1,0:T(8,128)(2,1)}, u32[]{:S(2)}, u32[]{:S(2)}) collective-permute-start(bf16[448,512]{1,0:T(8,128)(2,1)S(1)} %added.4), channel_id=1, source_target_pairs={{0,2},{2,0},{1,3},{3,1},{4,6},{6,4},{5,7},{7,5},{8,10},{10,8},{9,1... | collective-permute-start | bytes 1376264 | tf_op jit(solution)/shard_map/ppermute | solution.py:554
  17.2 0.8 copy-start.4
  18.0 9.7 %copy-start.10 = (s32[3]{0:T(128)S(1)}, s32[3]{0:T(128)}, u32[]{:S(2)}) copy-start(s32[3]{0:T(128)} %pad_add_fusion.here_ref.refs_0_) | copy-start | bytes 40
  24.5 4.3 %collective-permute-start.6 = (bf16[448,512]{1,0:T(8,128)(2,1)}, bf16[448,512]{1,0:T(8,128)(2,1)S(1)}, u32[]{:S(2)}, u32[]{:S(2)}) collective-permute-start(bf16[448,512]{1,0:T(8,128)(2,1)} %get-tuple-element.56), channel_id=1, source_target_pairs={{0,1},{1,0},{2,3},{3,2},{4,5},{5,4},{6,7},{7,6},{8,9},{9,8},{10,11... | collective-permute-start | bytes 1376264 | tf_op jit(solution)/shard_map/ppermute | solution.py:554
  24.6 16.0 %collective-permute-start.8 = (bf16[576,512]{1,0:T(8,128)(2,1)}, bf16[576,512]{1,0:T(8,128)(2,1)S(1)}, u32[]{:S(2)}, u32[]{:S(2)}) collective-permute-start(bf16[576,512]{1,0:T(8,128)(2,1)} %copy-done.4), channel_id=1, source_target_pairs={{0,2},{2,0},{1,3},{3,1},{4,6},{6,4},{5,7},{7,5},{8,10},{10,8},{9,1... | collective-permute-start | bytes 1769480 | tf_op jit(solution)/shard_map/ppermute | solution.py:554
  26.2 14.4 %collective-permute-start.7 = (bf16[576,512]{1,0:T(8,128)(2,1)}, bf16[576,512]{1,0:T(8,128)(2,1)S(1)}, u32[]{:S(2)}, u32[]{:S(2)}) collective-permute-start(bf16[576,512]{1,0:T(8,128)(2,1)} %get-tuple-element.58), channel_id=1, source_target_pairs={{0,1},{1,0},{2,3},{3,2},{4,5},{5,4},{6,7},{7,6},{8,9},{9,8},{10,11... | collective-permute-start | bytes 1769480 | tf_op jit(solution)/shard_map/ppermute | solution.py:554
  27.7 1.1 collective-permute-start.4
  28.9 1.0 copy-start.8
  31.9 14.6 %copy-start.13 = (s32[2]{0:T(128)S(1)}, s32[2]{0:T(128)}, u32[]{:S(2)}) copy-start(s32[2]{0:T(128)} %prompts_ref.1) | copy-start | bytes 28
  31.9 14.4 %collective-permute-start.9 = (bf16[448,512]{1,0:T(8,128)(2,1)}, bf16[448,512]{1,0:T(8,128)(2,1)}, u32[]{:S(2)}, u32[]{:S(2)}) collective-permute-start(bf16[448,512]{1,0:T(8,128)(2,1)} %added.6.rest_0_), channel_id=1, source_target_pairs={{0,4},{12,8},{1,5},{13,9},{2,6},{14,10},{3,7},{15,11},{16,20},{28,... | collective-permute-start | bytes 1376264 | tf_op jit(solution)/shard_map/ppermute | solution.py:551
  34.1 12.2 %collective-permute-start.11 = (bf16[448,512]{1,0:T(8,128)(2,1)}, bf16[448,512]{1,0:T(8,128)(2,1)}, u32[]{:S(2)}, u32[]{:S(2)}) collective-permute-start(bf16[448,512]{1,0:T(8,128)(2,1)} %added.6.rest_0_), channel_id=1, source_target_pairs={{4,8},{8,4},{5,9},{9,5},{6,10},{10,6},{7,11},{11,7},{20,24},{24,20... | collective-permute-start | bytes 1376264 | tf_op jit(solution)/shard_map/ppermute | solution.py:551
  40.6 1.1 copy-start.3
  43.2 21.5 %copy-start.2 = (bf16[4,64,512]{2,1,0:T(8,128)(2,1)S(1)}, bf16[4,64,512]{2,1,0:T(8,128)(2,1)}, u32[]{:S(2)}) copy-start(bf16[4,64,512]{2,1,0:T(8,128)(2,1)} %new_hbm.1) | copy-start | bytes 786436
  43.2 14.4 %collective-permute-start.10 = (bf16[576,512]{1,0:T(8,128)(2,1)}, bf16[576,512]{1,0:T(8,128)(2,1)}, u32[]{:S(2)}, u32[]{:S(2)}) collective-permute-start(bf16[576,512]{1,0:T(8,128)(2,1)} %added.7.rest_1_), channel_id=1, source_target_pairs={{0,4},{12,8},{1,5},{13,9},{2,6},{14,10},{3,7},{15,11},{16,20},{28,... | collective-permute-start | bytes 1769480 | tf_op jit(solution)/shard_map/ppermute | solution.py:551
  45.4 19.2 %copy-start.1 = (bf16[4,64,1280]{2,1,0:T(8,128)(2,1)S(1)}, bf16[4,64,1280]{2,1,0:T(8,128)(2,1)}, u32[]{:S(2)}) copy-start(bf16[4,64,1280]{2,1,0:T(8,128)(2,1)} %query_hbm) | copy-start | bytes 1966084
  45.4 17.9 %collective-permute-start.13 = (bf16[576,512]{1,0:T(8,128)(2,1)}, bf16[576,512]{1,0:T(8,128)(2,1)S(1)}, u32[]{:S(2)}, u32[]{:S(2)}) collective-permute-start(bf16[576,512]{1,0:T(8,128)(2,1)} %added.7.rest_1_), channel_id=1, source_target_pairs={{4,8},{8,4},{5,9},{9,5},{6,10},{10,6},{7,11},{11,7},{20,24},{24,20... | collective-permute-start | bytes 1769480 | tf_op jit(solution)/shard_map/ppermute | solution.py:551
  46.3 15.8 %collective-permute-start.12 = (bf16[448,512]{1,0:T(8,128)(2,1)}, bf16[448,512]{1,0:T(8,128)(2,1)S(1)}, u32[]{:S(2)}, u32[]{:S(2)}) collective-permute-start(bf16[448,512]{1,0:T(8,128)(2,1)} %copy-done.6), channel_id=1, source_target_pairs={{0,1},{1,0},{2,3},{3,2},{4,5},{5,4},{6,7},{7,6},{8,9},{9,8},{10,11... | collective-permute-start | bytes 1376264 | tf_op jit(solution)/shard_map/ppermute | solution.py:554
  46.5 40.8 %copy-start.11 = (s32[4]{0:T(128)S(1)}, s32[4]{0:T(128)}, u32[]{:S(2)}) copy-start(s32[4]{0:T(128)} %owners_ref.3) | copy-start | bytes 52
  46.5 40.8 %copy-start.12 = (s32[4]{0:T(128)S(1)}, s32[4]{0:T(128)}, u32[]{:S(2)}) copy-start(s32[4]{0:T(128)} %lengths_ref.3) | copy-start | bytes 52
  46.5 11.1 %collective-permute-start.16 = (s32[2]{0:T(128)S(1)}, s32[2]{0:T(128)S(1)}, u32[]{:S(2)}, u32[]{:S(2)}) collective-permute-start(s32[2]{0:T(128)S(1)} %copy-done.13), channel_id=1, source_target_pairs={{0,4},{12,8},{1,5},{13,9},{2,6},{14,10},{3,7},{15,11},{16,20},{28,... | collective-permute-start | bytes 32 | tf_op jit(solution)/shard_map/ppermute | solution.py:551
  57.6 24.6 %collective-permute-start.17 = (bf16[384,1280]{1,0:T(8,128)(2,1)S(1)}, bf16[384,1280]{1,0:T(8,128)(2,1)S(1)}, u32[]{:S(2)}, u32[]{:S(2)}) collective-permute-start(bf16[384,1280]{1,0:T(8,128)(2,1)S(1)} %constant_dynamic-slice_fusion), channel_id=1, source_target_pairs={{0,4},{12,8},{1,5},{13,9},{2,6},{14,10},{3,7},{15,11},{16,20},{28,... | collective-permute-start | bytes 2949128 | tf_op jit(solution)/shard_map/ppermute | solution.py:551
  63.4 23.9 %collective-permute-start.14 = (bf16[1024,512]{1,0:T(8,128)(2,1)S(1)}, bf16[1024,512]{1,0:T(8,128)(2,1)S(1)}, u32[]{:S(2)}, u32[]{:S(2)}) collective-permute-start(bf16[1024,512]{1,0:T(8,128)(2,1)S(1)} %stacked.1.rest_2_), channel_id=1, source_target_pairs={{4,8},{8,4},{5,9},{9,5},{6,10},{10,6},{7,11},{11,7},{20,24},{24,20... | collective-permute-start | bytes 3145736 | tf_op jit(solution)/shard_map/ppermute | solution.py:551
  64.1 23.1 %collective-permute-start.1 = (bf16[256,1280]{1,0:T(8,128)(2,1)}, bf16[256,1280]{1,0:T(8,128)(2,1)S(1)}, u32[]{:S(2)}, u32[]{:S(2)}) collective-permute-start(bf16[256,1280]{1,0:T(8,128)(2,1)} %collective-permute-done.refs_3_.refs_2_), channel_id=1, source_target_pairs={{0,16},{16,0},{1,17},{17,1},{2,18},{18,2},{3,19},{19,3},{4,20},{20... | collective-permute-start | bytes 1966088 | tf_op jit(solution)/shard_map/ppermute | solution.py:578
  82.2 22.3 %collective-permute-start.18 = (bf16[4,64,1792]{2,1,0:T(8,128)(2,1)S(1)}, bf16[4,64,1792]{2,1,0:T(8,128)(2,1)S(1)}, u32[]{:S(2)}, u32[]{:S(2)}) collective-permute-start(bf16[4,64,1792]{2,1,0:T(8,128)(2,1)S(1)} %pad_maximum_fusion), channel_id=1, source_target_pairs={{0,4},{12,8},{1,5},{13,9},{2,6},{14,10},{3,7},{15,11},{16,20},{28,... | collective-permute-start | bytes 2752520 | tf_op jit(solution)/shard_map/ppermute | solution.py:551
  86.7 25.7 %collective-permute-start.19 = (bf16[384,1280]{1,0:T(8,128)(2,1)S(1)}, bf16[384,1280]{1,0:T(8,128)(2,1)S(1)}, u32[]{:S(2)}, u32[]{:S(2)}) collective-permute-start(bf16[384,1280]{1,0:T(8,128)(2,1)S(1)} %collective-permute-done.17.refs_4_.refs_3_), channel_id=1, source_target_pairs={{0,16},{16,0},{1,17},{17,1},{2,18},{18,2},{3,19},{19,3},{4,20},{20... | collective-permute-start | bytes 2949128 | tf_op jit(solution)/shard_map/ppermute | solution.py:578
  92.5 19.9 %collective-permute-start.15 = (bf16[4,64,1280]{2,1,0:T(8,128)(2,1)S(1)}, bf16[4,64,1280]{2,1,0:T(8,128)(2,1)S(1)}, u32[]{:S(2)}, u32[]{:S(2)}) collective-permute-start(bf16[4,64,1280]{2,1,0:T(8,128)(2,1)S(1)} %attend.2.refs_0_), channel_id=1, source_target_pairs={{4,8},{8,4},{5,9},{9,5},{6,10},{10,6},{7,11},{11,7},{20,24},{24,20... | collective-permute-start | bytes 1966088 | tf_op jit(solution)/shard_map/ppermute | solution.py:551
  111.4 10.8 %collective-permute-start.21 = (bf16[4,64,1280]{2,1,0:T(8,128)(2,1)S(1)}, bf16[4,64,1280]{2,1,0:T(8,128)(2,1)S(1)}, u32[]{:S(2)}, u32[]{:S(2)}) collective-permute-start(bf16[4,64,1280]{2,1,0:T(8,128)(2,1)S(1)} %attend.3.refs_1_), channel_id=1, source_target_pairs={{4,8},{8,4},{5,9},{9,5},{6,10},{10,6},{7,11},{11,7},{20,24},{24,20... | collective-permute-start | bytes 1966088 | tf_op jit(solution)/shard_map/ppermute | solution.py:551
  117.6 4.7 %collective-permute-start.22 = (bf16[4,64,1280]{2,1,0:T(8,128)(2,1)S(1)}, bf16[4,64,1280]{2,1,0:T(8,128)(2,1)S(1)}, u32[]{:S(2)}, u32[]{:S(2)}) collective-permute-start(bf16[4,64,1280]{2,1,0:T(8,128)(2,1)S(1)} %get-tuple-element.72), channel_id=1, source_target_pairs={{0,1},{1,0},{2,3},{3,2},{4,5},{5,4},{6,7},{7,6},{8,9},{9,8},{10,11... | collective-permute-start | bytes 1966088 | tf_op jit(solution)/shard_map/ppermute | solution.py:554
  117.7 4.7 %collective-permute-start.23 = (bf16[4,64,1280]{2,1,0:T(8,128)(2,1)S(1)}, bf16[4,64,1280]{2,1,0:T(8,128)(2,1)S(1)}, u32[]{:S(2)}, u32[]{:S(2)}) collective-permute-start(bf16[4,64,1280]{2,1,0:T(8,128)(2,1)S(1)} %get-tuple-element.73), channel_id=1, source_target_pairs={{0,1},{1,0},{2,3},{3,2},{4,5},{5,4},{6,7},{7,6},{8,9},{9,8},{10,11... | collective-permute-start | bytes 1966088 | tf_op jit(solution)/shard_map/ppermute | solution.py:554
  122.2 2.4 %collective-permute-start.24 = (bf16[4,64,1280]{2,1,0:T(8,128)(2,1)}, bf16[4,64,1280]{2,1,0:T(8,128)(2,1)S(1)}, u32[]{:S(2)}, u32[]{:S(2)}) collective-permute-start(bf16[4,64,1280]{2,1,0:T(8,128)(2,1)} %get-tuple-element.84.refs_1_), channel_id=1, source_target_pairs={{0,1},{1,0},{2,3},{3,2},{4,5},{5,4},{6,7},{7,6},{8,9},{9,8},{10,11... | collective-permute-start | bytes 1966088 | tf_op jit(solution)/shard_map/ppermute | solution.py:554
  123.0 17.1 %collective-permute-start.26 = (bf16[2,128,1280]{2,1,0:T(8,128)(2,1)S(1)}, bf16[2,128,1280]{2,1,0:T(8,128)(2,1)S(1)}, u32[]{:S(2)}, u32[]{:S(2)}) collective-permute-start(bf16[2,128,1280]{2,1,0:T(8,128)(2,1)S(1)} %added_half.3), channel_id=1, source_target_pairs={{0,2},{2,0},{1,3},{3,1},{4,6},{6,4},{5,7},{7,5},{8,10},{10,8},{9,1... | collective-permute-start | bytes 1966088 | tf_op jit(solution)/shard_map/ppermute | solution.py:554
  127.8 12.4 %collective-permute-start.25 = (bf16[4,64,1280]{2,1,0:T(8,128)(2,1)S(1)}, bf16[4,64,1280]{2,1,0:T(8,128)(2,1)S(1)}, u32[]{:S(2)}, u32[]{:S(2)}) collective-permute-start(bf16[4,64,1280]{2,1,0:T(8,128)(2,1)S(1)} %get-tuple-element.77), channel_id=1, source_target_pairs={{0,1},{1,0},{2,3},{3,2},{4,5},{5,4},{6,7},{7,6},{8,9},{9,8},{10,11... | collective-permute-start | bytes 1966088 | tf_op jit(solution)/shard_map/ppermute | solution.py:554
  128.1 14.3 %collective-permute-start.20 = (bf16[4,64,1280]{2,1,0:T(8,128)(2,1)S(1)}, bf16[4,64,1280]{2,1,0:T(8,128)(2,1)S(1)}, u32[]{:S(2)}, u32[]{:S(2)}) collective-permute-start(bf16[4,64,1280]{2,1,0:T(8,128)(2,1)S(1)} %get-tuple-element.71), channel_id=1, source_target_pairs={{0,1},{1,0},{2,3},{3,2},{4,5},{5,4},{6,7},{7,6},{8,9},{9,8},{10,11... | collective-permute-start | bytes 1966088 | tf_op jit(solution)/shard_map/ppermute | solution.py:554
  140.2 2.2 %collective-permute-start.27 = (bf16[4,64,1280]{2,1,0:T(8,128)(2,1)S(1)}, bf16[4,64,1280]{2,1,0:T(8,128)(2,1)S(1)}, u32[]{:S(2)}, u32[]{:S(2)}) collective-permute-start(bf16[4,64,1280]{2,1,0:T(8,128)(2,1)S(1)} %attend.2.refs_0_), channel_id=1, source_target_pairs={{0,1},{1,0},{2,3},{3,2},{4,5},{5,4},{6,7},{7,6},{8,9},{9,8},{10,11... | collective-permute-start | bytes 1966088 | tf_op jit(solution)/shard_map/ppermute | solution.py:554
  140.8 10.2 %collective-permute-start.29 = (bf16[2,64,1280]{2,1,0:T(8,128)(2,1)S(1)}, bf16[2,64,1280]{2,1,0:T(8,128)(2,1)S(1)}, u32[]{:S(2)}, u32[]{:S(2)}) collective-permute-start(bf16[2,64,1280]{2,1,0:T(8,128)(2,1)S(1)} %added_half.4), channel_id=1, source_target_pairs={{0,2},{2,0},{1,3},{3,1},{4,6},{6,4},{5,7},{7,5},{8,10},{10,8},{9,1... | collective-permute-start | bytes 983048 | tf_op jit(solution)/shard_map/ppermute | solution.py:554
  143.7 10.6 %collective-permute-start.28 = (bf16[4,32,1280]{2,1,0:T(8,128)(2,1)S(1)}, bf16[4,32,1280]{2,1,0:T(8,128)(2,1)S(1)}, u32[]{:S(2)}, u32[]{:S(2)}) collective-permute-start(bf16[4,32,1280]{2,1,0:T(8,128)(2,1)S(1)} %get-tuple-element.82.refs_1_), channel_id=1, source_target_pairs={{6,4},{7,5},{8,10},{9,11},{22,20},{23,21},{24,26},{25,27}} | collective-permute-start | bytes 983048 | tf_op jit(solution)/shard_map/ppermute | solution.py:533
  145.4 9.0 %collective-permute-start.32 = (bf16[2,64,1280]{2,1,0:T(8,128)(2,1)S(1)}, bf16[2,64,1280]{2,1,0:T(8,128)(2,1)S(1)}, u32[]{:S(2)}, u32[]{:S(2)}) collective-permute-start(bf16[2,64,1280]{2,1,0:T(8,128)(2,1)S(1)} %get-tuple-element.85), channel_id=1, source_target_pairs={{4,8},{5,9},{10,6},{11,7},{6,0},{7,1},{8,14},{9,15},{20,24},{21,25... | collective-permute-start | bytes 983048 | tf_op jit(solution)/shard_map/ppermute | solution.py:524
  146.1 9.0 %collective-permute-start.33 = (bf16[2,64,1280]{2,1,0:T(8,128)(2,1)S(1)}, bf16[2,64,1280]{2,1,0:T(8,128)(2,1)S(1)}, u32[]{:S(2)}, u32[]{:S(2)}) collective-permute-start(bf16[2,64,1280]{2,1,0:T(8,128)(2,1)S(1)} %get-tuple-element.86), channel_id=1, source_target_pairs={{6,8},{7,9},{8,6},{9,7},{4,0},{5,1},{10,14},{11,15},{22,24},{23,25... | collective-permute-start | bytes 983048 | tf_op jit(solution)/shard_map/ppermute | solution.py:524
  151.7 23.2 %collective-permute-start.35 = (bf16[2,64,1280]{2,1,0:T(8,128)(2,1)S(1)}, bf16[2,64,1280]{2,1,0:T(8,128)(2,1)}, u32[]{:S(2)}, u32[]{:S(2)}) collective-permute-start(bf16[2,64,1280]{2,1,0:T(8,128)(2,1)S(1)} %added_half.5), channel_id=1, source_target_pairs={{6,12},{7,13},{8,2},{9,3},{22,28},{23,29},{24,18},{25,19}} | collective-permute-start | bytes 983048 | tf_op jit(solution)/shard_map/ppermute | solution.py:524
  153.0 21.9 %collective-permute-start.34 = (bf16[2,64,1280]{2,1,0:T(8,128)(2,1)S(1)}, bf16[2,64,1280]{2,1,0:T(8,128)(2,1)}, u32[]{:S(2)}, u32[]{:S(2)}) collective-permute-start(bf16[2,64,1280]{2,1,0:T(8,128)(2,1)S(1)} %added_half.5), channel_id=1, source_target_pairs={{4,12},{5,13},{10,2},{11,3},{20,28},{21,29},{26,18},{27,19}} | collective-permute-start | bytes 983048 | tf_op jit(solution)/shard_map/ppermute | solution.py:524
  154.3 21.8 %collective-permute-start.31 = (bf16[4,64,1280]{2,1,0:T(8,128)(2,1)}, bf16[4,64,1280]{2,1,0:T(8,128)(2,1)S(1)}, u32[]{:S(2)}, u32[]{:S(2)}) collective-permute-start(bf16[4,64,1280]{2,1,0:T(8,128)(2,1)} %get-tuple-element.84.refs_1_), channel_id=1, source_target_pairs={{0,1},{1,0},{2,3},{3,2},{4,5},{5,4},{6,7},{7,6},{8,9},{9,8},{10,11... | collective-permute-start | bytes 1966088 | tf_op jit(solution)/shard_map/ppermute | solution.py:554
  154.4 21.6 %collective-permute-start.30 = (bf16[4,32,1280]{2,1,0:T(8,128)(2,1)S(1)}, bf16[4,32,1280]{2,1,0:T(8,128)(2,1)S(1)}, u32[]{:S(2)}, u32[]{:S(2)}) collective-permute-start(bf16[4,32,1280]{2,1,0:T(8,128)(2,1)S(1)} %get-tuple-element.83.refs_2_), channel_id=1, source_target_pairs={{6,4},{7,5},{8,10},{9,11},{22,20},{23,21},{24,26},{25,27}} | collective-permute-start | bytes 983048 | tf_op jit(solution)/shard_map/ppermute | solution.py:533

commit v7 on v6

--- a/solution.py
+++ b/solution.py
@@ -423,30 +423,45 @@
     return run_small(body, "added", here, parts, parts[0].shape, limit=limit)[0]
 
 
-def added_pieces(here, one, two, pieces, waits_for):
-    steps, rows, columns = one.shape
-    piece = rows // pieces
-
-    def body(_, one_ref, two_ref, *outs):
+def added_pieces(here, one, two, cuts, waits_for):
+    steps, _, columns = one.shape
+    places = [slice(low, high) for low, high in zip(cuts[:-1], cuts[1:])]
+
+    def body(_, one_ref, two_ref, *refs):
+        outs = refs[len(waits_for) :]
         total = one_ref[...].astype(jnp.float32) + two_ref[...].astype(jnp.float32)
         total = total.astype(jnp.bfloat16)
-        for at, out in enumerate(outs):
-            out[...] = total[:, at * piece : (at + 1) * piece]
-
-    shape = (steps, piece, columns)
-    return run_small(body, "added_pieces", here, (one, two), shape, pieces, waits_for=waits_for)
+        for place, out in zip(places, outs):
+            out[...] = total[:, place]
+
+    in_vmem = pl.BlockSpec(memory_space=pltpu.VMEM)
+    return pl.pallas_call(
+        body,
+        in_specs=[pl.BlockSpec(memory_space=pltpu.SMEM)]
+        + [in_vmem] * 2
+        + [pl.BlockSpec(memory_space=pltpu.HBM)] * len(waits_for),
+        out_specs=[in_vmem] * len(places),
+        out_shape=[
+            jax.ShapeDtypeStruct((steps, place.stop - place.start, columns), jnp.bfloat16)
+            for place in places
+        ],
+        compiler_params=compiler_params(),
+        cost_estimate=small_cost(),
+        name="added_pieces",
+    )(here, one, two, *waits_for)
 
 
 def joined(here, ones, twos, waits_for):
-    steps, piece, columns = ones[0].shape
+    steps, _, columns = ones[0].shape
     count = len(ones)
+    ends = [sum(one.shape[1] for one in ones[:at]) for at in range(count + 1)]
 
     def body(_, *refs):
         for at in range(count):
             total = refs[at][...].astype(jnp.float32) + refs[count + at][...].astype(jnp.float32)
-            refs[-1][:, at * piece : (at + 1) * piece] = total.astype(jnp.bfloat16)
-
-    shape = (steps, count * piece, columns)
+            refs[-1][:, ends[at] : ends[at + 1]] = total.astype(jnp.bfloat16)
+
+    shape = (steps, ends[-1], columns)
     return run_small(body, "joined", here, (*ones, *twos), shape, waits_for=waits_for)[0]
 
 
@@ -642,7 +657,7 @@
         here,
         own_keep,
         after(own_arrived[0], beyond_leaving),
-        2,
+        (0, own_rows.shape[1] * 3 // 4, own_rows.shape[1]),
         waits_for=(beside(own_rows, both_crossed),),
     )
     own_crossed = [

time: 178 us -> 187 us (1.051)
  waiting for transfers between devices: 80.4 us -> 86.8 us
  starting transfers between devices: 39.1 us -> 44 us
  Pallas kernels: 50.1 us -> 47.4 us
    ppermute x11, starting transfers between devices: 25.2 us -> 30.8 us  [on_samp(): return lax.ppermute(value, 'samp', pairs)]
    ppermute x4, waiting for transfers between devices: 19.8 us -> 23.6 us  [sent_home(): lax.ppermute(value, ('samp', 'head'), [pair for part in pairs for pair in...]
    ppermute x17, waiting for transfers between devices: 23.6 us -> 26.7 us  [on_head(): return lax.ppermute(value, 'head', pairs)]
    pallas_call x2, Pallas kernels: 12.1 us -> 9.89 us  [attend(): pl.pallas_call(body, in_specs=[in_smem] * 4 + [in_hbm] * (2 + len(page_pa...]
    pallas_call x11 -> x10, Pallas kernels: 12.3 us -> 10.8 us  [run_small(): pl.pallas_call(whole, in_specs=[pl.BlockSpec(memory_space=pltpu.SMEM)] +...]
    unnamed x28 -> x26, local copies, waits for them, and re-layouts: 3.96 us -> 3.35 us
  transfers between devices with their start and end apart: 36 -> 36, of which waited for: 9 -> 12; matrix products, arithmetic and copies ran while one was open for 1% -> 1% of each run, Pallas kernels for 24% -> 21%
where the time goes in v7:
time: 187 us; the launch traced here: 185 us
  waiting for transfers between devices  86.8 us (46%)
  Pallas kernels  47.4 us (25%)
  starting transfers between devices  44 us (24%)
  local copies, waits for them, and re-layouts  3.47 us (2%)
  other arithmetic  2.78 us (1%)
    ppermute x11, waiting for transfers between devices, on_samp(): return lax.ppermute(value, 'samp', pairs)  36.5 us
    ppermute x11, starting transfers between devices, on_samp(): return lax.ppermute(value, 'samp', pairs)  30.8 us
    ppermute x17, waiting for transfers between devices, on_head(): return lax.ppermute(value, 'head', pairs)  26.7 us
    ppermute x4, waiting for transfers between devices, sent_home(): lax.ppermute(value, ('samp', 'head'), [pair for part in pairs for pair in...  23.6 us
    pallas_call x2, Pallas kernels, project(): pl.pallas_call(body, in_specs=[pl.BlockSpec(memory_space=pltpu.SMEM), in_...  13 us
    pallas_call x3, Pallas kernels, spread(): pl.pallas_call(body, in_specs=[pl.BlockSpec(memory_space=pltpu.SMEM)] + [...  12.5 us
    pallas_call x10, Pallas kernels, run_small(): pl.pallas_call(whole, in_specs=[pl.BlockSpec(memory_space=pltpu.SMEM)] +...  10.8 us
    pallas_call x2, Pallas kernels, attend(): pl.pallas_call(body, in_specs=[in_smem] * 4 + [in_hbm] * (2 + len(page_pa...  9.89 us
  transfers between devices with their start and end apart: 36, of which 12 were waited for; matrix products, arithmetic and copies ran while one was open for 1% of the time, Pallas kernels for 21%

profile of v7, /device:TPU:6, one launch (start us, length us, event | category | flops | bytes accessed | tf_op | source)
XLA Modules:
  0.0 184.9 jit_solution(2152887359422554033)
XLA Ops:
  0.0 0.6 pad_add_fusion.here_ref.refs_0_._
  0.6 6.5 %project.2 = (bf16[448,512]{1,0:T(8,128)(2,1)}, bf16[576,512]{1,0:T(8,128)(2,1)}, bf16[448,512]{1,0:T(8,128)(2,1)}, bf16[576,512]{1,0:T(8,128)(2,1)}) custom-call(s32[3]{0:T(128)} %pad_add_fusion.here_ref.refs_0_._, bf16[1024,1280]{1,0:T(8,128)(2,1)} %bitcast.4, bf16[1280,2048]{1,0:T(8,128)(2,1)} %weight_hbm.3), custom_call_target="tpu_custom_call" | custom-call | flops 64 | bytes 64 | tf_op jit(solution)/shard_map/project/pallas_call | solution.py:190
  7.2 0.5 collective-permute-start.2
  7.7 2.4 %collective-permute-done.2.refs_2_ = bf16[448,512]{1,0:T(8,128)(2,1)S(1)} collective-permute-done((bf16[448,512]{1,0:T(8,128)(2,1)}, bf16[448,512]{1,0:T(8,128)(2,1)S(1)}, u32[]{:S(2)}, u32[]{:S(2)}) %collective-permute-start.2) | collective-permute-done | bytes 458784 | tf_op jit(solution)/shard_map/ppermute | solution.py:569
  10.0 1.0 copy-done.6
  11.0 0.6 added.4
  11.7 1.2 copy-done.4
  12.9 1.5 added.5
  14.5 0.5 collective-permute-start.8
  15.0 6.5 %project.3 = (bf16[448,512]{1,0:T(8,128)(2,1)}, bf16[576,512]{1,0:T(8,128)(2,1)}, bf16[448,512]{1,0:T(8,128)(2,1)}, bf16[576,512]{1,0:T(8,128)(2,1)}) custom-call(s32[3]{0:T(128)} %pad_add_fusion.here_ref.refs_0_._, bf16[1024,1280]{1,0:T(8,128)(2,1)} %bitcast.5, bf16[1280,2048]{1,0:T(8,128)(2,1)} %weight_hbm.3), custom_call_target="tpu_custom_call" | custom-call | flops 64 | bytes 64 | tf_op jit(solution)/shard_map/project/pallas_call | solution.py:190
  21.7 4.4 %collective-permute-start = (bf16[256,1280]{1,0:T(8,128)(2,1)S(1)}, bf16[256,1280]{1,0:T(8,128)(2,1)}, u32[]{:S(2)}, u32[]{:S(2)}) collective-permute-start(bf16[256,1280]{1,0:T(8,128)(2,1)S(1)} %constant_dynamic-slice_fusion.1), channel_id=1, source_target_pairs={{0,4},{12,8},{1,5},{13,9},{2,6},{14,10},{3,7},{15,11},{16,20},{28,... | collective-permute-start | bytes 1966088 | tf_op jit(solution)/shard_map/ppermute | solution.py:566
  26.0 1.4 collective-permute-start.3
  27.4 3.5 %collective-permute-done.8.refs_3_ = bf16[576,512]{1,0:T(8,128)(2,1)} collective-permute-done((bf16[576,512]{1,0:T(8,128)(2,1)}, bf16[576,512]{1,0:T(8,128)(2,1)}, u32[]{:S(2)}, u32[]{:S(2)}) %collective-permute-start.8) | collective-permute-done | bytes 589856 | tf_op jit(solution)/shard_map/ppermute | solution.py:569
  30.9 1.1 copy-done.3
  32.0 2.1 %added.7.rest_1_ = bf16[576,512]{1,0:T(8,128)(2,1)} custom-call(s32[3]{0:T(128)S(1)} %copy-done.9, bf16[576,512]{1,0:T(8,128)(2,1)S(1)} %copy-done.3, bf16[576,512]{1,0:T(8,128)(2,1)S(1)} %collective-permute-done.7.refs_2_, bf16[576,512]{1,0:T(8,128)(2,1)} %collective-permute-done.8.refs_3_), custom_call_target="tpu_custom_call" | custom-call | flops 64 | bytes 64 | tf_op jit(solution)/shard_map/added/pallas_call | solution.py:403
  34.2 4.3 %collective-permute-start.10 = (bf16[576,512]{1,0:T(8,128)(2,1)}, bf16[576,512]{1,0:T(8,128)(2,1)}, u32[]{:S(2)}, u32[]{:S(2)}) collective-permute-start(bf16[576,512]{1,0:T(8,128)(2,1)} %added.7.rest_1_), channel_id=1, source_target_pairs={{0,4},{12,8},{1,5},{13,9},{2,6},{14,10},{3,7},{15,11},{16,20},{28,... | collective-permute-start | bytes 1769480 | tf_op jit(solution)/shard_map/ppermute | solution.py:566
  38.5 1.4 collective-permute-done.3.refs_3_
  39.9 1.1 collective-permute-done.4.refs_0_
  41.0 1.5 added.6.rest_0_
  42.5 4.4 %collective-permute-start.9 = (bf16[448,512]{1,0:T(8,128)(2,1)}, bf16[448,512]{1,0:T(8,128)(2,1)}, u32[]{:S(2)}, u32[]{:S(2)}) collective-permute-start(bf16[448,512]{1,0:T(8,128)(2,1)} %added.6.rest_0_), channel_id=1, source_target_pairs={{0,4},{12,8},{1,5},{13,9},{2,6},{14,10},{3,7},{15,11},{16,20},{28,... | collective-permute-start | bytes 1376264 | tf_op jit(solution)/shard_map/ppermute | solution.py:566
  46.9 1.4 collective-permute-start.11
  48.3 0.8 collective-permute-start.13
  49.3 4.3 %collective-permute-start.16 = (s32[2]{0:T(128)S(1)}, s32[2]{0:T(128)S(1)}, u32[]{:S(2)}, u32[]{:S(2)}) collective-permute-start(s32[2]{0:T(128)S(1)} %copy-done.12), channel_id=1, source_target_pairs={{0,4},{12,8},{1,5},{13,9},{2,6},{14,10},{3,7},{15,11},{16,20},{28,... | collective-permute-start | bytes 32 | tf_op jit(solution)/shard_map/ppermute | solution.py:566
  53.5 8.9 %collective-permute-done.16.prompts_ref = s32[2]{0:T(128)S(1)} collective-permute-done((s32[2]{0:T(128)S(1)}, s32[2]{0:T(128)S(1)}, u32[]{:S(2)}, u32[]{:S(2)}) %collective-permute-start.16) | collective-permute-done | bytes 40 | tf_op jit(solution)/shard_map/ppermute | solution.py:566
  62.4 4.4 %collective-permute-start.17 = (bf16[384,1280]{1,0:T(8,128)(2,1)S(1)}, bf16[384,1280]{1,0:T(8,128)(2,1)S(1)}, u32[]{:S(2)}, u32[]{:S(2)}) collective-permute-start(bf16[384,1280]{1,0:T(8,128)(2,1)S(1)} %constant_dynamic-slice_fusion), channel_id=1, source_target_pairs={{0,4},{12,8},{1,5},{13,9},{2,6},{14,10},{3,7},{15,11},{16,20},{28,... | collective-permute-start | bytes 2949128 | tf_op jit(solution)/shard_map/ppermute | solution.py:566
  66.9 2.0 %collective-permute-done.12.refs_3_ = bf16[448,512]{1,0:T(8,128)(2,1)S(1)} collective-permute-done((bf16[448,512]{1,0:T(8,128)(2,1)}, bf16[448,512]{1,0:T(8,128)(2,1)S(1)}, u32[]{:S(2)}, u32[]{:S(2)}) %collective-permute-start.12) | collective-permute-done | bytes 458784 | tf_op jit(solution)/shard_map/ppermute | solution.py:569
  68.9 1.3 stacked.1.rest_2_
  70.2 0.7 collective-permute-start.14
  71.0 0.6 collective-permute-start.1
  71.5 16.1 %collective-permute-done.17.refs_4_.refs_3_ = bf16[384,1280]{1,0:T(8,128)(2,1)S(1)} collective-permute-done((bf16[384,1280]{1,0:T(8,128)(2,1)S(1)}, bf16[384,1280]{1,0:T(8,128)(2,1)S(1)}, u32[]{:S(2)}, u32[]{:S(2)}) %collective-permute-start.17) | collective-permute-done | bytes 983072 | tf_op jit(solution)/shard_map/ppermute | solution.py:566
  87.6 0.5 collective-permute-start.19
  88.2 4.4 %collective-permute-start.18 = (bf16[4,64,1792]{2,1,0:T(8,128)(2,1)S(1)}, bf16[4,64,1792]{2,1,0:T(8,128)(2,1)S(1)}, u32[]{:S(2)}, u32[]{:S(2)}) collective-permute-start(bf16[4,64,1792]{2,1,0:T(8,128)(2,1)S(1)} %pad_maximum_fusion), channel_id=1, source_target_pairs={{0,4},{12,8},{1,5},{13,9},{2,6},{14,10},{3,7},{15,11},{16,20},{28,... | collective-permute-start | bytes 2752520 | tf_op jit(solution)/shard_map/ppermute | solution.py:566
  92.7 5.9 %attend.2.refs_0_ = bf16[4,64,1280]{2,1,0:T(8,128)(2,1)S(1)} custom-call(s32[3]{0:T(128)S(1)} %copy-done.9, s32[2]{0:T(128)S(1)} %copy-done.12, s32[4]{0:T(128)S(1)} %copy-done.10, s32[4]{0:T(128)S(1)} %copy-done.11, bf16[4,64,1280]{2,1,0:T(8,128)(2,1)S(1)} %copy-done.1, bf16[4,64,512]{2,1,0:T(8,128)(2,1)S(1)} %copy-done.2, bf16[448,512]{1,0:T(8,128)(2,1)} %added.6.rest_0_, ...), custom_call_target="tpu_custom_call" | custom-call | flops 64 | bytes 64 | tf_op jit(solution)/shard_map/attend/pallas_call | solution.py:323
  98.6 0.7 collective-permute-start.15
  99.3 11.5 %collective-permute-done.18.query_hbm.new_hbm = bf16[4,64,1792]{2,1,0:T(8,128)(2,1)S(1)} collective-permute-done((bf16[4,64,1792]{2,1,0:T(8,128)(2,1)S(1)}, bf16[4,64,1792]{2,1,0:T(8,128)(2,1)S(1)}, u32[]{:S(2)}, u32[]{:S(2)}) %collective-permute-start.18) | collective-permute-done | bytes 917536 | tf_op jit(solution)/shard_map/ppermute | solution.py:566
  110.8 4.0 %attend.3.refs_1_ = bf16[4,64,1280]{2,1,0:T(8,128)(2,1)S(1)} custom-call(s32[3]{0:T(128)S(1)} %copy-done.9, s32[2]{0:T(128)S(1)} %collective-permute-done.16.prompts_ref, s32[4]{0:T(128)S(1)} %copy-done.10, s32[4]{0:T(128)S(1)} %copy-done.11, bf16[4,64,1792]{2,1,0:T(8,128)(2,1)S(1)} %collective-permute-done.18.query_hbm.new_hbm, ...), custom_call_target="tpu_custom_call" | custom-call | flops 64 | bytes 64 | tf_op jit(solution)/shard_map/attend/pallas_call | solution.py:323
  114.8 1.0 collective-permute-start.21
  115.8 5.1 %spread.3 = (bf16[4,128,1280]{2,1,0:T(8,128)(2,1)S(1)}, bf16[4,64,1280]{2,1,0:T(8,128)(2,1)S(1)}, bf16[4,64,1280]{2,1,0:T(8,128)(2,1)S(1)}) custom-call(s32[3]{0:T(128)S(1)} %copy-done.9, bf16[4,64,1280]{2,1,0:T(8,128)(2,1)S(1)} %collective-permute-done.15.refs_0_, bf16[4,64,1280]{2,1,0:T(8,128)(2,1)S(1)} %attend.3.refs_1_, bf16[1280,1280]{1,0:T(8,128)(2,1)S(1)} %copy-done, ...), custom_call_target="tpu_custom_call" | custom-call | flops 64 | bytes 64 | tf_op jit(solution)/shard_map/spread/pallas_call | solution.py:383
  121.0 0.5 collective-permute-start.23
  121.5 4.1 %spread.4 = (bf16[4,64,1280]{2,1,0:T(8,128)(2,1)}, bf16[4,64,1280]{2,1,0:T(8,128)(2,1)S(1)}) custom-call(s32[3]{0:T(128)S(1)} %copy-done.9, bf16[4,64,1280]{2,1,0:T(8,128)(2,1)S(1)} %attend.2.refs_0_, bf16[1280,1280]{1,0:T(8,128)(2,1)S(1)} %copy-done, bf16[256,1280]{1,0:T(8,128)(2,1)} %collective-permute-done.refs_3_.refs_2_, ...), custom_call_target="tpu_custom_call" | custom-call | flops 64 | bytes 64 | tf_op jit(solution)/shard_map/spread/pallas_call | solution.py:383
  125.6 0.1 collective-permute-start.24
  125.7 0.7 added_half.3
  126.4 1.4 collective-permute-start.26
  127.8 0.1 collective-permute-done.24.refs_6_
  127.9 3.2 %spread.5 = (bf16[4,64,1280]{2,1,0:T(8,128)(2,1)S(1)}, bf16[4,64,1280]{2,1,0:T(8,128)(2,1)S(1)}) custom-call(s32[3]{0:T(128)S(1)} %copy-done.9, bf16[4,64,1280]{2,1,0:T(8,128)(2,1)S(1)} %collective-permute-done.21.refs_0_, bf16[1280,1280]{1,0:T(8,128)(2,1)S(1)} %copy-done, bf16[256,1280]{1,0:T(8,128)(2,1)} %collective-permute-done.refs_3_.refs_2_, ...), custom_call_target="tpu_custom_call" | custom-call | flops 64 | bytes 64 | tf_op jit(solution)/shard_map/spread/pallas_call | solution.py:383
  131.2 0.2 collective-permute-start.25
  131.4 0.4 collective-permute-start.20
  131.7 11.8 %collective-permute-done.26.refs_4_ = bf16[2,128,1280]{2,1,0:T(8,128)(2,1)S(1)} collective-permute-done((bf16[2,128,1280]{2,1,0:T(8,128)(2,1)S(1)}, bf16[2,128,1280]{2,1,0:T(8,128)(2,1)S(1)}, u32[]{:S(2)}, u32[]{:S(2)}) %collective-permute-start.26) | collective-permute-done | bytes 655392 | tf_op jit(solution)/shard_map/ppermute | solution.py:569
  143.6 0.6 added_half.4
  144.2 1.4 collective-permute-start.29
  145.6 1.3 added_pieces.1
  147.0 0.7 collective-permute-start.28
  147.7 1.0 added_halves.1
  148.7 0.7 collective-permute-start.32
  149.4 0.7 collective-permute-start.33
  150.1 4.3 %collective-permute-done.29.refs_3_ = bf16[2,64,1280]{2,1,0:T(8,128)(2,1)S(1)} collective-permute-done((bf16[2,64,1280]{2,1,0:T(8,128)(2,1)S(1)}, bf16[2,64,1280]{2,1,0:T(8,128)(2,1)S(1)}, u32[]{:S(2)}, u32[]{:S(2)}) %collective-permute-start.29) | collective-permute-done | bytes 327712 | tf_op jit(solution)/shard_map/ppermute | solution.py:569
  154.4 0.7 added_half.5
  155.1 1.3 collective-permute-start.35
  156.4 1.3 collective-permute-start.34
  157.8 0.7 collective-permute-start.30
  158.5 23.6 %collective-permute-done.35 = bf16[2,64,1280]{2,1,0:T(8,128)(2,1)} collective-permute-done((bf16[2,64,1280]{2,1,0:T(8,128)(2,1)S(1)}, bf16[2,64,1280]{2,1,0:T(8,128)(2,1)}, u32[]{:S(2)}, u32[]{:S(2)}) %collective-permute-start.35) | collective-permute-done | bytes 327712 | tf_op jit(solution)/shard_map/ppermute | solution.py:539
  182.0 1.2 select_select_fusion.1
  183.2 0.7 joined.1
  183.9 1.0 fusion
  (58 shorter events, 0.7 us)
Async XLA Ops:
  0.6 9.4 %copy-start.8 = (s32[3]{0:T(128)S(1)}, s32[3]{0:T(128)}, u32[]{:S(2)}) copy-start(s32[3]{0:T(128)} %pad_add_fusion.here_ref.refs_0_._) | copy-start | bytes 40
  7.1 4.6 %collective-permute-start.5 = (bf16[576,512]{1,0:T(8,128)(2,1)}, bf16[576,512]{1,0:T(8,128)(2,1)S(1)}, u32[]{:S(2)}, u32[]{:S(2)}) collective-permute-start(bf16[576,512]{1,0:T(8,128)(2,1)} %get-tuple-element.52), channel_id=1, source_target_pairs={{0,1},{1,0},{2,3},{3,2},{4,5},{5,4},{6,7},{7,6},{8,9},{9,8},{10,11... | collective-permute-start | bytes 1769480 | tf_op jit(solution)/shard_map/ppermute | solution.py:569
  7.2 2.9 %collective-permute-start.2 = (bf16[448,512]{1,0:T(8,128)(2,1)}, bf16[448,512]{1,0:T(8,128)(2,1)S(1)}, u32[]{:S(2)}, u32[]{:S(2)}) collective-permute-start(bf16[448,512]{1,0:T(8,128)(2,1)} %get-tuple-element.46), channel_id=1, source_target_pairs={{0,1},{1,0},{2,3},{3,2},{4,5},{5,4},{6,7},{7,6},{8,9},{9,8},{10,11... | collective-permute-start | bytes 1376264 | tf_op jit(solution)/shard_map/ppermute | solution.py:569
  10.0 1.0 copy-start.6
  11.7 14.4 %copy-start.5 = (bf16[448,512]{1,0:T(8,128)(2,1)}, bf16[448,512]{1,0:T(8,128)(2,1)S(1)}, u32[]{:S(2)}) copy-start(bf16[448,512]{1,0:T(8,128)(2,1)S(1)} %added.4) | copy-start | bytes 1376260
  11.7 1.2 copy-start.4
  14.4 7.2 %copy-start = (bf16[1280,1280]{1,0:T(8,128)(2,1)S(1)}, bf16[1280,1280]{1,0:T(8,128)(2,1)}, u32[]{:S(2)}) copy-start(bf16[1280,1280]{1,0:T(8,128)(2,1)} %refs_1_.3) | copy-start | bytes 9830404
  14.4 16.5 %copy-start.9 = (s32[3]{0:T(128)S(1)}, s32[3]{0:T(128)}, u32[]{:S(2)}) copy-start(s32[3]{0:T(128)} %pad_add_fusion.here_ref.refs_0_._) | copy-start | bytes 40
  14.5 16.5 %collective-permute-start.8 = (bf16[576,512]{1,0:T(8,128)(2,1)}, bf16[576,512]{1,0:T(8,128)(2,1)}, u32[]{:S(2)}, u32[]{:S(2)}) collective-permute-start(bf16[576,512]{1,0:T(8,128)(2,1)} %added.5), channel_id=1, source_target_pairs={{0,2},{2,0},{1,3},{3,1},{4,6},{6,4},{5,7},{7,5},{8,10},{10,8},{9,1... | collective-permute-start | bytes 1769480 | tf_op jit(solution)/shard_map/ppermute | solution.py:569
  21.5 19.5 %copy-start.7 = (bf16[448,512]{1,0:T(8,128)(2,1)S(1)}, bf16[448,512]{1,0:T(8,128)(2,1)}, u32[]{:S(2)}) copy-start(bf16[448,512]{1,0:T(8,128)(2,1)} %get-tuple-element.55.refs_1_) | copy-start | bytes 1376260
  21.5 9.4 %collective-permute-start.7 = (bf16[576,512]{1,0:T(8,128)(2,1)}, bf16[576,512]{1,0:T(8,128)(2,1)S(1)}, u32[]{:S(2)}, u32[]{:S(2)}) collective-permute-start(bf16[576,512]{1,0:T(8,128)(2,1)} %get-tuple-element.58), channel_id=1, source_target_pairs={{0,1},{1,0},{2,3},{3,2},{4,5},{5,4},{6,7},{7,6},{8,9},{9,8},{10,11... | collective-permute-start | bytes 1769480 | tf_op jit(solution)/shard_map/ppermute | solution.py:569
  21.7 20.8 %collective-permute-start = (bf16[256,1280]{1,0:T(8,128)(2,1)S(1)}, bf16[256,1280]{1,0:T(8,128)(2,1)}, u32[]{:S(2)}, u32[]{:S(2)}) collective-permute-start(bf16[256,1280]{1,0:T(8,128)(2,1)S(1)} %constant_dynamic-slice_fusion.1), channel_id=1, source_target_pairs={{0,4},{12,8},{1,5},{13,9},{2,6},{14,10},{3,7},{15,11},{16,20},{28,... | collective-permute-start | bytes 1966088 | tf_op jit(solution)/shard_map/ppermute | solution.py:566
  26.0 13.8 %collective-permute-start.3 = (bf16[448,512]{1,0:T(8,128)(2,1)S(1)}, bf16[448,512]{1,0:T(8,128)(2,1)S(1)}, u32[]{:S(2)}, u32[]{:S(2)}) collective-permute-start(bf16[448,512]{1,0:T(8,128)(2,1)S(1)} %added.4), channel_id=1, source_target_pairs={{0,2},{2,0},{1,3},{3,1},{4,6},{6,4},{5,7},{7,5},{8,10},{10,8},{9,1... | collective-permute-start | bytes 1376264 | tf_op jit(solution)/shard_map/ppermute | solution.py:569
  27.4 13.6 %collective-permute-start.6 = (bf16[448,512]{1,0:T(8,128)(2,1)}, bf16[448,512]{1,0:T(8,128)(2,1)S(1)}, u32[]{:S(2)}, u32[]{:S(2)}) collective-permute-start(bf16[448,512]{1,0:T(8,128)(2,1)} %get-tuple-element.56), channel_id=1, source_target_pairs={{0,1},{1,0},{2,3},{3,2},{4,5},{5,4},{6,7},{7,6},{8,9},{9,8},{10,11... | collective-permute-start | bytes 1376264 | tf_op jit(solution)/shard_map/ppermute | solution.py:569
  30.9 1.1 copy-start.3
  32.0 17.2 %copy-start.12 = (s32[2]{0:T(128)S(1)}, s32[2]{0:T(128)}, u32[]{:S(2)}) copy-start(s32[2]{0:T(128)} %prompts_ref.1) | copy-start | bytes 28
  34.2 28.2 %collective-permute-start.10 = (bf16[576,512]{1,0:T(8,128)(2,1)}, bf16[576,512]{1,0:T(8,128)(2,1)}, u32[]{:S(2)}, u32[]{:S(2)}) collective-permute-start(bf16[576,512]{1,0:T(8,128)(2,1)} %added.7.rest_1_), channel_id=1, source_target_pairs={{0,4},{12,8},{1,5},{13,9},{2,6},{14,10},{3,7},{15,11},{16,20},{28,... | collective-permute-start | bytes 1769480 | tf_op jit(solution)/shard_map/ppermute | solution.py:566
  39.9 1.1 collective-permute-start.4
  42.5 45.6 %copy-start.2 = (bf16[4,64,512]{2,1,0:T(8,128)(2,1)S(1)}, bf16[4,64,512]{2,1,0:T(8,128)(2,1)}, u32[]{:S(2)}) copy-start(bf16[4,64,512]{2,1,0:T(8,128)(2,1)} %new_hbm.1) | copy-start | bytes 786436
  42.5 24.3 %collective-permute-start.9 = (bf16[448,512]{1,0:T(8,128)(2,1)}, bf16[448,512]{1,0:T(8,128)(2,1)}, u32[]{:S(2)}, u32[]{:S(2)}) collective-permute-start(bf16[448,512]{1,0:T(8,128)(2,1)} %added.6.rest_0_), channel_id=1, source_target_pairs={{0,4},{12,8},{1,5},{13,9},{2,6},{14,10},{3,7},{15,11},{16,20},{28,... | collective-permute-start | bytes 1376264 | tf_op jit(solution)/shard_map/ppermute | solution.py:566
  46.9 20.0 %collective-permute-start.11 = (bf16[448,512]{1,0:T(8,128)(2,1)}, bf16[448,512]{1,0:T(8,128)(2,1)}, u32[]{:S(2)}, u32[]{:S(2)}) collective-permute-start(bf16[448,512]{1,0:T(8,128)(2,1)} %added.6.rest_0_), channel_id=1, source_target_pairs={{4,8},{8,4},{5,9},{9,5},{6,10},{10,6},{7,11},{11,7},{20,24},{24,20... | collective-permute-start | bytes 1376264 | tf_op jit(solution)/shard_map/ppermute | solution.py:566
  48.3 39.8 %copy-start.1 = (bf16[4,64,1280]{2,1,0:T(8,128)(2,1)S(1)}, bf16[4,64,1280]{2,1,0:T(8,128)(2,1)}, u32[]{:S(2)}) copy-start(bf16[4,64,1280]{2,1,0:T(8,128)(2,1)} %query_hbm) | copy-start | bytes 1966084
  48.3 21.9 %collective-permute-start.13 = (bf16[576,512]{1,0:T(8,128)(2,1)}, bf16[576,512]{1,0:T(8,128)(2,1)S(1)}, u32[]{:S(2)}, u32[]{:S(2)}) collective-permute-start(bf16[576,512]{1,0:T(8,128)(2,1)} %added.7.rest_1_), channel_id=1, source_target_pairs={{4,8},{8,4},{5,9},{9,5},{6,10},{10,6},{7,11},{11,7},{20,24},{24,20... | collective-permute-start | bytes 1769480 | tf_op jit(solution)/shard_map/ppermute | solution.py:566
  49.2 43.4 %copy-start.10 = (s32[4]{0:T(128)S(1)}, s32[4]{0:T(128)}, u32[]{:S(2)}) copy-start(s32[4]{0:T(128)} %owners_ref.3) | copy-start | bytes 52
  49.2 43.4 %copy-start.11 = (s32[4]{0:T(128)S(1)}, s32[4]{0:T(128)}, u32[]{:S(2)}) copy-start(s32[4]{0:T(128)} %lengths_ref.3) | copy-start | bytes 52
  49.3 13.1 %collective-permute-start.16 = (s32[2]{0:T(128)S(1)}, s32[2]{0:T(128)S(1)}, u32[]{:S(2)}, u32[]{:S(2)}) collective-permute-start(s32[2]{0:T(128)S(1)} %copy-done.12), channel_id=1, source_target_pairs={{0,4},{12,8},{1,5},{13,9},{2,6},{14,10},{3,7},{15,11},{16,20},{28,... | collective-permute-start | bytes 32 | tf_op jit(solution)/shard_map/ppermute | solution.py:566
  62.4 25.2 %collective-permute-start.17 = (bf16[384,1280]{1,0:T(8,128)(2,1)S(1)}, bf16[384,1280]{1,0:T(8,128)(2,1)S(1)}, u32[]{:S(2)}, u32[]{:S(2)}) collective-permute-start(bf16[384,1280]{1,0:T(8,128)(2,1)S(1)} %constant_dynamic-slice_fusion), channel_id=1, source_target_pairs={{0,4},{12,8},{1,5},{13,9},{2,6},{14,10},{3,7},{15,11},{16,20},{28,... | collective-permute-start | bytes 2949128 | tf_op jit(solution)/shard_map/ppermute | solution.py:566
  66.8 2.1 %collective-permute-start.12 = (bf16[448,512]{1,0:T(8,128)(2,1)}, bf16[448,512]{1,0:T(8,128)(2,1)S(1)}, u32[]{:S(2)}, u32[]{:S(2)}) collective-permute-start(bf16[448,512]{1,0:T(8,128)(2,1)} %copy-done.5), channel_id=1, source_target_pairs={{0,1},{1,0},{2,3},{3,2},{4,5},{5,4},{6,7},{7,6},{8,9},{9,8},{10,11... | collective-permute-start | bytes 1376264 | tf_op jit(solution)/shard_map/ppermute | solution.py:569
  70.2 22.4 %collective-permute-start.14 = (bf16[1024,512]{1,0:T(8,128)(2,1)S(1)}, bf16[1024,512]{1,0:T(8,128)(2,1)S(1)}, u32[]{:S(2)}, u32[]{:S(2)}) collective-permute-start(bf16[1024,512]{1,0:T(8,128)(2,1)S(1)} %stacked.1.rest_2_), channel_id=1, source_target_pairs={{4,8},{8,4},{5,9},{9,5},{6,10},{10,6},{7,11},{11,7},{20,24},{24,20... | collective-permute-start | bytes 3145736 | tf_op jit(solution)/shard_map/ppermute | solution.py:566
  71.0 21.7 %collective-permute-start.1 = (bf16[256,1280]{1,0:T(8,128)(2,1)}, bf16[256,1280]{1,0:T(8,128)(2,1)S(1)}, u32[]{:S(2)}, u32[]{:S(2)}) collective-permute-start(bf16[256,1280]{1,0:T(8,128)(2,1)} %collective-permute-done.refs_3_.refs_2_), channel_id=1, source_target_pairs={{0,16},{16,0},{1,17},{17,1},{2,18},{18,2},{3,19},{19,3},{4,20},{20... | collective-permute-start | bytes 1966088 | tf_op jit(solution)/shard_map/ppermute | solution.py:593
  87.6 28.2 %collective-permute-start.19 = (bf16[384,1280]{1,0:T(8,128)(2,1)S(1)}, bf16[384,1280]{1,0:T(8,128)(2,1)S(1)}, u32[]{:S(2)}, u32[]{:S(2)}) collective-permute-start(bf16[384,1280]{1,0:T(8,128)(2,1)S(1)} %collective-permute-done.17.refs_4_.refs_3_), channel_id=1, source_target_pairs={{0,16},{16,0},{1,17},{17,1},{2,18},{18,2},{3,19},{19,3},{4,20},{20... | collective-permute-start | bytes 2949128 | tf_op jit(solution)/shard_map/ppermute | solution.py:593
  88.2 22.7 %collective-permute-start.18 = (bf16[4,64,1792]{2,1,0:T(8,128)(2,1)S(1)}, bf16[4,64,1792]{2,1,0:T(8,128)(2,1)S(1)}, u32[]{:S(2)}, u32[]{:S(2)}) collective-permute-start(bf16[4,64,1792]{2,1,0:T(8,128)(2,1)S(1)} %pad_maximum_fusion), channel_id=1, source_target_pairs={{0,4},{12,8},{1,5},{13,9},{2,6},{14,10},{3,7},{15,11},{16,20},{28,... | collective-permute-start | bytes 2752520 | tf_op jit(solution)/shard_map/ppermute | solution.py:566
  98.6 17.2 %collective-permute-start.15 = (bf16[4,64,1280]{2,1,0:T(8,128)(2,1)S(1)}, bf16[4,64,1280]{2,1,0:T(8,128)(2,1)S(1)}, u32[]{:S(2)}, u32[]{:S(2)}) collective-permute-start(bf16[4,64,1280]{2,1,0:T(8,128)(2,1)S(1)} %attend.2.refs_0_), channel_id=1, source_target_pairs={{4,8},{8,4},{5,9},{9,5},{6,10},{10,6},{7,11},{11,7},{20,24},{24,20... | collective-permute-start | bytes 1966088 | tf_op jit(solution)/shard_map/ppermute | solution.py:566
  114.8 10.8 %collective-permute-start.21 = (bf16[4,64,1280]{2,1,0:T(8,128)(2,1)S(1)}, bf16[4,64,1280]{2,1,0:T(8,128)(2,1)S(1)}, u32[]{:S(2)}, u32[]{:S(2)}) collective-permute-start(bf16[4,64,1280]{2,1,0:T(8,128)(2,1)S(1)} %attend.3.refs_1_), channel_id=1, source_target_pairs={{4,8},{8,4},{5,9},{9,5},{6,10},{10,6},{7,11},{11,7},{20,24},{24,20... | collective-permute-start | bytes 1966088 | tf_op jit(solution)/shard_map/ppermute | solution.py:566
  120.9 4.7 %collective-permute-start.22 = (bf16[4,64,1280]{2,1,0:T(8,128)(2,1)S(1)}, bf16[4,64,1280]{2,1,0:T(8,128)(2,1)S(1)}, u32[]{:S(2)}, u32[]{:S(2)}) collective-permute-start(bf16[4,64,1280]{2,1,0:T(8,128)(2,1)S(1)} %get-tuple-element.72), channel_id=1, source_target_pairs={{0,1},{1,0},{2,3},{3,2},{4,5},{5,4},{6,7},{7,6},{8,9},{9,8},{10,11... | collective-permute-start | bytes 1966088 | tf_op jit(solution)/shard_map/ppermute | solution.py:569
  121.0 4.7 %collective-permute-start.23 = (bf16[4,64,1280]{2,1,0:T(8,128)(2,1)S(1)}, bf16[4,64,1280]{2,1,0:T(8,128)(2,1)S(1)}, u32[]{:S(2)}, u32[]{:S(2)}) collective-permute-start(bf16[4,64,1280]{2,1,0:T(8,128)(2,1)S(1)} %get-tuple-element.73), channel_id=1, source_target_pairs={{0,1},{1,0},{2,3},{3,2},{4,5},{5,4},{6,7},{7,6},{8,9},{9,8},{10,11... | collective-permute-start | bytes 1966088 | tf_op jit(solution)/shard_map/ppermute | solution.py:569
  125.6 2.3 %collective-permute-start.24 = (bf16[4,64,1280]{2,1,0:T(8,128)(2,1)}, bf16[4,64,1280]{2,1,0:T(8,128)(2,1)S(1)}, u32[]{:S(2)}, u32[]{:S(2)}) collective-permute-start(bf16[4,64,1280]{2,1,0:T(8,128)(2,1)} %get-tuple-element.84.one_ref), channel_id=1, source_target_pairs={{0,1},{1,0},{2,3},{3,2},{4,5},{5,4},{6,7},{7,6},{8,9},{9,8},{10,11... | collective-permute-start | bytes 1966088 | tf_op jit(solution)/shard_map/ppermute | solution.py:569
  126.4 17.1 %collective-permute-start.26 = (bf16[2,128,1280]{2,1,0:T(8,128)(2,1)S(1)}, bf16[2,128,1280]{2,1,0:T(8,128)(2,1)S(1)}, u32[]{:S(2)}, u32[]{:S(2)}) collective-permute-start(bf16[2,128,1280]{2,1,0:T(8,128)(2,1)S(1)} %added_half.3), channel_id=1, source_target_pairs={{0,2},{2,0},{1,3},{3,1},{4,6},{6,4},{5,7},{7,5},{8,10},{10,8},{9,1... | collective-permute-start | bytes 1966088 | tf_op jit(solution)/shard_map/ppermute | solution.py:569
  131.2 12.4 %collective-permute-start.25 = (bf16[4,64,1280]{2,1,0:T(8,128)(2,1)S(1)}, bf16[4,64,1280]{2,1,0:T(8,128)(2,1)S(1)}, u32[]{:S(2)}, u32[]{:S(2)}) collective-permute-start(bf16[4,64,1280]{2,1,0:T(8,128)(2,1)S(1)} %get-tuple-element.77), channel_id=1, source_target_pairs={{0,1},{1,0},{2,3},{3,2},{4,5},{5,4},{6,7},{7,6},{8,9},{9,8},{10,11... | collective-permute-start | bytes 1966088 | tf_op jit(solution)/shard_map/ppermute | solution.py:569
  131.4 14.3 %collective-permute-start.20 = (bf16[4,64,1280]{2,1,0:T(8,128)(2,1)S(1)}, bf16[4,64,1280]{2,1,0:T(8,128)(2,1)S(1)}, u32[]{:S(2)}, u32[]{:S(2)}) collective-permute-start(bf16[4,64,1280]{2,1,0:T(8,128)(2,1)S(1)} %get-tuple-element.71), channel_id=1, source_target_pairs={{0,1},{1,0},{2,3},{3,2},{4,5},{5,4},{6,7},{7,6},{8,9},{9,8},{10,11... | collective-permute-start | bytes 1966088 | tf_op jit(solution)/shard_map/ppermute | solution.py:569
  143.6 2.1 %collective-permute-start.27 = (bf16[4,64,1280]{2,1,0:T(8,128)(2,1)S(1)}, bf16[4,64,1280]{2,1,0:T(8,128)(2,1)S(1)}, u32[]{:S(2)}, u32[]{:S(2)}) collective-permute-start(bf16[4,64,1280]{2,1,0:T(8,128)(2,1)S(1)} %attend.2.refs_0_), channel_id=1, source_target_pairs={{0,1},{1,0},{2,3},{3,2},{4,5},{5,4},{6,7},{7,6},{8,9},{9,8},{10,11... | collective-permute-start | bytes 1966088 | tf_op jit(solution)/shard_map/ppermute | solution.py:569
  144.2 10.2 %collective-permute-start.29 = (bf16[2,64,1280]{2,1,0:T(8,128)(2,1)S(1)}, bf16[2,64,1280]{2,1,0:T(8,128)(2,1)S(1)}, u32[]{:S(2)}, u32[]{:S(2)}) collective-permute-start(bf16[2,64,1280]{2,1,0:T(8,128)(2,1)S(1)} %added_half.4), channel_id=1, source_target_pairs={{0,2},{2,0},{1,3},{3,1},{4,6},{6,4},{5,7},{7,5},{8,10},{10,8},{9,1... | collective-permute-start | bytes 983048 | tf_op jit(solution)/shard_map/ppermute | solution.py:569
  147.0 10.7 %collective-permute-start.28 = (bf16[4,48,1280]{2,1,0:T(8,128)(2,1)S(1)}, bf16[4,48,1280]{2,1,0:T(8,128)(2,1)S(1)}, u32[]{:S(2)}, u32[]{:S(2)}) collective-permute-start(bf16[4,48,1280]{2,1,0:T(8,128)(2,1)S(1)} %get-tuple-element.82.refs_1_), channel_id=1, source_target_pairs={{6,4},{7,5},{8,10},{9,11},{22,20},{23,21},{24,26},{25,27}} | collective-permute-start | bytes 1474568 | tf_op jit(solution)/shard_map/ppermute | solution.py:548
  148.7 9.1 %collective-permute-start.32 = (bf16[2,64,1280]{2,1,0:T(8,128)(2,1)S(1)}, bf16[2,64,1280]{2,1,0:T(8,128)(2,1)S(1)}, u32[]{:S(2)}, u32[]{:S(2)}) collective-permute-start(bf16[2,64,1280]{2,1,0:T(8,128)(2,1)S(1)} %get-tuple-element.85), channel_id=1, source_target_pairs={{4,8},{5,9},{10,6},{11,7},{6,0},{7,1},{8,14},{9,15},{20,24},{21,25... | collective-permute-start | bytes 983048 | tf_op jit(solution)/shard_map/ppermute | solution.py:539
  149.4 9.1 %collective-permute-start.33 = (bf16[2,64,1280]{2,1,0:T(8,128)(2,1)S(1)}, bf16[2,64,1280]{2,1,0:T(8,128)(2,1)S(1)}, u32[]{:S(2)}, u32[]{:S(2)}) collective-permute-start(bf16[2,64,1280]{2,1,0:T(8,128)(2,1)S(1)} %get-tuple-element.86), channel_id=1, source_target_pairs={{6,8},{7,9},{8,6},{9,7},{4,0},{5,1},{10,14},{11,15},{22,24},{23,25... | collective-permute-start | bytes 983048 | tf_op jit(solution)/shard_map/ppermute | solution.py:539
  155.1 27.0 %collective-permute-start.35 = (bf16[2,64,1280]{2,1,0:T(8,128)(2,1)S(1)}, bf16[2,64,1280]{2,1,0:T(8,128)(2,1)}, u32[]{:S(2)}, u32[]{:S(2)}) collective-permute-start(bf16[2,64,1280]{2,1,0:T(8,128)(2,1)S(1)} %added_half.5), channel_id=1, source_target_pairs={{6,12},{7,13},{8,2},{9,3},{22,28},{23,29},{24,18},{25,19}} | collective-permute-start | bytes 983048 | tf_op jit(solution)/shard_map/ppermute | solution.py:539
  156.4 25.7 %collective-permute-start.34 = (bf16[2,64,1280]{2,1,0:T(8,128)(2,1)S(1)}, bf16[2,64,1280]{2,1,0:T(8,128)(2,1)}, u32[]{:S(2)}, u32[]{:S(2)}) collective-permute-start(bf16[2,64,1280]{2,1,0:T(8,128)(2,1)S(1)} %added_half.5), channel_id=1, source_target_pairs={{4,12},{5,13},{10,2},{11,3},{20,28},{21,29},{26,18},{27,19}} | collective-permute-start | bytes 983048 | tf_op jit(solution)/shard_map/ppermute | solution.py:539
  157.7 25.6 %collective-permute-start.31 = (bf16[4,64,1280]{2,1,0:T(8,128)(2,1)}, bf16[4,64,1280]{2,1,0:T(8,128)(2,1)S(1)}, u32[]{:S(2)}, u32[]{:S(2)}) collective-permute-start(bf16[4,64,1280]{2,1,0:T(8,128)(2,1)} %get-tuple-element.84.one_ref), channel_id=1, source_target_pairs={{0,1},{1,0},{2,3},{3,2},{4,5},{5,4},{6,7},{7,6},{8,9},{9,8},{10,11... | collective-permute-start | bytes 1966088 | tf_op jit(solution)/shard_map/ppermute | solution.py:569
  157.8 25.4 %collective-permute-start.30 = (bf16[4,16,1280]{2,1,0:T(8,128)(2,1)S(1)}, bf16[4,16,1280]{2,1,0:T(8,128)(2,1)S(1)}, u32[]{:S(2)}, u32[]{:S(2)}) collective-permute-start(bf16[4,16,1280]{2,1,0:T(8,128)(2,1)S(1)} %get-tuple-element.83.refs_2_), channel_id=1, source_target_pairs={{6,4},{7,5},{8,10},{9,11},{22,20},{23,21},{24,26},{25,27}} | collective-permute-start | bytes 491528 | tf_op jit(solution)/shard_map/ppermute | solution.py:548
